TPU v7x, 256 devices: a whole 4x4x8 slice. The times are simulated.
256 devices in a mesh: tile: 16 (over x_hi, z), map: 8 (over y, core), dp: 2 (over x_lo).
Axes of the slice: x: 4 (x_hi: 2, x_lo: 2; x = x_hi * 2 + x_lo), y: 4, z: 8, core: 2. Of those that a mesh axis runs over, the one named last changes fastest.
Arguments:
- frames: bfloat16 [3, 320, 128, 768], P(None, 'tile', None, 'dp'), may hold values from -6 to 6
- weights: bfloat16 [128, 972, 1024], P('tile', None, 'map'), may hold values from -0.1875 to 0.1875
- offsets: int32 [128, 2], P('tile'), may hold values from 0 to 110, as said below
Outputs:
- grad: float32 [128, 972, 1024], P('tile', 'dp', 'map')
- new_weights: bfloat16 [128, 972, 1024], P('tile', None, 'map')
Inputs may be any that keep to these rules, and one draw needn't show every extreme that they name: offsets[c, 0] lies in 0 to 19 and offsets[c, 1] in 0 to 110; in every tile some column has both at their largest and some has both at zero.
All inputs are finite; a program needn't handle non-finite values.
Results may differ from a plain program's by a relative error of at most 0.017.
Values may be sent and summed in bfloat16 or wider, within the bound.
No kernel may reach another device: no remote copies, remote signals or barrier semaphores. Data moves between devices by JAX's collectives and lax.ppermute only.
A program may use at most 128 MiB of HBM per device.

v0:
```python
import jax
import jax.numpy as jnp
from jax import lax
from jax.sharding import PartitionSpec as P

FIELD = 18
POOL = 5


smoothing = 1.0
sparsity = 3.0
learn_rate = 0.1


def from_behind(x, axis, by):
    count = lax.axis_size(axis)
    pairs = [(i, i + by) for i in range(count) if 0 <= i + by < count]
    return lax.ppermute(x, axis, pairs)


def from_behind_2(x, axis, by):
    count = lax.axis_size(axis)
    return lax.ppermute(x, axis, [(i, (i + by) % count) for i in range(count)])


def for_sending(x):
    return jax.tree.map(lambda a: a.astype(jnp.bfloat16) if a.dtype == jnp.float32 else a, x)


def window_total(extended, length):
    total = extended[:, :, 0:length]
    for shift_no in range(1, POOL):
        total = total + extended[:, :, shift_no : shift_no + length]
    return total


def per_device(frames, weights, offsets):
    channels, rows_here, pixels_wide, num_frames = frames.shape
    num_cols, inner, maps_here = weights.shape
    margin = POOL - 1
    upper = from_behind(frames[:, : FIELD - 1, :, :], "tile", -1)
    tall = jnp.concatenate([frames, upper], axis=1)
    zero = jnp.int32(0)

    def cut_patch(place):
        piece = lax.dynamic_slice(
            tall, (zero, place[0], place[1], zero), (channels, FIELD, FIELD, num_frames)
        )
        return piece.reshape(inner, num_frames)

    patches = jax.vmap(cut_patch)(offsets)
    responses = jnp.einsum("cif,cim->cfm", patches, weights, preferred_element_type=jnp.float32)
    responses_b = responses.astype(jnp.bfloat16)
    term = jnp.einsum(
        "cim,cfm->cif", weights, responses_b, preferred_element_type=jnp.float32
    ).astype(jnp.bfloat16)
    term = lax.optimization_barrier(term).astype(jnp.float32)
    rebuilt = lax.psum(term.astype(jnp.bfloat16), "map").astype(jnp.float32)
    error_b = (rebuilt - patches.astype(jnp.float32)).astype(jnp.bfloat16)
    back = jnp.einsum("cif,cim->cfm", error_b, weights, preferred_element_type=jnp.float32)
    squares = responses * responses
    next_head = from_behind_2(squares[:, :, :margin].astype(jnp.bfloat16), "map", -1).astype(
        jnp.float32
    )
    extended = jnp.concatenate([squares, next_head], axis=2)
    inverse = 1.0 / jnp.sqrt(smoothing + window_total(extended, maps_here))
    prior_tail = from_behind_2(for_sending(inverse[:, :, maps_here - margin :]), "map", 1)
    inverse_wide = jnp.concatenate([prior_tail, inverse], axis=2)
    spread = inverse_wide[:, :, margin : margin + maps_here]
    for shift_no in range(1, POOL):
        spread = spread + inverse_wide[:, :, margin - shift_no : margin - shift_no + maps_here]
    mixed = (back + sparsity * responses * spread).astype(jnp.bfloat16)
    total_frames = num_frames * lax.axis_size("dp")
    grad_part = (
        jnp.einsum("cif,cfm->cim", patches, mixed, preferred_element_type=jnp.float32)
        + jnp.einsum("cif,cfm->cim", error_b, responses_b, preferred_element_type=jnp.float32)
    ) * (1.0 / total_frames)
    half = inner // lax.axis_size("dp")
    grad_piece = lax.psum_scatter(
        grad_part.astype(jnp.bfloat16), "dp", scatter_dimension=1, tiled=True
    ).astype(jnp.float32)
    own = lax.dynamic_slice_in_dim(weights, lax.axis_index("dp") * half, half, 1)
    fresh_piece = (own.astype(jnp.float32) - learn_rate * grad_piece).astype(jnp.bfloat16)
    new_weights = lax.all_gather(fresh_piece, "dp", axis=1, tiled=True)
    return (grad_piece, new_weights)


def solution(mesh):
    placed = (P(None, "tile", None, "dp"), P("tile", None, "map"), P("tile", None))
    return jax.shard_map(
        per_device,
        mesh=mesh,
        in_specs=placed,
        out_specs=(P("tile", "dp", "map"), P("tile", None, "map")),
        check_vma=False,
    )
```

profile of v0, /device:TPU:4, one launch (start us, length us, event | category | flops | bytes accessed | tf_op | source)
XLA Modules:
  0.0 385.8 jit_solution(17459266435725603926)
XLA Ops:
  7.2 5.6 %slice.41 = bf16[3,17,128,384]{3,2,1,0:T(8,128)(2,1)} slice(bf16[3,20,128,384]{3,2,1,0:T(8,128)(2,1)} %param.3), slice={[0:3], [0:17], [0:128], [0:384]} | slice | bytes 10027008 | tf_op jit(solution)/shard_map/slice | solution.py:41
  12.8 7.7 %collective-permute-start = (bf16[3,17,128,384]{3,2,1,0:T(8,128)(2,1)}, bf16[3,17,128,384]{3,2,1,0:T(8,128)(2,1)}, u32[]{:S(2)}, u32[]{:S(2)}) collective-permute-start(bf16[3,17,128,384]{3,2,1,0:T(8,128)(2,1)} %slice.41), channel_id=1, source_target_pairs={{16,0},{32,16},{48,32},{64,48},{80,64},{96,80},{112,96},{128,112},... | collective-permute-start | bytes 15040520 | tf_op jit(solution)/shard_map/ppermute | solution.py:18
  20.5 107.6 %collective-permute-done = bf16[3,17,128,384]{3,2,1,0:T(8,128)(2,1)} collective-permute-done((bf16[3,17,128,384]{3,2,1,0:T(8,128)(2,1)}, bf16[3,17,128,384]{3,2,1,0:T(8,128)(2,1)}, u32[]{:S(2)}, u32[]{:S(2)}) %collective-permute-start) | collective-permute-done | bytes 5013536 | tf_op jit(solution)/shard_map/ppermute | solution.py:18
  128.2 9.7 %pad_maximum_fusion = bf16[3,37,128,384]{3,2,1,0:T(8,128)(2,1)} fusion(bf16[3,17,128,384]{3,2,1,0:T(8,128)(2,1)} %collective-permute-done, bf16[3,20,128,384]{3,2,1,0:T(8,128)(2,1)} %param.3), kind=kLoop, calls=%fused_computation.3 | loop fusion | flops 5455872 | bytes 21823488 | tf_op jit(solution)/shard_map/concatenate | solution.py:42
  137.9 36.3 %while.1 = (s32[]{:T(128)}, bf16[3,37,128,384]{3,2,1,0:T(8,128)(2,1)}, s32[8,4]{0,1:T(4,128)S(1)}, bf16[8,3,18,18,384]{4,3,2,1,0:T(8,128)(2,1)}, s32[]{:T(128)}) while((s32[]{:T(128)}, bf16[3,37,128,384]{3,2,1,0:T(8,128)(2,1)}, s32[8,4]{0,1:T(4,128)S(1)}, bf16[8,3,18,18,384]{4,3,2,1,0:T(8,128)(2,1)}, s32[]{:T(128)}) %tuple.28), condition=%wide.while_cond, body=%wide.while_body.sunk | while | flops 2 | bytes 1992305 | solution.py:46
  137.9 0.1 constant_dynamic-slice_fusion.2
  137.9 0.5 fusion.40
  138.5 3.9 %bitcast_dynamic-update-slice_fusion.2 = bf16[8,3,18,18,384]{4,3,2,1,0:T(8,128)(2,1)} fusion(bf16[8,3,18,18,384]{4,3,2,1,0:T(8,128)(2,1)} %get-tuple-element.67, s32[]{:T(128)} %get-tuple-element.64, bf16[3,37,128,384]{3,2,1,0:T(8,128)(2,1)} %get-tuple-element.70, s32[]{:T(128)} %bitcast.11, s32[]{:T(128)} %bitcast.12), kind=kLoop, calls=%fused_computation.clone.1 | loop fusion | bytes 1992192 | tf_op jit(solution)/shard_map/vmap()/gather
  142.4 0.1 constant_dynamic-slice_fusion.2
  142.5 0.5 fusion.40
  143.0 3.9 %bitcast_dynamic-update-slice_fusion.2 = bf16[8,3,18,18,384]{4,3,2,1,0:T(8,128)(2,1)} fusion(bf16[8,3,18,18,384]{4,3,2,1,0:T(8,128)(2,1)} %get-tuple-element.67, s32[]{:T(128)} %get-tuple-element.64, bf16[3,37,128,384]{3,2,1,0:T(8,128)(2,1)} %get-tuple-element.70, s32[]{:T(128)} %bitcast.11, s32[]{:T(128)} %bitcast.12), kind=kLoop, calls=%fused_computation.clone.1 | loop fusion | bytes 1992192 | tf_op jit(solution)/shard_map/vmap()/gather
  146.9 0.1 constant_dynamic-slice_fusion.2
  146.9 0.5 fusion.40
  147.5 4.0 %bitcast_dynamic-update-slice_fusion.2 = bf16[8,3,18,18,384]{4,3,2,1,0:T(8,128)(2,1)} fusion(bf16[8,3,18,18,384]{4,3,2,1,0:T(8,128)(2,1)} %get-tuple-element.67, s32[]{:T(128)} %get-tuple-element.64, bf16[3,37,128,384]{3,2,1,0:T(8,128)(2,1)} %get-tuple-element.70, s32[]{:T(128)} %bitcast.11, s32[]{:T(128)} %bitcast.12), kind=kLoop, calls=%fused_computation.clone.1 | loop fusion | bytes 1992192 | tf_op jit(solution)/shard_map/vmap()/gather
  151.4 0.1 constant_dynamic-slice_fusion.2
  151.5 0.5 fusion.40
  152.0 4.0 %bitcast_dynamic-update-slice_fusion.2 = bf16[8,3,18,18,384]{4,3,2,1,0:T(8,128)(2,1)} fusion(bf16[8,3,18,18,384]{4,3,2,1,0:T(8,128)(2,1)} %get-tuple-element.67, s32[]{:T(128)} %get-tuple-element.64, bf16[3,37,128,384]{3,2,1,0:T(8,128)(2,1)} %get-tuple-element.70, s32[]{:T(128)} %bitcast.11, s32[]{:T(128)} %bitcast.12), kind=kLoop, calls=%fused_computation.clone.1 | loop fusion | bytes 1992192 | tf_op jit(solution)/shard_map/vmap()/gather
  156.0 0.1 constant_dynamic-slice_fusion.2
  156.0 0.5 fusion.40
  156.6 4.0 %bitcast_dynamic-update-slice_fusion.2 = bf16[8,3,18,18,384]{4,3,2,1,0:T(8,128)(2,1)} fusion(bf16[8,3,18,18,384]{4,3,2,1,0:T(8,128)(2,1)} %get-tuple-element.67, s32[]{:T(128)} %get-tuple-element.64, bf16[3,37,128,384]{3,2,1,0:T(8,128)(2,1)} %get-tuple-element.70, s32[]{:T(128)} %bitcast.11, s32[]{:T(128)} %bitcast.12), kind=kLoop, calls=%fused_computation.clone.1 | loop fusion | bytes 1992192 | tf_op jit(solution)/shard_map/vmap()/gather
  160.6 0.1 constant_dynamic-slice_fusion.2
  160.6 0.5 fusion.40
  161.2 3.9 %bitcast_dynamic-update-slice_fusion.2 = bf16[8,3,18,18,384]{4,3,2,1,0:T(8,128)(2,1)} fusion(bf16[8,3,18,18,384]{4,3,2,1,0:T(8,128)(2,1)} %get-tuple-element.67, s32[]{:T(128)} %get-tuple-element.64, bf16[3,37,128,384]{3,2,1,0:T(8,128)(2,1)} %get-tuple-element.70, s32[]{:T(128)} %bitcast.11, s32[]{:T(128)} %bitcast.12), kind=kLoop, calls=%fused_computation.clone.1 | loop fusion | bytes 1992192 | tf_op jit(solution)/shard_map/vmap()/gather
  165.1 0.1 constant_dynamic-slice_fusion.2
  165.2 0.5 fusion.40
  165.7 4.0 %bitcast_dynamic-update-slice_fusion.2 = bf16[8,3,18,18,384]{4,3,2,1,0:T(8,128)(2,1)} fusion(bf16[8,3,18,18,384]{4,3,2,1,0:T(8,128)(2,1)} %get-tuple-element.67, s32[]{:T(128)} %get-tuple-element.64, bf16[3,37,128,384]{3,2,1,0:T(8,128)(2,1)} %get-tuple-element.70, s32[]{:T(128)} %bitcast.11, s32[]{:T(128)} %bitcast.12), kind=kLoop, calls=%fused_computation.clone.1 | loop fusion | bytes 1992192 | tf_op jit(solution)/shard_map/vmap()/gather
  169.7 0.1 constant_dynamic-slice_fusion.2
  169.7 0.5 fusion.40
  170.2 4.0 %bitcast_dynamic-update-slice_fusion.2 = bf16[8,3,18,18,384]{4,3,2,1,0:T(8,128)(2,1)} fusion(bf16[8,3,18,18,384]{4,3,2,1,0:T(8,128)(2,1)} %get-tuple-element.67, s32[]{:T(128)} %get-tuple-element.64, bf16[3,37,128,384]{3,2,1,0:T(8,128)(2,1)} %get-tuple-element.70, s32[]{:T(128)} %bitcast.11, s32[]{:T(128)} %bitcast.12), kind=kLoop, calls=%fused_computation.clone.1 | loop fusion | bytes 1992192 | tf_op jit(solution)/shard_map/vmap()/gather
  174.2 4.9 %copy.25 = bf16[8,3,18,18,384]{4,0,3,2,1:T(8,128)(2,1)S(1)} copy(bf16[8,3,18,18,384]{4,3,2,1,0:T(8,128)(2,1)} %get-tuple-element.9) | data formatting | bytes 11943936 | tf_op jit(solution)/shard_map/vmap()/gather | solution.py:46
  179.1 2.4 fusion.38
  181.5 0.3 copy-done
  181.8 4.3 %convert_bitcast_fusion = bf16[8,972,384]{2,1,0:T(8,128)(2,1)} fusion(bf16[8,972,128]{2,0,1:T(8,128)(2,1)S(1)} %copy-done.1, f32[8,384,128]{1,2,0:T(8,128)S(1)} %get-tuple-element.29), kind=kOutput, calls=%fused_computation.4 | convolution fusion | flops 767791104 | bytes 9535488 | tf_op jit(solution)/shard_map/cim,cfm->cif/dot_general | solution.py:54
  186.1 0.2 reduce-scatter.2.cloned.1.call-start
  186.3 1.6 collective-permute-start.1
  187.9 1.5 collective-permute-done.1
  189.5 0.8 fusion.19
  190.2 1.1 copy-done.3
  191.4 0.1 collective-permute-start.2
  191.5 4.4 %collective-permute-done.2 = bf16[8,384,4]{1,2,0:T(4,128)(2,1)S(1)} collective-permute-done((bf16[8,384,4]{1,2,0:T(4,128)(2,1)S(1)}, bf16[8,384,4]{1,2,0:T(4,128)(2,1)S(1)}, u32[]{:S(2)}, u32[]{:S(2)}) %collective-permute-start.2) | collective-permute-done | bytes 24608 | tf_op jit(solution)/shard_map/ppermute | solution.py:23
  195.9 77.7 %all-reduce.2.cloned.1.call-done = bf16[8,972,384]{2,1,0:T(8,128)(2,1)} async-done(((bf16[8,972,384]{2,1,0:T(8,128)(2,1)}), bf16[8,972,384]{2,1,0:T(8,128)(2,1)}) %all-reduce.2.cloned.1.call-update) | async-done | bytes 5971984 | tf_op jit(solution)/shard_map/psum | solution.py:58
  273.5 16.2 %fusion.2 = f32[8,972,128]{2,1,0:T(8,128)} fusion(bf16[8,972,384]{2,0,1:T(8,128)(2,1)} %bitcast.14, f32[8,384,4]{1,2,0:T(4,128)S(1)} %convert_element_type.50, f32[8,384,128]{1,2,0:T(8,128)} %copy-done.3, f32[8,384,128]{1,2,0:T(8,128)S(1)} %get-tuple-element.29, bf16[8,972,384]{2,1,0:T(8,128)(2,1)} %all-reduce.2.cloned.1.call-done, ...), kind=kOutput, calls=%fused_computation.7 | convolution fusion | flops 1545486336 | bytes 27107328 | tf_op jit(solution)/shard_map/cif,cfm->cim/dot_general | solution.py:75
  289.7 7.8 %multiply_convert_fusion = bf16[8,972,128]{2,1,0:T(8,128)(2,1)S(1)} fusion(f32[8,972,128]{2,1,0:T(8,128)} %fusion.2, bf16[8,972,384]{2,1,0:T(8,128)(2,1)} %all-reduce.2.cloned.1.call-done, bf16[8,972,384]{2,0,1:T(8,128)(2,1)} %bitcast.15, f32[8,384,128]{1,2,0:T(8,128)S(1)} %get-tuple-element.29), kind=kOutput, calls=%fused_computation.9 | convolution fusion | flops 779735040 | bytes 19488768 | tf_op jit(solution)/shard_map/cif,cfm->cim/dot_general | solution.py:76
  297.6 1.8 copy.36
  299.5 35.5 %reduce-scatter.2.cloned.1.call-done = bf16[8,486,128]{2,0,1:T(8,128)(2,1)} async-done(((bf16[8,972,128]{2,0,1:T(8,128)(2,1)}), bf16[8,486,128]{2,0,1:T(8,128)(2,1)}) %reduce-scatter.2.cloned.1.call-update) | async-done | bytes 995344 | tf_op jit(solution)/shard_map/reduce_scatter | solution.py:79
  335.0 3.1 subtract_convert_fusion.1
  338.1 38.1 %all-gather.2.cloned.1.call-done = bf16[8,972,128]{2,0,1:T(8,128)(2,1)} async-done(((bf16[8,486,128]{2,0,1:T(8,128)(2,1)}), bf16[8,972,128]{2,0,1:T(8,128)(2,1)}) %all-gather.2.cloned.1.call-update) | async-done | bytes 1990672 | tf_op jit(solution)/shard_map/all_gather | solution.py:84
  376.3 3.0 copy.75
  (21 shorter events, 0.2 us)
Async XLA Ops:
  7.2 13.3 %copy-start.4 = (s32[8,2]{0,1:T(2,128)S(1)}, s32[8,2]{0,1:T(2,128)}, u32[]{:S(2)}) copy-start(s32[8,2]{0,1:T(2,128)} %param.5) | copy-start | bytes 196
  7.2 266.4 %all-reduce.2.cloned.1.call-start = ((), (), s32[]{:S(2)}) async-start(), calls=%async_computation.1 | async-start | bytes 11993088 | tf_op jit(solution)/shard_map/psum | solution.py:58
  12.8 115.4 %collective-permute-start = (bf16[3,17,128,384]{3,2,1,0:T(8,128)(2,1)}, bf16[3,17,128,384]{3,2,1,0:T(8,128)(2,1)}, u32[]{:S(2)}, u32[]{:S(2)}) collective-permute-start(bf16[3,17,128,384]{3,2,1,0:T(8,128)(2,1)} %slice.41), channel_id=1, source_target_pairs={{16,0},{32,16},{48,32},{64,48},{80,64},{96,80},{112,96},{128,112},... | collective-permute-start | bytes 15040520 | tf_op jit(solution)/shard_map/ppermute | solution.py:18
  174.2 4.9 %copy-start.1 = (bf16[8,972,128]{2,0,1:T(8,128)(2,1)S(1)}, bf16[8,972,128]{2,0,1:T(8,128)(2,1)}, u32[]{:S(2)}) copy-start(bf16[8,972,128]{2,0,1:T(8,128)(2,1)} %param.4) | copy-start | bytes 5971972
  179.1 2.7 copy-start
  186.1 148.9 %reduce-scatter.2.cloned.1.call-start = ((), (), s32[]{:S(2)}) async-start(), calls=%async_computation.2 | async-start | bytes 2985984 | tf_op jit(solution)/shard_map/reduce_scatter | solution.py:79
  186.3 3.1 collective-permute-start.1
  190.2 1.1 copy-start.3
  191.4 4.5 %collective-permute-start.2 = (bf16[8,384,4]{1,2,0:T(4,128)(2,1)S(1)}, bf16[8,384,4]{1,2,0:T(4,128)(2,1)S(1)}, u32[]{:S(2)}, u32[]{:S(2)}) collective-permute-start(bf16[8,384,4]{1,2,0:T(4,128)(2,1)S(1)} %slice.159), channel_id=1, source_target_pairs={{0,2},{2,4},{4,6},{6,8},{8,10},{10,12},{12,14},{14,0},{1,3},{3,5},... | collective-permute-start | bytes 73736 | tf_op jit(solution)/shard_map/ppermute | solution.py:23
  299.4 35.6 %copy-start.2 = (bf16[8,972,128]{2,0,1:T(8,128)(2,1)S(1)}, bf16[8,972,128]{2,0,1:T(8,128)(2,1)}, u32[]{:S(2)}) copy-start(bf16[8,972,128]{2,0,1:T(8,128)(2,1)} %param.4) | copy-start | bytes 5971972
  299.4 76.9 %all-gather.2.cloned.1.call-start = ((), (), s32[]{:S(2)}) async-start(), calls=%async_computation.3 | async-start | bytes 2985984 | tf_op jit(solution)/shard_map/all_gather | solution.py:84
Sparse Core Ops, SparseCore 0:
  186.2 87.2 all-reduce.1
  299.5 35.4 reduce-scatter.1
  338.2 37.9 all-gather.1
where the time goes:
time: 388 us; the launch traced here: 386 us
  waiting for transfers between devices  265 us (68%)
  local copies, waits for them, and re-layouts  52.9 us (14%)
  matrix products  30.7 us (8%)
  between operations  13.9 us (4%)
  other arithmetic  13.6 us (4%)
  starting transfers between devices  9.7 us (2%)
    ppermute x1, waiting for transfers between devices, from_behind(): return lax.ppermute(x, axis, pairs)  108 us
    psum x1, waiting for transfers between devices, per_device(): rebuilt = lax.psum(term.astype(jnp.bfloat16), 'map').astype(jnp.float32)  77.7 us
    all_gather x1, waiting for transfers between devices, per_device(): new_weights = lax.all_gather(fresh_piece, 'dp', axis=1, tiled=True)  38.1 us
    gather x24, local copies, waits for them, and re-layouts  36.3 us
    reduce_scatter x1, waiting for transfers between devices, per_device(): lax.psum_scatter(grad_part.astype(jnp.bfloat16), 'dp', scatter_dimension=...  35.5 us
    dot_general x1, matrix products, per_device(): jnp.einsum('cif,cfm->cim', patches, mixed, preferred_element_type=jnp.flo...  16.2 us
    concatenate x1, other arithmetic, per_device(): tall = jnp.concatenate([frames, upper], axis=1)  9.7 us
    dot_general x1, matrix products, per_device(): jnp.einsum('cif,cfm->cim', error_b, responses_b, preferred_element_type=j...  7.85 us
  transfers between devices with their start and end apart: 6, of which 6 were waited for; matrix products, arithmetic and copies ran while one was open for 0% of the time, Pallas kernels for 0%

commit v1 on v0

v1 whole, which is shorter than its diff:
```python
import jax
import jax.numpy as jnp
from jax import lax
from jax.sharding import PartitionSpec as P

FIELD = 18
POOL = 5
CORES = 2

smoothing = 1.0
sparsity = 3.0
learn_rate = 0.1

AXES = ("tile", "map", "dp")


def table(mesh_shape, move):
    tiles, maps, dps = mesh_shape
    pairs = []
    for t in range(tiles):
        for y in range(maps // CORES):
            for k in range(CORES):
                for d in range(dps):
                    to = move(t, y, k, d)
                    if to is None:
                        continue
                    t2, y2, k2, d2 = to
                    if not 0 <= t2 < tiles:
                        continue
                    y2 = y2 % (maps // CORES)
                    source = (t * maps + y * CORES + k) * dps + d
                    target = (t2 * maps + y2 * CORES + k2) * dps + d2
                    pairs.append((source, target))
    return pairs


def cut(frames, place, above):
    channels, rows_here, wide, count = frames.shape
    zero = jnp.int32(0)
    strip = lax.dynamic_slice(
        frames, (zero, zero, place[1], zero), (channels, rows_here, FIELD, count)
    )
    if above:
        strip = jnp.pad(strip, ((0, 0), (0, FIELD - 1), (0, 0), (0, 0)))
    else:
        strip = jnp.pad(strip, ((0, 0), (rows_here, 0), (0, 0), (0, 0)))
    piece = lax.dynamic_slice(
        strip, (zero, place[0], zero, zero), (channels, FIELD, FIELD, count)
    )
    return piece.reshape(channels * FIELD * FIELD, count)


def ring_sum(x, step):
    total = x
    for shift in range(1, POOL):
        total = total + jnp.roll(x, step * shift, axis=1)
    return total


def column_step(patch, weight, total_frames):
    responses = jnp.einsum("if,im->fm", patch, weight, preferred_element_type=jnp.float32)
    responses_b = responses.astype(jnp.bfloat16)
    rebuilt = jnp.einsum("im,fm->if", weight, responses_b, preferred_element_type=jnp.float32)
    error_b = (rebuilt - patch.astype(jnp.float32)).astype(jnp.bfloat16)
    back = jnp.einsum("if,im->fm", error_b, weight, preferred_element_type=jnp.float32)
    inverse = 1.0 / jnp.sqrt(smoothing + ring_sum(responses * responses, -1))
    spread = ring_sum(inverse, 1)
    mixed = (back + sparsity * responses * spread).astype(jnp.bfloat16)
    return (
        jnp.einsum("if,fm->im", patch, mixed, preferred_element_type=jnp.float32)
        + jnp.einsum("if,fm->im", error_b, responses_b, preferred_element_type=jnp.float32)
    ) * (1.0 / total_frames)


def per_device(mesh_shape, frames, weights, offsets):
    num_cols, inner, maps_here = weights.shape
    rows_y = mesh_shape[1] // CORES
    group = lax.axis_index("map")
    y, k, d = group // CORES, group % CORES, lax.axis_index("dp")

    def send(x, move):
        return lax.ppermute(x, AXES, table(mesh_shape, move))

    upper_offsets = send(offsets, lambda t, y, k, d: (t + 1, y, k, d))
    lent = CORES * y + k
    below = cut(frames, upper_offsets[lent], False)
    above = cut(frames, offsets[lent], True)
    below = send(below, lambda t, y, k, d: (t - 1, y, d, k))
    above_in = send(above, lambda t, y, k, d: (t, y, d, k) if k != d else None)
    patch = jnp.where(k == d, above, above_in) + below

    own = []
    for s in range(rows_y):
        target = (y - s) % rows_y
        block = lax.dynamic_index_in_dim(weights, CORES * target + d, 0, keepdims=False)
        if s:
            block = send(block, lambda t, y, k, d: (t, y - s, k, d))
        own.append(block)
    own = jnp.stack(own, 1)
    other = send(own, lambda t, y, k, d: (t, y, 1 - k, d))
    low, high = jnp.where(k == 0, own, other), jnp.where(k == 0, other, own)
    weight = jnp.stack([low, high], 2).reshape(inner, -1)

    grad = column_step(patch, weight, frames.shape[3] * CORES)

    grad = grad.reshape(inner, rows_y, CORES, maps_here)
    low, high = grad[:, :, 0], grad[:, :, 1]
    away = jnp.where(k == 0, high, low).astype(jnp.bfloat16)
    home = jnp.where(k == 0, low, high)
    both = home + send(away, lambda t, y, k, d: (t, y, 1 - k, d)).astype(jnp.float32)
    both = both.astype(jnp.bfloat16)
    arrived = []
    for s in range(rows_y):
        block = both[:, s]
        if s:
            block = send(block, lambda t, y, k, d: (t, y + s, k, d))
        arrived.append(block)
    arrived = jnp.stack(arrived)
    crossed = send(arrived, lambda t, y, k, d: (t, y, k, 1 - d))
    order = (y - jnp.arange(rows_y)) % rows_y
    arrived, crossed = arrived[order], crossed[order]
    low, high = jnp.where(d == 0, arrived, crossed), jnp.where(d == 0, crossed, arrived)
    full = jnp.stack([low, high], 1).reshape(num_cols, inner, maps_here).astype(jnp.float32)
    half = inner // mesh_shape[2]
    new_weights = (weights.astype(jnp.float32) - learn_rate * full).astype(jnp.bfloat16)
    return lax.dynamic_slice_in_dim(full, d * half, half, 1), new_weights


def solution(mesh):
    mesh_shape = tuple(mesh.shape[a] for a in AXES)
    placed = (P(None, "tile", None, "dp"), P("tile", None, "map"), P("tile", None))

    def run(frames, weights, offsets):
        return per_device(mesh_shape, frames, weights, offsets)

    return jax.shard_map(
        run,
        mesh=mesh,
        in_specs=placed,
        out_specs=(P("tile", "dp", "map"), P("tile", None, "map")),
        check_vma=False,
    )
```

time: 388 us -> 145 us (0.37)
  waiting for transfers between devices: 265 us -> 48.5 us
  matrix products: 30.7 us -> 15.7 us
  starting transfers between devices: 9.7 us -> 23.8 us
  local copies, waits for them, and re-layouts: 52.9 us -> 39.5 us
  other arithmetic: 13.6 us -> 7.54 us
  between operations: 13.9 us -> 8.79 us
    psum x1 -> x0, waiting for transfers between devices: 77.7 us -> none  [per_device(): rebuilt = lax.psum(term.astype(jnp.bfloat16), 'map').astype(jnp.float32)]
    ppermute x3 -> x12, waiting for transfers between devices: 113 us -> 48.5 us  [send(): return lax.ppermute(x, AXES, table(mesh_shape, move))]
    gather x25 -> x2, local copies, waits for them, and re-layouts: 41.2 us -> 1.48 us  [per_device(): arrived, crossed = (arrived[order], crossed[order])]
    all_gather x1 -> x0, waiting for transfers between devices: 38.1 us -> none  [per_device(): new_weights = lax.all_gather(fresh_piece, 'dp', axis=1, tiled=True)]
    reduce_scatter x1 -> x0, waiting for transfers between devices: 35.5 us -> none  [per_device(): lax.psum_scatter(grad_part.astype(jnp.bfloat16), 'dp', scatter_dimension=...]
    dot_general x4, matrix products: 30.7 us -> 15.7 us  [the longest x1 8.65 us: column_step(): jnp.einsum('if,fm->im', patch, mixed, preferred_element_type=jnp.float32)]
    ppermute x3 -> x12, starting transfers between devices: 9.4 us -> 23.8 us  [send(): return lax.ppermute(x, AXES, table(mesh_shape, move))]
    concatenate x2 -> x0, other arithmetic: 9.71 us -> none  [the longest x1 9.7 us: per_device(): tall = jnp.concatenate([frames, upper], axis=1)]
  transfers between devices with their start and end apart: 6 -> 12, of which waited for: 6 -> 5; matrix products, arithmetic and copies ran while one was open for 0% -> 9% of each run, Pallas kernels for 0% -> 0%
where the time goes in v1:
time: 145 us; the launch traced here: 144 us
  waiting for transfers between devices  48.5 us (33%)
  local copies, waits for them, and re-layouts  39.5 us (27%)
  starting transfers between devices  23.8 us (16%)
  matrix products  15.7 us (11%)
  between operations  8.79 us (6%)
  other arithmetic  7.54 us (5%)
    ppermute x12, waiting for transfers between devices, send(): return lax.ppermute(x, AXES, table(mesh_shape, move))  48.5 us
    ppermute x12, starting transfers between devices, send(): return lax.ppermute(x, AXES, table(mesh_shape, move))  23.8 us
    dot_general x1, matrix products, column_step(): jnp.einsum('if,fm->im', patch, mixed, preferred_element_type=jnp.float32)  8.65 us
    slice x1, local copies, waits for them, and re-layouts, per_device(): low, high = (grad[:, :, 0], grad[:, :, 1])  6.75 us
    unnamed x15, local copies, waits for them, and re-layouts  6.56 us
    reshape x1, local copies, waits for them, and re-layouts, per_device(): grad = grad.reshape(inner, rows_y, CORES, maps_here)  6.33 us
    another operation x1, local copies, waits for them, and re-layouts, per_device(): weight = jnp.stack([low, high], 2).reshape(inner, -1)  3.91 us
    slice x12, local copies, waits for them, and re-layouts, ring_sum(): total = total + jnp.roll(x, step * shift, axis=1)  3.84 us
  transfers between devices with their start and end apart: 12, of which 5 were waited for; matrix products, arithmetic and copies ran while one was open for 9% of the time, Pallas kernels for 0%

profile of v1, /device:TPU:4, one launch (start us, length us, event | category | flops | bytes accessed | tf_op | source)
XLA Modules:
  0.0 143.9 jit_solution(13826943765262624861)
XLA Ops:
  0.6 3.8 %collective-permute-start.1 = (s32[8,2]{0,1:T(2,128)}, s32[8,2]{0,1:T(2,128)S(1)}, u32[]{:S(2)}, u32[]{:S(2)}) collective-permute-start(s32[8,2]{0,1:T(2,128)} %param.5), channel_id=1, source_target_pairs={{0,16},{1,17},{2,18},{3,19},{4,20},{5,21},{6,22},{7,23},{8,24},{9,... | collective-permute-start | bytes 200 | tf_op jit(solution)/shard_map/ppermute | solution.py:82
  4.6 1.8 %copy.48 = bf16[8,972,128]{2,1,0:T(8,128)(2,1)S(1)} copy(bf16[8,972,128]{2,0,1:T(8,128)(2,1)} %param.4) | data formatting | bytes 3981312 | tf_op args[1]
  6.4 0.9 dynamic-slice_bitcast_fusion.3
  7.3 1.6 %collective-permute-start.5 = (bf16[972,128]{1,0:T(8,128)(2,1)}, bf16[972,128]{1,0:T(8,128)(2,1)S(1)}, u32[]{:S(2)}, u32[]{:S(2)}) collective-permute-start(bf16[972,128]{1,0:T(8,128)(2,1)} %get-tuple-element.15), channel_id=1, source_target_pairs={{0,4},{1,5},{2,6},{3,7},{4,8},{5,9},{6,10},{7,11},{8,12},{9,13},{1... | collective-permute-start | bytes 746504 | tf_op jit(solution)/shard_map/ppermute | solution.py:82
  8.9 1.7 %collective-permute-start.3 = (bf16[972,128]{1,0:T(8,128)(2,1)}, bf16[972,128]{1,0:T(8,128)(2,1)S(1)}, u32[]{:S(2)}, u32[]{:S(2)}) collective-permute-start(bf16[972,128]{1,0:T(8,128)(2,1)} %get-tuple-element.17), channel_id=1, source_target_pairs={{0,12},{1,13},{2,14},{3,15},{4,0},{5,1},{6,2},{7,3},{8,4},{9,5},{1... | collective-permute-start | bytes 746504 | tf_op jit(solution)/shard_map/ppermute | solution.py:82
  10.5 2.0 %collective-permute-start.4 = (bf16[972,128]{1,0:T(8,128)(2,1)}, bf16[972,128]{1,0:T(8,128)(2,1)S(1)}, u32[]{:S(2)}, u32[]{:S(2)}) collective-permute-start(bf16[972,128]{1,0:T(8,128)(2,1)} %get-tuple-element.16), channel_id=1, source_target_pairs={{0,8},{1,9},{2,10},{3,11},{4,12},{5,13},{6,14},{7,15},{8,0},{9,1},... | collective-permute-start | bytes 746504 | tf_op jit(solution)/shard_map/ppermute | solution.py:82
  12.6 0.5 fusion.23
  17.1 0.5 fusion.24
  21.5 3.1 %constant_dynamic-slice_fusion.3 = (bf16[3,20,18,384]{3,2,1,0:T(8,128)(2,1)S(1)}, bf16[3,20,18,384]{3,2,1,0:T(8,128)(2,1)S(1)}) fusion(bf16[3,20,128,384]{3,2,1,0:T(8,128)(2,1)} %param.3, s32[]{:T(128)S(6)} %select_n.157, s32[]{:T(128)S(6)} %select_n.160), kind=kLoop, calls=%fused_computation.51 | loop fusion | bytes 3317768 | tf_op jit(solution)/shard_map/dynamic_slice | solution.py:40
  24.8 1.1 reshape.109
  25.9 5.8 %collective-permute-start.2 = (bf16[972,384]{1,0:T(8,128)(2,1)}, bf16[972,384]{1,0:T(8,128)(2,1)}, u32[]{:S(2)}, u32[]{:S(2)}) collective-permute-start(bf16[972,384]{1,0:T(8,128)(2,1)} %reshape.109), channel_id=1, source_target_pairs={{16,0},{17,2},{18,1},{19,3},{20,4},{21,6},{22,5},{23,7},{24,8},{25... | collective-permute-start | bytes 2239496 | tf_op jit(solution)/shard_map/ppermute | solution.py:82
  32.2 0.7 collective-permute-start
  33.1 1.3 copy.52
  34.4 1.4 collective-permute-start.6
  35.8 12.9 %collective-permute-done.2 = bf16[972,384]{1,0:T(8,128)(2,1)} collective-permute-done((bf16[972,384]{1,0:T(8,128)(2,1)}, bf16[972,384]{1,0:T(8,128)(2,1)}, u32[]{:S(2)}, u32[]{:S(2)}) %collective-permute-start.2) | collective-permute-done | bytes 746528 | tf_op jit(solution)/shard_map/ppermute | solution.py:82
  48.6 1.3 select_add_fusion
  49.9 1.8 %select_bitcast_fusion.3 = (bf16[972,4,1,128]{3,0,1,2:T(8,128)(2,1)S(1)}, bf16[972,4,1,128]{3,0,1,2:T(8,128)(2,1)S(1)}) fusion(pred[]{:T(512)S(6)} %eq.22, bf16[972,4,128]{2,1,0:T(4,128)(2,1)} %collective-permute-done.6, bf16[972,1,128]{2,0,1:T(8,128)(2,1)S(1)} %bitcast.63, bf16[972,1,128]{2,0,1:T(8,128)(2,1)S(1)} %bitcast.67, ...), kind=kLoop, calls=%fused_computation.32 | loop fusion | flops 2488320 | bytes 3981313 | tf_op jit(solution)/shard_map/stack | solution.py:102
  51.7 1.5 %pad_maximum_fusion = bf16[972,4,2,128]{3,0,1,2:T(8,128)(2,1)} fusion(bf16[972,4,1,128]{3,0,1,2:T(8,128)(2,1)S(1)} %get-tuple-element.19, bf16[972,4,1,128]{3,0,1,2:T(8,128)(2,1)S(1)} %get-tuple-element.18), kind=kLoop, calls=%fused_computation.6 | loop fusion | flops 995328 | bytes 3981312 | tf_op jit(solution)/shard_map/stack | solution.py:102
  53.2 3.9 %copy.55 = bf16[972,4,2,128]{0,3,2,1:T(8,128)(2,1)} copy(bf16[972,4,2,128]{3,0,1,2:T(8,128)(2,1)} %pad_maximum_fusion) | data formatting | bytes 3981312 | tf_op jit(solution)/shard_map/stack | solution.py:102
  57.1 2.6 %fusion.25 = (f32[384,1024]{1,0:T(8,128)S(1)}, f32[384,1024]{1,0:T(8,128)S(1)}) fusion(bf16[972,384]{1,0:T(8,128)(2,1)S(1)} %select_add_fusion, bf16[972,1024]{0,1:T(8,128)(2,1)} %bitcast.59), kind=kOutput, calls=%fused_computation.63 | convolution fusion | flops 764805120 | bytes 5882880 | tf_op jit(solution)/shard_map/if,im->fm/dot_general | solution.py:61
  59.7 0.5 slice.128
  60.2 0.5 slice.130
  60.6 0.5 slice.132
  61.1 0.5 slice.134
  61.7 1.0 fusion.5
  63.0 0.8 slice.140
  63.8 0.8 slice.142
  64.6 1.3 fusion.16
  66.0 3.1 %fusion.12 = f32[972,1024]{1,0:T(8,128)} fusion(f32[972,384]{1,0:T(8,128)S(1)} %fusion.16, bf16[972,384]{1,0:T(8,128)(2,1)S(1)} %copy-done.2, f32[384,1024]{1,0:T(8,128)S(1)} %get-tuple-element.29), kind=kOutput, calls=%fused_computation.25 | convolution fusion | flops 765924864 | bytes 7793664 | tf_op jit(solution)/shard_map/if,fm->im/dot_general | solution.py:71
  69.1 8.6 %add_multiply_fusion = f32[972,1024]{1,0:T(8,128)} fusion(f32[972,1024]{1,0:T(8,128)} %fusion.12, bf16[972,384]{1,0:T(8,128)(2,1)} %copy-done.1, f32[384,1024]{1,0:T(8,128)S(1)} %fusion.5, f32[384,1023]{1,0:T(8,128)S(1)} %bitcast.54, f32[384,1]{1,0:T(8,128)S(1)} %slice.136, f32[384,1022]{1,0:T(8,128)S(1)} %bitcast.55, f32[384,2]{1,0:T(8,128)S(1)} %slice.138, ...), kind=kOutput, calls=%fused_computation.3 | convolution fusion | flops 1536652800 | bytes 21629952 | tf_op jit(solution)/shard_map/if,fm->im/dot_general | solution.py:70
  77.8 6.3 %reshape.111 = f32[972,4,2,128]{3,2,1,0:T(2,128)} reshape(f32[972,1024]{1,0:T(8,128)} %add_multiply_fusion) | data formatting | bytes 7962624 | tf_op jit(solution)/shard_map/reshape | solution.py:106
  84.1 6.8 %fusion.22 = (f32[972,4,1,128]{3,2,1,0:T(1,128)S(1)}, f32[972,4,1,128]{3,2,1,0:T(1,128)S(1)}) fusion(f32[972,4,2,128]{3,2,1,0:T(2,128)} %reshape.111), kind=kLoop, calls=%fused_computation.60 | loop fusion | bytes 7962624 | tf_op jit(solution)/shard_map/slice | solution.py:107
  91.7 2.1 %collective-permute-start.7 = (bf16[972,4,128]{2,1,0:T(4,128)(2,1)S(1)}, bf16[972,4,128]{2,1,0:T(4,128)(2,1)S(1)}, u32[]{:S(2)}, u32[]{:S(2)}) collective-permute-start(bf16[972,4,128]{2,1,0:T(4,128)(2,1)S(1)} %copy.58), channel_id=1, source_target_pairs={{0,2},{1,3},{2,0},{3,1},{4,6},{5,7},{6,4},{7,5},{8,10},{9,11},{10,... | collective-permute-start | bytes 2985992 | tf_op jit(solution)/shard_map/ppermute | solution.py:82
  93.8 2.2 %collective-permute-done.7 = bf16[972,4,128]{2,1,0:T(4,128)(2,1)S(1)} collective-permute-done((bf16[972,4,128]{2,1,0:T(4,128)(2,1)S(1)}, bf16[972,4,128]{2,1,0:T(4,128)(2,1)S(1)}, u32[]{:S(2)}, u32[]{:S(2)}) %collective-permute-start.7) | collective-permute-done | bytes 995360 | tf_op jit(solution)/shard_map/ppermute | solution.py:82
  96.4 0.8 collective-permute-start.8
  97.2 1.9 %collective-permute-start.9 = (bf16[972,128]{1,0:T(8,128)(2,1)S(1)}, bf16[972,128]{1,0:T(8,128)(2,1)S(1)}, u32[]{:S(2)}, u32[]{:S(2)}) collective-permute-start(bf16[972,128]{1,0:T(8,128)(2,1)S(1)} %get-tuple-element.22), channel_id=1, source_target_pairs={{0,8},{1,9},{2,10},{3,11},{4,12},{5,13},{6,14},{7,15},{8,0},{9,1},... | collective-permute-start | bytes 746504 | tf_op jit(solution)/shard_map/ppermute | solution.py:82
  99.1 1.5 %collective-permute-start.10 = (bf16[972,128]{1,0:T(8,128)(2,1)S(1)}, bf16[972,128]{1,0:T(8,128)(2,1)S(1)}, u32[]{:S(2)}, u32[]{:S(2)}) collective-permute-start(bf16[972,128]{1,0:T(8,128)(2,1)S(1)} %get-tuple-element.21), channel_id=1, source_target_pairs={{0,12},{1,13},{2,14},{3,15},{4,0},{5,1},{6,2},{7,3},{8,4},{9,5},{1... | collective-permute-start | bytes 746504 | tf_op jit(solution)/shard_map/ppermute | solution.py:82
  100.6 10.8 %collective-permute-done.8 = bf16[972,128]{1,0:T(8,128)(2,1)S(1)} collective-permute-done((bf16[972,128]{1,0:T(8,128)(2,1)S(1)}, bf16[972,128]{1,0:T(8,128)(2,1)S(1)}, u32[]{:S(2)}, u32[]{:S(2)}) %collective-permute-start.8) | collective-permute-done | bytes 248864 | tf_op jit(solution)/shard_map/ppermute | solution.py:82
  111.4 0.6 collective-permute-done.10
  112.1 1.3 copy.60
  113.5 0.6 collective-permute-start.11
  114.1 0.7 gather_fusion
  114.9 22.0 %collective-permute-done.11 = bf16[4,972,128]{2,0,1:T(4,128)(2,1)S(1)} collective-permute-done((bf16[4,972,128]{2,0,1:T(4,128)(2,1)}, bf16[4,972,128]{2,0,1:T(4,128)(2,1)S(1)}, u32[]{:S(2)}, u32[]{:S(2)}) %collective-permute-start.11) | collective-permute-done | bytes 995360 | tf_op jit(solution)/shard_map/ppermute | solution.py:82
  137.0 0.7 gather_fusion.1
  138.4 1.3 copy-done.3
  139.7 0.5 subtract_convert_fusion
  140.4 1.6 %copy.64 = f32[8,486,128]{2,0,1:T(8,128)} copy(f32[8,486,128]{2,1,0:T(8,128)S(1)} %constant_dynamic-slice_fusion) | data formatting | bytes 3981312
  142.1 1.8 %copy.65 = bf16[8,972,128]{2,0,1:T(8,128)(2,1)} copy(bf16[8,972,128]{2,1,0:T(8,128)(2,1)S(1)} %subtract_convert_fusion) | data formatting | bytes 3981312
  (42 shorter events, 3.7 us)
Async XLA Ops:
  0.6 16.4 %collective-permute-start.1 = (s32[8,2]{0,1:T(2,128)}, s32[8,2]{0,1:T(2,128)S(1)}, u32[]{:S(2)}, u32[]{:S(2)}) collective-permute-start(s32[8,2]{0,1:T(2,128)} %param.5), channel_id=1, source_target_pairs={{0,16},{1,17},{2,18},{3,19},{4,20},{5,21},{6,22},{7,23},{8,24},{9,... | collective-permute-start | bytes 200 | tf_op jit(solution)/shard_map/ppermute | solution.py:82
  6.4 6.1 %copy-start.5 = (s32[8,2]{0,1:T(2,128)S(1)}, s32[8,2]{0,1:T(2,128)}, u32[]{:S(2)}) copy-start(s32[8,2]{0,1:T(2,128)} %param.5) | copy-start | bytes 196
  7.3 25.6 %collective-permute-start.5 = (bf16[972,128]{1,0:T(8,128)(2,1)}, bf16[972,128]{1,0:T(8,128)(2,1)S(1)}, u32[]{:S(2)}, u32[]{:S(2)}) collective-permute-start(bf16[972,128]{1,0:T(8,128)(2,1)} %get-tuple-element.15), channel_id=1, source_target_pairs={{0,4},{1,5},{2,6},{3,7},{4,8},{5,9},{6,10},{7,11},{8,12},{9,13},{1... | collective-permute-start | bytes 746504 | tf_op jit(solution)/shard_map/ppermute | solution.py:82
  8.9 24.0 %collective-permute-start.3 = (bf16[972,128]{1,0:T(8,128)(2,1)}, bf16[972,128]{1,0:T(8,128)(2,1)S(1)}, u32[]{:S(2)}, u32[]{:S(2)}) collective-permute-start(bf16[972,128]{1,0:T(8,128)(2,1)} %get-tuple-element.17), channel_id=1, source_target_pairs={{0,12},{1,13},{2,14},{3,15},{4,0},{5,1},{6,2},{7,3},{8,4},{9,5},{1... | collective-permute-start | bytes 746504 | tf_op jit(solution)/shard_map/ppermute | solution.py:82
  10.5 22.4 %collective-permute-start.4 = (bf16[972,128]{1,0:T(8,128)(2,1)}, bf16[972,128]{1,0:T(8,128)(2,1)S(1)}, u32[]{:S(2)}, u32[]{:S(2)}) collective-permute-start(bf16[972,128]{1,0:T(8,128)(2,1)} %get-tuple-element.16), channel_id=1, source_target_pairs={{0,8},{1,9},{2,10},{3,11},{4,12},{5,13},{6,14},{7,15},{8,0},{9,1},... | collective-permute-start | bytes 746504 | tf_op jit(solution)/shard_map/ppermute | solution.py:82
  25.9 22.7 %collective-permute-start.2 = (bf16[972,384]{1,0:T(8,128)(2,1)}, bf16[972,384]{1,0:T(8,128)(2,1)}, u32[]{:S(2)}, u32[]{:S(2)}) collective-permute-start(bf16[972,384]{1,0:T(8,128)(2,1)} %reshape.109), channel_id=1, source_target_pairs={{16,0},{17,2},{18,1},{19,3},{20,4},{21,6},{22,5},{23,7},{24,8},{25... | collective-permute-start | bytes 2239496 | tf_op jit(solution)/shard_map/ppermute | solution.py:82
  32.2 16.4 %collective-permute-start = (bf16[972,384]{1,0:T(8,128)(2,1)S(1)}, bf16[972,384]{1,0:T(8,128)(2,1)S(1)}, u32[]{:S(2)}, u32[]{:S(2)}) collective-permute-start(bf16[972,384]{1,0:T(8,128)(2,1)S(1)} %reshape.108), channel_id=1, source_target_pairs={{1,2},{2,1},{5,6},{6,5},{9,10},{10,9},{13,14},{14,13},{17,18},{18,... | collective-permute-start | bytes 2239496 | tf_op jit(solution)/shard_map/ppermute | solution.py:82
  34.4 15.5 %collective-permute-start.6 = (bf16[972,4,128]{2,1,0:T(4,128)(2,1)}, bf16[972,4,128]{2,1,0:T(4,128)(2,1)}, u32[]{:S(2)}, u32[]{:S(2)}) collective-permute-start(bf16[972,4,128]{2,1,0:T(4,128)(2,1)} %copy.52), channel_id=1, source_target_pairs={{0,2},{1,3},{2,0},{3,1},{4,6},{5,7},{6,4},{7,5},{8,10},{9,11},{10,... | collective-permute-start | bytes 2985992 | tf_op jit(solution)/shard_map/ppermute | solution.py:82
  49.9 7.2 %copy-start.1 = (bf16[972,384]{1,0:T(8,128)(2,1)}, bf16[972,384]{1,0:T(8,128)(2,1)S(1)}, u32[]{:S(2)}) copy-start(bf16[972,384]{1,0:T(8,128)(2,1)S(1)} %select_add_fusion) | copy-start | bytes 2239492
  61.7 2.9 %copy-start = (bf16[972,4,2,128]{0,3,2,1:T(8,128)(2,1)S(1)}, bf16[972,4,2,128]{0,3,2,1:T(8,128)(2,1)}, u32[]{:S(2)}) copy-start(bf16[972,4,2,128]{0,3,2,1:T(8,128)(2,1)} %copy.55) | copy-start | bytes 5971972
  64.6 1.3 copy-start.2
  66.0 3.1 %copy-start.4 = (f32[972,384]{1,0:T(8,128)}, f32[972,384]{1,0:T(8,128)S(1)}, u32[]{:S(2)}) copy-start(f32[972,384]{1,0:T(8,128)S(1)} %fusion.16) | copy-start | bytes 4478980
  91.7 4.3 %collective-permute-start.7 = (bf16[972,4,128]{2,1,0:T(4,128)(2,1)S(1)}, bf16[972,4,128]{2,1,0:T(4,128)(2,1)S(1)}, u32[]{:S(2)}, u32[]{:S(2)}) collective-permute-start(bf16[972,4,128]{2,1,0:T(4,128)(2,1)S(1)} %copy.58), channel_id=1, source_target_pairs={{0,2},{1,3},{2,0},{3,1},{4,6},{5,7},{6,4},{7,5},{8,10},{9,11},{10,... | collective-permute-start | bytes 2985992 | tf_op jit(solution)/shard_map/ppermute | solution.py:82
  96.4 15.0 %collective-permute-start.8 = (bf16[972,128]{1,0:T(8,128)(2,1)S(1)}, bf16[972,128]{1,0:T(8,128)(2,1)S(1)}, u32[]{:S(2)}, u32[]{:S(2)}) collective-permute-start(bf16[972,128]{1,0:T(8,128)(2,1)S(1)} %get-tuple-element.23), channel_id=1, source_target_pairs={{0,4},{1,5},{2,6},{3,7},{4,8},{5,9},{6,10},{7,11},{8,12},{9,13},{1... | collective-permute-start | bytes 746504 | tf_op jit(solution)/shard_map/ppermute | solution.py:82
  97.2 14.2 %collective-permute-start.9 = (bf16[972,128]{1,0:T(8,128)(2,1)S(1)}, bf16[972,128]{1,0:T(8,128)(2,1)S(1)}, u32[]{:S(2)}, u32[]{:S(2)}) collective-permute-start(bf16[972,128]{1,0:T(8,128)(2,1)S(1)} %get-tuple-element.22), channel_id=1, source_target_pairs={{0,8},{1,9},{2,10},{3,11},{4,12},{5,13},{6,14},{7,15},{8,0},{9,1},... | collective-permute-start | bytes 746504 | tf_op jit(solution)/shard_map/ppermute | solution.py:82
  99.1 13.0 %collective-permute-start.10 = (bf16[972,128]{1,0:T(8,128)(2,1)S(1)}, bf16[972,128]{1,0:T(8,128)(2,1)S(1)}, u32[]{:S(2)}, u32[]{:S(2)}) collective-permute-start(bf16[972,128]{1,0:T(8,128)(2,1)S(1)} %get-tuple-element.21), channel_id=1, source_target_pairs={{0,12},{1,13},{2,14},{3,15},{4,0},{5,1},{6,2},{7,3},{8,4},{9,5},{1... | collective-permute-start | bytes 746504 | tf_op jit(solution)/shard_map/ppermute | solution.py:82
  113.5 23.4 %collective-permute-start.11 = (bf16[4,972,128]{2,0,1:T(4,128)(2,1)}, bf16[4,972,128]{2,0,1:T(4,128)(2,1)S(1)}, u32[]{:S(2)}, u32[]{:S(2)}) collective-permute-start(bf16[4,972,128]{2,0,1:T(4,128)(2,1)} %copy.60), channel_id=1, source_target_pairs={{0,1},{1,0},{2,3},{3,2},{4,5},{5,4},{6,7},{7,6},{8,9},{9,8},{10,11... | collective-permute-start | bytes 2985992 | tf_op jit(solution)/shard_map/ppermute | solution.py:82
  138.1 1.6 %copy-start.3 = (bf16[8,972,128]{2,0,1:T(8,128)(2,1)S(1)}, bf16[8,972,128]{2,0,1:T(8,128)(2,1)}, u32[]{:S(2)}) copy-start(bf16[8,972,128]{2,0,1:T(8,128)(2,1)} %param.4) | copy-start | bytes 5971972

commit v2 on v1

v2 whole, which is shorter than its diff:
```python
import functools

import jax
import jax.numpy as jnp
from jax import lax
from jax.experimental import pallas as pl
from jax.experimental.pallas import tpu as pltpu
from jax.sharding import PartitionSpec as P

FIELD = 18
POOL = 5
CORES = 2
STRIP = 48
SUB = 8
LANES = 128
MIB = 1 << 20

smoothing = 1.0
sparsity = 3.0
learn_rate = 0.1

AXES = ("tile", "map", "dp")
F32, BF16 = jnp.float32, jnp.bfloat16
VMEM = pl.BlockSpec(memory_space=pltpu.VMEM)
SMEM = pl.BlockSpec(memory_space=pltpu.SMEM)
ANY = pl.BlockSpec(memory_space=pl.ANY)
HBM = pl.BlockSpec(memory_space=pltpu.HBM)


def table(mesh_shape, move):
    tiles, maps, dps = mesh_shape
    rows_y = maps // CORES
    pairs = []
    for t in range(tiles):
        for y in range(rows_y):
            for k in range(CORES):
                for d in range(dps):
                    to = move(t, y, k, d)
                    if to is None or not 0 <= to[0] < tiles:
                        continue
                    t2, y2, k2, d2 = to
                    source = (t * maps + y * CORES + k) * dps + d
                    target = (t2 * maps + (y2 % rows_y) * CORES + k2) * dps + d2
                    pairs.append((source, target))
    return pairs


def params(mib):
    return pltpu.CompilerParams(vmem_limit_bytes=mib * MIB)


def cut_kernel(above, offsets, frames, *refs):
    out, strip, flat, sem = refs[-4:]
    channels, rows_here, wide, count = frames.shape
    column = lax.axis_index("map")
    top, left = offsets[column, 0], offsets[column, 1]
    base = jnp.minimum(left // 16 * 16, wide - STRIP)
    base = pl.multiple_of(base, 16)
    first = jnp.minimum(top, rows_here - FIELD) if above else 0
    copy = pltpu.make_async_copy(
        frames.at[:, pl.ds(first, FIELD), pl.ds(base, STRIP), :], strip, sem
    )
    copy.start()
    copy.wait()
    back = lax.rem(STRIP - (left - base), STRIP)
    for channel in range(channels):
        for r in range(FIELD):
            row = top + r - (first if above else rows_here)
            valid = (row < FIELD) if above else (row >= 0)
            row = jnp.clip(row, 0, FIELD - 1)
            x = strip[channel, row].astype(F32)
            x = pltpu.roll(x, back, 0)[: FIELD + 6]
            x = jnp.where(valid, x, 0.0)
            flat[pl.ds((channel * FIELD + r) * FIELD, FIELD + 6), :] = x
    inner = channels * FIELD * FIELD
    out[...] = flat[pl.ds(0, inner), :].astype(BF16)


def cut(frames, offsets, above, after=()):
    channels, rows_here, wide, count = frames.shape
    inner = channels * FIELD * FIELD
    return pl.pallas_call(
        functools.partial(cut_kernel, above),
        out_shape=jax.ShapeDtypeStruct((inner, count), BF16),
        in_specs=[SMEM, HBM] + [ANY] * len(after),
        out_specs=VMEM,
        scratch_shapes=[
            pltpu.VMEM((channels, FIELD, STRIP, count), BF16),
            pltpu.VMEM((inner + 12, count), F32),
            pltpu.SemaphoreType.DMA,
        ],
        compiler_params=params(16 if above else 58),
        name="cut_above" if above else "cut_below",
    )(offsets, frames, *after)


def blocks_kernel(rows_y, dps, flat, after, *refs):
    outs, wide = refs[:-1], refs[-1]
    inner = outs[0].shape[0]
    y, d = lax.axis_index("map") // CORES, lax.axis_index("dp")
    wide[...] = flat[...].astype(F32)
    for s in range(rows_y):
        column = dps * lax.rem(y + rows_y - s, rows_y) + d
        outs[s][...] = wide[pl.ds(column, inner, stride=rows_y * dps), :].astype(BF16)


def blocks(weights, rows_y, dps, after):
    num_cols, inner, here = weights.shape
    flat = weights.transpose(1, 0, 2).reshape(inner * num_cols, here)
    return pl.pallas_call(
        functools.partial(blocks_kernel, rows_y, dps),
        out_shape=[jax.ShapeDtypeStruct((inner, here), BF16)] * rows_y,
        in_specs=[VMEM, ANY],
        out_specs=[VMEM] * rows_y,
        scratch_shapes=[pltpu.VMEM(flat.shape, F32)],
        compiler_params=params(16),
        name="blocks",
    )(flat, after)


def filters_kernel(own, other, weight, turned):
    k = lax.rem(lax.axis_index("map"), CORES)
    for block, core in ((own[...], k), (other[...], 1 - k)):
        at = pl.multiple_of(core * LANES, LANES)
        weight[:, pl.ds(at, LANES)] = block
        turned[pl.ds(at, LANES), :] = block.T


def filters(own, other):
    inner, here = own.shape
    return pl.pallas_call(
        filters_kernel,
        out_shape=[
            jax.ShapeDtypeStruct((inner, CORES * here), BF16),
            jax.ShapeDtypeStruct((CORES * here, inner), BF16),
        ],
        in_specs=[VMEM] * 2,
        out_specs=[VMEM] * 2,
        compiler_params=params(8),
        name="filters",
    )(own, other)


def dot(a, b):
    return jnp.dot(a, b, preferred_element_type=F32)


def column_kernel(rows_y, above, above_in, below, *refs):
    weight, turned = refs[:rows_y], refs[rows_y : 2 * rows_y]
    pe, mr, res, sq, inv = refs[2 * rows_y :]
    inner, count = above.shape
    tile = weight[0].shape[1]
    maps = rows_y * tile
    mine = lax.rem(lax.axis_index("map"), CORES) == lax.axis_index("dp")

    @pl.when(mine)
    def _():
        pe[:, pl.ds(0, count)] = above[...] + below[...]

    @pl.when(jnp.logical_not(mine))
    def _():
        pe[:, pl.ds(0, count)] = above_in[...] + below[...]

    patch = pe[:, pl.ds(0, count)]
    for m in range(0, maps, tile):
        r = dot(turned[m // tile][...], patch)
        res[pl.ds(m, tile), :] = r
        mr[pl.ds(m, tile), pl.ds(count, count)] = r.astype(BF16)
        sq[pl.ds(m, tile), :] = r * r
    sq[pl.ds(maps, SUB), :] = sq[pl.ds(0, SUB), :]

    steps = -(-inner // tile)
    for n in range(steps):
        low, high = n * tile, min(inner, (n + 1) * tile)
        rows = pl.ds(low, high - low)
        error = -pe[rows, pl.ds(0, count)].astype(F32)
        for p in range(rows_y):
            error += dot(weight[p][rows, :], mr[pl.ds(p * tile, tile), pl.ds(count, count)])
        pe[rows, pl.ds(count, count)] = error.astype(BF16)
    for m in range(0, maps, tile):
        total = sq[pl.ds(m, tile), :]
        for i in range(1, POOL):
            total = total + sq[pl.ds(m + i, tile), :]
        inv[pl.ds(SUB + m, tile), :] = lax.rsqrt(smoothing + total)
    inv[pl.ds(0, SUB), :] = inv[pl.ds(maps, SUB), :]
    error_b = pe[:, pl.ds(count, count)]
    for m in range(0, maps, tile):
        back = dot(turned[m // tile][...], error_b)
        spread = inv[pl.ds(SUB + m, tile), :]
        for i in range(1, POOL):
            spread = spread + inv[pl.ds(SUB + m - i, tile), :]
        mixed = back + sparsity * res[pl.ds(m, tile), :] * spread
        mr[pl.ds(m, tile), pl.ds(0, count)] = mixed.astype(BF16)


def column(above, above_in, below, weight, turned):
    inner, count = above.shape
    rows_y = len(weight)
    maps = rows_y * weight[0].shape[1]
    return pl.pallas_call(
        functools.partial(column_kernel, rows_y),
        out_shape=[
            jax.ShapeDtypeStruct((inner, 2 * count), BF16),
            jax.ShapeDtypeStruct((maps, 2 * count), BF16),
        ],
        in_specs=[VMEM] * (3 + 2 * rows_y),
        out_specs=[VMEM] * 2,
        scratch_shapes=[
            pltpu.VMEM((maps, count), F32),
            pltpu.VMEM((maps + SUB, count), F32),
            pltpu.VMEM((maps + SUB, count), F32),
        ],
        compiler_params=params(40),
        name="column",
    )(above, above_in, below, *weight, *turned)


def piece_kernel(p, scale, pe, mr, home, away):
    inner = pe.shape[0]
    first = lax.rem(lax.axis_index("map"), CORES) == 0
    tile = 256
    groups = mr[pl.ds(CORES * LANES * p, CORES * LANES), :]
    for n in range(0, inner, tile):
        rows = pl.ds(n, min(tile, inner - n))
        g = lax.dot_general(
            pe[rows, :], groups, (((1,), (1,)), ((), ())), preferred_element_type=F32
        )
        g = g * scale
        low, high = g[:, :LANES], g[:, LANES:]
        home[rows, :] = jnp.where(first, low, high)
        away[rows, :] = jnp.where(first, high, low).astype(BF16)


def piece(p, pe, mr):
    inner, depth = pe.shape
    return pl.pallas_call(
        functools.partial(piece_kernel, p, 1.0 / depth),
        out_shape=[
            jax.ShapeDtypeStruct((inner, LANES), F32),
            jax.ShapeDtypeStruct((inner, LANES), BF16),
        ],
        in_specs=[VMEM] * 2,
        out_specs=[VMEM] * 2,
        compiler_params=params(16),
        name="piece",
    )(pe, mr)


def finish_kernel(rows_y, dps, *refs):
    arrived, crossed = refs[:rows_y], refs[rows_y : 2 * rows_y]
    weights, grad, fresh, full = refs[2 * rows_y :]
    inner = arrived[0].shape[0]
    num_cols = rows_y * dps
    y, d = lax.axis_index("map") // CORES, lax.axis_index("dp")
    for s in range(rows_y):
        row = lax.rem(y + rows_y - s, rows_y)
        for block, part in ((arrived[s], d), (crossed[s], 1 - d)):
            full[pl.ds(dps * row + part, inner, stride=num_cols), :] = block[...].astype(F32)
    some = inner * num_cols // dps
    grad[...] = full[pl.ds(pl.multiple_of(d * some, SUB), some), :]
    fresh[...] = (weights[...].astype(F32) - learn_rate * full[...]).astype(BF16)


def finish(arrived, crossed, weights, dps):
    inner, here = arrived[0].shape
    num_cols = weights.shape[0]
    rows = inner * num_cols
    flat = weights.transpose(1, 0, 2).reshape(rows, here)
    grad, fresh = pl.pallas_call(
        functools.partial(finish_kernel, len(arrived), dps),
        out_shape=[
            jax.ShapeDtypeStruct((rows // dps, here), F32),
            jax.ShapeDtypeStruct((rows, here), BF16),
        ],
        in_specs=[VMEM] * (2 * len(arrived) + 1),
        out_specs=[VMEM] * 2,
        scratch_shapes=[pltpu.VMEM((rows, here), F32)],
        compiler_params=params(32),
        name="finish",
    )(*arrived, *crossed, flat)
    grad = grad.reshape(inner // dps, num_cols, here).transpose(1, 0, 2)
    return grad, fresh.reshape(inner, num_cols, here).transpose(1, 0, 2)


def per_device(mesh_shape, frames, weights, offsets):
    rows_y = mesh_shape[1] // CORES
    def send(x, move):
        return lax.ppermute(x, AXES, table(mesh_shape, move))

    upper_offsets = send(offsets, lambda t, y, k, d: (t + 1, y, k, d))
    below = cut(frames, upper_offsets, False)
    own = blocks(weights, rows_y, mesh_shape[2], below)
    above = cut(frames, offsets, True, own[:1])
    below = send(below, lambda t, y, k, d: (t - 1, y, d, k))
    above_in = send(above, lambda t, y, k, d: (t, y, d, k) if k != d else None)

    weight, turned = [], []
    for s in range(rows_y):
        block = own[s]
        if s:
            block = send(block, lambda t, y, k, d: (t, y - s, k, d))
        other = send(block, lambda t, y, k, d: (t, y, 1 - k, d))
        pair = filters(block, other)
        weight.append(pair[0])
        turned.append(pair[1])

    pe, mr = column(above, above_in, below, weight, turned)

    arrived, crossed = [], []
    for s in range(rows_y):
        home, away = piece(s, pe, mr)
        away = send(away, lambda t, y, k, d: (t, y, 1 - k, d))
        block = (home + away.astype(F32)).astype(BF16)
        if s:
            block = send(block, lambda t, y, k, d: (t, y + s, k, d))
        arrived.append(block)
        crossed.append(send(block, lambda t, y, k, d: (t, y, k, 1 - d)))
    return finish(arrived, crossed, weights, mesh_shape[2])


def solution(mesh):
    mesh_shape = tuple(mesh.shape[a] for a in AXES)
    placed = (P(None, "tile", None, "dp"), P("tile", None, "map"), P("tile", None))

    def run(frames, weights, offsets):
        return per_device(mesh_shape, frames, weights, offsets)

    return jax.shard_map(
        run,
        mesh=mesh,
        in_specs=placed,
        out_specs=(P("tile", "dp", "map"), P("tile", None, "map")),
        check_vma=False,
    )
```

time: 145 us -> 86.2 us (0.59)
  local copies, waits for them, and re-layouts: 39.5 us -> 4.02 us
  Pallas kernels: 0 us -> 19.4 us
  matrix products: 15.7 us -> 0 us
  waiting for transfers between devices: 48.5 us -> 38.3 us
  between operations: 8.79 us -> 0.81 us
  other arithmetic: 7.54 us -> 0.25 us
    pallas_call x0 -> x13, Pallas kernels: none -> 19.4 us  [the longest x2 7.15 us: cut(): pl.pallas_call(functools.partial(cut_kernel, above), out_shape=jax.ShapeD...]
    dot_general x4 -> x0, matrix products: 15.7 us -> none  [the longest x1 8.65 us: column_step(): jnp.einsum('if,fm->im', patch, mixed, preferred_element_type=jnp.float32)]
    slice x15 -> x0, local copies, waits for them, and re-layouts: 11.7 us -> none  [the longest x1 6.75 us: per_device(): low, high = (grad[:, :, 0], grad[:, :, 1])]
    ppermute x12 -> x21, waiting for transfers between devices: 48.5 us -> 38.3 us  [send(): return lax.ppermute(x, AXES, table(mesh_shape, move))]
    reshape x3 -> x0, local copies, waits for them, and re-layouts: 7.65 us -> none  [the longest x1 6.33 us: per_device(): grad = grad.reshape(inner, rows_y, CORES, maps_here)]
    another operation x5 -> x0, local copies, waits for them, and re-layouts: 7.52 us -> none  [the longest x1 3.91 us: per_device(): weight = jnp.stack([low, high], 2).reshape(inner, -1)]
    dynamic_slice x6 -> x0, local copies, waits for them, and re-layouts: 3.83 us -> none  [the longest x1 3.07 us: cut(): lax.dynamic_slice(frames, (zero, zero, place[1], zero), (channels, rows_h...]
    another operation x4 -> x0, other arithmetic: 3.51 us -> none  [the longest x2 3.25 us: per_device(): weight = jnp.stack([low, high], 2).reshape(inner, -1)]
  transfers between devices with their start and end apart: 12 -> 21, of which waited for: 5 -> 13; matrix products, arithmetic and copies ran while one was open for 9% -> 0% of each run, Pallas kernels for 0% -> 6%
where the time goes in v2:
time: 86.2 us; the launch traced here: 85.3 us
  waiting for transfers between devices  38.3 us (44%)
  starting transfers between devices  22.5 us (26%)
  Pallas kernels  19.4 us (23%)
  local copies, waits for them, and re-layouts  4.02 us (5%)
    ppermute x21, waiting for transfers between devices, send(): return lax.ppermute(x, AXES, table(mesh_shape, move))  38.3 us
    ppermute x21, starting transfers between devices, send(): return lax.ppermute(x, AXES, table(mesh_shape, move))  22.5 us
    pallas_call x2, Pallas kernels, cut(): pl.pallas_call(functools.partial(cut_kernel, above), out_shape=jax.ShapeD...  7.15 us
    pallas_call x1, Pallas kernels, column(): pl.pallas_call(functools.partial(column_kernel, rows_y), out_shape=[jax.S...  4.39 us
    unnamed x11, local copies, waits for them, and re-layouts  4.02 us
    pallas_call x1, Pallas kernels, finish(): pl.pallas_call(functools.partial(finish_kernel, len(arrived), dps), out_s...  3.65 us
    pallas_call x4, Pallas kernels, piece(): pl.pallas_call(functools.partial(piece_kernel, p, 1.0 / depth), out_shape...  2.43 us
  transfers between devices with their start and end apart: 21, of which 13 were waited for; matrix products, arithmetic and copies ran while one was open for 0% of the time, Pallas kernels for 6%

profile of v2, /device:TPU:4, one launch (start us, length us, event | category | flops | bytes accessed | tf_op | source)
XLA Modules:
  0.0 85.3 jit_solution(926866547687743886)
XLA Ops:
  0.6 0.8 copy.6.offsets
  1.4 3.8 %collective-permute-start = (s32[8,2]{1,0:T(8,128)S(1)}, s32[8,2]{1,0:T(8,128)S(1)}, u32[]{:S(2)}, u32[]{:S(2)}) collective-permute-start(s32[8,2]{1,0:T(8,128)S(1)} %copy.6.offsets), channel_id=1, source_target_pairs={{0,16},{1,17},{2,18},{3,19},{4,20},{5,21},{6,22},{7,23},{8,24},{9,... | collective-permute-start | bytes 200 | tf_op jit(solution)/shard_map/ppermute | solution.py:288
  5.2 5.5 %collective-permute-done.offsets = s32[8,2]{1,0:T(8,128)S(1)} collective-permute-done((s32[8,2]{1,0:T(8,128)S(1)}, s32[8,2]{1,0:T(8,128)S(1)}, u32[]{:S(2)}, u32[]{:S(2)}) %collective-permute-start) | collective-permute-done | bytes 96 | tf_op jit(solution)/shard_map/ppermute | solution.py:288
  10.7 0.6 copy-done.4
  11.3 5.0 %cut_below.1.after = bf16[972,384]{1,0:T(8,128)(2,1)} custom-call(s32[8,2]{1,0:T(8,128)} %copy-done.4, bf16[3,20,128,384]{3,2,1,0:T(8,128)(2,1)} %frames.3), custom_call_target="tpu_custom_call" | custom-call | tf_op jit(solution)/shard_map/cut_below/pallas_call | solution.py:82
  16.3 1.5 %copy-done.1 = bf16[8,972,128]{2,0,1:T(8,128)(2,1)S(1)} copy-done((bf16[8,972,128]{2,0,1:T(8,128)(2,1)S(1)}, bf16[8,972,128]{2,0,1:T(8,128)(2,1)}, u32[]{:S(2)}) %copy-start.1) | copy-done | bytes 1990680
  17.8 1.1 %copy-done.3 = bf16[972,384]{1,0:T(8,128)(2,1)S(1)} copy-done((bf16[972,384]{1,0:T(8,128)(2,1)S(1)}, bf16[972,384]{1,0:T(8,128)(2,1)}, u32[]{:S(2)}) %copy-start.3) | copy-done | bytes 746520
  19.0 0.8 blocks.1
  19.7 3.1 %collective-permute-start.4 = (bf16[972,128]{1,0:T(8,128)(2,1)S(1)}, bf16[972,128]{1,0:T(8,128)(2,1)S(1)}, u32[]{:S(2)}, u32[]{:S(2)}) collective-permute-start(bf16[972,128]{1,0:T(8,128)(2,1)S(1)} %get-tuple-element.28), channel_id=1, source_target_pairs={{0,12},{1,13},{2,14},{3,15},{4,0},{5,1},{6,2},{7,3},{8,4},{9,5},{1... | collective-permute-start | bytes 746504 | tf_op jit(solution)/shard_map/ppermute | solution.py:288
  22.8 3.9 %collective-permute-start.2 = (bf16[972,384]{1,0:T(8,128)(2,1)S(1)}, bf16[972,384]{1,0:T(8,128)(2,1)S(1)}, u32[]{:S(2)}, u32[]{:S(2)}) collective-permute-start(bf16[972,384]{1,0:T(8,128)(2,1)S(1)} %copy-done.3), channel_id=1, source_target_pairs={{16,0},{17,2},{18,1},{19,3},{20,4},{21,6},{22,5},{23,7},{24,8},{25... | collective-permute-start | bytes 2239496 | tf_op jit(solution)/shard_map/ppermute | solution.py:288
  26.8 2.1 %cut_above.1.above = bf16[972,384]{1,0:T(8,128)(2,1)S(1)} custom-call(s32[8,2]{1,0:T(8,128)S(1)} %copy.6.offsets, bf16[3,20,128,384]{3,2,1,0:T(8,128)(2,1)S(1)} %copy-done, bf16[972,128]{1,0:T(8,128)(2,1)S(1)} %get-tuple-element.26.refs_0_.own), custom_call_target="tpu_custom_call" | custom-call | tf_op jit(solution)/shard_map/cut_above/pallas_call | solution.py:82
  28.9 0.7 collective-permute-start.1
  29.7 2.2 %collective-permute-start.6 = (bf16[972,128]{1,0:T(8,128)(2,1)S(1)}, bf16[972,128]{1,0:T(8,128)(2,1)S(1)}, u32[]{:S(2)}, u32[]{:S(2)}) collective-permute-start(bf16[972,128]{1,0:T(8,128)(2,1)S(1)} %get-tuple-element.30), channel_id=1, source_target_pairs={{0,8},{1,9},{2,10},{3,11},{4,12},{5,13},{6,14},{7,15},{8,0},{9,1},... | collective-permute-start | bytes 746504 | tf_op jit(solution)/shard_map/ppermute | solution.py:288
  31.9 0.9 collective-permute-start.3
  32.7 12.1 %collective-permute-done.8.own = bf16[972,128]{1,0:T(8,128)(2,1)S(1)} collective-permute-done((bf16[972,128]{1,0:T(8,128)(2,1)S(1)}, bf16[972,128]{1,0:T(8,128)(2,1)S(1)}, u32[]{:S(2)}, u32[]{:S(2)}) %collective-permute-start.8) | collective-permute-done | bytes 248864 | tf_op jit(solution)/shard_map/ppermute | solution.py:288
  44.8 0.2 collective-permute-start.9
  45.0 0.3 collective-permute-start.7
  45.3 0.2 collective-permute-start.5
  45.5 0.2 filters.4
  45.8 0.6 collective-permute-done.9.other
  46.3 0.2 filters.7
  46.6 0.1 collective-permute-done.7.other
  46.7 0.2 filters.6
  46.9 0.1 collective-permute-done.5.other
  47.0 0.2 filters.5
  47.3 4.4 %column.1 = (bf16[972,768]{1,0:T(8,128)(2,1)S(1)}, bf16[1024,768]{1,0:T(8,128)(2,1)S(1)}) custom-call(bf16[972,384]{1,0:T(8,128)(2,1)S(1)} %cut_above.1.above, bf16[972,384]{1,0:T(8,128)(2,1)S(1)} %collective-permute-done.1.above_in, bf16[972,384]{1,0:T(8,128)(2,1)S(1)} %collective-permute-done.2.below, bf16[972,256]{1,0:T(8,128)(2,1)S(1)} %get-tuple-element.27.refs_0_, ...), custom_call_target="tpu_custom_call" | custom-call | tf_op jit(solution)/shard_map/column/pallas_call | solution.py:200
  51.7 0.6 piece.7
  52.3 0.3 collective-permute-start.15
  52.6 0.6 piece.6
  53.2 0.6 piece.5
  53.8 0.6 piece.4
  54.4 0.4 collective-permute-start.13
  54.9 0.2 collective-permute-start.11
  55.0 0.3 collective-permute-start.10
  55.5 0.5 collective-permute-done.13
  56.2 0.2 collective-permute-done.11
  56.4 1.4 %collective-permute-start.12 = (bf16[972,128]{1,0:T(8,128)(2,1)S(1)}, bf16[972,128]{1,0:T(8,128)(2,1)S(1)}, u32[]{:S(2)}, u32[]{:S(2)}) collective-permute-start(bf16[972,128]{1,0:T(8,128)(2,1)S(1)} %add_convert_fusion.2), channel_id=1, source_target_pairs={{0,4},{1,5},{2,6},{3,7},{4,8},{5,9},{6,10},{7,11},{8,12},{9,13},{1... | collective-permute-start | bytes 746504 | tf_op jit(solution)/shard_map/ppermute | solution.py:288
  57.9 1.1 %collective-permute-start.17 = (bf16[972,128]{1,0:T(8,128)(2,1)S(1)}, bf16[972,128]{1,0:T(8,128)(2,1)S(1)}, u32[]{:S(2)}, u32[]{:S(2)}) collective-permute-start(bf16[972,128]{1,0:T(8,128)(2,1)S(1)} %add_convert_fusion.3.refs_0_), channel_id=1, source_target_pairs={{0,1},{1,0},{2,3},{3,2},{4,5},{5,4},{6,7},{7,6},{8,9},{9,8},{10,11... | collective-permute-start | bytes 746504 | tf_op jit(solution)/shard_map/ppermute | solution.py:288
  59.1 5.3 %collective-permute-done.16.refs_3_ = bf16[972,128]{1,0:T(8,128)(2,1)S(1)} collective-permute-done((bf16[972,128]{1,0:T(8,128)(2,1)S(1)}, bf16[972,128]{1,0:T(8,128)(2,1)S(1)}, u32[]{:S(2)}, u32[]{:S(2)}) %collective-permute-start.16) | collective-permute-done | bytes 248864 | tf_op jit(solution)/shard_map/ppermute | solution.py:288
  64.4 1.0 %collective-permute-start.20 = (bf16[972,128]{1,0:T(8,128)(2,1)S(1)}, bf16[972,128]{1,0:T(8,128)(2,1)S(1)}, u32[]{:S(2)}, u32[]{:S(2)}) collective-permute-start(bf16[972,128]{1,0:T(8,128)(2,1)S(1)} %collective-permute-done.16.refs_3_), channel_id=1, source_target_pairs={{0,1},{1,0},{2,3},{3,2},{4,5},{5,4},{6,7},{7,6},{8,9},{9,8},{10,11... | collective-permute-start | bytes 746504 | tf_op jit(solution)/shard_map/ppermute | solution.py:288
  65.4 1.2 %collective-permute-done.14.refs_2_ = bf16[972,128]{1,0:T(8,128)(2,1)S(1)} collective-permute-done((bf16[972,128]{1,0:T(8,128)(2,1)S(1)}, bf16[972,128]{1,0:T(8,128)(2,1)S(1)}, u32[]{:S(2)}, u32[]{:S(2)}) %collective-permute-start.14) | collective-permute-done | bytes 248864 | tf_op jit(solution)/shard_map/ppermute | solution.py:288
  66.6 1.3 %collective-permute-start.19 = (bf16[972,128]{1,0:T(8,128)(2,1)S(1)}, bf16[972,128]{1,0:T(8,128)(2,1)S(1)}, u32[]{:S(2)}, u32[]{:S(2)}) collective-permute-start(bf16[972,128]{1,0:T(8,128)(2,1)S(1)} %collective-permute-done.14.refs_2_), channel_id=1, source_target_pairs={{0,1},{1,0},{2,3},{3,2},{4,5},{5,4},{6,7},{7,6},{8,9},{9,8},{10,11... | collective-permute-start | bytes 746504 | tf_op jit(solution)/shard_map/ppermute | solution.py:288
  67.9 3.5 %collective-permute-done.12.refs_1_ = bf16[972,128]{1,0:T(8,128)(2,1)S(1)} collective-permute-done((bf16[972,128]{1,0:T(8,128)(2,1)S(1)}, bf16[972,128]{1,0:T(8,128)(2,1)S(1)}, u32[]{:S(2)}, u32[]{:S(2)}) %collective-permute-start.12) | collective-permute-done | bytes 248864 | tf_op jit(solution)/shard_map/ppermute | solution.py:288
  71.3 1.0 %collective-permute-start.18 = (bf16[972,128]{1,0:T(8,128)(2,1)S(1)}, bf16[972,128]{1,0:T(8,128)(2,1)S(1)}, u32[]{:S(2)}, u32[]{:S(2)}) collective-permute-start(bf16[972,128]{1,0:T(8,128)(2,1)S(1)} %collective-permute-done.12.refs_1_), channel_id=1, source_target_pairs={{0,1},{1,0},{2,3},{3,2},{4,5},{5,4},{6,7},{7,6},{8,9},{9,8},{10,11... | collective-permute-start | bytes 746504 | tf_op jit(solution)/shard_map/ppermute | solution.py:288
  72.3 1.1 %collective-permute-done.20.refs_7_ = bf16[972,128]{1,0:T(8,128)(2,1)S(1)} collective-permute-done((bf16[972,128]{1,0:T(8,128)(2,1)S(1)}, bf16[972,128]{1,0:T(8,128)(2,1)S(1)}, u32[]{:S(2)}, u32[]{:S(2)}) %collective-permute-start.20) | collective-permute-done | bytes 248864 | tf_op jit(solution)/shard_map/ppermute | solution.py:288
  73.4 5.2 %collective-permute-done.19.refs_6_ = bf16[972,128]{1,0:T(8,128)(2,1)S(1)} collective-permute-done((bf16[972,128]{1,0:T(8,128)(2,1)S(1)}, bf16[972,128]{1,0:T(8,128)(2,1)S(1)}, u32[]{:S(2)}, u32[]{:S(2)}) %collective-permute-start.19) | collective-permute-done | bytes 248864 | tf_op jit(solution)/shard_map/ppermute | solution.py:288
  78.6 3.1 %collective-permute-done.18.refs_5_ = bf16[972,128]{1,0:T(8,128)(2,1)S(1)} collective-permute-done((bf16[972,128]{1,0:T(8,128)(2,1)S(1)}, bf16[972,128]{1,0:T(8,128)(2,1)S(1)}, u32[]{:S(2)}, u32[]{:S(2)}) %collective-permute-start.18) | collective-permute-done | bytes 248864 | tf_op jit(solution)/shard_map/ppermute | solution.py:288
  81.6 3.6 %finish.1 = (f32[3888,128]{1,0:T(8,128)}, bf16[7776,128]{1,0:T(8,128)(2,1)}) custom-call(bf16[972,128]{1,0:T(8,128)(2,1)S(1)} %add_convert_fusion.3.refs_0_, bf16[972,128]{1,0:T(8,128)(2,1)S(1)} %collective-permute-done.12.refs_1_, bf16[972,128]{1,0:T(8,128)(2,1)S(1)} %collective-permute-done.14.refs_2_, ...), custom_call_target="tpu_custom_call" | custom-call | tf_op jit(solution)/shard_map/finish/pallas_call | solution.py:269
  (22 shorter events, 0.5 us)
Async XLA Ops:
  1.4 9.3 %collective-permute-start = (s32[8,2]{1,0:T(8,128)S(1)}, s32[8,2]{1,0:T(8,128)S(1)}, u32[]{:S(2)}, u32[]{:S(2)}) collective-permute-start(s32[8,2]{1,0:T(8,128)S(1)} %copy.6.offsets), channel_id=1, source_target_pairs={{0,16},{1,17},{2,18},{3,19},{4,20},{5,21},{6,22},{7,23},{8,24},{9,... | collective-permute-start | bytes 200 | tf_op jit(solution)/shard_map/ppermute | solution.py:288
  10.7 0.6 copy-start.4
  11.3 15.5 %copy-start = (bf16[3,20,128,384]{3,2,1,0:T(8,128)(2,1)S(1)}, bf16[3,20,128,384]{3,2,1,0:T(8,128)(2,1)}, u32[]{:S(2)}) copy-start(bf16[3,20,128,384]{3,2,1,0:T(8,128)(2,1)} %frames.3) | copy-start | bytes 17694724
  16.3 1.6 %copy-start.1 = (bf16[8,972,128]{2,0,1:T(8,128)(2,1)S(1)}, bf16[8,972,128]{2,0,1:T(8,128)(2,1)}, u32[]{:S(2)}) copy-start(bf16[8,972,128]{2,0,1:T(8,128)(2,1)} %param.4) | copy-start | bytes 5971972
  17.8 1.1 %copy-start.3 = (bf16[972,384]{1,0:T(8,128)(2,1)S(1)}, bf16[972,384]{1,0:T(8,128)(2,1)}, u32[]{:S(2)}) copy-start(bf16[972,384]{1,0:T(8,128)(2,1)} %cut_below.1.after) | copy-start | bytes 2239492
  19.7 12.2 %collective-permute-start.4 = (bf16[972,128]{1,0:T(8,128)(2,1)S(1)}, bf16[972,128]{1,0:T(8,128)(2,1)S(1)}, u32[]{:S(2)}, u32[]{:S(2)}) collective-permute-start(bf16[972,128]{1,0:T(8,128)(2,1)S(1)} %get-tuple-element.28), channel_id=1, source_target_pairs={{0,12},{1,13},{2,14},{3,15},{4,0},{5,1},{6,2},{7,3},{8,4},{9,5},{1... | collective-permute-start | bytes 746504 | tf_op jit(solution)/shard_map/ppermute | solution.py:288
  22.8 24.5 %collective-permute-start.2 = (bf16[972,384]{1,0:T(8,128)(2,1)S(1)}, bf16[972,384]{1,0:T(8,128)(2,1)S(1)}, u32[]{:S(2)}, u32[]{:S(2)}) collective-permute-start(bf16[972,384]{1,0:T(8,128)(2,1)S(1)} %copy-done.3), channel_id=1, source_target_pairs={{16,0},{17,2},{18,1},{19,3},{20,4},{21,6},{22,5},{23,7},{24,8},{25... | collective-permute-start | bytes 2239496 | tf_op jit(solution)/shard_map/ppermute | solution.py:288
  28.9 18.4 %collective-permute-start.1 = (bf16[972,384]{1,0:T(8,128)(2,1)S(1)}, bf16[972,384]{1,0:T(8,128)(2,1)S(1)}, u32[]{:S(2)}, u32[]{:S(2)}) collective-permute-start(bf16[972,384]{1,0:T(8,128)(2,1)S(1)} %cut_above.1.above), channel_id=1, source_target_pairs={{1,2},{2,1},{5,6},{6,5},{9,10},{10,9},{13,14},{14,13},{17,18},{18,... | collective-permute-start | bytes 2239496 | tf_op jit(solution)/shard_map/ppermute | solution.py:288
  29.6 15.2 %collective-permute-start.8 = (bf16[972,128]{1,0:T(8,128)(2,1)S(1)}, bf16[972,128]{1,0:T(8,128)(2,1)S(1)}, u32[]{:S(2)}, u32[]{:S(2)}) collective-permute-start(bf16[972,128]{1,0:T(8,128)(2,1)S(1)} %get-tuple-element.32), channel_id=1, source_target_pairs={{0,4},{1,5},{2,6},{3,7},{4,8},{5,9},{6,10},{7,11},{8,12},{9,13},{1... | collective-permute-start | bytes 746504 | tf_op jit(solution)/shard_map/ppermute | solution.py:288
  29.7 15.3 %collective-permute-start.6 = (bf16[972,128]{1,0:T(8,128)(2,1)S(1)}, bf16[972,128]{1,0:T(8,128)(2,1)S(1)}, u32[]{:S(2)}, u32[]{:S(2)}) collective-permute-start(bf16[972,128]{1,0:T(8,128)(2,1)S(1)} %get-tuple-element.30), channel_id=1, source_target_pairs={{0,8},{1,9},{2,10},{3,11},{4,12},{5,13},{6,14},{7,15},{8,0},{9,1},... | collective-permute-start | bytes 746504 | tf_op jit(solution)/shard_map/ppermute | solution.py:288
  31.9 13.4 %collective-permute-start.3 = (bf16[972,128]{1,0:T(8,128)(2,1)S(1)}, bf16[972,128]{1,0:T(8,128)(2,1)S(1)}, u32[]{:S(2)}, u32[]{:S(2)}) collective-permute-start(bf16[972,128]{1,0:T(8,128)(2,1)S(1)} %get-tuple-element.26.refs_0_.own), channel_id=1, source_target_pairs={{0,2},{1,3},{2,0},{3,1},{4,6},{5,7},{6,4},{7,5},{8,10},{9,11},{10,... | collective-permute-start | bytes 746504 | tf_op jit(solution)/shard_map/ppermute | solution.py:288
  44.8 1.5 %collective-permute-start.9 = (bf16[972,128]{1,0:T(8,128)(2,1)S(1)}, bf16[972,128]{1,0:T(8,128)(2,1)S(1)}, u32[]{:S(2)}, u32[]{:S(2)}) collective-permute-start(bf16[972,128]{1,0:T(8,128)(2,1)S(1)} %collective-permute-done.8.own), channel_id=1, source_target_pairs={{0,2},{1,3},{2,0},{3,1},{4,6},{5,7},{6,4},{7,5},{8,10},{9,11},{10,... | collective-permute-start | bytes 746504 | tf_op jit(solution)/shard_map/ppermute | solution.py:288
  45.0 1.7 %collective-permute-start.7 = (bf16[972,128]{1,0:T(8,128)(2,1)S(1)}, bf16[972,128]{1,0:T(8,128)(2,1)S(1)}, u32[]{:S(2)}, u32[]{:S(2)}) collective-permute-start(bf16[972,128]{1,0:T(8,128)(2,1)S(1)} %collective-permute-done.6.own), channel_id=1, source_target_pairs={{0,2},{1,3},{2,0},{3,1},{4,6},{5,7},{6,4},{7,5},{8,10},{9,11},{10,... | collective-permute-start | bytes 746504 | tf_op jit(solution)/shard_map/ppermute | solution.py:288
  45.3 1.7 %collective-permute-start.5 = (bf16[972,128]{1,0:T(8,128)(2,1)S(1)}, bf16[972,128]{1,0:T(8,128)(2,1)S(1)}, u32[]{:S(2)}, u32[]{:S(2)}) collective-permute-start(bf16[972,128]{1,0:T(8,128)(2,1)S(1)} %collective-permute-done.4.own), channel_id=1, source_target_pairs={{0,2},{1,3},{2,0},{3,1},{4,6},{5,7},{6,4},{7,5},{8,10},{9,11},{10,... | collective-permute-start | bytes 746504 | tf_op jit(solution)/shard_map/ppermute | solution.py:288
  52.3 3.0 %collective-permute-start.15 = (bf16[972,128]{1,0:T(8,128)(2,1)S(1)}, bf16[972,128]{1,0:T(8,128)(2,1)S(1)}, u32[]{:S(2)}, u32[]{:S(2)}) collective-permute-start(bf16[972,128]{1,0:T(8,128)(2,1)S(1)} %get-tuple-element.47), channel_id=1, source_target_pairs={{0,2},{1,3},{2,0},{3,1},{4,6},{5,7},{6,4},{7,5},{8,10},{9,11},{10,... | collective-permute-start | bytes 746504 | tf_op jit(solution)/shard_map/ppermute | solution.py:288
  54.4 1.6 %collective-permute-start.13 = (bf16[972,128]{1,0:T(8,128)(2,1)S(1)}, bf16[972,128]{1,0:T(8,128)(2,1)S(1)}, u32[]{:S(2)}, u32[]{:S(2)}) collective-permute-start(bf16[972,128]{1,0:T(8,128)(2,1)S(1)} %get-tuple-element.45), channel_id=1, source_target_pairs={{0,2},{1,3},{2,0},{3,1},{4,6},{5,7},{6,4},{7,5},{8,10},{9,11},{10,... | collective-permute-start | bytes 746504 | tf_op jit(solution)/shard_map/ppermute | solution.py:288
  54.9 1.5 %collective-permute-start.11 = (bf16[972,128]{1,0:T(8,128)(2,1)S(1)}, bf16[972,128]{1,0:T(8,128)(2,1)S(1)}, u32[]{:S(2)}, u32[]{:S(2)}) collective-permute-start(bf16[972,128]{1,0:T(8,128)(2,1)S(1)} %get-tuple-element.43), channel_id=1, source_target_pairs={{0,2},{1,3},{2,0},{3,1},{4,6},{5,7},{6,4},{7,5},{8,10},{9,11},{10,... | collective-permute-start | bytes 746504 | tf_op jit(solution)/shard_map/ppermute | solution.py:288
  55.0 2.9 %collective-permute-start.10 = (bf16[972,128]{1,0:T(8,128)(2,1)S(1)}, bf16[972,128]{1,0:T(8,128)(2,1)S(1)}, u32[]{:S(2)}, u32[]{:S(2)}) collective-permute-start(bf16[972,128]{1,0:T(8,128)(2,1)S(1)} %get-tuple-element.41), channel_id=1, source_target_pairs={{0,2},{1,3},{2,0},{3,1},{4,6},{5,7},{6,4},{7,5},{8,10},{9,11},{10,... | collective-permute-start | bytes 746504 | tf_op jit(solution)/shard_map/ppermute | solution.py:288
  55.4 26.3 %copy-start.2 = (bf16[8,972,128]{2,0,1:T(8,128)(2,1)S(1)}, bf16[8,972,128]{2,0,1:T(8,128)(2,1)}, u32[]{:S(2)}) copy-start(bf16[8,972,128]{2,0,1:T(8,128)(2,1)} %param.4) | copy-start | bytes 5971972
  55.4 9.0 %collective-permute-start.16 = (bf16[972,128]{1,0:T(8,128)(2,1)S(1)}, bf16[972,128]{1,0:T(8,128)(2,1)S(1)}, u32[]{:S(2)}, u32[]{:S(2)}) collective-permute-start(bf16[972,128]{1,0:T(8,128)(2,1)S(1)} %add_convert_fusion), channel_id=1, source_target_pairs={{0,12},{1,13},{2,14},{3,15},{4,0},{5,1},{6,2},{7,3},{8,4},{9,5},{1... | collective-permute-start | bytes 746504 | tf_op jit(solution)/shard_map/ppermute | solution.py:288
  56.1 10.5 %collective-permute-start.14 = (bf16[972,128]{1,0:T(8,128)(2,1)S(1)}, bf16[972,128]{1,0:T(8,128)(2,1)S(1)}, u32[]{:S(2)}, u32[]{:S(2)}) collective-permute-start(bf16[972,128]{1,0:T(8,128)(2,1)S(1)} %add_convert_fusion.1), channel_id=1, source_target_pairs={{0,8},{1,9},{2,10},{3,11},{4,12},{5,13},{6,14},{7,15},{8,0},{9,1},... | collective-permute-start | bytes 746504 | tf_op jit(solution)/shard_map/ppermute | solution.py:288
  56.4 14.9 %collective-permute-start.12 = (bf16[972,128]{1,0:T(8,128)(2,1)S(1)}, bf16[972,128]{1,0:T(8,128)(2,1)S(1)}, u32[]{:S(2)}, u32[]{:S(2)}) collective-permute-start(bf16[972,128]{1,0:T(8,128)(2,1)S(1)} %add_convert_fusion.2), channel_id=1, source_target_pairs={{0,4},{1,5},{2,6},{3,7},{4,8},{5,9},{6,10},{7,11},{8,12},{9,13},{1... | collective-permute-start | bytes 746504 | tf_op jit(solution)/shard_map/ppermute | solution.py:288
  57.9 14.4 %collective-permute-start.17 = (bf16[972,128]{1,0:T(8,128)(2,1)S(1)}, bf16[972,128]{1,0:T(8,128)(2,1)S(1)}, u32[]{:S(2)}, u32[]{:S(2)}) collective-permute-start(bf16[972,128]{1,0:T(8,128)(2,1)S(1)} %add_convert_fusion.3.refs_0_), channel_id=1, source_target_pairs={{0,1},{1,0},{2,3},{3,2},{4,5},{5,4},{6,7},{7,6},{8,9},{9,8},{10,11... | collective-permute-start | bytes 746504 | tf_op jit(solution)/shard_map/ppermute | solution.py:288
  64.4 9.0 %collective-permute-start.20 = (bf16[972,128]{1,0:T(8,128)(2,1)S(1)}, bf16[972,128]{1,0:T(8,128)(2,1)S(1)}, u32[]{:S(2)}, u32[]{:S(2)}) collective-permute-start(bf16[972,128]{1,0:T(8,128)(2,1)S(1)} %collective-permute-done.16.refs_3_), channel_id=1, source_target_pairs={{0,1},{1,0},{2,3},{3,2},{4,5},{5,4},{6,7},{7,6},{8,9},{9,8},{10,11... | collective-permute-start | bytes 746504 | tf_op jit(solution)/shard_map/ppermute | solution.py:288
  66.6 12.0 %collective-permute-start.19 = (bf16[972,128]{1,0:T(8,128)(2,1)S(1)}, bf16[972,128]{1,0:T(8,128)(2,1)S(1)}, u32[]{:S(2)}, u32[]{:S(2)}) collective-permute-start(bf16[972,128]{1,0:T(8,128)(2,1)S(1)} %collective-permute-done.14.refs_2_), channel_id=1, source_target_pairs={{0,1},{1,0},{2,3},{3,2},{4,5},{5,4},{6,7},{7,6},{8,9},{9,8},{10,11... | collective-permute-start | bytes 746504 | tf_op jit(solution)/shard_map/ppermute | solution.py:288
  71.3 10.3 %collective-permute-start.18 = (bf16[972,128]{1,0:T(8,128)(2,1)S(1)}, bf16[972,128]{1,0:T(8,128)(2,1)S(1)}, u32[]{:S(2)}, u32[]{:S(2)}) collective-permute-start(bf16[972,128]{1,0:T(8,128)(2,1)S(1)} %collective-permute-done.12.refs_1_), channel_id=1, source_target_pairs={{0,1},{1,0},{2,3},{3,2},{4,5},{5,4},{6,7},{7,6},{8,9},{9,8},{10,11... | collective-permute-start | bytes 746504 | tf_op jit(solution)/shard_map/ppermute | solution.py:288

commit v3 on v2

--- a/solution.py
+++ b/solution.py
@@ -14,6 +14,8 @@
 SUB = 8
 LANES = 128
 MIB = 1 << 20
+CUT_MIB = 50
+OUT_ROWS = 2048
 
 smoothing = 1.0
 sparsity = 3.0
@@ -49,21 +51,28 @@
     return pltpu.CompilerParams(vmem_limit_bytes=mib * MIB)
 
 
-def cut_kernel(above, offsets, frames, *refs):
-    out, strip, flat, sem = refs[-4:]
+def cut_kernel(above, places, frames, *refs):
+    out, token, strip, flat, sems = refs[-5:]
     channels, rows_here, wide, count = frames.shape
     column = lax.axis_index("map")
-    top, left = offsets[column, 0], offsets[column, 1]
+    top, left = places[0, column], places[1, column]
     base = jnp.minimum(left // 16 * 16, wide - STRIP)
     base = pl.multiple_of(base, 16)
     first = jnp.minimum(top, rows_here - FIELD) if above else 0
-    copy = pltpu.make_async_copy(
-        frames.at[:, pl.ds(first, FIELD), pl.ds(base, STRIP), :], strip, sem
-    )
-    copy.start()
-    copy.wait()
+    copies = [
+        pltpu.make_async_copy(
+            frames.at[channel, pl.ds(first, FIELD), pl.ds(base, STRIP), :],
+            strip.at[channel],
+            sems.at[channel],
+        )
+        for channel in range(channels)
+    ]
+    for copy in copies:
+        copy.start()
+    token[...] = jnp.zeros_like(token)
     back = lax.rem(STRIP - (left - base), STRIP)
     for channel in range(channels):
+        copies[channel].wait()
         for r in range(FIELD):
             row = top + r - (first if above else rows_here)
             valid = (row < FIELD) if above else (row >= 0)
@@ -76,26 +85,29 @@
     out[...] = flat[pl.ds(0, inner), :].astype(BF16)
 
 
-def cut(frames, offsets, above, after=()):
+def cut(frames, places, above, after=()):
     channels, rows_here, wide, count = frames.shape
     inner = channels * FIELD * FIELD
     return pl.pallas_call(
         functools.partial(cut_kernel, above),
-        out_shape=jax.ShapeDtypeStruct((inner, count), BF16),
+        out_shape=[
+            jax.ShapeDtypeStruct((inner, count), BF16),
+            jax.ShapeDtypeStruct((SUB, LANES), F32),
+        ],
         in_specs=[SMEM, HBM] + [ANY] * len(after),
-        out_specs=VMEM,
+        out_specs=[VMEM] * 2,
         scratch_shapes=[
             pltpu.VMEM((channels, FIELD, STRIP, count), BF16),
             pltpu.VMEM((inner + 12, count), F32),
-            pltpu.SemaphoreType.DMA,
-        ],
-        compiler_params=params(16 if above else 58),
+            pltpu.SemaphoreType.DMA((channels,)),
+        ],
+        compiler_params=params(CUT_MIB),
         name="cut_above" if above else "cut_below",
-    )(offsets, frames, *after)
-
-
-def blocks_kernel(rows_y, dps, flat, after, *refs):
-    outs, wide = refs[:-1], refs[-1]
+    )(places, frames, *after)
+
+
+def blocks_kernel(rows_y, dps, flat, *refs):
+    outs, wide = refs[-1 - rows_y : -1], refs[-1]
     inner = outs[0].shape[0]
     y, d = lax.axis_index("map") // CORES, lax.axis_index("dp")
     wide[...] = flat[...].astype(F32)
@@ -104,18 +116,18 @@
         outs[s][...] = wide[pl.ds(column, inner, stride=rows_y * dps), :].astype(BF16)
 
 
-def blocks(weights, rows_y, dps, after):
+def blocks(weights, rows_y, dps, after=()):
     num_cols, inner, here = weights.shape
     flat = weights.transpose(1, 0, 2).reshape(inner * num_cols, here)
     return pl.pallas_call(
         functools.partial(blocks_kernel, rows_y, dps),
         out_shape=[jax.ShapeDtypeStruct((inner, here), BF16)] * rows_y,
-        in_specs=[VMEM, ANY],
+        in_specs=[VMEM] + [ANY] * len(after),
         out_specs=[VMEM] * rows_y,
         scratch_shapes=[pltpu.VMEM(flat.shape, F32)],
         compiler_params=params(16),
         name="blocks",
-    )(flat, after)
+    )(flat, *after)
 
 
 def filters_kernel(own, other, weight, turned):
@@ -246,38 +258,75 @@
     )(pe, mr)
 
 
-def finish_kernel(rows_y, dps, *refs):
-    arrived, crossed = refs[:rows_y], refs[rows_y : 2 * rows_y]
-    weights, grad, fresh, full = refs[2 * rows_y :]
-    inner = arrived[0].shape[0]
-    num_cols = rows_y * dps
+def place_pieces(full, shifts, refs, rows_y, dps):
     y, d = lax.axis_index("map") // CORES, lax.axis_index("dp")
-    for s in range(rows_y):
+    inner = refs[0].shape[0]
+    for n, s in enumerate(shifts):
         row = lax.rem(y + rows_y - s, rows_y)
-        for block, part in ((arrived[s], d), (crossed[s], 1 - d)):
-            full[pl.ds(dps * row + part, inner, stride=num_cols), :] = block[...].astype(F32)
-    some = inner * num_cols // dps
-    grad[...] = full[pl.ds(pl.multiple_of(d * some, SUB), some), :]
-    fresh[...] = (weights[...].astype(F32) - learn_rate * full[...]).astype(BF16)
-
-
-def finish(arrived, crossed, weights, dps):
-    inner, here = arrived[0].shape
-    num_cols = weights.shape[0]
+        for block, part in ((refs[2 * n], d), (refs[2 * n + 1], 1 - d)):
+            at = pl.ds(dps * row + part, inner, stride=rows_y * dps)
+            full[at, :] = block[...].astype(F32)
+
+
+def gather_kernel(rows_y, dps, shifts, *refs):
+    place_pieces(refs[-1], shifts, refs[:-1], rows_y, dps)
+
+
+def gather(pieces, shifts, rows_y, dps):
+    inner, here = pieces[0].shape
+    return pl.pallas_call(
+        functools.partial(gather_kernel, rows_y, dps, shifts),
+        out_shape=jax.ShapeDtypeStruct((inner * rows_y * dps, here), F32),
+        in_specs=[VMEM] * len(pieces),
+        out_specs=VMEM,
+        compiler_params=params(8),
+        name="gather",
+    )(*pieces)
+
+
+def finish_kernel(rows_y, dps, shifts, *refs):
+    pieces, weights, early = refs[: 2 * len(shifts)], refs[-8], refs[-7]
+    grad, fresh, full, new, grad_sem, sems = refs[-6:]
+    full[...] = early[...]
+    place_pieces(full, shifts, pieces, rows_y, dps)
+    rows = full.shape[0]
+    some = rows // dps
+    at = pl.multiple_of(lax.axis_index("dp") * some, SUB)
+    grad_copy = pltpu.make_async_copy(full.at[pl.ds(at, some), :], grad, grad_sem)
+    grad_copy.start()
+    copies = []
+    for n, low in enumerate(range(0, rows, OUT_ROWS)):
+        part = pl.ds(low, min(OUT_ROWS, rows - low))
+        new[part, :] = (weights[part, :].astype(F32) - learn_rate * full[part, :]).astype(BF16)
+        copy = pltpu.make_async_copy(new.at[part, :], fresh.at[part, :], sems.at[n])
+        copy.start()
+        copies.append(copy)
+    grad_copy.wait()
+    for copy in copies:
+        copy.wait()
+
+
+def finish(pieces, shifts, weights, full, rows_y, dps):
+    num_cols, inner, here = weights.shape
     rows = inner * num_cols
     flat = weights.transpose(1, 0, 2).reshape(rows, here)
     grad, fresh = pl.pallas_call(
-        functools.partial(finish_kernel, len(arrived), dps),
+        functools.partial(finish_kernel, rows_y, dps, shifts),
         out_shape=[
             jax.ShapeDtypeStruct((rows // dps, here), F32),
             jax.ShapeDtypeStruct((rows, here), BF16),
         ],
-        in_specs=[VMEM] * (2 * len(arrived) + 1),
-        out_specs=[VMEM] * 2,
-        scratch_shapes=[pltpu.VMEM((rows, here), F32)],
-        compiler_params=params(32),
+        in_specs=[VMEM] * (len(pieces) + 2),
+        out_specs=[HBM, HBM],
+        scratch_shapes=[
+            pltpu.VMEM((rows, here), F32),
+            pltpu.VMEM((rows, here), BF16),
+            pltpu.SemaphoreType.DMA,
+            pltpu.SemaphoreType.DMA((-(-rows // OUT_ROWS),)),
+        ],
+        compiler_params=params(16),
         name="finish",
-    )(*arrived, *crossed, flat)
+    )(*pieces, flat, full)
     grad = grad.reshape(inner // dps, num_cols, here).transpose(1, 0, 2)
     return grad, fresh.reshape(inner, num_cols, here).transpose(1, 0, 2)
 
@@ -287,10 +336,12 @@
     def send(x, move):
         return lax.ppermute(x, AXES, table(mesh_shape, move))
 
-    upper_offsets = send(offsets, lambda t, y, k, d: (t + 1, y, k, d))
-    below = cut(frames, upper_offsets, False)
-    own = blocks(weights, rows_y, mesh_shape[2], below)
-    above = cut(frames, offsets, True, own[:1])
+    dps = mesh_shape[2]
+    places = offsets.T
+    upper = send(places, lambda t, y, k, d: (t + 1, y, k, d))
+    below, token = cut(frames, upper, False)
+    own = blocks(weights, rows_y, dps, (token,))
+    above, token = cut(frames, places, True, (own[0],))
     below = send(below, lambda t, y, k, d: (t - 1, y, d, k))
     above_in = send(above, lambda t, y, k, d: (t, y, d, k) if k != d else None)
 
@@ -306,16 +357,17 @@
 
     pe, mr = column(above, above_in, below, weight, turned)
 
-    arrived, crossed = [], []
-    for s in range(rows_y):
+    pieces = {}
+    for s in (1, 0, 3, 2):
         home, away = piece(s, pe, mr)
         away = send(away, lambda t, y, k, d: (t, y, 1 - k, d))
         block = (home + away.astype(F32)).astype(BF16)
         if s:
             block = send(block, lambda t, y, k, d: (t, y + s, k, d))
-        arrived.append(block)
-        crossed.append(send(block, lambda t, y, k, d: (t, y, k, 1 - d)))
-    return finish(arrived, crossed, weights, mesh_shape[2])
+        pieces[s] = [block, send(block, lambda t, y, k, d: (t, y, k, 1 - d))]
+    early, late = (0, 1, 3), (2,)
+    full = gather(sum([pieces[s] for s in early], []), early, rows_y, dps)
+    return finish(sum([pieces[s] for s in late], []), late, weights, full, rows_y, dps)
 
 
 def solution(mesh):

time: 86.2 us -> 81.9 us (0.950)
  local copies, waits for them, and re-layouts: 4.02 us -> 0.01 us
  waiting for transfers between devices: 38.3 us -> 40.2 us
  Pallas kernels: 19.4 us -> 17.9 us
    unnamed x11 -> x4, local copies, waits for them, and re-layouts: 4.02 us -> 0.01 us
    ppermute x21, waiting for transfers between devices: 38.3 us -> 40.2 us  [send(): return lax.ppermute(x, AXES, table(mesh_shape, move))]
    pallas_call x3 -> x4, Pallas kernels: 10.8 us -> 9.29 us  [the longest x2 5.98 us: cut(): pl.pallas_call(functools.partial(cut_kernel, above), out_shape=[jax.Shape...]
  transfers between devices with their start and end apart: 21 -> 21, of which waited for: 13 -> 10; matrix products, arithmetic and copies ran while one was open for 0% -> 0% of each run, Pallas kernels for 6% -> 8%
where the time goes in v3:
time: 81.9 us; the launch traced here: 81.7 us
  waiting for transfers between devices  40.2 us (49%)
  starting transfers between devices  22.3 us (27%)
  Pallas kernels  17.9 us (22%)
  between operations  1 us (1%)
    ppermute x21, waiting for transfers between devices, send(): return lax.ppermute(x, AXES, table(mesh_shape, move))  40.2 us
    ppermute x21, starting transfers between devices, send(): return lax.ppermute(x, AXES, table(mesh_shape, move))  22.3 us
    pallas_call x2, Pallas kernels, cut(): pl.pallas_call(functools.partial(cut_kernel, above), out_shape=[jax.Shape...  5.98 us
    pallas_call x1, Pallas kernels, column(): pl.pallas_call(functools.partial(column_kernel, rows_y), out_shape=[jax.S...  4.38 us
    pallas_call x1, Pallas kernels, finish(): pl.pallas_call(functools.partial(finish_kernel, rows_y, dps, shifts), out...  2.5 us
    pallas_call x4, Pallas kernels, piece(): pl.pallas_call(functools.partial(piece_kernel, p, 1.0 / depth), out_shape...  2.43 us
  transfers between devices with their start and end apart: 21, of which 10 were waited for; matrix products, arithmetic and copies ran while one was open for 0% of the time, Pallas kernels for 8%

profile of v3, /device:TPU:4, one launch (start us, length us, event | category | flops | bytes accessed | tf_op | source)
XLA Modules:
  0.0 81.7 jit_solution(11227195496559864547)
XLA Ops:
  0.6 4.0 %collective-permute-start = (s32[2,8]{1,0:T(2,128)}, s32[2,8]{1,0:T(2,128)S(1)}, u32[]{:S(2)}, u32[]{:S(2)}) collective-permute-start(s32[2,8]{1,0:T(2,128)} %bitcast.12), channel_id=1, source_target_pairs={{0,16},{1,17},{2,18},{3,19},{4,20},{5,21},{6,22},{7,23},{8,24},{9,... | collective-permute-start | bytes 200 | tf_op jit(solution)/shard_map/ppermute | solution.py:337
  4.6 5.6 %collective-permute-done.places = s32[2,8]{1,0:T(2,128)S(1)} collective-permute-done((s32[2,8]{1,0:T(2,128)}, s32[2,8]{1,0:T(2,128)S(1)}, u32[]{:S(2)}, u32[]{:S(2)}) %collective-permute-start) | collective-permute-done | bytes 96 | tf_op jit(solution)/shard_map/ppermute | solution.py:337
  10.2 2.9 %cut_below.1 = (bf16[972,384]{1,0:T(8,128)(2,1)S(1)}, f32[8,128]{1,0:T(8,128)S(1)}) custom-call(s32[2,8]{1,0:T(2,128)S(1)} %collective-permute-done.places, bf16[3,20,128,384]{3,2,1,0:T(8,128)(2,1)} %frames.3), custom_call_target="tpu_custom_call" | custom-call | tf_op jit(solution)/shard_map/cut_below/pallas_call | solution.py:91
  13.2 0.8 blocks.1
  14.0 3.1 %collective-permute-start.4 = (bf16[972,128]{1,0:T(8,128)(2,1)S(1)}, bf16[972,128]{1,0:T(8,128)(2,1)S(1)}, u32[]{:S(2)}, u32[]{:S(2)}) collective-permute-start(bf16[972,128]{1,0:T(8,128)(2,1)S(1)} %get-tuple-element.34), channel_id=1, source_target_pairs={{0,12},{1,13},{2,14},{3,15},{4,0},{5,1},{6,2},{7,3},{8,4},{9,5},{1... | collective-permute-start | bytes 746504 | tf_op jit(solution)/shard_map/ppermute | solution.py:337
  17.1 3.9 %collective-permute-start.2 = (bf16[972,384]{1,0:T(8,128)(2,1)S(1)}, bf16[972,384]{1,0:T(8,128)(2,1)S(1)}, u32[]{:S(2)}, u32[]{:S(2)}) collective-permute-start(bf16[972,384]{1,0:T(8,128)(2,1)S(1)} %get-tuple-element.32), channel_id=1, source_target_pairs={{16,0},{17,2},{18,1},{19,3},{20,4},{21,6},{22,5},{23,7},{24,8},{25... | collective-permute-start | bytes 2239496 | tf_op jit(solution)/shard_map/ppermute | solution.py:337
  21.0 3.0 %cut_above.1 = (bf16[972,384]{1,0:T(8,128)(2,1)S(1)}, f32[8,128]{1,0:T(8,128)}) custom-call(s32[2,8]{1,0:T(2,128)S(1)} %bitcast.13, bf16[3,20,128,384]{3,2,1,0:T(8,128)(2,1)} %frames.3, bf16[972,128]{1,0:T(8,128)(2,1)S(1)} %get-tuple-element.30.refs_0_.own), custom_call_target="tpu_custom_call" | custom-call | tf_op jit(solution)/shard_map/cut_above/pallas_call | solution.py:91
  24.1 0.7 collective-permute-start.1
  24.8 0.1 collective-permute-start.8
  24.9 2.2 %collective-permute-start.6 = (bf16[972,128]{1,0:T(8,128)(2,1)S(1)}, bf16[972,128]{1,0:T(8,128)(2,1)S(1)}, u32[]{:S(2)}, u32[]{:S(2)}) collective-permute-start(bf16[972,128]{1,0:T(8,128)(2,1)S(1)} %get-tuple-element.36), channel_id=1, source_target_pairs={{0,8},{1,9},{2,10},{3,11},{4,12},{5,13},{6,14},{7,15},{8,0},{9,1},... | collective-permute-start | bytes 746504 | tf_op jit(solution)/shard_map/ppermute | solution.py:337
  27.1 0.9 %collective-permute-start.3 = (bf16[972,128]{1,0:T(8,128)(2,1)S(1)}, bf16[972,128]{1,0:T(8,128)(2,1)S(1)}, u32[]{:S(2)}, u32[]{:S(2)}) collective-permute-start(bf16[972,128]{1,0:T(8,128)(2,1)S(1)} %get-tuple-element.30.refs_0_.own), channel_id=1, source_target_pairs={{0,2},{1,3},{2,0},{3,1},{4,6},{5,7},{6,4},{7,5},{8,10},{9,11},{10,... | collective-permute-start | bytes 746504 | tf_op jit(solution)/shard_map/ppermute | solution.py:337
  27.9 12.1 %collective-permute-done.8.own = bf16[972,128]{1,0:T(8,128)(2,1)S(1)} collective-permute-done((bf16[972,128]{1,0:T(8,128)(2,1)S(1)}, bf16[972,128]{1,0:T(8,128)(2,1)S(1)}, u32[]{:S(2)}, u32[]{:S(2)}) %collective-permute-start.8) | collective-permute-done | bytes 248864 | tf_op jit(solution)/shard_map/ppermute | solution.py:337
  40.0 0.2 collective-permute-start.9
  40.2 0.3 collective-permute-start.7
  40.5 0.2 collective-permute-start.5
  40.7 0.3 filters.4
  40.9 0.6 collective-permute-done.9.other
  41.5 0.2 filters.7
  41.7 0.1 collective-permute-done.7.other
  41.8 0.2 filters.6
  42.1 0.1 collective-permute-done.5.other
  42.2 0.2 filters.5
  42.5 4.4 %column.1 = (bf16[972,768]{1,0:T(8,128)(2,1)S(1)}, bf16[1024,768]{1,0:T(8,128)(2,1)S(1)}) custom-call(bf16[972,384]{1,0:T(8,128)(2,1)S(1)} %get-tuple-element.31.above, bf16[972,384]{1,0:T(8,128)(2,1)S(1)} %collective-permute-done.1.above_in, bf16[972,384]{1,0:T(8,128)(2,1)S(1)} %collective-permute-done.2.below, ...), custom_call_target="tpu_custom_call" | custom-call | tf_op jit(solution)/shard_map/column/pallas_call | solution.py:212
  46.9 0.6 piece.7
  47.5 0.3 collective-permute-start.18
  47.7 0.6 piece.6
  48.3 0.6 piece.5
  49.0 0.6 piece.4
  49.6 0.4 collective-permute-start.15
  50.0 0.2 collective-permute-start.13
  50.2 0.3 collective-permute-start.10
  50.5 0.1 add_convert_fusion
  50.6 0.1 collective-permute-start.19
  50.7 0.5 collective-permute-done.15
  51.2 0.1 add_convert_fusion.1
  51.2 1.6 %collective-permute-start.16 = (bf16[972,128]{1,0:T(8,128)(2,1)S(1)}, bf16[972,128]{1,0:T(8,128)(2,1)S(1)}, u32[]{:S(2)}, u32[]{:S(2)}) collective-permute-start(bf16[972,128]{1,0:T(8,128)(2,1)S(1)} %add_convert_fusion.1), channel_id=1, source_target_pairs={{0,4},{1,5},{2,6},{3,7},{4,8},{5,9},{6,10},{7,11},{8,12},{9,13},{1... | collective-permute-start | bytes 746504 | tf_op jit(solution)/shard_map/ppermute | solution.py:337
  52.9 0.1 collective-permute-start.11
  53.0 0.1 add_convert_fusion.2.refs_0_
  53.1 1.3 %collective-permute-start.14 = (bf16[972,128]{1,0:T(8,128)(2,1)S(1)}, bf16[972,128]{1,0:T(8,128)(2,1)S(1)}, u32[]{:S(2)}, u32[]{:S(2)}) collective-permute-start(bf16[972,128]{1,0:T(8,128)(2,1)S(1)} %add_convert_fusion.2.refs_0_), channel_id=1, source_target_pairs={{0,1},{1,0},{2,3},{3,2},{4,5},{5,4},{6,7},{7,6},{8,9},{9,8},{10,11... | collective-permute-start | bytes 746504 | tf_op jit(solution)/shard_map/ppermute | solution.py:337
  54.4 5.2 %collective-permute-done.19.refs_4_ = bf16[972,128]{1,0:T(8,128)(2,1)S(1)} collective-permute-done((bf16[972,128]{1,0:T(8,128)(2,1)S(1)}, bf16[972,128]{1,0:T(8,128)(2,1)S(1)}, u32[]{:S(2)}, u32[]{:S(2)}) %collective-permute-start.19) | collective-permute-done | bytes 248864 | tf_op jit(solution)/shard_map/ppermute | solution.py:337
  59.5 0.5 collective-permute-start.20
  60.1 6.1 %collective-permute-done.16.refs_2_ = bf16[972,128]{1,0:T(8,128)(2,1)S(1)} collective-permute-done((bf16[972,128]{1,0:T(8,128)(2,1)S(1)}, bf16[972,128]{1,0:T(8,128)(2,1)S(1)}, u32[]{:S(2)}, u32[]{:S(2)}) %collective-permute-start.16) | collective-permute-done | bytes 248864 | tf_op jit(solution)/shard_map/ppermute | solution.py:337
  66.2 0.5 collective-permute-start.17
  66.7 1.5 %collective-permute-start.12 = (bf16[972,128]{1,0:T(8,128)(2,1)S(1)}, bf16[972,128]{1,0:T(8,128)(2,1)S(1)}, u32[]{:S(2)}, u32[]{:S(2)}) collective-permute-start(bf16[972,128]{1,0:T(8,128)(2,1)S(1)} %collective-permute-done.11.refs_0_), channel_id=1, source_target_pairs={{0,1},{1,0},{2,3},{3,2},{4,5},{5,4},{6,7},{7,6},{8,9},{9,8},{10,11... | collective-permute-start | bytes 746504 | tf_op jit(solution)/shard_map/ppermute | solution.py:337
  68.2 6.9 %collective-permute-done.17.refs_3_ = bf16[972,128]{1,0:T(8,128)(2,1)S(1)} collective-permute-done((bf16[972,128]{1,0:T(8,128)(2,1)S(1)}, bf16[972,128]{1,0:T(8,128)(2,1)S(1)}, u32[]{:S(2)}, u32[]{:S(2)}) %collective-permute-start.17) | collective-permute-done | bytes 248864 | tf_op jit(solution)/shard_map/ppermute | solution.py:337
  75.1 0.8 gather.1.refs_3_
  76.0 3.0 %collective-permute-done.12.refs_1_ = bf16[972,128]{1,0:T(8,128)(2,1)S(1)} collective-permute-done((bf16[972,128]{1,0:T(8,128)(2,1)S(1)}, bf16[972,128]{1,0:T(8,128)(2,1)S(1)}, u32[]{:S(2)}, u32[]{:S(2)}) %collective-permute-start.12) | collective-permute-done | bytes 248864 | tf_op jit(solution)/shard_map/ppermute | solution.py:337
  79.0 2.5 %finish.1 = (f32[3888,128]{1,0:T(8,128)}, bf16[7776,128]{1,0:T(8,128)(2,1)}) custom-call(bf16[972,128]{1,0:T(8,128)(2,1)S(1)} %collective-permute-done.11.refs_0_, bf16[972,128]{1,0:T(8,128)(2,1)S(1)} %collective-permute-done.12.refs_1_, bf16[7776,128]{1,0:T(8,128)(2,1)S(1)} %bitcast.11, f32[7776,128]{1,0:T(8,128)S(1)} %gather.1.refs_3_), custom_call_target="tpu_custom_call" | custom-call | tf_op jit(solution)/shard_map/finish/pallas_call | solution.py:313
  (16 shorter events, 0.1 us)
Async XLA Ops:
  0.6 12.6 %copy-start = (bf16[8,972,128]{2,0,1:T(8,128)(2,1)S(1)}, bf16[8,972,128]{2,0,1:T(8,128)(2,1)}, u32[]{:S(2)}) copy-start(bf16[8,972,128]{2,0,1:T(8,128)(2,1)} %param.4) | copy-start | bytes 5971972
  0.6 9.6 %collective-permute-start = (s32[2,8]{1,0:T(2,128)}, s32[2,8]{1,0:T(2,128)S(1)}, u32[]{:S(2)}, u32[]{:S(2)}) collective-permute-start(s32[2,8]{1,0:T(2,128)} %bitcast.12), channel_id=1, source_target_pairs={{0,16},{1,17},{2,18},{3,19},{4,20},{5,21},{6,22},{7,23},{8,24},{9,... | collective-permute-start | bytes 200 | tf_op jit(solution)/shard_map/ppermute | solution.py:337
  13.2 7.8 %copy-start.1 = (s32[8,2]{0,1:T(2,128)S(1)}, s32[8,2]{0,1:T(2,128)}, u32[]{:S(2)}) copy-start(s32[8,2]{0,1:T(2,128)} %param.5) | copy-start | bytes 196
  14.0 13.1 %collective-permute-start.4 = (bf16[972,128]{1,0:T(8,128)(2,1)S(1)}, bf16[972,128]{1,0:T(8,128)(2,1)S(1)}, u32[]{:S(2)}, u32[]{:S(2)}) collective-permute-start(bf16[972,128]{1,0:T(8,128)(2,1)S(1)} %get-tuple-element.34), channel_id=1, source_target_pairs={{0,12},{1,13},{2,14},{3,15},{4,0},{5,1},{6,2},{7,3},{8,4},{9,5},{1... | collective-permute-start | bytes 746504 | tf_op jit(solution)/shard_map/ppermute | solution.py:337
  17.1 25.4 %collective-permute-start.2 = (bf16[972,384]{1,0:T(8,128)(2,1)S(1)}, bf16[972,384]{1,0:T(8,128)(2,1)S(1)}, u32[]{:S(2)}, u32[]{:S(2)}) collective-permute-start(bf16[972,384]{1,0:T(8,128)(2,1)S(1)} %get-tuple-element.32), channel_id=1, source_target_pairs={{16,0},{17,2},{18,1},{19,3},{20,4},{21,6},{22,5},{23,7},{24,8},{25... | collective-permute-start | bytes 2239496 | tf_op jit(solution)/shard_map/ppermute | solution.py:337
  24.1 18.4 %collective-permute-start.1 = (bf16[972,384]{1,0:T(8,128)(2,1)S(1)}, bf16[972,384]{1,0:T(8,128)(2,1)S(1)}, u32[]{:S(2)}, u32[]{:S(2)}) collective-permute-start(bf16[972,384]{1,0:T(8,128)(2,1)S(1)} %get-tuple-element.31.above), channel_id=1, source_target_pairs={{1,2},{2,1},{5,6},{6,5},{9,10},{10,9},{13,14},{14,13},{17,18},{18,... | collective-permute-start | bytes 2239496 | tf_op jit(solution)/shard_map/ppermute | solution.py:337
  24.8 15.2 %collective-permute-start.8 = (bf16[972,128]{1,0:T(8,128)(2,1)S(1)}, bf16[972,128]{1,0:T(8,128)(2,1)S(1)}, u32[]{:S(2)}, u32[]{:S(2)}) collective-permute-start(bf16[972,128]{1,0:T(8,128)(2,1)S(1)} %get-tuple-element.38), channel_id=1, source_target_pairs={{0,4},{1,5},{2,6},{3,7},{4,8},{5,9},{6,10},{7,11},{8,12},{9,13},{1... | collective-permute-start | bytes 746504 | tf_op jit(solution)/shard_map/ppermute | solution.py:337
  24.9 15.3 %collective-permute-start.6 = (bf16[972,128]{1,0:T(8,128)(2,1)S(1)}, bf16[972,128]{1,0:T(8,128)(2,1)S(1)}, u32[]{:S(2)}, u32[]{:S(2)}) collective-permute-start(bf16[972,128]{1,0:T(8,128)(2,1)S(1)} %get-tuple-element.36), channel_id=1, source_target_pairs={{0,8},{1,9},{2,10},{3,11},{4,12},{5,13},{6,14},{7,15},{8,0},{9,1},... | collective-permute-start | bytes 746504 | tf_op jit(solution)/shard_map/ppermute | solution.py:337
  27.1 13.4 %collective-permute-start.3 = (bf16[972,128]{1,0:T(8,128)(2,1)S(1)}, bf16[972,128]{1,0:T(8,128)(2,1)S(1)}, u32[]{:S(2)}, u32[]{:S(2)}) collective-permute-start(bf16[972,128]{1,0:T(8,128)(2,1)S(1)} %get-tuple-element.30.refs_0_.own), channel_id=1, source_target_pairs={{0,2},{1,3},{2,0},{3,1},{4,6},{5,7},{6,4},{7,5},{8,10},{9,11},{10,... | collective-permute-start | bytes 746504 | tf_op jit(solution)/shard_map/ppermute | solution.py:337
  40.0 1.5 %collective-permute-start.9 = (bf16[972,128]{1,0:T(8,128)(2,1)S(1)}, bf16[972,128]{1,0:T(8,128)(2,1)S(1)}, u32[]{:S(2)}, u32[]{:S(2)}) collective-permute-start(bf16[972,128]{1,0:T(8,128)(2,1)S(1)} %collective-permute-done.8.own), channel_id=1, source_target_pairs={{0,2},{1,3},{2,0},{3,1},{4,6},{5,7},{6,4},{7,5},{8,10},{9,11},{10,... | collective-permute-start | bytes 746504 | tf_op jit(solution)/shard_map/ppermute | solution.py:337
  40.2 1.7 %collective-permute-start.7 = (bf16[972,128]{1,0:T(8,128)(2,1)S(1)}, bf16[972,128]{1,0:T(8,128)(2,1)S(1)}, u32[]{:S(2)}, u32[]{:S(2)}) collective-permute-start(bf16[972,128]{1,0:T(8,128)(2,1)S(1)} %collective-permute-done.6.own), channel_id=1, source_target_pairs={{0,2},{1,3},{2,0},{3,1},{4,6},{5,7},{6,4},{7,5},{8,10},{9,11},{10,... | collective-permute-start | bytes 746504 | tf_op jit(solution)/shard_map/ppermute | solution.py:337
  40.5 1.7 %collective-permute-start.5 = (bf16[972,128]{1,0:T(8,128)(2,1)S(1)}, bf16[972,128]{1,0:T(8,128)(2,1)S(1)}, u32[]{:S(2)}, u32[]{:S(2)}) collective-permute-start(bf16[972,128]{1,0:T(8,128)(2,1)S(1)} %collective-permute-done.4.own), channel_id=1, source_target_pairs={{0,2},{1,3},{2,0},{3,1},{4,6},{5,7},{6,4},{7,5},{8,10},{9,11},{10,... | collective-permute-start | bytes 746504 | tf_op jit(solution)/shard_map/ppermute | solution.py:337
  47.5 3.0 %collective-permute-start.18 = (bf16[972,128]{1,0:T(8,128)(2,1)S(1)}, bf16[972,128]{1,0:T(8,128)(2,1)S(1)}, u32[]{:S(2)}, u32[]{:S(2)}) collective-permute-start(bf16[972,128]{1,0:T(8,128)(2,1)S(1)} %get-tuple-element.53), channel_id=1, source_target_pairs={{0,2},{1,3},{2,0},{3,1},{4,6},{5,7},{6,4},{7,5},{8,10},{9,11},{10,... | collective-permute-start | bytes 746504 | tf_op jit(solution)/shard_map/ppermute | solution.py:337
  49.6 1.6 %collective-permute-start.15 = (bf16[972,128]{1,0:T(8,128)(2,1)S(1)}, bf16[972,128]{1,0:T(8,128)(2,1)S(1)}, u32[]{:S(2)}, u32[]{:S(2)}) collective-permute-start(bf16[972,128]{1,0:T(8,128)(2,1)S(1)} %get-tuple-element.51), channel_id=1, source_target_pairs={{0,2},{1,3},{2,0},{3,1},{4,6},{5,7},{6,4},{7,5},{8,10},{9,11},{10,... | collective-permute-start | bytes 746504 | tf_op jit(solution)/shard_map/ppermute | solution.py:337
  50.0 3.0 %collective-permute-start.13 = (bf16[972,128]{1,0:T(8,128)(2,1)S(1)}, bf16[972,128]{1,0:T(8,128)(2,1)S(1)}, u32[]{:S(2)}, u32[]{:S(2)}) collective-permute-start(bf16[972,128]{1,0:T(8,128)(2,1)S(1)} %get-tuple-element.49), channel_id=1, source_target_pairs={{0,2},{1,3},{2,0},{3,1},{4,6},{5,7},{6,4},{7,5},{8,10},{9,11},{10,... | collective-permute-start | bytes 746504 | tf_op jit(solution)/shard_map/ppermute | solution.py:337
  50.2 2.7 %collective-permute-start.10 = (bf16[972,128]{1,0:T(8,128)(2,1)S(1)}, bf16[972,128]{1,0:T(8,128)(2,1)S(1)}, u32[]{:S(2)}, u32[]{:S(2)}) collective-permute-start(bf16[972,128]{1,0:T(8,128)(2,1)S(1)} %get-tuple-element.47), channel_id=1, source_target_pairs={{0,2},{1,3},{2,0},{3,1},{4,6},{5,7},{6,4},{7,5},{8,10},{9,11},{10,... | collective-permute-start | bytes 746504 | tf_op jit(solution)/shard_map/ppermute | solution.py:337
  50.6 9.0 %collective-permute-start.19 = (bf16[972,128]{1,0:T(8,128)(2,1)S(1)}, bf16[972,128]{1,0:T(8,128)(2,1)S(1)}, u32[]{:S(2)}, u32[]{:S(2)}) collective-permute-start(bf16[972,128]{1,0:T(8,128)(2,1)S(1)} %add_convert_fusion), channel_id=1, source_target_pairs={{0,12},{1,13},{2,14},{3,15},{4,0},{5,1},{6,2},{7,3},{8,4},{9,5},{1... | collective-permute-start | bytes 746504 | tf_op jit(solution)/shard_map/ppermute | solution.py:337
  51.2 14.9 %collective-permute-start.16 = (bf16[972,128]{1,0:T(8,128)(2,1)S(1)}, bf16[972,128]{1,0:T(8,128)(2,1)S(1)}, u32[]{:S(2)}, u32[]{:S(2)}) collective-permute-start(bf16[972,128]{1,0:T(8,128)(2,1)S(1)} %add_convert_fusion.1), channel_id=1, source_target_pairs={{0,4},{1,5},{2,6},{3,7},{4,8},{5,9},{6,10},{7,11},{8,12},{9,13},{1... | collective-permute-start | bytes 746504 | tf_op jit(solution)/shard_map/ppermute | solution.py:337
  52.9 13.8 %collective-permute-start.11 = (bf16[972,128]{1,0:T(8,128)(2,1)S(1)}, bf16[972,128]{1,0:T(8,128)(2,1)S(1)}, u32[]{:S(2)}, u32[]{:S(2)}) collective-permute-start(bf16[972,128]{1,0:T(8,128)(2,1)S(1)} %add_convert_fusion.3), channel_id=1, source_target_pairs={{0,8},{1,9},{2,10},{3,11},{4,12},{5,13},{6,14},{7,15},{8,0},{9,1},... | collective-permute-start | bytes 746504 | tf_op jit(solution)/shard_map/ppermute | solution.py:337
  53.1 15.1 %collective-permute-start.14 = (bf16[972,128]{1,0:T(8,128)(2,1)S(1)}, bf16[972,128]{1,0:T(8,128)(2,1)S(1)}, u32[]{:S(2)}, u32[]{:S(2)}) collective-permute-start(bf16[972,128]{1,0:T(8,128)(2,1)S(1)} %add_convert_fusion.2.refs_0_), channel_id=1, source_target_pairs={{0,1},{1,0},{2,3},{3,2},{4,5},{5,4},{6,7},{7,6},{8,9},{9,8},{10,11... | collective-permute-start | bytes 746504 | tf_op jit(solution)/shard_map/ppermute | solution.py:337
  59.5 8.7 %collective-permute-start.20 = (bf16[972,128]{1,0:T(8,128)(2,1)S(1)}, bf16[972,128]{1,0:T(8,128)(2,1)S(1)}, u32[]{:S(2)}, u32[]{:S(2)}) collective-permute-start(bf16[972,128]{1,0:T(8,128)(2,1)S(1)} %collective-permute-done.19.refs_4_), channel_id=1, source_target_pairs={{0,1},{1,0},{2,3},{3,2},{4,5},{5,4},{6,7},{7,6},{8,9},{9,8},{10,11... | collective-permute-start | bytes 746504 | tf_op jit(solution)/shard_map/ppermute | solution.py:337
  66.2 9.0 %collective-permute-start.17 = (bf16[972,128]{1,0:T(8,128)(2,1)S(1)}, bf16[972,128]{1,0:T(8,128)(2,1)S(1)}, u32[]{:S(2)}, u32[]{:S(2)}) collective-permute-start(bf16[972,128]{1,0:T(8,128)(2,1)S(1)} %collective-permute-done.16.refs_2_), channel_id=1, source_target_pairs={{0,1},{1,0},{2,3},{3,2},{4,5},{5,4},{6,7},{7,6},{8,9},{9,8},{10,11... | collective-permute-start | bytes 746504 | tf_op jit(solution)/shard_map/ppermute | solution.py:337
  66.7 12.3 %collective-permute-start.12 = (bf16[972,128]{1,0:T(8,128)(2,1)S(1)}, bf16[972,128]{1,0:T(8,128)(2,1)S(1)}, u32[]{:S(2)}, u32[]{:S(2)}) collective-permute-start(bf16[972,128]{1,0:T(8,128)(2,1)S(1)} %collective-permute-done.11.refs_0_), channel_id=1, source_target_pairs={{0,1},{1,0},{2,3},{3,2},{4,5},{5,4},{6,7},{7,6},{8,9},{9,8},{10,11... | collective-permute-start | bytes 746504 | tf_op jit(solution)/shard_map/ppermute | solution.py:337

commit v4 on v3

--- a/solution.py
+++ b/solution.py
@@ -52,11 +52,11 @@
 
 
 def cut_kernel(above, places, frames, *refs):
-    out, token, strip, flat, sems = refs[-5:]
-    channels, rows_here, wide, count = frames.shape
+    out, token, strip, wide, flat, sems = refs[-6:]
+    channels, rows_here, across, count = frames.shape
     column = lax.axis_index("map")
     top, left = places[0, column], places[1, column]
-    base = jnp.minimum(left // 16 * 16, wide - STRIP)
+    base = jnp.minimum(left // 16 * 16, across - STRIP)
     base = pl.multiple_of(base, 16)
     first = jnp.minimum(top, rows_here - FIELD) if above else 0
     copies = [
@@ -70,17 +70,21 @@
     for copy in copies:
         copy.start()
     token[...] = jnp.zeros_like(token)
-    back = lax.rem(STRIP - (left - base), STRIP)
+    shift = left - base
     for channel in range(channels):
         copies[channel].wait()
+        for n in range(count // LANES):
+            lanes = strip[channel, :, :, pl.ds(n * LANES, LANES)]
+            wide[n] = lanes.reshape(FIELD * STRIP, LANES).astype(F32)
         for r in range(FIELD):
             row = top + r - (first if above else rows_here)
             valid = (row < FIELD) if above else (row >= 0)
             row = jnp.clip(row, 0, FIELD - 1)
-            x = strip[channel, row].astype(F32)
-            x = pltpu.roll(x, back, 0)[: FIELD + 6]
-            x = jnp.where(valid, x, 0.0)
-            flat[pl.ds((channel * FIELD + r) * FIELD, FIELD + 6), :] = x
+            for n in range(count // LANES):
+                x = wide[n, pl.ds(row * STRIP + shift, FIELD), :]
+                x = jnp.where(valid, x, 0.0)
+                at = pl.ds((channel * FIELD + r) * FIELD, FIELD)
+                flat[at, pl.ds(n * LANES, LANES)] = x
     inner = channels * FIELD * FIELD
     out[...] = flat[pl.ds(0, inner), :].astype(BF16)
 
@@ -98,7 +102,8 @@
         out_specs=[VMEM] * 2,
         scratch_shapes=[
             pltpu.VMEM((channels, FIELD, STRIP, count), BF16),
-            pltpu.VMEM((inner + 12, count), F32),
+            pltpu.VMEM((count // LANES, FIELD * STRIP, LANES), F32),
+            pltpu.VMEM((inner, count), F32),
             pltpu.SemaphoreType.DMA((channels,)),
         ],
         compiler_params=params(CUT_MIB),
@@ -153,27 +158,41 @@
     )(own, other)
 
 
+def join_kernel(above, above_in, below, patch):
+    mine = lax.rem(lax.axis_index("map"), CORES) == lax.axis_index("dp")
+
+    @pl.when(mine)
+    def _():
+        patch[...] = above[...] + below[...]
+
+    @pl.when(jnp.logical_not(mine))
+    def _():
+        patch[...] = above_in[...] + below[...]
+
+
+def join(above, above_in, below):
+    return pl.pallas_call(
+        join_kernel,
+        out_shape=jax.ShapeDtypeStruct(below.shape, BF16),
+        in_specs=[VMEM] * 3,
+        out_specs=VMEM,
+        compiler_params=params(8),
+        name="join",
+    )(above, above_in, below)
+
+
 def dot(a, b):
     return jnp.dot(a, b, preferred_element_type=F32)
 
 
-def column_kernel(rows_y, above, above_in, below, *refs):
+def column_kernel(rows_y, patch_in, *refs):
     weight, turned = refs[:rows_y], refs[rows_y : 2 * rows_y]
     pe, mr, res, sq, inv = refs[2 * rows_y :]
-    inner, count = above.shape
+    inner, count = patch_in.shape
     tile = weight[0].shape[1]
     maps = rows_y * tile
-    mine = lax.rem(lax.axis_index("map"), CORES) == lax.axis_index("dp")
-
-    @pl.when(mine)
-    def _():
-        pe[:, pl.ds(0, count)] = above[...] + below[...]
-
-    @pl.when(jnp.logical_not(mine))
-    def _():
-        pe[:, pl.ds(0, count)] = above_in[...] + below[...]
-
-    patch = pe[:, pl.ds(0, count)]
+    pe[:, pl.ds(0, count)] = patch_in[...]
+    patch = patch_in[...]
     for m in range(0, maps, tile):
         r = dot(turned[m // tile][...], patch)
         res[pl.ds(m, tile), :] = r
@@ -205,8 +224,8 @@
         mr[pl.ds(m, tile), pl.ds(0, count)] = mixed.astype(BF16)
 
 
-def column(above, above_in, below, weight, turned):
-    inner, count = above.shape
+def column(patch, weight, turned):
+    inner, count = patch.shape
     rows_y = len(weight)
     maps = rows_y * weight[0].shape[1]
     return pl.pallas_call(
@@ -215,7 +234,7 @@
             jax.ShapeDtypeStruct((inner, 2 * count), BF16),
             jax.ShapeDtypeStruct((maps, 2 * count), BF16),
         ],
-        in_specs=[VMEM] * (3 + 2 * rows_y),
+        in_specs=[VMEM] * (1 + 2 * rows_y),
         out_specs=[VMEM] * 2,
         scratch_shapes=[
             pltpu.VMEM((maps, count), F32),
@@ -224,38 +243,81 @@
         ],
         compiler_params=params(40),
         name="column",
-    )(above, above_in, below, *weight, *turned)
-
-
-def piece_kernel(p, scale, pe, mr, home, away):
+    )(patch, *weight, *turned)
+
+
+def padded(rows):
+    return -(-rows // 16) * 16
+
+
+def piece_kernel(shifts, scale, pe, mr, *refs):
+    home, away = refs[-2:]
     inner = pe.shape[0]
     first = lax.rem(lax.axis_index("map"), CORES) == 0
     tile = 256
-    groups = mr[pl.ds(CORES * LANES * p, CORES * LANES), :]
-    for n in range(0, inner, tile):
-        rows = pl.ds(n, min(tile, inner - n))
-        g = lax.dot_general(
-            pe[rows, :], groups, (((1,), (1,)), ((), ())), preferred_element_type=F32
-        )
-        g = g * scale
-        low, high = g[:, :LANES], g[:, LANES:]
-        home[rows, :] = jnp.where(first, low, high)
-        away[rows, :] = jnp.where(first, high, low).astype(BF16)
-
-
-def piece(p, pe, mr):
+    for i, p in enumerate(shifts):
+        groups = mr[pl.ds(CORES * LANES * p, CORES * LANES), :]
+        for n in range(0, inner, tile):
+            size = min(tile, inner - n)
+            g = lax.dot_general(
+                pe[pl.ds(n, size), :], groups, (((1,), (1,)), ((), ())),
+                preferred_element_type=F32,
+            )
+            g = g * scale
+            low, high = g[:, :LANES], g[:, LANES:]
+            rows = pl.ds(i * padded(inner) + n, size)
+            home[rows, :] = jnp.where(first, low, high)
+            away[rows, :] = jnp.where(first, high, low).astype(BF16)
+
+
+def piece(shifts, pe, mr, after=()):
     inner, depth = pe.shape
-    return pl.pallas_call(
-        functools.partial(piece_kernel, p, 1.0 / depth),
+    rows = len(shifts) * padded(inner)
+    return pl.pallas_call(
+        functools.partial(piece_kernel, shifts, 1.0 / depth),
         out_shape=[
-            jax.ShapeDtypeStruct((inner, LANES), F32),
-            jax.ShapeDtypeStruct((inner, LANES), BF16),
-        ],
-        in_specs=[VMEM] * 2,
+            jax.ShapeDtypeStruct((rows, LANES), F32),
+            jax.ShapeDtypeStruct((rows, LANES), BF16),
+        ],
+        in_specs=[VMEM] * 2 + [ANY] * len(after),
         out_specs=[VMEM] * 2,
         compiler_params=params(16),
         name="piece",
-    )(pe, mr)
+    )(pe, mr, *after)
+
+
+def total_kernel(count, home, away, *refs):
+    outs = refs[-count:]
+    inner = outs[0].shape[0]
+    for i, out in enumerate(outs):
+        rows = pl.ds(i * padded(inner), inner)
+        out[...] = (home[rows, :] + away[rows, :].astype(F32)).astype(BF16)
+
+
+def total(home, away, count, inner, after):
+    return pl.pallas_call(
+        functools.partial(total_kernel, count),
+        out_shape=[jax.ShapeDtypeStruct((inner, LANES), BF16)] * count,
+        in_specs=[VMEM] * 2 + [ANY] * len(after),
+        out_specs=[VMEM] * count,
+        compiler_params=params(8),
+        name="total",
+    )(home, away, *after)
+
+
+def follow_kernel(block, after, out):
+    out[...] = block[...]
+
+
+def follow(block, after):
+    return pl.pallas_call(
+        follow_kernel,
+        out_shape=jax.ShapeDtypeStruct(block.shape, block.dtype),
+        in_specs=[VMEM, ANY],
+        out_specs=VMEM,
+        compiler_params=params(4),
+        name="follow",
+    )(block, after)
 
 
 def place_pieces(full, shifts, refs, rows_y, dps):
@@ -339,11 +401,10 @@
     dps = mesh_shape[2]
     places = offsets.T
     upper = send(places, lambda t, y, k, d: (t + 1, y, k, d))
-    below, token = cut(frames, upper, False)
+    above, token = cut(frames, places, True)
+    below, token = cut(frames, upper, False, (token,))
     own = blocks(weights, rows_y, dps, (token,))
-    above, token = cut(frames, places, True, (own[0],))
     below = send(below, lambda t, y, k, d: (t - 1, y, d, k))
-    above_in = send(above, lambda t, y, k, d: (t, y, d, k) if k != d else None)
 
     weight, turned = [], []
     for s in range(rows_y):
@@ -354,17 +415,25 @@
         pair = filters(block, other)
         weight.append(pair[0])
         turned.append(pair[1])
-
-    pe, mr = column(above, above_in, below, weight, turned)
+    above_in = send(above, lambda t, y, k, d: (t, y, d, k) if k != d else None)
+
+    pe, mr = column(join(above, above_in, below), weight, turned)
 
     pieces = {}
-    for s in (1, 0, 3, 2):
-        home, away = piece(s, pe, mr)
+    inner = weights.shape[1]
+    after_piece, after_total = (), ()
+    for shifts in ((0,), (1, 3, 2)):
+        home, away = piece(shifts, pe, mr, after_piece)
+        after_piece = (away,)
         away = send(away, lambda t, y, k, d: (t, y, 1 - k, d))
-        block = (home + away.astype(F32)).astype(BF16)
-        if s:
-            block = send(block, lambda t, y, k, d: (t, y + s, k, d))
-        pieces[s] = [block, send(block, lambda t, y, k, d: (t, y, k, 1 - d))]
+        blocks_here = total(home, away, len(shifts), inner, after_total)
+        after_total = (blocks_here[0],)
+        for s, block in zip(shifts, blocks_here):
+            if s:
+                block = send(block, lambda t, y, k, d: (t, y + s, k, d))
+            if s == 1:
+                block = follow(block, pieces[0][1])
+            pieces[s] = [block, send(block, lambda t, y, k, d: (t, y, k, 1 - d))]
     early, late = (0, 1, 3), (2,)
     full = gather(sum([pieces[s] for s in early], []), early, rows_y, dps)
     return finish(sum([pieces[s] for s in late], []), late, weights, full, rows_y, dps)

time: 81.9 us -> 84.3 us (1.029)
  Pallas kernels: 17.9 us -> 16.4 us
  waiting for transfers between devices: 40.2 us -> 41.7 us
  starting transfers between devices: 22.3 us -> 23.6 us
    ppermute x21 -> x19, waiting for transfers between devices: 40.2 us -> 41.7 us  [send(): return lax.ppermute(x, AXES, table(mesh_shape, move))]
    pallas_call x2, Pallas kernels: 5.98 us -> 4.65 us  [cut(): pl.pallas_call(functools.partial(cut_kernel, above), out_shape=[jax.Shape...]
    ppermute x21 -> x19, starting transfers between devices: 22.3 us -> 23.6 us  [send(): return lax.ppermute(x, AXES, table(mesh_shape, move))]
    pallas_call x4 -> x6, Pallas kernels: 2.43 us -> 2.57 us  [the longest x2 2.06 us: piece(): pl.pallas_call(functools.partial(piece_kernel, shifts, 1.0 / depth), out_...]
  transfers between devices with their start and end apart: 21 -> 19, of which waited for: 10 -> 11; matrix products, arithmetic and copies ran while one was open for 0% -> 0% of each run, Pallas kernels for 8% -> 5%
where the time goes in v4:
time: 84.3 us; the launch traced here: 83.3 us
  waiting for transfers between devices  41.7 us (49%)
  starting transfers between devices  23.6 us (28%)
  Pallas kernels  16.4 us (19%)
  between operations  0.96 us (1%)
    ppermute x19, waiting for transfers between devices, send(): return lax.ppermute(x, AXES, table(mesh_shape, move))  41.7 us
    ppermute x19, starting transfers between devices, send(): return lax.ppermute(x, AXES, table(mesh_shape, move))  23.6 us
    pallas_call x2, Pallas kernels, cut(): pl.pallas_call(functools.partial(cut_kernel, above), out_shape=[jax.Shape...  4.65 us
    pallas_call x1, Pallas kernels, column(): pl.pallas_call(functools.partial(column_kernel, rows_y), out_shape=[jax.S...  4.08 us
    pallas_call x1, Pallas kernels, finish(): pl.pallas_call(functools.partial(finish_kernel, rows_y, dps, shifts), out...  2.5 us
    pallas_call x2, Pallas kernels, piece(): pl.pallas_call(functools.partial(piece_kernel, shifts, 1.0 / depth), out_...  2.06 us
  transfers between devices with their start and end apart: 19, of which 11 were waited for; matrix products, arithmetic and copies ran while one was open for 0% of the time, Pallas kernels for 5%

profile of v4, /device:TPU:4, one launch (start us, length us, event | category | flops | bytes accessed | tf_op | source)
XLA Modules:
  0.0 83.3 jit_solution(540660794405271034)
XLA Ops:
  0.6 3.8 %collective-permute-start.1 = (s32[2,8]{1,0:T(2,128)}, s32[2,8]{1,0:T(2,128)S(1)}, u32[]{:S(2)}, u32[]{:S(2)}) collective-permute-start(s32[2,8]{1,0:T(2,128)} %bitcast.12), channel_id=1, source_target_pairs={{0,16},{1,17},{2,18},{3,19},{4,20},{5,21},{6,22},{7,23},{8,24},{9,... | collective-permute-start | bytes 200 | tf_op jit(solution)/shard_map/ppermute | solution.py:399
  4.5 0.7 copy-done.1
  5.2 2.3 %cut_above.1 = (bf16[972,384]{1,0:T(8,128)(2,1)S(1)}, f32[8,128]{1,0:T(8,128)S(1)}) custom-call(s32[2,8]{1,0:T(2,128)S(1)} %bitcast.13, bf16[3,20,128,384]{3,2,1,0:T(8,128)(2,1)} %frames.3), custom_call_target="tpu_custom_call" | custom-call | tf_op jit(solution)/shard_map/cut_above/pallas_call | solution.py:95
  7.5 2.6 %collective-permute-done.1.places = s32[2,8]{1,0:T(2,128)S(1)} collective-permute-done((s32[2,8]{1,0:T(2,128)}, s32[2,8]{1,0:T(2,128)S(1)}, u32[]{:S(2)}, u32[]{:S(2)}) %collective-permute-start.1) | collective-permute-done | bytes 96 | tf_op jit(solution)/shard_map/ppermute | solution.py:399
  10.1 2.3 %cut_below.1 = (bf16[972,384]{1,0:T(8,128)(2,1)S(1)}, f32[8,128]{1,0:T(8,128)S(1)}) custom-call(s32[2,8]{1,0:T(2,128)S(1)} %collective-permute-done.1.places, bf16[3,20,128,384]{3,2,1,0:T(8,128)(2,1)} %frames.3, f32[8,128]{1,0:T(8,128)S(1)} %get-tuple-element.30.refs_0_), custom_call_target="tpu_custom_call" | custom-call | tf_op jit(solution)/shard_map/cut_below/pallas_call | solution.py:95
  12.4 0.8 blocks.1
  13.2 3.1 %collective-permute-start.4 = (bf16[972,128]{1,0:T(8,128)(2,1)S(1)}, bf16[972,128]{1,0:T(8,128)(2,1)S(1)}, u32[]{:S(2)}, u32[]{:S(2)}) collective-permute-start(bf16[972,128]{1,0:T(8,128)(2,1)S(1)} %get-tuple-element.35), channel_id=1, source_target_pairs={{0,12},{1,13},{2,14},{3,15},{4,0},{5,1},{6,2},{7,3},{8,4},{9,5},{1... | collective-permute-start | bytes 746504 | tf_op jit(solution)/shard_map/ppermute | solution.py:399
  16.3 0.7 collective-permute-start
  17.0 3.9 %collective-permute-start.2 = (bf16[972,384]{1,0:T(8,128)(2,1)S(1)}, bf16[972,384]{1,0:T(8,128)(2,1)S(1)}, u32[]{:S(2)}, u32[]{:S(2)}) collective-permute-start(bf16[972,384]{1,0:T(8,128)(2,1)S(1)} %get-tuple-element.31), channel_id=1, source_target_pairs={{16,0},{17,2},{18,1},{19,3},{20,4},{21,6},{22,5},{23,7},{24,8},{25... | collective-permute-start | bytes 2239496 | tf_op jit(solution)/shard_map/ppermute | solution.py:399
  21.0 0.1 collective-permute-start.8
  21.1 2.2 %collective-permute-start.6 = (bf16[972,128]{1,0:T(8,128)(2,1)S(1)}, bf16[972,128]{1,0:T(8,128)(2,1)S(1)}, u32[]{:S(2)}, u32[]{:S(2)}) collective-permute-start(bf16[972,128]{1,0:T(8,128)(2,1)S(1)} %get-tuple-element.37), channel_id=1, source_target_pairs={{0,8},{1,9},{2,10},{3,11},{4,12},{5,13},{6,14},{7,15},{8,0},{9,1},... | collective-permute-start | bytes 746504 | tf_op jit(solution)/shard_map/ppermute | solution.py:399
  23.3 0.9 %collective-permute-start.3 = (bf16[972,128]{1,0:T(8,128)(2,1)S(1)}, bf16[972,128]{1,0:T(8,128)(2,1)S(1)}, u32[]{:S(2)}, u32[]{:S(2)}) collective-permute-start(bf16[972,128]{1,0:T(8,128)(2,1)S(1)} %get-tuple-element.33.own), channel_id=1, source_target_pairs={{0,2},{1,3},{2,0},{3,1},{4,6},{5,7},{6,4},{7,5},{8,10},{9,11},{10,... | collective-permute-start | bytes 746504 | tf_op jit(solution)/shard_map/ppermute | solution.py:399
  24.1 12.0 %collective-permute-done.8.own = bf16[972,128]{1,0:T(8,128)(2,1)S(1)} collective-permute-done((bf16[972,128]{1,0:T(8,128)(2,1)S(1)}, bf16[972,128]{1,0:T(8,128)(2,1)S(1)}, u32[]{:S(2)}, u32[]{:S(2)}) %collective-permute-start.8) | collective-permute-done | bytes 248864 | tf_op jit(solution)/shard_map/ppermute | solution.py:399
  36.1 0.2 collective-permute-start.9
  36.3 0.0 collective-permute-done.6.own
  36.3 0.3 collective-permute-start.7
  36.7 0.2 collective-permute-start.5
  36.9 0.2 filters.4
  37.1 0.5 collective-permute-done.9.other
  37.7 0.2 filters.7
  37.9 0.1 collective-permute-done.7.other
  38.0 0.2 filters.6
  38.3 0.1 collective-permute-done.5.other
  38.4 0.2 filters.5
  38.6 0.0 collective-permute-done.above_in
  38.6 0.0 collective-permute-done.2.below
  38.6 0.3 join.1.patch_in
  39.0 4.1 %column.1 = (bf16[972,768]{1,0:T(8,128)(2,1)S(1)}, bf16[1024,768]{1,0:T(8,128)(2,1)S(1)}) custom-call(bf16[972,384]{1,0:T(8,128)(2,1)S(1)} %join.1.patch_in, bf16[972,256]{1,0:T(8,128)(2,1)S(1)} %get-tuple-element.34.refs_0_, bf16[972,256]{1,0:T(8,128)(2,1)S(1)} %get-tuple-element.36.refs_1_, bf16[972,256]{1,0:T(8,128)(2,1)S(1)} %get-tuple-element.38.refs_2_, ...), custom_call_target="tpu_custom_call" | custom-call | tf_op jit(solution)/shard_map/column/pallas_call | solution.py:231
  43.1 0.6 piece.2
  43.7 1.5 %piece.3 = (f32[2928,128]{1,0:T(8,128)S(1)}, bf16[2928,128]{1,0:T(8,128)(2,1)S(1)}) custom-call(bf16[972,768]{1,0:T(8,128)(2,1)S(1)} %get-tuple-element.45.pe, bf16[1024,768]{1,0:T(8,128)(2,1)S(1)} %get-tuple-element.46.mr, bf16[976,128]{1,0:T(8,128)(2,1)S(1)} %get-tuple-element.47.refs_0_), custom_call_target="tpu_custom_call" | custom-call | tf_op jit(solution)/shard_map/piece/pallas_call | solution.py:276
  45.1 0.3 collective-permute-start.10
  45.4 0.3 collective-permute-start.11
  45.7 2.1 %collective-permute-done.11.away = bf16[976,128]{1,0:T(8,128)(2,1)S(1)} collective-permute-done((bf16[976,128]{1,0:T(8,128)(2,1)S(1)}, bf16[976,128]{1,0:T(8,128)(2,1)S(1)}, u32[]{:S(2)}, u32[]{:S(2)}) %collective-permute-start.11) | collective-permute-done | bytes 249888 | tf_op jit(solution)/shard_map/ppermute | solution.py:399
  47.9 1.4 %collective-permute-start.14 = (bf16[972,128]{1,0:T(8,128)(2,1)S(1)}, bf16[972,128]{1,0:T(8,128)(2,1)S(1)}, u32[]{:S(2)}, u32[]{:S(2)}) collective-permute-start(bf16[972,128]{1,0:T(8,128)(2,1)S(1)} %total.2.refs_0_), channel_id=1, source_target_pairs={{0,1},{1,0},{2,3},{3,2},{4,5},{5,4},{6,7},{7,6},{8,9},{9,8},{10,11... | collective-permute-start | bytes 746504 | tf_op jit(solution)/shard_map/ppermute | solution.py:399
  49.3 0.0 collective-permute-done.10.away
  49.3 0.1 total.3
  49.4 0.1 collective-permute-start.15
  49.5 3.2 %collective-permute-start.17 = (bf16[972,128]{1,0:T(8,128)(2,1)S(1)}, bf16[972,128]{1,0:T(8,128)(2,1)S(1)}, u32[]{:S(2)}, u32[]{:S(2)}) collective-permute-start(bf16[972,128]{1,0:T(8,128)(2,1)S(1)} %get-tuple-element.53), channel_id=1, source_target_pairs={{0,12},{1,13},{2,14},{3,15},{4,0},{5,1},{6,2},{7,3},{8,4},{9,5},{1... | collective-permute-start | bytes 746504 | tf_op jit(solution)/shard_map/ppermute | solution.py:399
  52.8 3.3 %collective-permute-done.14.after.refs_1_ = bf16[972,128]{1,0:T(8,128)(2,1)S(1)} collective-permute-done((bf16[972,128]{1,0:T(8,128)(2,1)S(1)}, bf16[972,128]{1,0:T(8,128)(2,1)S(1)}, u32[]{:S(2)}, u32[]{:S(2)}) %collective-permute-start.14) | collective-permute-done | bytes 248864 | tf_op jit(solution)/shard_map/ppermute | solution.py:399
  56.1 7.8 %collective-permute-done.15.block = bf16[972,128]{1,0:T(8,128)(2,1)S(1)} collective-permute-done((bf16[972,128]{1,0:T(8,128)(2,1)S(1)}, bf16[972,128]{1,0:T(8,128)(2,1)S(1)}, u32[]{:S(2)}, u32[]{:S(2)}) %collective-permute-start.15) | collective-permute-done | bytes 248864 | tf_op jit(solution)/shard_map/ppermute | solution.py:399
  63.9 0.8 collective-permute-start.16
  64.7 1.3 %collective-permute-start.18 = (bf16[972,128]{1,0:T(8,128)(2,1)S(1)}, bf16[972,128]{1,0:T(8,128)(2,1)S(1)}, u32[]{:S(2)}, u32[]{:S(2)}) collective-permute-start(bf16[972,128]{1,0:T(8,128)(2,1)S(1)} %collective-permute-done.17.refs_4_), channel_id=1, source_target_pairs={{0,1},{1,0},{2,3},{3,2},{4,5},{5,4},{6,7},{7,6},{8,9},{9,8},{10,11... | collective-permute-start | bytes 746504 | tf_op jit(solution)/shard_map/ppermute | solution.py:399
  66.0 0.7 collective-permute-start.13
  66.8 6.2 %collective-permute-done.16.refs_3_ = bf16[972,128]{1,0:T(8,128)(2,1)S(1)} collective-permute-done((bf16[972,128]{1,0:T(8,128)(2,1)S(1)}, bf16[972,128]{1,0:T(8,128)(2,1)S(1)}, u32[]{:S(2)}, u32[]{:S(2)}) %collective-permute-start.16) | collective-permute-done | bytes 248864 | tf_op jit(solution)/shard_map/ppermute | solution.py:399
  73.0 5.0 %collective-permute-done.18.refs_5_ = bf16[972,128]{1,0:T(8,128)(2,1)S(1)} collective-permute-done((bf16[972,128]{1,0:T(8,128)(2,1)S(1)}, bf16[972,128]{1,0:T(8,128)(2,1)S(1)}, u32[]{:S(2)}, u32[]{:S(2)}) %collective-permute-start.18) | collective-permute-done | bytes 248864 | tf_op jit(solution)/shard_map/ppermute | solution.py:399
  78.0 0.8 gather.1.refs_3_
  78.8 1.9 %collective-permute-done.13.refs_1_ = bf16[972,128]{1,0:T(8,128)(2,1)S(1)} collective-permute-done((bf16[972,128]{1,0:T(8,128)(2,1)S(1)}, bf16[972,128]{1,0:T(8,128)(2,1)S(1)}, u32[]{:S(2)}, u32[]{:S(2)}) %collective-permute-start.13) | collective-permute-done | bytes 248864 | tf_op jit(solution)/shard_map/ppermute | solution.py:399
  80.7 2.5 %finish.1 = (f32[3888,128]{1,0:T(8,128)}, bf16[7776,128]{1,0:T(8,128)(2,1)}) custom-call(bf16[972,128]{1,0:T(8,128)(2,1)S(1)} %collective-permute-done.12.refs_0_, bf16[972,128]{1,0:T(8,128)(2,1)S(1)} %collective-permute-done.13.refs_1_, bf16[7776,128]{1,0:T(8,128)(2,1)S(1)} %bitcast.11, f32[7776,128]{1,0:T(8,128)S(1)} %gather.1.refs_3_), custom_call_target="tpu_custom_call" | custom-call | tf_op jit(solution)/shard_map/finish/pallas_call | solution.py:375
  (10 shorter events, 0.1 us)
Async XLA Ops:
  0.6 9.5 %collective-permute-start.1 = (s32[2,8]{1,0:T(2,128)}, s32[2,8]{1,0:T(2,128)S(1)}, u32[]{:S(2)}, u32[]{:S(2)}) collective-permute-start(s32[2,8]{1,0:T(2,128)} %bitcast.12), channel_id=1, source_target_pairs={{0,16},{1,17},{2,18},{3,19},{4,20},{5,21},{6,22},{7,23},{8,24},{9,... | collective-permute-start | bytes 200 | tf_op jit(solution)/shard_map/ppermute | solution.py:399
  4.5 0.7 copy-start.1
  10.1 2.4 %copy-start = (bf16[8,972,128]{2,0,1:T(8,128)(2,1)S(1)}, bf16[8,972,128]{2,0,1:T(8,128)(2,1)}, u32[]{:S(2)}) copy-start(bf16[8,972,128]{2,0,1:T(8,128)(2,1)} %param.4) | copy-start | bytes 5971972
  13.2 10.0 %collective-permute-start.4 = (bf16[972,128]{1,0:T(8,128)(2,1)S(1)}, bf16[972,128]{1,0:T(8,128)(2,1)S(1)}, u32[]{:S(2)}, u32[]{:S(2)}) collective-permute-start(bf16[972,128]{1,0:T(8,128)(2,1)S(1)} %get-tuple-element.35), channel_id=1, source_target_pairs={{0,12},{1,13},{2,14},{3,15},{4,0},{5,1},{6,2},{7,3},{8,4},{9,5},{1... | collective-permute-start | bytes 746504 | tf_op jit(solution)/shard_map/ppermute | solution.py:399
  16.3 22.3 %collective-permute-start = (bf16[972,384]{1,0:T(8,128)(2,1)S(1)}, bf16[972,384]{1,0:T(8,128)(2,1)S(1)}, u32[]{:S(2)}, u32[]{:S(2)}) collective-permute-start(bf16[972,384]{1,0:T(8,128)(2,1)S(1)} %get-tuple-element.29.above), channel_id=1, source_target_pairs={{1,2},{2,1},{5,6},{6,5},{9,10},{10,9},{13,14},{14,13},{17,18},{18,... | collective-permute-start | bytes 2239496 | tf_op jit(solution)/shard_map/ppermute | solution.py:399
  17.0 21.6 %collective-permute-start.2 = (bf16[972,384]{1,0:T(8,128)(2,1)S(1)}, bf16[972,384]{1,0:T(8,128)(2,1)S(1)}, u32[]{:S(2)}, u32[]{:S(2)}) collective-permute-start(bf16[972,384]{1,0:T(8,128)(2,1)S(1)} %get-tuple-element.31), channel_id=1, source_target_pairs={{16,0},{17,2},{18,1},{19,3},{20,4},{21,6},{22,5},{23,7},{24,8},{25... | collective-permute-start | bytes 2239496 | tf_op jit(solution)/shard_map/ppermute | solution.py:399
  21.0 15.2 %collective-permute-start.8 = (bf16[972,128]{1,0:T(8,128)(2,1)S(1)}, bf16[972,128]{1,0:T(8,128)(2,1)S(1)}, u32[]{:S(2)}, u32[]{:S(2)}) collective-permute-start(bf16[972,128]{1,0:T(8,128)(2,1)S(1)} %get-tuple-element.39), channel_id=1, source_target_pairs={{0,4},{1,5},{2,6},{3,7},{4,8},{5,9},{6,10},{7,11},{8,12},{9,13},{1... | collective-permute-start | bytes 746504 | tf_op jit(solution)/shard_map/ppermute | solution.py:399
  21.1 15.3 %collective-permute-start.6 = (bf16[972,128]{1,0:T(8,128)(2,1)S(1)}, bf16[972,128]{1,0:T(8,128)(2,1)S(1)}, u32[]{:S(2)}, u32[]{:S(2)}) collective-permute-start(bf16[972,128]{1,0:T(8,128)(2,1)S(1)} %get-tuple-element.37), channel_id=1, source_target_pairs={{0,8},{1,9},{2,10},{3,11},{4,12},{5,13},{6,14},{7,15},{8,0},{9,1},... | collective-permute-start | bytes 746504 | tf_op jit(solution)/shard_map/ppermute | solution.py:399
  23.3 13.4 %collective-permute-start.3 = (bf16[972,128]{1,0:T(8,128)(2,1)S(1)}, bf16[972,128]{1,0:T(8,128)(2,1)S(1)}, u32[]{:S(2)}, u32[]{:S(2)}) collective-permute-start(bf16[972,128]{1,0:T(8,128)(2,1)S(1)} %get-tuple-element.33.own), channel_id=1, source_target_pairs={{0,2},{1,3},{2,0},{3,1},{4,6},{5,7},{6,4},{7,5},{8,10},{9,11},{10,... | collective-permute-start | bytes 746504 | tf_op jit(solution)/shard_map/ppermute | solution.py:399
  36.1 1.5 %collective-permute-start.9 = (bf16[972,128]{1,0:T(8,128)(2,1)S(1)}, bf16[972,128]{1,0:T(8,128)(2,1)S(1)}, u32[]{:S(2)}, u32[]{:S(2)}) collective-permute-start(bf16[972,128]{1,0:T(8,128)(2,1)S(1)} %collective-permute-done.8.own), channel_id=1, source_target_pairs={{0,2},{1,3},{2,0},{3,1},{4,6},{5,7},{6,4},{7,5},{8,10},{9,11},{10,... | collective-permute-start | bytes 746504 | tf_op jit(solution)/shard_map/ppermute | solution.py:399
  36.3 1.7 %collective-permute-start.7 = (bf16[972,128]{1,0:T(8,128)(2,1)S(1)}, bf16[972,128]{1,0:T(8,128)(2,1)S(1)}, u32[]{:S(2)}, u32[]{:S(2)}) collective-permute-start(bf16[972,128]{1,0:T(8,128)(2,1)S(1)} %collective-permute-done.6.own), channel_id=1, source_target_pairs={{0,2},{1,3},{2,0},{3,1},{4,6},{5,7},{6,4},{7,5},{8,10},{9,11},{10,... | collective-permute-start | bytes 746504 | tf_op jit(solution)/shard_map/ppermute | solution.py:399
  36.7 1.7 %collective-permute-start.5 = (bf16[972,128]{1,0:T(8,128)(2,1)S(1)}, bf16[972,128]{1,0:T(8,128)(2,1)S(1)}, u32[]{:S(2)}, u32[]{:S(2)}) collective-permute-start(bf16[972,128]{1,0:T(8,128)(2,1)S(1)} %collective-permute-done.4.own), channel_id=1, source_target_pairs={{0,2},{1,3},{2,0},{3,1},{4,6},{5,7},{6,4},{7,5},{8,10},{9,11},{10,... | collective-permute-start | bytes 746504 | tf_op jit(solution)/shard_map/ppermute | solution.py:399
  45.1 4.2 %collective-permute-start.10 = (bf16[2928,128]{1,0:T(8,128)(2,1)S(1)}, bf16[2928,128]{1,0:T(8,128)(2,1)S(1)}, u32[]{:S(2)}, u32[]{:S(2)}) collective-permute-start(bf16[2928,128]{1,0:T(8,128)(2,1)S(1)} %get-tuple-element.49), channel_id=1, source_target_pairs={{0,2},{1,3},{2,0},{3,1},{4,6},{5,7},{6,4},{7,5},{8,10},{9,11},{10,... | collective-permute-start | bytes 2248712 | tf_op jit(solution)/shard_map/ppermute | solution.py:399
  45.4 2.4 %collective-permute-start.11 = (bf16[976,128]{1,0:T(8,128)(2,1)S(1)}, bf16[976,128]{1,0:T(8,128)(2,1)S(1)}, u32[]{:S(2)}, u32[]{:S(2)}) collective-permute-start(bf16[976,128]{1,0:T(8,128)(2,1)S(1)} %get-tuple-element.47.refs_0_), channel_id=1, source_target_pairs={{0,2},{1,3},{2,0},{3,1},{4,6},{5,7},{6,4},{7,5},{8,10},{9,11},{10,... | collective-permute-start | bytes 749576 | tf_op jit(solution)/shard_map/ppermute | solution.py:399
  47.9 8.2 %collective-permute-start.14 = (bf16[972,128]{1,0:T(8,128)(2,1)S(1)}, bf16[972,128]{1,0:T(8,128)(2,1)S(1)}, u32[]{:S(2)}, u32[]{:S(2)}) collective-permute-start(bf16[972,128]{1,0:T(8,128)(2,1)S(1)} %total.2.refs_0_), channel_id=1, source_target_pairs={{0,1},{1,0},{2,3},{3,2},{4,5},{5,4},{6,7},{7,6},{8,9},{9,8},{10,11... | collective-permute-start | bytes 746504 | tf_op jit(solution)/shard_map/ppermute | solution.py:399
  49.4 14.4 %collective-permute-start.15 = (bf16[972,128]{1,0:T(8,128)(2,1)S(1)}, bf16[972,128]{1,0:T(8,128)(2,1)S(1)}, u32[]{:S(2)}, u32[]{:S(2)}) collective-permute-start(bf16[972,128]{1,0:T(8,128)(2,1)S(1)} %get-tuple-element.52), channel_id=1, source_target_pairs={{0,4},{1,5},{2,6},{3,7},{4,8},{5,9},{6,10},{7,11},{8,12},{9,13},{1... | collective-permute-start | bytes 746504 | tf_op jit(solution)/shard_map/ppermute | solution.py:399
  49.5 15.2 %collective-permute-start.17 = (bf16[972,128]{1,0:T(8,128)(2,1)S(1)}, bf16[972,128]{1,0:T(8,128)(2,1)S(1)}, u32[]{:S(2)}, u32[]{:S(2)}) collective-permute-start(bf16[972,128]{1,0:T(8,128)(2,1)S(1)} %get-tuple-element.53), channel_id=1, source_target_pairs={{0,12},{1,13},{2,14},{3,15},{4,0},{5,1},{6,2},{7,3},{8,4},{9,5},{1... | collective-permute-start | bytes 746504 | tf_op jit(solution)/shard_map/ppermute | solution.py:399
  52.8 13.3 %collective-permute-start.12 = (bf16[972,128]{1,0:T(8,128)(2,1)S(1)}, bf16[972,128]{1,0:T(8,128)(2,1)S(1)}, u32[]{:S(2)}, u32[]{:S(2)}) collective-permute-start(bf16[972,128]{1,0:T(8,128)(2,1)S(1)} %get-tuple-element.51), channel_id=1, source_target_pairs={{0,8},{1,9},{2,10},{3,11},{4,12},{5,13},{6,14},{7,15},{8,0},{9,1},... | collective-permute-start | bytes 746504 | tf_op jit(solution)/shard_map/ppermute | solution.py:399
  63.9 9.1 %collective-permute-start.16 = (bf16[972,128]{1,0:T(8,128)(2,1)S(1)}, bf16[972,128]{1,0:T(8,128)(2,1)S(1)}, u32[]{:S(2)}, u32[]{:S(2)}) collective-permute-start(bf16[972,128]{1,0:T(8,128)(2,1)S(1)} %follow.1.refs_2_), channel_id=1, source_target_pairs={{0,1},{1,0},{2,3},{3,2},{4,5},{5,4},{6,7},{7,6},{8,9},{9,8},{10,11... | collective-permute-start | bytes 746504 | tf_op jit(solution)/shard_map/ppermute | solution.py:399
  64.7 13.3 %collective-permute-start.18 = (bf16[972,128]{1,0:T(8,128)(2,1)S(1)}, bf16[972,128]{1,0:T(8,128)(2,1)S(1)}, u32[]{:S(2)}, u32[]{:S(2)}) collective-permute-start(bf16[972,128]{1,0:T(8,128)(2,1)S(1)} %collective-permute-done.17.refs_4_), channel_id=1, source_target_pairs={{0,1},{1,0},{2,3},{3,2},{4,5},{5,4},{6,7},{7,6},{8,9},{9,8},{10,11... | collective-permute-start | bytes 746504 | tf_op jit(solution)/shard_map/ppermute | solution.py:399
  66.0 14.7 %collective-permute-start.13 = (bf16[972,128]{1,0:T(8,128)(2,1)S(1)}, bf16[972,128]{1,0:T(8,128)(2,1)S(1)}, u32[]{:S(2)}, u32[]{:S(2)}) collective-permute-start(bf16[972,128]{1,0:T(8,128)(2,1)S(1)} %collective-permute-done.12.refs_0_), channel_id=1, source_target_pairs={{0,1},{1,0},{2,3},{3,2},{4,5},{5,4},{6,7},{7,6},{8,9},{9,8},{10,11... | collective-permute-start | bytes 746504 | tf_op jit(solution)/shard_map/ppermute | solution.py:399

commit v5 on v4

--- a/solution.py
+++ b/solution.py
@@ -429,9 +429,12 @@
         blocks_here = total(home, away, len(shifts), inner, after_total)
         after_total = (blocks_here[0],)
         for s, block in zip(shifts, blocks_here):
+            if s == 2:
+                block = follow(block, first)
             if s:
                 block = send(block, lambda t, y, k, d: (t, y + s, k, d))
             if s == 1:
+                first = block
                 block = follow(block, pieces[0][1])
             pieces[s] = [block, send(block, lambda t, y, k, d: (t, y, k, 1 - d))]
     early, late = (0, 1, 3), (2,)

time: 84.3 us -> 79 us (0.937)
  waiting for transfers between devices: 41.7 us -> 36.3 us
    ppermute x19, waiting for transfers between devices: 41.7 us -> 36.3 us  [send(): return lax.ppermute(x, AXES, table(mesh_shape, move))]
where the time goes in v5:
time: 79 us; the launch traced here: 78.4 us
  waiting for transfers between devices  36.3 us (46%)
  starting transfers between devices  24 us (30%)
  Pallas kernels  16.4 us (21%)
  between operations  0.99 us (1%)
    ppermute x19, waiting for transfers between devices, send(): return lax.ppermute(x, AXES, table(mesh_shape, move))  36.3 us
    ppermute x19, starting transfers between devices, send(): return lax.ppermute(x, AXES, table(mesh_shape, move))  24 us
    pallas_call x2, Pallas kernels, cut(): pl.pallas_call(functools.partial(cut_kernel, above), out_shape=[jax.Shape...  4.65 us
    pallas_call x1, Pallas kernels, column(): pl.pallas_call(functools.partial(column_kernel, rows_y), out_shape=[jax.S...  4.09 us
    pallas_call x1, Pallas kernels, finish(): pl.pallas_call(functools.partial(finish_kernel, rows_y, dps, shifts), out...  2.5 us
    pallas_call x2, Pallas kernels, piece(): pl.pallas_call(functools.partial(piece_kernel, shifts, 1.0 / depth), out_...  2.06 us
  transfers between devices with their start and end apart: 19, of which 11 were waited for; matrix products, arithmetic and copies ran while one was open for 0% of the time, Pallas kernels for 5%

profile of v5, /device:TPU:4, one launch (start us, length us, event | category | flops | bytes accessed | tf_op | source)
XLA Modules:
  0.0 78.4 jit_solution(132483408609829531)
XLA Ops:
  0.6 3.8 %collective-permute-start.1 = (s32[2,8]{1,0:T(2,128)}, s32[2,8]{1,0:T(2,128)S(1)}, u32[]{:S(2)}, u32[]{:S(2)}) collective-permute-start(s32[2,8]{1,0:T(2,128)} %bitcast.12), channel_id=1, source_target_pairs={{0,16},{1,17},{2,18},{3,19},{4,20},{5,21},{6,22},{7,23},{8,24},{9,... | collective-permute-start | bytes 200 | tf_op jit(solution)/shard_map/ppermute | solution.py:399
  4.5 0.7 copy-done.1
  5.2 2.3 %cut_above.1 = (bf16[972,384]{1,0:T(8,128)(2,1)S(1)}, f32[8,128]{1,0:T(8,128)S(1)}) custom-call(s32[2,8]{1,0:T(2,128)S(1)} %bitcast.13, bf16[3,20,128,384]{3,2,1,0:T(8,128)(2,1)} %frames.3), custom_call_target="tpu_custom_call" | custom-call | tf_op jit(solution)/shard_map/cut_above/pallas_call | solution.py:95
  7.5 2.6 %collective-permute-done.1.places = s32[2,8]{1,0:T(2,128)S(1)} collective-permute-done((s32[2,8]{1,0:T(2,128)}, s32[2,8]{1,0:T(2,128)S(1)}, u32[]{:S(2)}, u32[]{:S(2)}) %collective-permute-start.1) | collective-permute-done | bytes 96 | tf_op jit(solution)/shard_map/ppermute | solution.py:399
  10.1 2.3 %cut_below.1 = (bf16[972,384]{1,0:T(8,128)(2,1)S(1)}, f32[8,128]{1,0:T(8,128)S(1)}) custom-call(s32[2,8]{1,0:T(2,128)S(1)} %collective-permute-done.1.places, bf16[3,20,128,384]{3,2,1,0:T(8,128)(2,1)} %frames.3, f32[8,128]{1,0:T(8,128)S(1)} %get-tuple-element.30.refs_0_), custom_call_target="tpu_custom_call" | custom-call | tf_op jit(solution)/shard_map/cut_below/pallas_call | solution.py:95
  12.4 0.8 blocks.1
  13.2 3.1 %collective-permute-start.4 = (bf16[972,128]{1,0:T(8,128)(2,1)S(1)}, bf16[972,128]{1,0:T(8,128)(2,1)S(1)}, u32[]{:S(2)}, u32[]{:S(2)}) collective-permute-start(bf16[972,128]{1,0:T(8,128)(2,1)S(1)} %get-tuple-element.35), channel_id=1, source_target_pairs={{0,12},{1,13},{2,14},{3,15},{4,0},{5,1},{6,2},{7,3},{8,4},{9,5},{1... | collective-permute-start | bytes 746504 | tf_op jit(solution)/shard_map/ppermute | solution.py:399
  16.3 0.7 collective-permute-start
  17.0 3.9 %collective-permute-start.2 = (bf16[972,384]{1,0:T(8,128)(2,1)S(1)}, bf16[972,384]{1,0:T(8,128)(2,1)S(1)}, u32[]{:S(2)}, u32[]{:S(2)}) collective-permute-start(bf16[972,384]{1,0:T(8,128)(2,1)S(1)} %get-tuple-element.31), channel_id=1, source_target_pairs={{16,0},{17,2},{18,1},{19,3},{20,4},{21,6},{22,5},{23,7},{24,8},{25... | collective-permute-start | bytes 2239496 | tf_op jit(solution)/shard_map/ppermute | solution.py:399
  21.0 0.1 collective-permute-start.8
  21.1 2.2 %collective-permute-start.6 = (bf16[972,128]{1,0:T(8,128)(2,1)S(1)}, bf16[972,128]{1,0:T(8,128)(2,1)S(1)}, u32[]{:S(2)}, u32[]{:S(2)}) collective-permute-start(bf16[972,128]{1,0:T(8,128)(2,1)S(1)} %get-tuple-element.37), channel_id=1, source_target_pairs={{0,8},{1,9},{2,10},{3,11},{4,12},{5,13},{6,14},{7,15},{8,0},{9,1},... | collective-permute-start | bytes 746504 | tf_op jit(solution)/shard_map/ppermute | solution.py:399
  23.2 0.9 %collective-permute-start.3 = (bf16[972,128]{1,0:T(8,128)(2,1)S(1)}, bf16[972,128]{1,0:T(8,128)(2,1)S(1)}, u32[]{:S(2)}, u32[]{:S(2)}) collective-permute-start(bf16[972,128]{1,0:T(8,128)(2,1)S(1)} %get-tuple-element.33.own), channel_id=1, source_target_pairs={{0,2},{1,3},{2,0},{3,1},{4,6},{5,7},{6,4},{7,5},{8,10},{9,11},{10,... | collective-permute-start | bytes 746504 | tf_op jit(solution)/shard_map/ppermute | solution.py:399
  24.1 12.1 %collective-permute-done.8.own = bf16[972,128]{1,0:T(8,128)(2,1)S(1)} collective-permute-done((bf16[972,128]{1,0:T(8,128)(2,1)S(1)}, bf16[972,128]{1,0:T(8,128)(2,1)S(1)}, u32[]{:S(2)}, u32[]{:S(2)}) %collective-permute-start.8) | collective-permute-done | bytes 248864 | tf_op jit(solution)/shard_map/ppermute | solution.py:399
  36.2 0.2 collective-permute-start.9
  36.4 0.3 collective-permute-start.7
  36.7 0.2 collective-permute-start.5
  36.9 0.2 filters.4
  37.1 0.6 collective-permute-done.9.other
  37.7 0.2 filters.7
  37.9 0.1 collective-permute-done.7.other
  38.1 0.2 filters.6
  38.3 0.1 collective-permute-done.5.other
  38.4 0.2 filters.5
  38.7 0.0 collective-permute-done.above_in
  38.7 0.0 collective-permute-done.2.below
  38.7 0.3 join.1.patch_in
  39.0 4.1 %column.1 = (bf16[972,768]{1,0:T(8,128)(2,1)S(1)}, bf16[1024,768]{1,0:T(8,128)(2,1)S(1)}) custom-call(bf16[972,384]{1,0:T(8,128)(2,1)S(1)} %join.1.patch_in, bf16[972,256]{1,0:T(8,128)(2,1)S(1)} %get-tuple-element.34.refs_0_, bf16[972,256]{1,0:T(8,128)(2,1)S(1)} %get-tuple-element.36.refs_1_, bf16[972,256]{1,0:T(8,128)(2,1)S(1)} %get-tuple-element.38.refs_2_, ...), custom_call_target="tpu_custom_call" | custom-call | tf_op jit(solution)/shard_map/column/pallas_call | solution.py:231
  43.1 0.6 piece.2
  43.7 1.5 %piece.3 = (f32[2928,128]{1,0:T(8,128)S(1)}, bf16[2928,128]{1,0:T(8,128)(2,1)S(1)}) custom-call(bf16[972,768]{1,0:T(8,128)(2,1)S(1)} %get-tuple-element.45.pe, bf16[1024,768]{1,0:T(8,128)(2,1)S(1)} %get-tuple-element.46.mr, bf16[976,128]{1,0:T(8,128)(2,1)S(1)} %get-tuple-element.47.refs_0_), custom_call_target="tpu_custom_call" | custom-call | tf_op jit(solution)/shard_map/piece/pallas_call | solution.py:276
  45.2 0.3 collective-permute-start.10
  45.5 0.3 collective-permute-start.11
  45.8 2.1 %collective-permute-done.11.away = bf16[976,128]{1,0:T(8,128)(2,1)S(1)} collective-permute-done((bf16[976,128]{1,0:T(8,128)(2,1)S(1)}, bf16[976,128]{1,0:T(8,128)(2,1)S(1)}, u32[]{:S(2)}, u32[]{:S(2)}) %collective-permute-start.11) | collective-permute-done | bytes 249888 | tf_op jit(solution)/shard_map/ppermute | solution.py:399
  47.9 0.1 total.3
  48.1 0.1 collective-permute-start.12
  48.1 1.4 %collective-permute-start.15 = (bf16[972,128]{1,0:T(8,128)(2,1)S(1)}, bf16[972,128]{1,0:T(8,128)(2,1)S(1)}, u32[]{:S(2)}, u32[]{:S(2)}) collective-permute-start(bf16[972,128]{1,0:T(8,128)(2,1)S(1)} %total.2.refs_0_), channel_id=1, source_target_pairs={{0,1},{1,0},{2,3},{3,2},{4,5},{5,4},{6,7},{7,6},{8,9},{9,8},{10,11... | collective-permute-start | bytes 746504 | tf_op jit(solution)/shard_map/ppermute | solution.py:399
  49.5 3.1 %collective-permute-start.17 = (bf16[972,128]{1,0:T(8,128)(2,1)S(1)}, bf16[972,128]{1,0:T(8,128)(2,1)S(1)}, u32[]{:S(2)}, u32[]{:S(2)}) collective-permute-start(bf16[972,128]{1,0:T(8,128)(2,1)S(1)} %get-tuple-element.53), channel_id=1, source_target_pairs={{0,12},{1,13},{2,14},{3,15},{4,0},{5,1},{6,2},{7,3},{8,4},{9,5},{1... | collective-permute-start | bytes 746504 | tf_op jit(solution)/shard_map/ppermute | solution.py:399
  52.7 4.8 %collective-permute-done.12.after.block = bf16[972,128]{1,0:T(8,128)(2,1)S(1)} collective-permute-done((bf16[972,128]{1,0:T(8,128)(2,1)S(1)}, bf16[972,128]{1,0:T(8,128)(2,1)S(1)}, u32[]{:S(2)}, u32[]{:S(2)}) %collective-permute-start.12) | collective-permute-done | bytes 248864 | tf_op jit(solution)/shard_map/ppermute | solution.py:399
  57.5 0.1 collective-permute-start.13
  57.6 0.0 collective-permute-done.15.after.refs_1_
  57.6 1.4 %collective-permute-start.16 = (bf16[972,128]{1,0:T(8,128)(2,1)S(1)}, bf16[972,128]{1,0:T(8,128)(2,1)S(1)}, u32[]{:S(2)}, u32[]{:S(2)}) collective-permute-start(bf16[972,128]{1,0:T(8,128)(2,1)S(1)} %follow.3.refs_2_), channel_id=1, source_target_pairs={{0,1},{1,0},{2,3},{3,2},{4,5},{5,4},{6,7},{7,6},{8,9},{9,8},{10,11... | collective-permute-start | bytes 746504 | tf_op jit(solution)/shard_map/ppermute | solution.py:399
  59.0 4.1 %collective-permute-done.17.refs_4_ = bf16[972,128]{1,0:T(8,128)(2,1)S(1)} collective-permute-done((bf16[972,128]{1,0:T(8,128)(2,1)S(1)}, bf16[972,128]{1,0:T(8,128)(2,1)S(1)}, u32[]{:S(2)}, u32[]{:S(2)}) %collective-permute-start.17) | collective-permute-done | bytes 248864 | tf_op jit(solution)/shard_map/ppermute | solution.py:399
  63.1 0.8 collective-permute-start.18
  63.9 2.5 %collective-permute-done.13.refs_0_ = bf16[972,128]{1,0:T(8,128)(2,1)S(1)} collective-permute-done((bf16[972,128]{1,0:T(8,128)(2,1)S(1)}, bf16[972,128]{1,0:T(8,128)(2,1)S(1)}, u32[]{:S(2)}, u32[]{:S(2)}) %collective-permute-start.13) | collective-permute-done | bytes 248864 | tf_op jit(solution)/shard_map/ppermute | solution.py:399
  66.4 1.2 %collective-permute-start.14 = (bf16[972,128]{1,0:T(8,128)(2,1)S(1)}, bf16[972,128]{1,0:T(8,128)(2,1)S(1)}, u32[]{:S(2)}, u32[]{:S(2)}) collective-permute-start(bf16[972,128]{1,0:T(8,128)(2,1)S(1)} %collective-permute-done.13.refs_0_), channel_id=1, source_target_pairs={{0,1},{1,0},{2,3},{3,2},{4,5},{5,4},{6,7},{7,6},{8,9},{9,8},{10,11... | collective-permute-start | bytes 746504 | tf_op jit(solution)/shard_map/ppermute | solution.py:399
  67.6 4.4 %collective-permute-done.18.refs_5_ = bf16[972,128]{1,0:T(8,128)(2,1)S(1)} collective-permute-done((bf16[972,128]{1,0:T(8,128)(2,1)S(1)}, bf16[972,128]{1,0:T(8,128)(2,1)S(1)}, u32[]{:S(2)}, u32[]{:S(2)}) %collective-permute-start.18) | collective-permute-done | bytes 248864 | tf_op jit(solution)/shard_map/ppermute | solution.py:399
  72.1 0.8 %gather.1.refs_3_ = f32[7776,128]{1,0:T(8,128)S(1)} custom-call(bf16[972,128]{1,0:T(8,128)(2,1)S(1)} %total.2.refs_0_, bf16[972,128]{1,0:T(8,128)(2,1)S(1)} %collective-permute-done.15.after.refs_1_, bf16[972,128]{1,0:T(8,128)(2,1)S(1)} %follow.3.refs_2_, bf16[972,128]{1,0:T(8,128)(2,1)S(1)} %collective-permute-done.16.refs_3_, ...), custom_call_target="tpu_custom_call" | custom-call | tf_op jit(solution)/shard_map/gather/pallas_call | solution.py:339
  72.9 2.9 %collective-permute-done.14.refs_1_ = bf16[972,128]{1,0:T(8,128)(2,1)S(1)} collective-permute-done((bf16[972,128]{1,0:T(8,128)(2,1)S(1)}, bf16[972,128]{1,0:T(8,128)(2,1)S(1)}, u32[]{:S(2)}, u32[]{:S(2)}) %collective-permute-start.14) | collective-permute-done | bytes 248864 | tf_op jit(solution)/shard_map/ppermute | solution.py:399
  75.7 2.5 %finish.1 = (f32[3888,128]{1,0:T(8,128)}, bf16[7776,128]{1,0:T(8,128)(2,1)}) custom-call(bf16[972,128]{1,0:T(8,128)(2,1)S(1)} %collective-permute-done.13.refs_0_, bf16[972,128]{1,0:T(8,128)(2,1)S(1)} %collective-permute-done.14.refs_1_, bf16[7776,128]{1,0:T(8,128)(2,1)S(1)} %bitcast.11, f32[7776,128]{1,0:T(8,128)S(1)} %gather.1.refs_3_), custom_call_target="tpu_custom_call" | custom-call | tf_op jit(solution)/shard_map/finish/pallas_call | solution.py:375
  (11 shorter events, 0.1 us)
Async XLA Ops:
  0.6 9.5 %collective-permute-start.1 = (s32[2,8]{1,0:T(2,128)}, s32[2,8]{1,0:T(2,128)S(1)}, u32[]{:S(2)}, u32[]{:S(2)}) collective-permute-start(s32[2,8]{1,0:T(2,128)} %bitcast.12), channel_id=1, source_target_pairs={{0,16},{1,17},{2,18},{3,19},{4,20},{5,21},{6,22},{7,23},{8,24},{9,... | collective-permute-start | bytes 200 | tf_op jit(solution)/shard_map/ppermute | solution.py:399
  4.5 0.7 copy-start.1
  10.1 2.4 %copy-start = (bf16[8,972,128]{2,0,1:T(8,128)(2,1)S(1)}, bf16[8,972,128]{2,0,1:T(8,128)(2,1)}, u32[]{:S(2)}) copy-start(bf16[8,972,128]{2,0,1:T(8,128)(2,1)} %param.4) | copy-start | bytes 5971972
  13.2 10.0 %collective-permute-start.4 = (bf16[972,128]{1,0:T(8,128)(2,1)S(1)}, bf16[972,128]{1,0:T(8,128)(2,1)S(1)}, u32[]{:S(2)}, u32[]{:S(2)}) collective-permute-start(bf16[972,128]{1,0:T(8,128)(2,1)S(1)} %get-tuple-element.35), channel_id=1, source_target_pairs={{0,12},{1,13},{2,14},{3,15},{4,0},{5,1},{6,2},{7,3},{8,4},{9,5},{1... | collective-permute-start | bytes 746504 | tf_op jit(solution)/shard_map/ppermute | solution.py:399
  16.3 22.3 %collective-permute-start = (bf16[972,384]{1,0:T(8,128)(2,1)S(1)}, bf16[972,384]{1,0:T(8,128)(2,1)S(1)}, u32[]{:S(2)}, u32[]{:S(2)}) collective-permute-start(bf16[972,384]{1,0:T(8,128)(2,1)S(1)} %get-tuple-element.29.above), channel_id=1, source_target_pairs={{1,2},{2,1},{5,6},{6,5},{9,10},{10,9},{13,14},{14,13},{17,18},{18,... | collective-permute-start | bytes 2239496 | tf_op jit(solution)/shard_map/ppermute | solution.py:399
  17.0 21.6 %collective-permute-start.2 = (bf16[972,384]{1,0:T(8,128)(2,1)S(1)}, bf16[972,384]{1,0:T(8,128)(2,1)S(1)}, u32[]{:S(2)}, u32[]{:S(2)}) collective-permute-start(bf16[972,384]{1,0:T(8,128)(2,1)S(1)} %get-tuple-element.31), channel_id=1, source_target_pairs={{16,0},{17,2},{18,1},{19,3},{20,4},{21,6},{22,5},{23,7},{24,8},{25... | collective-permute-start | bytes 2239496 | tf_op jit(solution)/shard_map/ppermute | solution.py:399
  21.0 15.2 %collective-permute-start.8 = (bf16[972,128]{1,0:T(8,128)(2,1)S(1)}, bf16[972,128]{1,0:T(8,128)(2,1)S(1)}, u32[]{:S(2)}, u32[]{:S(2)}) collective-permute-start(bf16[972,128]{1,0:T(8,128)(2,1)S(1)} %get-tuple-element.39), channel_id=1, source_target_pairs={{0,4},{1,5},{2,6},{3,7},{4,8},{5,9},{6,10},{7,11},{8,12},{9,13},{1... | collective-permute-start | bytes 746504 | tf_op jit(solution)/shard_map/ppermute | solution.py:399
  21.1 15.3 %collective-permute-start.6 = (bf16[972,128]{1,0:T(8,128)(2,1)S(1)}, bf16[972,128]{1,0:T(8,128)(2,1)S(1)}, u32[]{:S(2)}, u32[]{:S(2)}) collective-permute-start(bf16[972,128]{1,0:T(8,128)(2,1)S(1)} %get-tuple-element.37), channel_id=1, source_target_pairs={{0,8},{1,9},{2,10},{3,11},{4,12},{5,13},{6,14},{7,15},{8,0},{9,1},... | collective-permute-start | bytes 746504 | tf_op jit(solution)/shard_map/ppermute | solution.py:399
  23.2 13.4 %collective-permute-start.3 = (bf16[972,128]{1,0:T(8,128)(2,1)S(1)}, bf16[972,128]{1,0:T(8,128)(2,1)S(1)}, u32[]{:S(2)}, u32[]{:S(2)}) collective-permute-start(bf16[972,128]{1,0:T(8,128)(2,1)S(1)} %get-tuple-element.33.own), channel_id=1, source_target_pairs={{0,2},{1,3},{2,0},{3,1},{4,6},{5,7},{6,4},{7,5},{8,10},{9,11},{10,... | collective-permute-start | bytes 746504 | tf_op jit(solution)/shard_map/ppermute | solution.py:399
  36.2 1.5 %collective-permute-start.9 = (bf16[972,128]{1,0:T(8,128)(2,1)S(1)}, bf16[972,128]{1,0:T(8,128)(2,1)S(1)}, u32[]{:S(2)}, u32[]{:S(2)}) collective-permute-start(bf16[972,128]{1,0:T(8,128)(2,1)S(1)} %collective-permute-done.8.own), channel_id=1, source_target_pairs={{0,2},{1,3},{2,0},{3,1},{4,6},{5,7},{6,4},{7,5},{8,10},{9,11},{10,... | collective-permute-start | bytes 746504 | tf_op jit(solution)/shard_map/ppermute | solution.py:399
  36.4 1.7 %collective-permute-start.7 = (bf16[972,128]{1,0:T(8,128)(2,1)S(1)}, bf16[972,128]{1,0:T(8,128)(2,1)S(1)}, u32[]{:S(2)}, u32[]{:S(2)}) collective-permute-start(bf16[972,128]{1,0:T(8,128)(2,1)S(1)} %collective-permute-done.6.own), channel_id=1, source_target_pairs={{0,2},{1,3},{2,0},{3,1},{4,6},{5,7},{6,4},{7,5},{8,10},{9,11},{10,... | collective-permute-start | bytes 746504 | tf_op jit(solution)/shard_map/ppermute | solution.py:399
  36.7 1.7 %collective-permute-start.5 = (bf16[972,128]{1,0:T(8,128)(2,1)S(1)}, bf16[972,128]{1,0:T(8,128)(2,1)S(1)}, u32[]{:S(2)}, u32[]{:S(2)}) collective-permute-start(bf16[972,128]{1,0:T(8,128)(2,1)S(1)} %collective-permute-done.4.own), channel_id=1, source_target_pairs={{0,2},{1,3},{2,0},{3,1},{4,6},{5,7},{6,4},{7,5},{8,10},{9,11},{10,... | collective-permute-start | bytes 746504 | tf_op jit(solution)/shard_map/ppermute | solution.py:399
  45.2 2.7 %collective-permute-start.10 = (bf16[2928,128]{1,0:T(8,128)(2,1)S(1)}, bf16[2928,128]{1,0:T(8,128)(2,1)S(1)}, u32[]{:S(2)}, u32[]{:S(2)}) collective-permute-start(bf16[2928,128]{1,0:T(8,128)(2,1)S(1)} %get-tuple-element.49), channel_id=1, source_target_pairs={{0,2},{1,3},{2,0},{3,1},{4,6},{5,7},{6,4},{7,5},{8,10},{9,11},{10,... | collective-permute-start | bytes 2248712 | tf_op jit(solution)/shard_map/ppermute | solution.py:399
  45.5 2.4 %collective-permute-start.11 = (bf16[976,128]{1,0:T(8,128)(2,1)S(1)}, bf16[976,128]{1,0:T(8,128)(2,1)S(1)}, u32[]{:S(2)}, u32[]{:S(2)}) collective-permute-start(bf16[976,128]{1,0:T(8,128)(2,1)S(1)} %get-tuple-element.47.refs_0_), channel_id=1, source_target_pairs={{0,2},{1,3},{2,0},{3,1},{4,6},{5,7},{6,4},{7,5},{8,10},{9,11},{10,... | collective-permute-start | bytes 749576 | tf_op jit(solution)/shard_map/ppermute | solution.py:399
  48.1 9.4 %collective-permute-start.12 = (bf16[972,128]{1,0:T(8,128)(2,1)S(1)}, bf16[972,128]{1,0:T(8,128)(2,1)S(1)}, u32[]{:S(2)}, u32[]{:S(2)}) collective-permute-start(bf16[972,128]{1,0:T(8,128)(2,1)S(1)} %get-tuple-element.52), channel_id=1, source_target_pairs={{0,4},{1,5},{2,6},{3,7},{4,8},{5,9},{6,10},{7,11},{8,12},{9,13},{1... | collective-permute-start | bytes 746504 | tf_op jit(solution)/shard_map/ppermute | solution.py:399
  48.1 9.5 %collective-permute-start.15 = (bf16[972,128]{1,0:T(8,128)(2,1)S(1)}, bf16[972,128]{1,0:T(8,128)(2,1)S(1)}, u32[]{:S(2)}, u32[]{:S(2)}) collective-permute-start(bf16[972,128]{1,0:T(8,128)(2,1)S(1)} %total.2.refs_0_), channel_id=1, source_target_pairs={{0,1},{1,0},{2,3},{3,2},{4,5},{5,4},{6,7},{7,6},{8,9},{9,8},{10,11... | collective-permute-start | bytes 746504 | tf_op jit(solution)/shard_map/ppermute | solution.py:399
  49.5 13.6 %collective-permute-start.17 = (bf16[972,128]{1,0:T(8,128)(2,1)S(1)}, bf16[972,128]{1,0:T(8,128)(2,1)S(1)}, u32[]{:S(2)}, u32[]{:S(2)}) collective-permute-start(bf16[972,128]{1,0:T(8,128)(2,1)S(1)} %get-tuple-element.53), channel_id=1, source_target_pairs={{0,12},{1,13},{2,14},{3,15},{4,0},{5,1},{6,2},{7,3},{8,4},{9,5},{1... | collective-permute-start | bytes 746504 | tf_op jit(solution)/shard_map/ppermute | solution.py:399
  57.5 8.9 %collective-permute-start.13 = (bf16[972,128]{1,0:T(8,128)(2,1)S(1)}, bf16[972,128]{1,0:T(8,128)(2,1)S(1)}, u32[]{:S(2)}, u32[]{:S(2)}) collective-permute-start(bf16[972,128]{1,0:T(8,128)(2,1)S(1)} %follow.2), channel_id=1, source_target_pairs={{0,8},{1,9},{2,10},{3,11},{4,12},{5,13},{6,14},{7,15},{8,0},{9,1},... | collective-permute-start | bytes 746504 | tf_op jit(solution)/shard_map/ppermute | solution.py:399
  57.6 10.0 %collective-permute-start.16 = (bf16[972,128]{1,0:T(8,128)(2,1)S(1)}, bf16[972,128]{1,0:T(8,128)(2,1)S(1)}, u32[]{:S(2)}, u32[]{:S(2)}) collective-permute-start(bf16[972,128]{1,0:T(8,128)(2,1)S(1)} %follow.3.refs_2_), channel_id=1, source_target_pairs={{0,1},{1,0},{2,3},{3,2},{4,5},{5,4},{6,7},{7,6},{8,9},{9,8},{10,11... | collective-permute-start | bytes 746504 | tf_op jit(solution)/shard_map/ppermute | solution.py:399
  63.1 8.9 %collective-permute-start.18 = (bf16[972,128]{1,0:T(8,128)(2,1)S(1)}, bf16[972,128]{1,0:T(8,128)(2,1)S(1)}, u32[]{:S(2)}, u32[]{:S(2)}) collective-permute-start(bf16[972,128]{1,0:T(8,128)(2,1)S(1)} %collective-permute-done.17.refs_4_), channel_id=1, source_target_pairs={{0,1},{1,0},{2,3},{3,2},{4,5},{5,4},{6,7},{7,6},{8,9},{9,8},{10,11... | collective-permute-start | bytes 746504 | tf_op jit(solution)/shard_map/ppermute | solution.py:399
  66.4 9.3 %collective-permute-start.14 = (bf16[972,128]{1,0:T(8,128)(2,1)S(1)}, bf16[972,128]{1,0:T(8,128)(2,1)S(1)}, u32[]{:S(2)}, u32[]{:S(2)}) collective-permute-start(bf16[972,128]{1,0:T(8,128)(2,1)S(1)} %collective-permute-done.13.refs_0_), channel_id=1, source_target_pairs={{0,1},{1,0},{2,3},{3,2},{4,5},{5,4},{6,7},{7,6},{8,9},{9,8},{10,11... | collective-permute-start | bytes 746504 | tf_op jit(solution)/shard_map/ppermute | solution.py:399

commit v6 on v4

--- a/solution.py
+++ b/solution.py
@@ -401,8 +401,7 @@
     dps = mesh_shape[2]
     places = offsets.T
     upper = send(places, lambda t, y, k, d: (t + 1, y, k, d))
-    above, token = cut(frames, places, True)
-    below, token = cut(frames, upper, False, (token,))
+    below, token = cut(frames, upper, False)
     own = blocks(weights, rows_y, dps, (token,))
     below = send(below, lambda t, y, k, d: (t - 1, y, d, k))
 
@@ -415,6 +414,9 @@
         pair = filters(block, other)
         weight.append(pair[0])
         turned.append(pair[1])
+        if s == 0:
+            above, _ = cut(frames, places, True, (other,))
+    above_in = send(above, lambda t, y, k, d: (t, y, d, k) if k != d else None)
     above_in = send(above, lambda t, y, k, d: (t, y, d, k) if k != d else None)
 
     pe, mr = column(join(above, above_in, below), weight, turned)
@@ -429,10 +431,10 @@
         blocks_here = total(home, away, len(shifts), inner, after_total)
         after_total = (blocks_here[0],)
         for s, block in zip(shifts, blocks_here):
+            if s == 2:
+                block = follow(block, pieces[0][1])
             if s:
                 block = send(block, lambda t, y, k, d: (t, y + s, k, d))
-            if s == 1:
-                block = follow(block, pieces[0][1])
             pieces[s] = [block, send(block, lambda t, y, k, d: (t, y, k, 1 - d))]
     early, late = (0, 1, 3), (2,)
     full = gather(sum([pieces[s] for s in early], []), early, rows_y, dps)

time: 84.3 us -> 80.4 us (0.954)
  waiting for transfers between devices: 41.7 us -> 32 us
  starting transfers between devices: 23.6 us -> 30.3 us
    ppermute x19, waiting for transfers between devices: 41.7 us -> 32 us  [send(): return lax.ppermute(x, AXES, table(mesh_shape, move))]
    ppermute x19, starting transfers between devices: 23.6 us -> 30.3 us  [send(): return lax.ppermute(x, AXES, table(mesh_shape, move))]
  transfers between devices with their start and end apart: 19 -> 19, of which waited for: 11 -> 12; matrix products, arithmetic and copies ran while one was open for 0% -> 0% of each run, Pallas kernels for 5% -> 6%
where the time goes in v6:
time: 80.4 us; the launch traced here: 80.2 us
  waiting for transfers between devices  32 us (40%)
  starting transfers between devices  30.3 us (38%)
  Pallas kernels  16.9 us (21%)
  between operations  0.98 us (1%)
    ppermute x19, waiting for transfers between devices, send(): return lax.ppermute(x, AXES, table(mesh_shape, move))  32 us
    ppermute x19, starting transfers between devices, send(): return lax.ppermute(x, AXES, table(mesh_shape, move))  30.3 us
    pallas_call x2, Pallas kernels, cut(): pl.pallas_call(functools.partial(cut_kernel, above), out_shape=[jax.Shape...  5.15 us
    pallas_call x1, Pallas kernels, column(): pl.pallas_call(functools.partial(column_kernel, rows_y), out_shape=[jax.S...  4.11 us
    pallas_call x1, Pallas kernels, finish(): pl.pallas_call(functools.partial(finish_kernel, rows_y, dps, shifts), out...  2.5 us
    pallas_call x2, Pallas kernels, piece(): pl.pallas_call(functools.partial(piece_kernel, shifts, 1.0 / depth), out_...  2.07 us
  transfers between devices with their start and end apart: 19, of which 12 were waited for; matrix products, arithmetic and copies ran while one was open for 0% of the time, Pallas kernels for 6%

profile of v6, /device:TPU:4, one launch (start us, length us, event | category | flops | bytes accessed | tf_op | source)
XLA Modules:
  0.0 80.2 jit_solution(13387277745434050249)
XLA Ops:
  0.6 4.0 %collective-permute-start = (s32[2,8]{1,0:T(2,128)}, s32[2,8]{1,0:T(2,128)S(1)}, u32[]{:S(2)}, u32[]{:S(2)}) collective-permute-start(s32[2,8]{1,0:T(2,128)} %bitcast.12), channel_id=1, source_target_pairs={{0,16},{1,17},{2,18},{3,19},{4,20},{5,21},{6,22},{7,23},{8,24},{9,... | collective-permute-start | bytes 200 | tf_op jit(solution)/shard_map/ppermute | solution.py:399
  4.6 5.6 %collective-permute-done.places = s32[2,8]{1,0:T(2,128)S(1)} collective-permute-done((s32[2,8]{1,0:T(2,128)}, s32[2,8]{1,0:T(2,128)S(1)}, u32[]{:S(2)}, u32[]{:S(2)}) %collective-permute-start) | collective-permute-done | bytes 96 | tf_op jit(solution)/shard_map/ppermute | solution.py:399
  10.2 2.3 %cut_below.1 = (bf16[972,384]{1,0:T(8,128)(2,1)S(1)}, f32[8,128]{1,0:T(8,128)S(1)}) custom-call(s32[2,8]{1,0:T(2,128)S(1)} %collective-permute-done.places, bf16[3,20,128,384]{3,2,1,0:T(8,128)(2,1)} %frames.3), custom_call_target="tpu_custom_call" | custom-call | tf_op jit(solution)/shard_map/cut_below/pallas_call | solution.py:95
  12.6 0.0 copy-start.1
  12.6 0.8 blocks.1
  13.4 0.1 collective-permute-start.1
  13.5 3.9 %collective-permute-start.3 = (bf16[972,384]{1,0:T(8,128)(2,1)S(1)}, bf16[972,384]{1,0:T(8,128)(2,1)S(1)}, u32[]{:S(2)}, u32[]{:S(2)}) collective-permute-start(bf16[972,384]{1,0:T(8,128)(2,1)S(1)} %get-tuple-element.31), channel_id=1, source_target_pairs={{16,0},{17,2},{18,1},{19,3},{20,4},{21,6},{22,5},{23,7},{24,8},{25... | collective-permute-start | bytes 2239496 | tf_op jit(solution)/shard_map/ppermute | solution.py:399
  17.4 0.0 collective-permute-done.1.refs_0_.other
  17.4 2.8 %cut_above.1 = (bf16[972,384]{1,0:T(8,128)(2,1)S(1)}, f32[8,128]{1,0:T(8,128)}) custom-call(s32[2,8]{1,0:T(2,128)S(1)} %bitcast.13, bf16[3,20,128,384]{3,2,1,0:T(8,128)(2,1)} %frames.3, bf16[972,128]{1,0:T(8,128)(2,1)S(1)} %collective-permute-done.1.refs_0_.other), custom_call_target="tpu_custom_call" | custom-call | tf_op jit(solution)/shard_map/cut_above/pallas_call | solution.py:95
  20.3 0.7 collective-permute-start.2
  21.0 1.6 %collective-permute-start.8 = (bf16[972,128]{1,0:T(8,128)(2,1)S(1)}, bf16[972,128]{1,0:T(8,128)(2,1)S(1)}, u32[]{:S(2)}, u32[]{:S(2)}) collective-permute-start(bf16[972,128]{1,0:T(8,128)(2,1)S(1)} %get-tuple-element.37), channel_id=1, source_target_pairs={{0,4},{1,5},{2,6},{3,7},{4,8},{5,9},{6,10},{7,11},{8,12},{9,13},{1... | collective-permute-start | bytes 746504 | tf_op jit(solution)/shard_map/ppermute | solution.py:399
  22.6 2.9 %collective-permute-start.6 = (bf16[972,128]{1,0:T(8,128)(2,1)S(1)}, bf16[972,128]{1,0:T(8,128)(2,1)S(1)}, u32[]{:S(2)}, u32[]{:S(2)}) collective-permute-start(bf16[972,128]{1,0:T(8,128)(2,1)S(1)} %get-tuple-element.35), channel_id=1, source_target_pairs={{0,8},{1,9},{2,10},{3,11},{4,12},{5,13},{6,14},{7,15},{8,0},{9,1},... | collective-permute-start | bytes 746504 | tf_op jit(solution)/shard_map/ppermute | solution.py:399
  25.5 1.4 %collective-permute-start.4 = (bf16[972,128]{1,0:T(8,128)(2,1)S(1)}, bf16[972,128]{1,0:T(8,128)(2,1)S(1)}, u32[]{:S(2)}, u32[]{:S(2)}) collective-permute-start(bf16[972,128]{1,0:T(8,128)(2,1)S(1)} %get-tuple-element.33), channel_id=1, source_target_pairs={{0,12},{1,13},{2,14},{3,15},{4,0},{5,1},{6,2},{7,3},{8,4},{9,5},{1... | collective-permute-start | bytes 746504 | tf_op jit(solution)/shard_map/ppermute | solution.py:399
  26.9 2.6 %collective-permute-done.8.own = bf16[972,128]{1,0:T(8,128)(2,1)S(1)} collective-permute-done((bf16[972,128]{1,0:T(8,128)(2,1)S(1)}, bf16[972,128]{1,0:T(8,128)(2,1)S(1)}, u32[]{:S(2)}, u32[]{:S(2)}) %collective-permute-start.8) | collective-permute-done | bytes 248864 | tf_op jit(solution)/shard_map/ppermute | solution.py:399
  29.5 2.3 %collective-permute-start.9 = (bf16[972,128]{1,0:T(8,128)(2,1)S(1)}, bf16[972,128]{1,0:T(8,128)(2,1)S(1)}, u32[]{:S(2)}, u32[]{:S(2)}) collective-permute-start(bf16[972,128]{1,0:T(8,128)(2,1)S(1)} %collective-permute-done.8.own), channel_id=1, source_target_pairs={{0,2},{1,3},{2,0},{3,1},{4,6},{5,7},{6,4},{7,5},{8,10},{9,11},{10,... | collective-permute-start | bytes 746504 | tf_op jit(solution)/shard_map/ppermute | solution.py:399
  31.7 4.4 %collective-permute-done.6.own = bf16[972,128]{1,0:T(8,128)(2,1)S(1)} collective-permute-done((bf16[972,128]{1,0:T(8,128)(2,1)S(1)}, bf16[972,128]{1,0:T(8,128)(2,1)S(1)}, u32[]{:S(2)}, u32[]{:S(2)}) %collective-permute-start.6) | collective-permute-done | bytes 248864 | tf_op jit(solution)/shard_map/ppermute | solution.py:399
  36.1 1.5 %collective-permute-start.7 = (bf16[972,128]{1,0:T(8,128)(2,1)S(1)}, bf16[972,128]{1,0:T(8,128)(2,1)S(1)}, u32[]{:S(2)}, u32[]{:S(2)}) collective-permute-start(bf16[972,128]{1,0:T(8,128)(2,1)S(1)} %collective-permute-done.6.own), channel_id=1, source_target_pairs={{0,2},{1,3},{2,0},{3,1},{4,6},{5,7},{6,4},{7,5},{8,10},{9,11},{10,... | collective-permute-start | bytes 746504 | tf_op jit(solution)/shard_map/ppermute | solution.py:399
  37.6 0.0 collective-permute-start.5
  37.6 0.2 filters.4
  37.8 0.0 collective-permute-done.9.other
  37.8 0.2 filters.7
  38.1 0.6 collective-permute-done.7.other
  38.7 0.3 filters.6
  39.0 0.1 collective-permute-done.5.other
  39.1 0.3 filters.5
  39.4 0.3 join.1.patch_in
  39.7 4.1 %column.1 = (bf16[972,768]{1,0:T(8,128)(2,1)S(1)}, bf16[1024,768]{1,0:T(8,128)(2,1)S(1)}) custom-call(bf16[972,384]{1,0:T(8,128)(2,1)S(1)} %join.1.patch_in, bf16[972,256]{1,0:T(8,128)(2,1)S(1)} %get-tuple-element.32.refs_0_, bf16[972,256]{1,0:T(8,128)(2,1)S(1)} %get-tuple-element.34.refs_1_, bf16[972,256]{1,0:T(8,128)(2,1)S(1)} %get-tuple-element.36.refs_2_, ...), custom_call_target="tpu_custom_call" | custom-call | tf_op jit(solution)/shard_map/column/pallas_call | solution.py:231
  43.8 0.6 piece.2
  44.4 1.5 %piece.3 = (f32[2928,128]{1,0:T(8,128)S(1)}, bf16[2928,128]{1,0:T(8,128)(2,1)S(1)}) custom-call(bf16[972,768]{1,0:T(8,128)(2,1)S(1)} %get-tuple-element.43.pe, bf16[1024,768]{1,0:T(8,128)(2,1)S(1)} %get-tuple-element.44.mr, bf16[976,128]{1,0:T(8,128)(2,1)S(1)} %get-tuple-element.45.refs_0_), custom_call_target="tpu_custom_call" | custom-call | tf_op jit(solution)/shard_map/piece/pallas_call | solution.py:276
  45.9 0.5 collective-permute-start.10
  46.3 0.1 collective-permute-start.11
  46.5 2.1 %collective-permute-done.11.away = bf16[976,128]{1,0:T(8,128)(2,1)S(1)} collective-permute-done((bf16[976,128]{1,0:T(8,128)(2,1)S(1)}, bf16[976,128]{1,0:T(8,128)(2,1)S(1)}, u32[]{:S(2)}, u32[]{:S(2)}) %collective-permute-start.11) | collective-permute-done | bytes 249888 | tf_op jit(solution)/shard_map/ppermute | solution.py:399
  48.6 2.0 %collective-permute-start.12 = (bf16[972,128]{1,0:T(8,128)(2,1)S(1)}, bf16[972,128]{1,0:T(8,128)(2,1)S(1)}, u32[]{:S(2)}, u32[]{:S(2)}) collective-permute-start(bf16[972,128]{1,0:T(8,128)(2,1)S(1)} %total.2.refs_0_), channel_id=1, source_target_pairs={{0,1},{1,0},{2,3},{3,2},{4,5},{5,4},{6,7},{7,6},{8,9},{9,8},{10,11... | collective-permute-start | bytes 746504 | tf_op jit(solution)/shard_map/ppermute | solution.py:399
  50.6 0.1 total.3
  50.7 0.9 %collective-permute-start.15 = (bf16[972,128]{1,0:T(8,128)(2,1)S(1)}, bf16[972,128]{1,0:T(8,128)(2,1)S(1)}, u32[]{:S(2)}, u32[]{:S(2)}) collective-permute-start(bf16[972,128]{1,0:T(8,128)(2,1)S(1)} %get-tuple-element.50), channel_id=1, source_target_pairs={{0,4},{1,5},{2,6},{3,7},{4,8},{5,9},{6,10},{7,11},{8,12},{9,13},{1... | collective-permute-start | bytes 746504 | tf_op jit(solution)/shard_map/ppermute | solution.py:399
  51.6 2.4 %collective-permute-start.17 = (bf16[972,128]{1,0:T(8,128)(2,1)S(1)}, bf16[972,128]{1,0:T(8,128)(2,1)S(1)}, u32[]{:S(2)}, u32[]{:S(2)}) collective-permute-start(bf16[972,128]{1,0:T(8,128)(2,1)S(1)} %get-tuple-element.51), channel_id=1, source_target_pairs={{0,12},{1,13},{2,14},{3,15},{4,0},{5,1},{6,2},{7,3},{8,4},{9,5},{1... | collective-permute-start | bytes 746504 | tf_op jit(solution)/shard_map/ppermute | solution.py:399
  54.0 3.0 %collective-permute-done.12.after.refs_1_ = bf16[972,128]{1,0:T(8,128)(2,1)S(1)} collective-permute-done((bf16[972,128]{1,0:T(8,128)(2,1)S(1)}, bf16[972,128]{1,0:T(8,128)(2,1)S(1)}, u32[]{:S(2)}, u32[]{:S(2)}) %collective-permute-start.12) | collective-permute-done | bytes 248864 | tf_op jit(solution)/shard_map/ppermute | solution.py:399
  57.0 2.6 %collective-permute-start.13 = (bf16[972,128]{1,0:T(8,128)(2,1)S(1)}, bf16[972,128]{1,0:T(8,128)(2,1)S(1)}, u32[]{:S(2)}, u32[]{:S(2)}) collective-permute-start(bf16[972,128]{1,0:T(8,128)(2,1)S(1)} %follow.1), channel_id=1, source_target_pairs={{0,8},{1,9},{2,10},{3,11},{4,12},{5,13},{6,14},{7,15},{8,0},{9,1},... | collective-permute-start | bytes 746504 | tf_op jit(solution)/shard_map/ppermute | solution.py:399
  59.6 0.2 collective-permute-done.15.refs_2_
  59.8 1.2 %collective-permute-start.16 = (bf16[972,128]{1,0:T(8,128)(2,1)S(1)}, bf16[972,128]{1,0:T(8,128)(2,1)S(1)}, u32[]{:S(2)}, u32[]{:S(2)}) collective-permute-start(bf16[972,128]{1,0:T(8,128)(2,1)S(1)} %collective-permute-done.15.refs_2_), channel_id=1, source_target_pairs={{0,1},{1,0},{2,3},{3,2},{4,5},{5,4},{6,7},{7,6},{8,9},{9,8},{10,11... | collective-permute-start | bytes 746504 | tf_op jit(solution)/shard_map/ppermute | solution.py:399
  61.0 0.8 %collective-permute-start.18 = (bf16[972,128]{1,0:T(8,128)(2,1)S(1)}, bf16[972,128]{1,0:T(8,128)(2,1)S(1)}, u32[]{:S(2)}, u32[]{:S(2)}) collective-permute-start(bf16[972,128]{1,0:T(8,128)(2,1)S(1)} %collective-permute-done.17.refs_4_), channel_id=1, source_target_pairs={{0,1},{1,0},{2,3},{3,2},{4,5},{5,4},{6,7},{7,6},{8,9},{9,8},{10,11... | collective-permute-start | bytes 746504 | tf_op jit(solution)/shard_map/ppermute | solution.py:399
  61.8 4.3 %collective-permute-done.13.refs_0_ = bf16[972,128]{1,0:T(8,128)(2,1)S(1)} collective-permute-done((bf16[972,128]{1,0:T(8,128)(2,1)S(1)}, bf16[972,128]{1,0:T(8,128)(2,1)S(1)}, u32[]{:S(2)}, u32[]{:S(2)}) %collective-permute-start.13) | collective-permute-done | bytes 248864 | tf_op jit(solution)/shard_map/ppermute | solution.py:399
  66.1 1.4 %collective-permute-start.14 = (bf16[972,128]{1,0:T(8,128)(2,1)S(1)}, bf16[972,128]{1,0:T(8,128)(2,1)S(1)}, u32[]{:S(2)}, u32[]{:S(2)}) collective-permute-start(bf16[972,128]{1,0:T(8,128)(2,1)S(1)} %collective-permute-done.13.refs_0_), channel_id=1, source_target_pairs={{0,1},{1,0},{2,3},{3,2},{4,5},{5,4},{6,7},{7,6},{8,9},{9,8},{10,11... | collective-permute-start | bytes 746504 | tf_op jit(solution)/shard_map/ppermute | solution.py:399
  67.5 1.2 %collective-permute-done.16.refs_3_ = bf16[972,128]{1,0:T(8,128)(2,1)S(1)} collective-permute-done((bf16[972,128]{1,0:T(8,128)(2,1)S(1)}, bf16[972,128]{1,0:T(8,128)(2,1)S(1)}, u32[]{:S(2)}, u32[]{:S(2)}) %collective-permute-start.16) | collective-permute-done | bytes 248864 | tf_op jit(solution)/shard_map/ppermute | solution.py:399
  68.8 5.4 %collective-permute-done.18.refs_5_ = bf16[972,128]{1,0:T(8,128)(2,1)S(1)} collective-permute-done((bf16[972,128]{1,0:T(8,128)(2,1)S(1)}, bf16[972,128]{1,0:T(8,128)(2,1)S(1)}, u32[]{:S(2)}, u32[]{:S(2)}) %collective-permute-start.18) | collective-permute-done | bytes 248864 | tf_op jit(solution)/shard_map/ppermute | solution.py:399
  74.1 0.8 %gather.1.refs_3_ = f32[7776,128]{1,0:T(8,128)S(1)} custom-call(bf16[972,128]{1,0:T(8,128)(2,1)S(1)} %total.2.refs_0_, bf16[972,128]{1,0:T(8,128)(2,1)S(1)} %collective-permute-done.12.after.refs_1_, bf16[972,128]{1,0:T(8,128)(2,1)S(1)} %collective-permute-done.15.refs_2_, bf16[972,128]{1,0:T(8,128)(2,1)S(1)} %collective-permute-done.16.refs_3_, ...), custom_call_target="tpu_custom_call" | custom-call | tf_op jit(solution)/shard_map/gather/pallas_call | solution.py:339
  75.0 2.6 %collective-permute-done.14.refs_1_ = bf16[972,128]{1,0:T(8,128)(2,1)S(1)} collective-permute-done((bf16[972,128]{1,0:T(8,128)(2,1)S(1)}, bf16[972,128]{1,0:T(8,128)(2,1)S(1)}, u32[]{:S(2)}, u32[]{:S(2)}) %collective-permute-start.14) | collective-permute-done | bytes 248864 | tf_op jit(solution)/shard_map/ppermute | solution.py:399
  77.6 2.5 %finish.1 = (f32[3888,128]{1,0:T(8,128)}, bf16[7776,128]{1,0:T(8,128)(2,1)}) custom-call(bf16[972,128]{1,0:T(8,128)(2,1)S(1)} %collective-permute-done.13.refs_0_, bf16[972,128]{1,0:T(8,128)(2,1)S(1)} %collective-permute-done.14.refs_1_, bf16[7776,128]{1,0:T(8,128)(2,1)S(1)} %bitcast.11, f32[7776,128]{1,0:T(8,128)S(1)} %gather.1.refs_3_), custom_call_target="tpu_custom_call" | custom-call | tf_op jit(solution)/shard_map/finish/pallas_call | solution.py:375
  (10 shorter events, 0.1 us)
Async XLA Ops:
  0.6 11.9 %copy-start = (bf16[8,972,128]{2,0,1:T(8,128)(2,1)S(1)}, bf16[8,972,128]{2,0,1:T(8,128)(2,1)}, u32[]{:S(2)}) copy-start(bf16[8,972,128]{2,0,1:T(8,128)(2,1)} %param.4) | copy-start | bytes 5971972
  0.6 9.6 %collective-permute-start = (s32[2,8]{1,0:T(2,128)}, s32[2,8]{1,0:T(2,128)S(1)}, u32[]{:S(2)}, u32[]{:S(2)}) collective-permute-start(s32[2,8]{1,0:T(2,128)} %bitcast.12), channel_id=1, source_target_pairs={{0,16},{1,17},{2,18},{3,19},{4,20},{5,21},{6,22},{7,23},{8,24},{9,... | collective-permute-start | bytes 200 | tf_op jit(solution)/shard_map/ppermute | solution.py:399
  12.6 4.9 %copy-start.1 = (s32[8,2]{0,1:T(2,128)S(1)}, s32[8,2]{0,1:T(2,128)}, u32[]{:S(2)}) copy-start(s32[8,2]{0,1:T(2,128)} %param.5) | copy-start | bytes 196
  13.4 4.0 %collective-permute-start.1 = (bf16[972,128]{1,0:T(8,128)(2,1)S(1)}, bf16[972,128]{1,0:T(8,128)(2,1)S(1)}, u32[]{:S(2)}, u32[]{:S(2)}) collective-permute-start(bf16[972,128]{1,0:T(8,128)(2,1)S(1)} %get-tuple-element.29.own), channel_id=1, source_target_pairs={{0,2},{1,3},{2,0},{3,1},{4,6},{5,7},{6,4},{7,5},{8,10},{9,11},{10,... | collective-permute-start | bytes 746504 | tf_op jit(solution)/shard_map/ppermute | solution.py:399
  13.5 25.9 %collective-permute-start.3 = (bf16[972,384]{1,0:T(8,128)(2,1)S(1)}, bf16[972,384]{1,0:T(8,128)(2,1)S(1)}, u32[]{:S(2)}, u32[]{:S(2)}) collective-permute-start(bf16[972,384]{1,0:T(8,128)(2,1)S(1)} %get-tuple-element.31), channel_id=1, source_target_pairs={{16,0},{17,2},{18,1},{19,3},{20,4},{21,6},{22,5},{23,7},{24,8},{25... | collective-permute-start | bytes 2239496 | tf_op jit(solution)/shard_map/ppermute | solution.py:399
  20.3 19.1 %collective-permute-start.2 = (bf16[972,384]{1,0:T(8,128)(2,1)S(1)}, bf16[972,384]{1,0:T(8,128)(2,1)S(1)}, u32[]{:S(2)}, u32[]{:S(2)}) collective-permute-start(bf16[972,384]{1,0:T(8,128)(2,1)S(1)} %get-tuple-element.30.above), channel_id=1, source_target_pairs={{1,2},{2,1},{5,6},{6,5},{9,10},{10,9},{13,14},{14,13},{17,18},{18,... | collective-permute-start | bytes 2239496 | tf_op jit(solution)/shard_map/ppermute | solution.py:399
  21.0 8.5 %collective-permute-start.8 = (bf16[972,128]{1,0:T(8,128)(2,1)S(1)}, bf16[972,128]{1,0:T(8,128)(2,1)S(1)}, u32[]{:S(2)}, u32[]{:S(2)}) collective-permute-start(bf16[972,128]{1,0:T(8,128)(2,1)S(1)} %get-tuple-element.37), channel_id=1, source_target_pairs={{0,4},{1,5},{2,6},{3,7},{4,8},{5,9},{6,10},{7,11},{8,12},{9,13},{1... | collective-permute-start | bytes 746504 | tf_op jit(solution)/shard_map/ppermute | solution.py:399
  22.6 13.5 %collective-permute-start.6 = (bf16[972,128]{1,0:T(8,128)(2,1)S(1)}, bf16[972,128]{1,0:T(8,128)(2,1)S(1)}, u32[]{:S(2)}, u32[]{:S(2)}) collective-permute-start(bf16[972,128]{1,0:T(8,128)(2,1)S(1)} %get-tuple-element.35), channel_id=1, source_target_pairs={{0,8},{1,9},{2,10},{3,11},{4,12},{5,13},{6,14},{7,15},{8,0},{9,1},... | collective-permute-start | bytes 746504 | tf_op jit(solution)/shard_map/ppermute | solution.py:399
  25.5 12.1 %collective-permute-start.4 = (bf16[972,128]{1,0:T(8,128)(2,1)S(1)}, bf16[972,128]{1,0:T(8,128)(2,1)S(1)}, u32[]{:S(2)}, u32[]{:S(2)}) collective-permute-start(bf16[972,128]{1,0:T(8,128)(2,1)S(1)} %get-tuple-element.33), channel_id=1, source_target_pairs={{0,12},{1,13},{2,14},{3,15},{4,0},{5,1},{6,2},{7,3},{8,4},{9,5},{1... | collective-permute-start | bytes 746504 | tf_op jit(solution)/shard_map/ppermute | solution.py:399
  29.5 8.4 %collective-permute-start.9 = (bf16[972,128]{1,0:T(8,128)(2,1)S(1)}, bf16[972,128]{1,0:T(8,128)(2,1)S(1)}, u32[]{:S(2)}, u32[]{:S(2)}) collective-permute-start(bf16[972,128]{1,0:T(8,128)(2,1)S(1)} %collective-permute-done.8.own), channel_id=1, source_target_pairs={{0,2},{1,3},{2,0},{3,1},{4,6},{5,7},{6,4},{7,5},{8,10},{9,11},{10,... | collective-permute-start | bytes 746504 | tf_op jit(solution)/shard_map/ppermute | solution.py:399
  36.1 2.6 %collective-permute-start.7 = (bf16[972,128]{1,0:T(8,128)(2,1)S(1)}, bf16[972,128]{1,0:T(8,128)(2,1)S(1)}, u32[]{:S(2)}, u32[]{:S(2)}) collective-permute-start(bf16[972,128]{1,0:T(8,128)(2,1)S(1)} %collective-permute-done.6.own), channel_id=1, source_target_pairs={{0,2},{1,3},{2,0},{3,1},{4,6},{5,7},{6,4},{7,5},{8,10},{9,11},{10,... | collective-permute-start | bytes 746504 | tf_op jit(solution)/shard_map/ppermute | solution.py:399
  37.6 1.5 %collective-permute-start.5 = (bf16[972,128]{1,0:T(8,128)(2,1)S(1)}, bf16[972,128]{1,0:T(8,128)(2,1)S(1)}, u32[]{:S(2)}, u32[]{:S(2)}) collective-permute-start(bf16[972,128]{1,0:T(8,128)(2,1)S(1)} %collective-permute-done.4.own), channel_id=1, source_target_pairs={{0,2},{1,3},{2,0},{3,1},{4,6},{5,7},{6,4},{7,5},{8,10},{9,11},{10,... | collective-permute-start | bytes 746504 | tf_op jit(solution)/shard_map/ppermute | solution.py:399
  45.9 4.7 %collective-permute-start.10 = (bf16[2928,128]{1,0:T(8,128)(2,1)S(1)}, bf16[2928,128]{1,0:T(8,128)(2,1)S(1)}, u32[]{:S(2)}, u32[]{:S(2)}) collective-permute-start(bf16[2928,128]{1,0:T(8,128)(2,1)S(1)} %get-tuple-element.47), channel_id=1, source_target_pairs={{0,2},{1,3},{2,0},{3,1},{4,6},{5,7},{6,4},{7,5},{8,10},{9,11},{10,... | collective-permute-start | bytes 2248712 | tf_op jit(solution)/shard_map/ppermute | solution.py:399
  46.3 2.2 %collective-permute-start.11 = (bf16[976,128]{1,0:T(8,128)(2,1)S(1)}, bf16[976,128]{1,0:T(8,128)(2,1)S(1)}, u32[]{:S(2)}, u32[]{:S(2)}) collective-permute-start(bf16[976,128]{1,0:T(8,128)(2,1)S(1)} %get-tuple-element.45.refs_0_), channel_id=1, source_target_pairs={{0,2},{1,3},{2,0},{3,1},{4,6},{5,7},{6,4},{7,5},{8,10},{9,11},{10,... | collective-permute-start | bytes 749576 | tf_op jit(solution)/shard_map/ppermute | solution.py:399
  48.6 8.4 %collective-permute-start.12 = (bf16[972,128]{1,0:T(8,128)(2,1)S(1)}, bf16[972,128]{1,0:T(8,128)(2,1)S(1)}, u32[]{:S(2)}, u32[]{:S(2)}) collective-permute-start(bf16[972,128]{1,0:T(8,128)(2,1)S(1)} %total.2.refs_0_), channel_id=1, source_target_pairs={{0,1},{1,0},{2,3},{3,2},{4,5},{5,4},{6,7},{7,6},{8,9},{9,8},{10,11... | collective-permute-start | bytes 746504 | tf_op jit(solution)/shard_map/ppermute | solution.py:399
  50.7 9.1 %collective-permute-start.15 = (bf16[972,128]{1,0:T(8,128)(2,1)S(1)}, bf16[972,128]{1,0:T(8,128)(2,1)S(1)}, u32[]{:S(2)}, u32[]{:S(2)}) collective-permute-start(bf16[972,128]{1,0:T(8,128)(2,1)S(1)} %get-tuple-element.50), channel_id=1, source_target_pairs={{0,4},{1,5},{2,6},{3,7},{4,8},{5,9},{6,10},{7,11},{8,12},{9,13},{1... | collective-permute-start | bytes 746504 | tf_op jit(solution)/shard_map/ppermute | solution.py:399
  51.6 9.3 %collective-permute-start.17 = (bf16[972,128]{1,0:T(8,128)(2,1)S(1)}, bf16[972,128]{1,0:T(8,128)(2,1)S(1)}, u32[]{:S(2)}, u32[]{:S(2)}) collective-permute-start(bf16[972,128]{1,0:T(8,128)(2,1)S(1)} %get-tuple-element.51), channel_id=1, source_target_pairs={{0,12},{1,13},{2,14},{3,15},{4,0},{5,1},{6,2},{7,3},{8,4},{9,5},{1... | collective-permute-start | bytes 746504 | tf_op jit(solution)/shard_map/ppermute | solution.py:399
  57.0 9.1 %collective-permute-start.13 = (bf16[972,128]{1,0:T(8,128)(2,1)S(1)}, bf16[972,128]{1,0:T(8,128)(2,1)S(1)}, u32[]{:S(2)}, u32[]{:S(2)}) collective-permute-start(bf16[972,128]{1,0:T(8,128)(2,1)S(1)} %follow.1), channel_id=1, source_target_pairs={{0,8},{1,9},{2,10},{3,11},{4,12},{5,13},{6,14},{7,15},{8,0},{9,1},... | collective-permute-start | bytes 746504 | tf_op jit(solution)/shard_map/ppermute | solution.py:399
  59.8 9.0 %collective-permute-start.16 = (bf16[972,128]{1,0:T(8,128)(2,1)S(1)}, bf16[972,128]{1,0:T(8,128)(2,1)S(1)}, u32[]{:S(2)}, u32[]{:S(2)}) collective-permute-start(bf16[972,128]{1,0:T(8,128)(2,1)S(1)} %collective-permute-done.15.refs_2_), channel_id=1, source_target_pairs={{0,1},{1,0},{2,3},{3,2},{4,5},{5,4},{6,7},{7,6},{8,9},{9,8},{10,11... | collective-permute-start | bytes 746504 | tf_op jit(solution)/shard_map/ppermute | solution.py:399
  61.0 13.2 %collective-permute-start.18 = (bf16[972,128]{1,0:T(8,128)(2,1)S(1)}, bf16[972,128]{1,0:T(8,128)(2,1)S(1)}, u32[]{:S(2)}, u32[]{:S(2)}) collective-permute-start(bf16[972,128]{1,0:T(8,128)(2,1)S(1)} %collective-permute-done.17.refs_4_), channel_id=1, source_target_pairs={{0,1},{1,0},{2,3},{3,2},{4,5},{5,4},{6,7},{7,6},{8,9},{9,8},{10,11... | collective-permute-start | bytes 746504 | tf_op jit(solution)/shard_map/ppermute | solution.py:399
  66.1 11.4 %collective-permute-start.14 = (bf16[972,128]{1,0:T(8,128)(2,1)S(1)}, bf16[972,128]{1,0:T(8,128)(2,1)S(1)}, u32[]{:S(2)}, u32[]{:S(2)}) collective-permute-start(bf16[972,128]{1,0:T(8,128)(2,1)S(1)} %collective-permute-done.13.refs_0_), channel_id=1, source_target_pairs={{0,1},{1,0},{2,3},{3,2},{4,5},{5,4},{6,7},{7,6},{8,9},{9,8},{10,11... | collective-permute-start | bytes 746504 | tf_op jit(solution)/shard_map/ppermute | solution.py:399

commit v7 on v6

--- a/solution.py
+++ b/solution.py
@@ -401,21 +401,19 @@
     dps = mesh_shape[2]
     places = offsets.T
     upper = send(places, lambda t, y, k, d: (t + 1, y, k, d))
-    below, token = cut(frames, upper, False)
-    own = blocks(weights, rows_y, dps, (token,))
+    own = blocks(weights, rows_y, dps)
+    below, token = cut(frames, upper, False, (own[0],))
     below = send(below, lambda t, y, k, d: (t - 1, y, d, k))
 
+    own = [own[0]] + [
+        send(own[s], lambda t, y, k, d: (t, y - s, k, d)) for s in range(1, rows_y)
+    ]
+    above, _ = cut(frames, places, True, own[1:])
     weight, turned = [], []
-    for s in range(rows_y):
-        block = own[s]
-        if s:
-            block = send(block, lambda t, y, k, d: (t, y - s, k, d))
-        other = send(block, lambda t, y, k, d: (t, y, 1 - k, d))
-        pair = filters(block, other)
+    for block in own:
+        pair = filters(block, send(block, lambda t, y, k, d: (t, y, 1 - k, d)))
         weight.append(pair[0])
         turned.append(pair[1])
-        if s == 0:
-            above, _ = cut(frames, places, True, (other,))
     above_in = send(above, lambda t, y, k, d: (t, y, d, k) if k != d else None)
     above_in = send(above, lambda t, y, k, d: (t, y, d, k) if k != d else None)
 

time: 80.4 us -> 84.7 us (1.053)
  waiting for transfers between devices: 32 us -> 34.3 us
  local copies, waits for them, and re-layouts: 0.01 us -> 1.56 us
    ppermute x19, waiting for transfers between devices: 32 us -> 34.3 us  [send(): return lax.ppermute(x, AXES, table(mesh_shape, move))]
    unnamed x4 -> x6, local copies, waits for them, and re-layouts: 0.01 us -> 1.56 us
  transfers between devices with their start and end apart: 19 -> 19, of which waited for: 12 -> 11; matrix products, arithmetic and copies ran while one was open for 0% -> 0% of each run, Pallas kernels for 6% -> 9%
where the time goes in v7:
time: 84.7 us; the launch traced here: 84.5 us
  waiting for transfers between devices  34.3 us (40%)
  starting transfers between devices  30.2 us (36%)
  Pallas kernels  17.4 us (21%)
  local copies, waits for them, and re-layouts  1.56 us (2%)
  between operations  0.97 us (1%)
    ppermute x19, waiting for transfers between devices, send(): return lax.ppermute(x, AXES, table(mesh_shape, move))  34.3 us
    ppermute x19, starting transfers between devices, send(): return lax.ppermute(x, AXES, table(mesh_shape, move))  30.2 us
    pallas_call x2, Pallas kernels, cut(): pl.pallas_call(functools.partial(cut_kernel, above), out_shape=[jax.Shape...  5.65 us
    pallas_call x1, Pallas kernels, column(): pl.pallas_call(functools.partial(column_kernel, rows_y), out_shape=[jax.S...  4.09 us
    pallas_call x1, Pallas kernels, finish(): pl.pallas_call(functools.partial(finish_kernel, rows_y, dps, shifts), out...  2.5 us
    pallas_call x2, Pallas kernels, piece(): pl.pallas_call(functools.partial(piece_kernel, shifts, 1.0 / depth), out_...  2.07 us
  transfers between devices with their start and end apart: 19, of which 11 were waited for; matrix products, arithmetic and copies ran while one was open for 0% of the time, Pallas kernels for 9%

profile of v7, /device:TPU:4, one launch (start us, length us, event | category | flops | bytes accessed | tf_op | source)
XLA Modules:
  0.0 84.5 jit_solution(12860397858945884788)
XLA Ops:
  0.6 0.0 copy-start
  0.7 1.5 %copy-done = bf16[8,972,128]{2,0,1:T(8,128)(2,1)S(1)} copy-done((bf16[8,972,128]{2,0,1:T(8,128)(2,1)S(1)}, bf16[8,972,128]{2,0,1:T(8,128)(2,1)}, u32[]{:S(2)}) %copy-start) | copy-done | bytes 1990680
  2.2 0.8 blocks.1
  3.0 3.1 %collective-permute-start = (bf16[972,128]{1,0:T(8,128)(2,1)S(1)}, bf16[972,128]{1,0:T(8,128)(2,1)S(1)}, u32[]{:S(2)}, u32[]{:S(2)}) collective-permute-start(bf16[972,128]{1,0:T(8,128)(2,1)S(1)} %get-tuple-element.27), channel_id=1, source_target_pairs={{0,12},{1,13},{2,14},{3,15},{4,0},{5,1},{6,2},{7,3},{8,4},{9,5},{1... | collective-permute-start | bytes 746504 | tf_op jit(solution)/shard_map/ppermute | solution.py:399
  6.1 0.6 collective-permute-start.1
  6.7 1.0 %collective-permute-start.2 = (bf16[972,128]{1,0:T(8,128)(2,1)S(1)}, bf16[972,128]{1,0:T(8,128)(2,1)S(1)}, u32[]{:S(2)}, u32[]{:S(2)}) collective-permute-start(bf16[972,128]{1,0:T(8,128)(2,1)S(1)} %get-tuple-element.29), channel_id=1, source_target_pairs={{0,4},{1,5},{2,6},{3,7},{4,8},{5,9},{6,10},{7,11},{8,12},{9,13},{1... | collective-permute-start | bytes 746504 | tf_op jit(solution)/shard_map/ppermute | solution.py:399
  7.7 3.8 %collective-permute-start.4 = (s32[2,8]{1,0:T(2,128)S(1)}, s32[2,8]{1,0:T(2,128)S(1)}, u32[]{:S(2)}, u32[]{:S(2)}) collective-permute-start(s32[2,8]{1,0:T(2,128)S(1)} %bitcast.12), channel_id=1, source_target_pairs={{0,16},{1,17},{2,18},{3,19},{4,20},{5,21},{6,22},{7,23},{8,24},{9,... | collective-permute-start | bytes 200 | tf_op jit(solution)/shard_map/ppermute | solution.py:399
  11.5 5.4 %collective-permute-done.4.places = s32[2,8]{1,0:T(2,128)S(1)} collective-permute-done((s32[2,8]{1,0:T(2,128)S(1)}, s32[2,8]{1,0:T(2,128)S(1)}, u32[]{:S(2)}, u32[]{:S(2)}) %collective-permute-start.4) | collective-permute-done | bytes 96 | tf_op jit(solution)/shard_map/ppermute | solution.py:399
  16.9 2.8 %cut_below.1 = (bf16[972,384]{1,0:T(8,128)(2,1)S(1)}, f32[8,128]{1,0:T(8,128)}) custom-call(s32[2,8]{1,0:T(2,128)S(1)} %collective-permute-done.4.places, bf16[3,20,128,384]{3,2,1,0:T(8,128)(2,1)} %frames.3, bf16[972,128]{1,0:T(8,128)(2,1)S(1)} %get-tuple-element.31.refs_0_.own), custom_call_target="tpu_custom_call" | custom-call | tf_op jit(solution)/shard_map/cut_below/pallas_call | solution.py:95
  19.7 3.9 %collective-permute-start.5 = (bf16[972,384]{1,0:T(8,128)(2,1)S(1)}, bf16[972,384]{1,0:T(8,128)(2,1)S(1)}, u32[]{:S(2)}, u32[]{:S(2)}) collective-permute-start(bf16[972,384]{1,0:T(8,128)(2,1)S(1)} %get-tuple-element.32), channel_id=1, source_target_pairs={{16,0},{17,2},{18,1},{19,3},{20,4},{21,6},{22,5},{23,7},{24,8},{25... | collective-permute-start | bytes 2239496 | tf_op jit(solution)/shard_map/ppermute | solution.py:399
  23.7 0.0 collective-permute-done.refs_0_.own
  23.7 2.8 %cut_above.1 = (bf16[972,384]{1,0:T(8,128)(2,1)S(1)}, f32[8,128]{1,0:T(8,128)}) custom-call(s32[2,8]{1,0:T(2,128)S(1)} %bitcast.13, bf16[3,20,128,384]{3,2,1,0:T(8,128)(2,1)} %frames.3, bf16[972,128]{1,0:T(8,128)(2,1)S(1)} %collective-permute-done.refs_0_.own, bf16[972,128]{1,0:T(8,128)(2,1)S(1)} %collective-permute-done.1.refs_1_.own, ...), custom_call_target="tpu_custom_call" | custom-call | tf_op jit(solution)/shard_map/cut_above/pallas_call | solution.py:95
  26.5 0.7 collective-permute-start.3
  27.3 1.5 %collective-permute-start.6 = (bf16[972,128]{1,0:T(8,128)(2,1)S(1)}, bf16[972,128]{1,0:T(8,128)(2,1)S(1)}, u32[]{:S(2)}, u32[]{:S(2)}) collective-permute-start(bf16[972,128]{1,0:T(8,128)(2,1)S(1)} %get-tuple-element.31.refs_0_.own), channel_id=1, source_target_pairs={{0,2},{1,3},{2,0},{3,1},{4,6},{5,7},{6,4},{7,5},{8,10},{9,11},{10,... | collective-permute-start | bytes 746504 | tf_op jit(solution)/shard_map/ppermute | solution.py:399
  28.7 0.1 collective-permute-start.9
  28.9 0.4 collective-permute-start.8
  29.3 0.6 collective-permute-done.6.other
  29.9 0.4 collective-permute-start.7
  30.3 0.2 filters.4
  30.5 0.3 filters.7
  30.8 0.3 filters.6
  31.0 0.4 collective-permute-done.7.other
  31.4 0.2 filters.5
  31.7 8.6 %collective-permute-done.5.below = bf16[972,384]{1,0:T(8,128)(2,1)S(1)} collective-permute-done((bf16[972,384]{1,0:T(8,128)(2,1)S(1)}, bf16[972,384]{1,0:T(8,128)(2,1)S(1)}, u32[]{:S(2)}, u32[]{:S(2)}) %collective-permute-start.5) | collective-permute-done | bytes 746528 | tf_op jit(solution)/shard_map/ppermute | solution.py:399
  40.3 0.3 join.1.patch_in
  40.6 4.1 %column.1 = (bf16[972,768]{1,0:T(8,128)(2,1)S(1)}, bf16[1024,768]{1,0:T(8,128)(2,1)S(1)}) custom-call(bf16[972,384]{1,0:T(8,128)(2,1)S(1)} %join.1.patch_in, bf16[972,256]{1,0:T(8,128)(2,1)S(1)} %get-tuple-element.33.refs_0_, bf16[972,256]{1,0:T(8,128)(2,1)S(1)} %get-tuple-element.34.refs_1_, bf16[972,256]{1,0:T(8,128)(2,1)S(1)} %get-tuple-element.35.refs_2_, ...), custom_call_target="tpu_custom_call" | custom-call | tf_op jit(solution)/shard_map/column/pallas_call | solution.py:231
  44.7 0.6 piece.2
  45.4 1.5 %piece.3 = (f32[2928,128]{1,0:T(8,128)S(1)}, bf16[2928,128]{1,0:T(8,128)(2,1)S(1)}) custom-call(bf16[972,768]{1,0:T(8,128)(2,1)S(1)} %get-tuple-element.41.pe, bf16[1024,768]{1,0:T(8,128)(2,1)S(1)} %get-tuple-element.42.mr, bf16[976,128]{1,0:T(8,128)(2,1)S(1)} %get-tuple-element.43.refs_0_), custom_call_target="tpu_custom_call" | custom-call | tf_op jit(solution)/shard_map/piece/pallas_call | solution.py:276
  46.8 3.4 %collective-permute-start.10 = (bf16[2928,128]{1,0:T(8,128)(2,1)S(1)}, bf16[2928,128]{1,0:T(8,128)(2,1)S(1)}, u32[]{:S(2)}, u32[]{:S(2)}) collective-permute-start(bf16[2928,128]{1,0:T(8,128)(2,1)S(1)} %get-tuple-element.45), channel_id=1, source_target_pairs={{0,2},{1,3},{2,0},{3,1},{4,6},{5,7},{6,4},{7,5},{8,10},{9,11},{10,... | collective-permute-start | bytes 2248712 | tf_op jit(solution)/shard_map/ppermute | solution.py:399
  50.2 0.1 collective-permute-start.11
  50.3 2.1 %collective-permute-done.11.away = bf16[976,128]{1,0:T(8,128)(2,1)S(1)} collective-permute-done((bf16[976,128]{1,0:T(8,128)(2,1)S(1)}, bf16[976,128]{1,0:T(8,128)(2,1)S(1)}, u32[]{:S(2)}, u32[]{:S(2)}) %collective-permute-start.11) | collective-permute-done | bytes 249888 | tf_op jit(solution)/shard_map/ppermute | solution.py:399
  52.5 2.4 %collective-permute-start.12 = (bf16[972,128]{1,0:T(8,128)(2,1)S(1)}, bf16[972,128]{1,0:T(8,128)(2,1)S(1)}, u32[]{:S(2)}, u32[]{:S(2)}) collective-permute-start(bf16[972,128]{1,0:T(8,128)(2,1)S(1)} %total.2.refs_0_), channel_id=1, source_target_pairs={{0,1},{1,0},{2,3},{3,2},{4,5},{5,4},{6,7},{7,6},{8,9},{9,8},{10,11... | collective-permute-start | bytes 746504 | tf_op jit(solution)/shard_map/ppermute | solution.py:399
  54.9 0.1 total.3
  55.1 2.0 %collective-permute-start.15 = (bf16[972,128]{1,0:T(8,128)(2,1)S(1)}, bf16[972,128]{1,0:T(8,128)(2,1)S(1)}, u32[]{:S(2)}, u32[]{:S(2)}) collective-permute-start(bf16[972,128]{1,0:T(8,128)(2,1)S(1)} %get-tuple-element.48), channel_id=1, source_target_pairs={{0,4},{1,5},{2,6},{3,7},{4,8},{5,9},{6,10},{7,11},{8,12},{9,13},{1... | collective-permute-start | bytes 746504 | tf_op jit(solution)/shard_map/ppermute | solution.py:399
  57.0 1.4 %collective-permute-start.17 = (bf16[972,128]{1,0:T(8,128)(2,1)S(1)}, bf16[972,128]{1,0:T(8,128)(2,1)S(1)}, u32[]{:S(2)}, u32[]{:S(2)}) collective-permute-start(bf16[972,128]{1,0:T(8,128)(2,1)S(1)} %get-tuple-element.49), channel_id=1, source_target_pairs={{0,12},{1,13},{2,14},{3,15},{4,0},{5,1},{6,2},{7,3},{8,4},{9,5},{1... | collective-permute-start | bytes 746504 | tf_op jit(solution)/shard_map/ppermute | solution.py:399
  58.4 2.9 %collective-permute-done.12.after.refs_1_ = bf16[972,128]{1,0:T(8,128)(2,1)S(1)} collective-permute-done((bf16[972,128]{1,0:T(8,128)(2,1)S(1)}, bf16[972,128]{1,0:T(8,128)(2,1)S(1)}, u32[]{:S(2)}, u32[]{:S(2)}) %collective-permute-start.12) | collective-permute-done | bytes 248864 | tf_op jit(solution)/shard_map/ppermute | solution.py:399
  61.3 0.0 copy-start.1
  61.3 2.0 %collective-permute-start.13 = (bf16[972,128]{1,0:T(8,128)(2,1)S(1)}, bf16[972,128]{1,0:T(8,128)(2,1)S(1)}, u32[]{:S(2)}, u32[]{:S(2)}) collective-permute-start(bf16[972,128]{1,0:T(8,128)(2,1)S(1)} %follow.1), channel_id=1, source_target_pairs={{0,8},{1,9},{2,10},{3,11},{4,12},{5,13},{6,14},{7,15},{8,0},{9,1},... | collective-permute-start | bytes 746504 | tf_op jit(solution)/shard_map/ppermute | solution.py:399
  63.3 0.8 %collective-permute-done.15.refs_2_ = bf16[972,128]{1,0:T(8,128)(2,1)S(1)} collective-permute-done((bf16[972,128]{1,0:T(8,128)(2,1)S(1)}, bf16[972,128]{1,0:T(8,128)(2,1)S(1)}, u32[]{:S(2)}, u32[]{:S(2)}) %collective-permute-start.15) | collective-permute-done | bytes 248864 | tf_op jit(solution)/shard_map/ppermute | solution.py:399
  64.2 0.9 %collective-permute-start.16 = (bf16[972,128]{1,0:T(8,128)(2,1)S(1)}, bf16[972,128]{1,0:T(8,128)(2,1)S(1)}, u32[]{:S(2)}, u32[]{:S(2)}) collective-permute-start(bf16[972,128]{1,0:T(8,128)(2,1)S(1)} %collective-permute-done.15.refs_2_), channel_id=1, source_target_pairs={{0,1},{1,0},{2,3},{3,2},{4,5},{5,4},{6,7},{7,6},{8,9},{9,8},{10,11... | collective-permute-start | bytes 746504 | tf_op jit(solution)/shard_map/ppermute | solution.py:399
  65.1 1.1 %collective-permute-start.18 = (bf16[972,128]{1,0:T(8,128)(2,1)S(1)}, bf16[972,128]{1,0:T(8,128)(2,1)S(1)}, u32[]{:S(2)}, u32[]{:S(2)}) collective-permute-start(bf16[972,128]{1,0:T(8,128)(2,1)S(1)} %collective-permute-done.17.refs_4_), channel_id=1, source_target_pairs={{0,1},{1,0},{2,3},{3,2},{4,5},{5,4},{6,7},{7,6},{8,9},{9,8},{10,11... | collective-permute-start | bytes 746504 | tf_op jit(solution)/shard_map/ppermute | solution.py:399
  66.2 4.3 %collective-permute-done.13.refs_0_ = bf16[972,128]{1,0:T(8,128)(2,1)S(1)} collective-permute-done((bf16[972,128]{1,0:T(8,128)(2,1)S(1)}, bf16[972,128]{1,0:T(8,128)(2,1)S(1)}, u32[]{:S(2)}, u32[]{:S(2)}) %collective-permute-start.13) | collective-permute-done | bytes 248864 | tf_op jit(solution)/shard_map/ppermute | solution.py:399
  70.5 1.4 %collective-permute-start.14 = (bf16[972,128]{1,0:T(8,128)(2,1)S(1)}, bf16[972,128]{1,0:T(8,128)(2,1)S(1)}, u32[]{:S(2)}, u32[]{:S(2)}) collective-permute-start(bf16[972,128]{1,0:T(8,128)(2,1)S(1)} %collective-permute-done.13.refs_0_), channel_id=1, source_target_pairs={{0,1},{1,0},{2,3},{3,2},{4,5},{5,4},{6,7},{7,6},{8,9},{9,8},{10,11... | collective-permute-start | bytes 746504 | tf_op jit(solution)/shard_map/ppermute | solution.py:399
  71.9 1.2 %collective-permute-done.16.refs_3_ = bf16[972,128]{1,0:T(8,128)(2,1)S(1)} collective-permute-done((bf16[972,128]{1,0:T(8,128)(2,1)S(1)}, bf16[972,128]{1,0:T(8,128)(2,1)S(1)}, u32[]{:S(2)}, u32[]{:S(2)}) %collective-permute-start.16) | collective-permute-done | bytes 248864 | tf_op jit(solution)/shard_map/ppermute | solution.py:399
  73.1 5.4 %collective-permute-done.18.refs_5_ = bf16[972,128]{1,0:T(8,128)(2,1)S(1)} collective-permute-done((bf16[972,128]{1,0:T(8,128)(2,1)S(1)}, bf16[972,128]{1,0:T(8,128)(2,1)S(1)}, u32[]{:S(2)}, u32[]{:S(2)}) %collective-permute-start.18) | collective-permute-done | bytes 248864 | tf_op jit(solution)/shard_map/ppermute | solution.py:399
  78.5 0.8 gather.1.refs_3_
  79.3 2.5 %collective-permute-done.14.refs_1_ = bf16[972,128]{1,0:T(8,128)(2,1)S(1)} collective-permute-done((bf16[972,128]{1,0:T(8,128)(2,1)S(1)}, bf16[972,128]{1,0:T(8,128)(2,1)S(1)}, u32[]{:S(2)}, u32[]{:S(2)}) %collective-permute-start.14) | collective-permute-done | bytes 248864 | tf_op jit(solution)/shard_map/ppermute | solution.py:399
  81.8 2.5 %finish.1 = (f32[3888,128]{1,0:T(8,128)}, bf16[7776,128]{1,0:T(8,128)(2,1)}) custom-call(bf16[972,128]{1,0:T(8,128)(2,1)S(1)} %collective-permute-done.13.refs_0_, bf16[972,128]{1,0:T(8,128)(2,1)S(1)} %collective-permute-done.14.refs_1_, bf16[7776,128]{1,0:T(8,128)(2,1)S(1)} %bitcast.11, f32[7776,128]{1,0:T(8,128)S(1)} %gather.1.refs_3_), custom_call_target="tpu_custom_call" | custom-call | tf_op jit(solution)/shard_map/finish/pallas_call | solution.py:375
  (12 shorter events, 0.1 us)
Async XLA Ops:
  0.6 7.0 %copy-start.2 = (s32[8,2]{0,1:T(2,128)S(1)}, s32[8,2]{0,1:T(2,128)}, u32[]{:S(2)}) copy-start(s32[8,2]{0,1:T(2,128)} %param.5) | copy-start | bytes 196
  0.6 1.6 %copy-start = (bf16[8,972,128]{2,0,1:T(8,128)(2,1)S(1)}, bf16[8,972,128]{2,0,1:T(8,128)(2,1)}, u32[]{:S(2)}) copy-start(bf16[8,972,128]{2,0,1:T(8,128)(2,1)} %param.4) | copy-start | bytes 5971972
  3.0 20.7 %collective-permute-start = (bf16[972,128]{1,0:T(8,128)(2,1)S(1)}, bf16[972,128]{1,0:T(8,128)(2,1)S(1)}, u32[]{:S(2)}, u32[]{:S(2)}) collective-permute-start(bf16[972,128]{1,0:T(8,128)(2,1)S(1)} %get-tuple-element.27), channel_id=1, source_target_pairs={{0,12},{1,13},{2,14},{3,15},{4,0},{5,1},{6,2},{7,3},{8,4},{9,5},{1... | collective-permute-start | bytes 746504 | tf_op jit(solution)/shard_map/ppermute | solution.py:399
  6.1 17.6 %collective-permute-start.1 = (bf16[972,128]{1,0:T(8,128)(2,1)S(1)}, bf16[972,128]{1,0:T(8,128)(2,1)S(1)}, u32[]{:S(2)}, u32[]{:S(2)}) collective-permute-start(bf16[972,128]{1,0:T(8,128)(2,1)S(1)} %get-tuple-element.28), channel_id=1, source_target_pairs={{0,8},{1,9},{2,10},{3,11},{4,12},{5,13},{6,14},{7,15},{8,0},{9,1},... | collective-permute-start | bytes 746504 | tf_op jit(solution)/shard_map/ppermute | solution.py:399
  6.7 17.0 %collective-permute-start.2 = (bf16[972,128]{1,0:T(8,128)(2,1)S(1)}, bf16[972,128]{1,0:T(8,128)(2,1)S(1)}, u32[]{:S(2)}, u32[]{:S(2)}) collective-permute-start(bf16[972,128]{1,0:T(8,128)(2,1)S(1)} %get-tuple-element.29), channel_id=1, source_target_pairs={{0,4},{1,5},{2,6},{3,7},{4,8},{5,9},{6,10},{7,11},{8,12},{9,13},{1... | collective-permute-start | bytes 746504 | tf_op jit(solution)/shard_map/ppermute | solution.py:399
  7.7 9.2 %collective-permute-start.4 = (s32[2,8]{1,0:T(2,128)S(1)}, s32[2,8]{1,0:T(2,128)S(1)}, u32[]{:S(2)}, u32[]{:S(2)}) collective-permute-start(s32[2,8]{1,0:T(2,128)S(1)} %bitcast.12), channel_id=1, source_target_pairs={{0,16},{1,17},{2,18},{3,19},{4,20},{5,21},{6,22},{7,23},{8,24},{9,... | collective-permute-start | bytes 200 | tf_op jit(solution)/shard_map/ppermute | solution.py:399
  19.7 20.6 %collective-permute-start.5 = (bf16[972,384]{1,0:T(8,128)(2,1)S(1)}, bf16[972,384]{1,0:T(8,128)(2,1)S(1)}, u32[]{:S(2)}, u32[]{:S(2)}) collective-permute-start(bf16[972,384]{1,0:T(8,128)(2,1)S(1)} %get-tuple-element.32), channel_id=1, source_target_pairs={{16,0},{17,2},{18,1},{19,3},{20,4},{21,6},{22,5},{23,7},{24,8},{25... | collective-permute-start | bytes 2239496 | tf_op jit(solution)/shard_map/ppermute | solution.py:399
  26.5 13.8 %collective-permute-start.3 = (bf16[972,384]{1,0:T(8,128)(2,1)S(1)}, bf16[972,384]{1,0:T(8,128)(2,1)S(1)}, u32[]{:S(2)}, u32[]{:S(2)}) collective-permute-start(bf16[972,384]{1,0:T(8,128)(2,1)S(1)} %get-tuple-element.30.above), channel_id=1, source_target_pairs={{1,2},{2,1},{5,6},{6,5},{9,10},{10,9},{13,14},{14,13},{17,18},{18,... | collective-permute-start | bytes 2239496 | tf_op jit(solution)/shard_map/ppermute | solution.py:399
  27.3 2.6 %collective-permute-start.6 = (bf16[972,128]{1,0:T(8,128)(2,1)S(1)}, bf16[972,128]{1,0:T(8,128)(2,1)S(1)}, u32[]{:S(2)}, u32[]{:S(2)}) collective-permute-start(bf16[972,128]{1,0:T(8,128)(2,1)S(1)} %get-tuple-element.31.refs_0_.own), channel_id=1, source_target_pairs={{0,2},{1,3},{2,0},{3,1},{4,6},{5,7},{6,4},{7,5},{8,10},{9,11},{10,... | collective-permute-start | bytes 746504 | tf_op jit(solution)/shard_map/ppermute | solution.py:399
  28.7 1.8 %collective-permute-start.9 = (bf16[972,128]{1,0:T(8,128)(2,1)S(1)}, bf16[972,128]{1,0:T(8,128)(2,1)S(1)}, u32[]{:S(2)}, u32[]{:S(2)}) collective-permute-start(bf16[972,128]{1,0:T(8,128)(2,1)S(1)} %collective-permute-done.2.refs_2_.own), channel_id=1, source_target_pairs={{0,2},{1,3},{2,0},{3,1},{4,6},{5,7},{6,4},{7,5},{8,10},{9,11},{10,... | collective-permute-start | bytes 746504 | tf_op jit(solution)/shard_map/ppermute | solution.py:399
  28.9 1.9 %collective-permute-start.8 = (bf16[972,128]{1,0:T(8,128)(2,1)S(1)}, bf16[972,128]{1,0:T(8,128)(2,1)S(1)}, u32[]{:S(2)}, u32[]{:S(2)}) collective-permute-start(bf16[972,128]{1,0:T(8,128)(2,1)S(1)} %collective-permute-done.1.refs_1_.own), channel_id=1, source_target_pairs={{0,2},{1,3},{2,0},{3,1},{4,6},{5,7},{6,4},{7,5},{8,10},{9,11},{10,... | collective-permute-start | bytes 746504 | tf_op jit(solution)/shard_map/ppermute | solution.py:399
  29.9 1.5 %collective-permute-start.7 = (bf16[972,128]{1,0:T(8,128)(2,1)S(1)}, bf16[972,128]{1,0:T(8,128)(2,1)S(1)}, u32[]{:S(2)}, u32[]{:S(2)}) collective-permute-start(bf16[972,128]{1,0:T(8,128)(2,1)S(1)} %collective-permute-done.refs_0_.own), channel_id=1, source_target_pairs={{0,2},{1,3},{2,0},{3,1},{4,6},{5,7},{6,4},{7,5},{8,10},{9,11},{10,... | collective-permute-start | bytes 746504 | tf_op jit(solution)/shard_map/ppermute | solution.py:399
  46.8 8.1 %collective-permute-start.10 = (bf16[2928,128]{1,0:T(8,128)(2,1)S(1)}, bf16[2928,128]{1,0:T(8,128)(2,1)S(1)}, u32[]{:S(2)}, u32[]{:S(2)}) collective-permute-start(bf16[2928,128]{1,0:T(8,128)(2,1)S(1)} %get-tuple-element.45), channel_id=1, source_target_pairs={{0,2},{1,3},{2,0},{3,1},{4,6},{5,7},{6,4},{7,5},{8,10},{9,11},{10,... | collective-permute-start | bytes 2248712 | tf_op jit(solution)/shard_map/ppermute | solution.py:399
  50.2 2.2 %collective-permute-start.11 = (bf16[976,128]{1,0:T(8,128)(2,1)S(1)}, bf16[976,128]{1,0:T(8,128)(2,1)S(1)}, u32[]{:S(2)}, u32[]{:S(2)}) collective-permute-start(bf16[976,128]{1,0:T(8,128)(2,1)S(1)} %get-tuple-element.43.refs_0_), channel_id=1, source_target_pairs={{0,2},{1,3},{2,0},{3,1},{4,6},{5,7},{6,4},{7,5},{8,10},{9,11},{10,... | collective-permute-start | bytes 749576 | tf_op jit(solution)/shard_map/ppermute | solution.py:399
  52.5 8.8 %collective-permute-start.12 = (bf16[972,128]{1,0:T(8,128)(2,1)S(1)}, bf16[972,128]{1,0:T(8,128)(2,1)S(1)}, u32[]{:S(2)}, u32[]{:S(2)}) collective-permute-start(bf16[972,128]{1,0:T(8,128)(2,1)S(1)} %total.2.refs_0_), channel_id=1, source_target_pairs={{0,1},{1,0},{2,3},{3,2},{4,5},{5,4},{6,7},{7,6},{8,9},{9,8},{10,11... | collective-permute-start | bytes 746504 | tf_op jit(solution)/shard_map/ppermute | solution.py:399
  55.1 9.1 %collective-permute-start.15 = (bf16[972,128]{1,0:T(8,128)(2,1)S(1)}, bf16[972,128]{1,0:T(8,128)(2,1)S(1)}, u32[]{:S(2)}, u32[]{:S(2)}) collective-permute-start(bf16[972,128]{1,0:T(8,128)(2,1)S(1)} %get-tuple-element.48), channel_id=1, source_target_pairs={{0,4},{1,5},{2,6},{3,7},{4,8},{5,9},{6,10},{7,11},{8,12},{9,13},{1... | collective-permute-start | bytes 746504 | tf_op jit(solution)/shard_map/ppermute | solution.py:399
  57.0 8.0 %collective-permute-start.17 = (bf16[972,128]{1,0:T(8,128)(2,1)S(1)}, bf16[972,128]{1,0:T(8,128)(2,1)S(1)}, u32[]{:S(2)}, u32[]{:S(2)}) collective-permute-start(bf16[972,128]{1,0:T(8,128)(2,1)S(1)} %get-tuple-element.49), channel_id=1, source_target_pairs={{0,12},{1,13},{2,14},{3,15},{4,0},{5,1},{6,2},{7,3},{8,4},{9,5},{1... | collective-permute-start | bytes 746504 | tf_op jit(solution)/shard_map/ppermute | solution.py:399
  61.3 20.5 %copy-start.1 = (bf16[8,972,128]{2,0,1:T(8,128)(2,1)S(1)}, bf16[8,972,128]{2,0,1:T(8,128)(2,1)}, u32[]{:S(2)}) copy-start(bf16[8,972,128]{2,0,1:T(8,128)(2,1)} %param.4) | copy-start | bytes 5971972
  61.3 9.2 %collective-permute-start.13 = (bf16[972,128]{1,0:T(8,128)(2,1)S(1)}, bf16[972,128]{1,0:T(8,128)(2,1)S(1)}, u32[]{:S(2)}, u32[]{:S(2)}) collective-permute-start(bf16[972,128]{1,0:T(8,128)(2,1)S(1)} %follow.1), channel_id=1, source_target_pairs={{0,8},{1,9},{2,10},{3,11},{4,12},{5,13},{6,14},{7,15},{8,0},{9,1},... | collective-permute-start | bytes 746504 | tf_op jit(solution)/shard_map/ppermute | solution.py:399
  64.2 9.0 %collective-permute-start.16 = (bf16[972,128]{1,0:T(8,128)(2,1)S(1)}, bf16[972,128]{1,0:T(8,128)(2,1)S(1)}, u32[]{:S(2)}, u32[]{:S(2)}) collective-permute-start(bf16[972,128]{1,0:T(8,128)(2,1)S(1)} %collective-permute-done.15.refs_2_), channel_id=1, source_target_pairs={{0,1},{1,0},{2,3},{3,2},{4,5},{5,4},{6,7},{7,6},{8,9},{9,8},{10,11... | collective-permute-start | bytes 746504 | tf_op jit(solution)/shard_map/ppermute | solution.py:399
  65.1 13.4 %collective-permute-start.18 = (bf16[972,128]{1,0:T(8,128)(2,1)S(1)}, bf16[972,128]{1,0:T(8,128)(2,1)S(1)}, u32[]{:S(2)}, u32[]{:S(2)}) collective-permute-start(bf16[972,128]{1,0:T(8,128)(2,1)S(1)} %collective-permute-done.17.refs_4_), channel_id=1, source_target_pairs={{0,1},{1,0},{2,3},{3,2},{4,5},{5,4},{6,7},{7,6},{8,9},{9,8},{10,11... | collective-permute-start | bytes 746504 | tf_op jit(solution)/shard_map/ppermute | solution.py:399
  70.5 11.3 %collective-permute-start.14 = (bf16[972,128]{1,0:T(8,128)(2,1)S(1)}, bf16[972,128]{1,0:T(8,128)(2,1)S(1)}, u32[]{:S(2)}, u32[]{:S(2)}) collective-permute-start(bf16[972,128]{1,0:T(8,128)(2,1)S(1)} %collective-permute-done.13.refs_0_), channel_id=1, source_target_pairs={{0,1},{1,0},{2,3},{3,2},{4,5},{5,4},{6,7},{7,6},{8,9},{9,8},{10,11... | collective-permute-start | bytes 746504 | tf_op jit(solution)/shard_map/ppermute | solution.py:399

commit v8 on v4

--- a/solution.py
+++ b/solution.py
@@ -401,9 +401,9 @@
     dps = mesh_shape[2]
     places = offsets.T
     upper = send(places, lambda t, y, k, d: (t + 1, y, k, d))
+    own = blocks(weights, rows_y, dps)
     above, token = cut(frames, places, True)
     below, token = cut(frames, upper, False, (token,))
-    own = blocks(weights, rows_y, dps, (token,))
     below = send(below, lambda t, y, k, d: (t - 1, y, d, k))
 
     weight, turned = [], []
@@ -429,10 +429,10 @@
         blocks_here = total(home, away, len(shifts), inner, after_total)
         after_total = (blocks_here[0],)
         for s, block in zip(shifts, blocks_here):
+            if s == 2:
+                block = follow(block, pieces[0][1])
             if s:
                 block = send(block, lambda t, y, k, d: (t, y + s, k, d))
-            if s == 1:
-                block = follow(block, pieces[0][1])
             pieces[s] = [block, send(block, lambda t, y, k, d: (t, y, k, 1 - d))]
     early, late = (0, 1, 3), (2,)
     full = gather(sum([pieces[s] for s in early], []), early, rows_y, dps)

time: 84.3 us -> 80.3 us (0.953)
  waiting for transfers between devices: 41.7 us -> 34.3 us
  starting transfers between devices: 23.6 us -> 25.2 us
  local copies, waits for them, and re-layouts: 0.69 us -> 1.56 us
    ppermute x19, waiting for transfers between devices: 41.7 us -> 34.3 us  [send(): return lax.ppermute(x, AXES, table(mesh_shape, move))]
    ppermute x19, starting transfers between devices: 23.6 us -> 25.2 us  [send(): return lax.ppermute(x, AXES, table(mesh_shape, move))]
    unnamed x4 -> x6, local copies, waits for them, and re-layouts: 0.69 us -> 1.56 us
  transfers between devices with their start and end apart: 19 -> 19, of which waited for: 11 -> 12; matrix products, arithmetic and copies ran while one was open for 0% -> 0% of each run, Pallas kernels for 5% -> 10%
where the time goes in v8:
time: 80.3 us; the launch traced here: 79 us
  waiting for transfers between devices  34.3 us (43%)
  starting transfers between devices  25.2 us (31%)
  Pallas kernels  16.9 us (21%)
  local copies, waits for them, and re-layouts  1.56 us (2%)
  between operations  0.98 us (1%)
    ppermute x19, waiting for transfers between devices, send(): return lax.ppermute(x, AXES, table(mesh_shape, move))  34.3 us
    ppermute x19, starting transfers between devices, send(): return lax.ppermute(x, AXES, table(mesh_shape, move))  25.2 us
    pallas_call x2, Pallas kernels, cut(): pl.pallas_call(functools.partial(cut_kernel, above), out_shape=[jax.Shape...  5.16 us
    pallas_call x1, Pallas kernels, column(): pl.pallas_call(functools.partial(column_kernel, rows_y), out_shape=[jax.S...  4.09 us
    pallas_call x1, Pallas kernels, finish(): pl.pallas_call(functools.partial(finish_kernel, rows_y, dps, shifts), out...  2.5 us
    pallas_call x2, Pallas kernels, piece(): pl.pallas_call(functools.partial(piece_kernel, shifts, 1.0 / depth), out_...  2.06 us
  transfers between devices with their start and end apart: 19, of which 12 were waited for; matrix products, arithmetic and copies ran while one was open for 0% of the time, Pallas kernels for 10%

profile of v8, /device:TPU:4, one launch (start us, length us, event | category | flops | bytes accessed | tf_op | source)
XLA Modules:
  0.0 79.0 jit_solution(2169670011581117088)
XLA Ops:
  0.6 3.8 %collective-permute-start.1 = (s32[2,8]{1,0:T(2,128)}, s32[2,8]{1,0:T(2,128)S(1)}, u32[]{:S(2)}, u32[]{:S(2)}) collective-permute-start(s32[2,8]{1,0:T(2,128)} %bitcast.12), channel_id=1, source_target_pairs={{0,16},{1,17},{2,18},{3,19},{4,20},{5,21},{6,22},{7,23},{8,24},{9,... | collective-permute-start | bytes 200 | tf_op jit(solution)/shard_map/ppermute | solution.py:399
  4.5 0.0 copy-start
  4.5 1.5 %copy-done = bf16[8,972,128]{2,0,1:T(8,128)(2,1)S(1)} copy-done((bf16[8,972,128]{2,0,1:T(8,128)(2,1)S(1)}, bf16[8,972,128]{2,0,1:T(8,128)(2,1)}, u32[]{:S(2)}) %copy-start) | copy-done | bytes 1990680
  6.0 0.8 blocks.1
  6.8 3.1 %collective-permute-start.4 = (bf16[972,128]{1,0:T(8,128)(2,1)S(1)}, bf16[972,128]{1,0:T(8,128)(2,1)S(1)}, u32[]{:S(2)}, u32[]{:S(2)}) collective-permute-start(bf16[972,128]{1,0:T(8,128)(2,1)S(1)} %get-tuple-element.33), channel_id=1, source_target_pairs={{0,12},{1,13},{2,14},{3,15},{4,0},{5,1},{6,2},{7,3},{8,4},{9,5},{1... | collective-permute-start | bytes 746504 | tf_op jit(solution)/shard_map/ppermute | solution.py:399
  9.9 2.3 %cut_above.1 = (bf16[972,384]{1,0:T(8,128)(2,1)S(1)}, f32[8,128]{1,0:T(8,128)S(1)}) custom-call(s32[2,8]{1,0:T(2,128)S(1)} %bitcast.13, bf16[3,20,128,384]{3,2,1,0:T(8,128)(2,1)} %frames.3), custom_call_target="tpu_custom_call" | custom-call | tf_op jit(solution)/shard_map/cut_above/pallas_call | solution.py:95
  12.2 0.7 collective-permute-start
  13.0 2.8 %cut_below.1 = (bf16[972,384]{1,0:T(8,128)(2,1)S(1)}, f32[8,128]{1,0:T(8,128)}) custom-call(s32[2,8]{1,0:T(2,128)S(1)} %collective-permute-done.1.places, bf16[3,20,128,384]{3,2,1,0:T(8,128)(2,1)} %frames.3, f32[8,128]{1,0:T(8,128)S(1)} %get-tuple-element.29.refs_0_), custom_call_target="tpu_custom_call" | custom-call | tf_op jit(solution)/shard_map/cut_below/pallas_call | solution.py:95
  15.8 5.8 %collective-permute-start.2 = (bf16[972,384]{1,0:T(8,128)(2,1)S(1)}, bf16[972,384]{1,0:T(8,128)(2,1)S(1)}, u32[]{:S(2)}, u32[]{:S(2)}) collective-permute-start(bf16[972,384]{1,0:T(8,128)(2,1)S(1)} %get-tuple-element.30), channel_id=1, source_target_pairs={{16,0},{17,2},{18,1},{19,3},{20,4},{21,6},{22,5},{23,7},{24,8},{25... | collective-permute-start | bytes 2239496 | tf_op jit(solution)/shard_map/ppermute | solution.py:399
  21.6 0.1 collective-permute-start.8
  21.7 2.2 %collective-permute-start.6 = (bf16[972,128]{1,0:T(8,128)(2,1)S(1)}, bf16[972,128]{1,0:T(8,128)(2,1)S(1)}, u32[]{:S(2)}, u32[]{:S(2)}) collective-permute-start(bf16[972,128]{1,0:T(8,128)(2,1)S(1)} %get-tuple-element.35), channel_id=1, source_target_pairs={{0,8},{1,9},{2,10},{3,11},{4,12},{5,13},{6,14},{7,15},{8,0},{9,1},... | collective-permute-start | bytes 746504 | tf_op jit(solution)/shard_map/ppermute | solution.py:399
  23.9 0.8 %collective-permute-start.3 = (bf16[972,128]{1,0:T(8,128)(2,1)S(1)}, bf16[972,128]{1,0:T(8,128)(2,1)S(1)}, u32[]{:S(2)}, u32[]{:S(2)}) collective-permute-start(bf16[972,128]{1,0:T(8,128)(2,1)S(1)} %get-tuple-element.31.own), channel_id=1, source_target_pairs={{0,2},{1,3},{2,0},{3,1},{4,6},{5,7},{6,4},{7,5},{8,10},{9,11},{10,... | collective-permute-start | bytes 746504 | tf_op jit(solution)/shard_map/ppermute | solution.py:399
  24.7 12.2 %collective-permute-done.8.own = bf16[972,128]{1,0:T(8,128)(2,1)S(1)} collective-permute-done((bf16[972,128]{1,0:T(8,128)(2,1)S(1)}, bf16[972,128]{1,0:T(8,128)(2,1)S(1)}, u32[]{:S(2)}, u32[]{:S(2)}) %collective-permute-start.8) | collective-permute-done | bytes 248864 | tf_op jit(solution)/shard_map/ppermute | solution.py:399
  36.9 0.1 collective-permute-start.9
  37.0 0.4 collective-permute-start.7
  37.4 0.1 collective-permute-start.5
  37.5 0.2 filters.4
  37.7 0.6 collective-permute-done.9.other
  38.4 0.2 filters.7
  38.6 0.1 collective-permute-done.7.other
  38.7 0.3 filters.6
  39.0 0.1 collective-permute-done.5.other
  39.1 0.2 filters.5
  39.4 0.3 join.1.patch_in
  39.7 4.1 %column.1 = (bf16[972,768]{1,0:T(8,128)(2,1)S(1)}, bf16[1024,768]{1,0:T(8,128)(2,1)S(1)}) custom-call(bf16[972,384]{1,0:T(8,128)(2,1)S(1)} %join.1.patch_in, bf16[972,256]{1,0:T(8,128)(2,1)S(1)} %get-tuple-element.32.refs_0_, bf16[972,256]{1,0:T(8,128)(2,1)S(1)} %get-tuple-element.34.refs_1_, bf16[972,256]{1,0:T(8,128)(2,1)S(1)} %get-tuple-element.36.refs_2_, ...), custom_call_target="tpu_custom_call" | custom-call | tf_op jit(solution)/shard_map/column/pallas_call | solution.py:231
  43.8 0.6 piece.2
  44.4 1.5 %piece.3 = (f32[2928,128]{1,0:T(8,128)S(1)}, bf16[2928,128]{1,0:T(8,128)(2,1)S(1)}) custom-call(bf16[972,768]{1,0:T(8,128)(2,1)S(1)} %get-tuple-element.43.pe, bf16[1024,768]{1,0:T(8,128)(2,1)S(1)} %get-tuple-element.44.mr, bf16[976,128]{1,0:T(8,128)(2,1)S(1)} %get-tuple-element.45.refs_0_), custom_call_target="tpu_custom_call" | custom-call | tf_op jit(solution)/shard_map/piece/pallas_call | solution.py:276
  45.9 0.2 collective-permute-start.10
  46.1 0.4 collective-permute-start.11
  46.5 2.1 %collective-permute-done.11.away = bf16[976,128]{1,0:T(8,128)(2,1)S(1)} collective-permute-done((bf16[976,128]{1,0:T(8,128)(2,1)S(1)}, bf16[976,128]{1,0:T(8,128)(2,1)S(1)}, u32[]{:S(2)}, u32[]{:S(2)}) %collective-permute-start.11) | collective-permute-done | bytes 249888 | tf_op jit(solution)/shard_map/ppermute | solution.py:399
  48.6 0.8 collective-permute-start.12
  49.4 0.1 total.3
  49.5 0.1 collective-permute-start.15
  49.6 3.2 %collective-permute-start.17 = (bf16[972,128]{1,0:T(8,128)(2,1)S(1)}, bf16[972,128]{1,0:T(8,128)(2,1)S(1)}, u32[]{:S(2)}, u32[]{:S(2)}) collective-permute-start(bf16[972,128]{1,0:T(8,128)(2,1)S(1)} %get-tuple-element.51), channel_id=1, source_target_pairs={{0,12},{1,13},{2,14},{3,15},{4,0},{5,1},{6,2},{7,3},{8,4},{9,5},{1... | collective-permute-start | bytes 746504 | tf_op jit(solution)/shard_map/ppermute | solution.py:399
  52.8 3.9 %collective-permute-done.12.after.refs_1_ = bf16[972,128]{1,0:T(8,128)(2,1)S(1)} collective-permute-done((bf16[972,128]{1,0:T(8,128)(2,1)S(1)}, bf16[972,128]{1,0:T(8,128)(2,1)S(1)}, u32[]{:S(2)}, u32[]{:S(2)}) %collective-permute-start.12) | collective-permute-done | bytes 248864 | tf_op jit(solution)/shard_map/ppermute | solution.py:399
  56.8 0.0 copy-start.1
  56.8 0.1 collective-permute-start.13
  56.9 1.7 %collective-permute-done.15.refs_2_ = bf16[972,128]{1,0:T(8,128)(2,1)S(1)} collective-permute-done((bf16[972,128]{1,0:T(8,128)(2,1)S(1)}, bf16[972,128]{1,0:T(8,128)(2,1)S(1)}, u32[]{:S(2)}, u32[]{:S(2)}) %collective-permute-start.15) | collective-permute-done | bytes 248864 | tf_op jit(solution)/shard_map/ppermute | solution.py:399
  58.7 1.3 %collective-permute-start.16 = (bf16[972,128]{1,0:T(8,128)(2,1)S(1)}, bf16[972,128]{1,0:T(8,128)(2,1)S(1)}, u32[]{:S(2)}, u32[]{:S(2)}) collective-permute-start(bf16[972,128]{1,0:T(8,128)(2,1)S(1)} %collective-permute-done.15.refs_2_), channel_id=1, source_target_pairs={{0,1},{1,0},{2,3},{3,2},{4,5},{5,4},{6,7},{7,6},{8,9},{9,8},{10,11... | collective-permute-start | bytes 746504 | tf_op jit(solution)/shard_map/ppermute | solution.py:399
  59.9 3.4 %collective-permute-done.17.refs_4_ = bf16[972,128]{1,0:T(8,128)(2,1)S(1)} collective-permute-done((bf16[972,128]{1,0:T(8,128)(2,1)S(1)}, bf16[972,128]{1,0:T(8,128)(2,1)S(1)}, u32[]{:S(2)}, u32[]{:S(2)}) %collective-permute-start.17) | collective-permute-done | bytes 248864 | tf_op jit(solution)/shard_map/ppermute | solution.py:399
  63.3 1.3 %collective-permute-start.18 = (bf16[972,128]{1,0:T(8,128)(2,1)S(1)}, bf16[972,128]{1,0:T(8,128)(2,1)S(1)}, u32[]{:S(2)}, u32[]{:S(2)}) collective-permute-start(bf16[972,128]{1,0:T(8,128)(2,1)S(1)} %collective-permute-done.17.refs_4_), channel_id=1, source_target_pairs={{0,1},{1,0},{2,3},{3,2},{4,5},{5,4},{6,7},{7,6},{8,9},{9,8},{10,11... | collective-permute-start | bytes 746504 | tf_op jit(solution)/shard_map/ppermute | solution.py:399
  64.6 1.1 %collective-permute-done.13.refs_0_ = bf16[972,128]{1,0:T(8,128)(2,1)S(1)} collective-permute-done((bf16[972,128]{1,0:T(8,128)(2,1)S(1)}, bf16[972,128]{1,0:T(8,128)(2,1)S(1)}, u32[]{:S(2)}, u32[]{:S(2)}) %collective-permute-start.13) | collective-permute-done | bytes 248864 | tf_op jit(solution)/shard_map/ppermute | solution.py:399
  65.7 0.8 collective-permute-start.14
  66.4 1.2 %collective-permute-done.16.refs_3_ = bf16[972,128]{1,0:T(8,128)(2,1)S(1)} collective-permute-done((bf16[972,128]{1,0:T(8,128)(2,1)S(1)}, bf16[972,128]{1,0:T(8,128)(2,1)S(1)}, u32[]{:S(2)}, u32[]{:S(2)}) %collective-permute-start.16) | collective-permute-done | bytes 248864 | tf_op jit(solution)/shard_map/ppermute | solution.py:399
  67.6 5.4 %collective-permute-done.18.refs_5_ = bf16[972,128]{1,0:T(8,128)(2,1)S(1)} collective-permute-done((bf16[972,128]{1,0:T(8,128)(2,1)S(1)}, bf16[972,128]{1,0:T(8,128)(2,1)S(1)}, u32[]{:S(2)}, u32[]{:S(2)}) %collective-permute-start.18) | collective-permute-done | bytes 248864 | tf_op jit(solution)/shard_map/ppermute | solution.py:399
  73.0 0.8 %gather.1.refs_3_ = f32[7776,128]{1,0:T(8,128)S(1)} custom-call(bf16[972,128]{1,0:T(8,128)(2,1)S(1)} %total.2.refs_0_, bf16[972,128]{1,0:T(8,128)(2,1)S(1)} %collective-permute-done.12.after.refs_1_, bf16[972,128]{1,0:T(8,128)(2,1)S(1)} %collective-permute-done.15.refs_2_, bf16[972,128]{1,0:T(8,128)(2,1)S(1)} %collective-permute-done.16.refs_3_, ...), custom_call_target="tpu_custom_call" | custom-call | tf_op jit(solution)/shard_map/gather/pallas_call | solution.py:339
  73.8 2.5 %collective-permute-done.14.refs_1_ = bf16[972,128]{1,0:T(8,128)(2,1)S(1)} collective-permute-done((bf16[972,128]{1,0:T(8,128)(2,1)S(1)}, bf16[972,128]{1,0:T(8,128)(2,1)S(1)}, u32[]{:S(2)}, u32[]{:S(2)}) %collective-permute-start.14) | collective-permute-done | bytes 248864 | tf_op jit(solution)/shard_map/ppermute | solution.py:399
  76.3 2.5 %finish.1 = (f32[3888,128]{1,0:T(8,128)}, bf16[7776,128]{1,0:T(8,128)(2,1)}) custom-call(bf16[972,128]{1,0:T(8,128)(2,1)S(1)} %collective-permute-done.13.refs_0_, bf16[972,128]{1,0:T(8,128)(2,1)S(1)} %collective-permute-done.14.refs_1_, bf16[7776,128]{1,0:T(8,128)(2,1)S(1)} %bitcast.11, f32[7776,128]{1,0:T(8,128)S(1)} %gather.1.refs_3_), custom_call_target="tpu_custom_call" | custom-call | tf_op jit(solution)/shard_map/finish/pallas_call | solution.py:375
  (12 shorter events, 0.1 us)
Async XLA Ops:
  0.6 9.3 %copy-start.2 = (s32[8,2]{0,1:T(2,128)S(1)}, s32[8,2]{0,1:T(2,128)}, u32[]{:S(2)}) copy-start(s32[8,2]{0,1:T(2,128)} %param.5) | copy-start | bytes 196
  0.6 12.3 %collective-permute-start.1 = (s32[2,8]{1,0:T(2,128)}, s32[2,8]{1,0:T(2,128)S(1)}, u32[]{:S(2)}, u32[]{:S(2)}) collective-permute-start(s32[2,8]{1,0:T(2,128)} %bitcast.12), channel_id=1, source_target_pairs={{0,16},{1,17},{2,18},{3,19},{4,20},{5,21},{6,22},{7,23},{8,24},{9,... | collective-permute-start | bytes 200 | tf_op jit(solution)/shard_map/ppermute | solution.py:399
  4.5 1.6 %copy-start = (bf16[8,972,128]{2,0,1:T(8,128)(2,1)S(1)}, bf16[8,972,128]{2,0,1:T(8,128)(2,1)}, u32[]{:S(2)}) copy-start(bf16[8,972,128]{2,0,1:T(8,128)(2,1)} %param.4) | copy-start | bytes 5971972
  6.8 17.1 %collective-permute-start.4 = (bf16[972,128]{1,0:T(8,128)(2,1)S(1)}, bf16[972,128]{1,0:T(8,128)(2,1)S(1)}, u32[]{:S(2)}, u32[]{:S(2)}) collective-permute-start(bf16[972,128]{1,0:T(8,128)(2,1)S(1)} %get-tuple-element.33), channel_id=1, source_target_pairs={{0,12},{1,13},{2,14},{3,15},{4,0},{5,1},{6,2},{7,3},{8,4},{9,5},{1... | collective-permute-start | bytes 746504 | tf_op jit(solution)/shard_map/ppermute | solution.py:399
  12.2 27.1 %collective-permute-start = (bf16[972,384]{1,0:T(8,128)(2,1)S(1)}, bf16[972,384]{1,0:T(8,128)(2,1)S(1)}, u32[]{:S(2)}, u32[]{:S(2)}) collective-permute-start(bf16[972,384]{1,0:T(8,128)(2,1)S(1)} %get-tuple-element.28.above), channel_id=1, source_target_pairs={{1,2},{2,1},{5,6},{6,5},{9,10},{10,9},{13,14},{14,13},{17,18},{18,... | collective-permute-start | bytes 2239496 | tf_op jit(solution)/shard_map/ppermute | solution.py:399
  15.8 23.5 %collective-permute-start.2 = (bf16[972,384]{1,0:T(8,128)(2,1)S(1)}, bf16[972,384]{1,0:T(8,128)(2,1)S(1)}, u32[]{:S(2)}, u32[]{:S(2)}) collective-permute-start(bf16[972,384]{1,0:T(8,128)(2,1)S(1)} %get-tuple-element.30), channel_id=1, source_target_pairs={{16,0},{17,2},{18,1},{19,3},{20,4},{21,6},{22,5},{23,7},{24,8},{25... | collective-permute-start | bytes 2239496 | tf_op jit(solution)/shard_map/ppermute | solution.py:399
  21.6 15.3 %collective-permute-start.8 = (bf16[972,128]{1,0:T(8,128)(2,1)S(1)}, bf16[972,128]{1,0:T(8,128)(2,1)S(1)}, u32[]{:S(2)}, u32[]{:S(2)}) collective-permute-start(bf16[972,128]{1,0:T(8,128)(2,1)S(1)} %get-tuple-element.37), channel_id=1, source_target_pairs={{0,4},{1,5},{2,6},{3,7},{4,8},{5,9},{6,10},{7,11},{8,12},{9,13},{1... | collective-permute-start | bytes 746504 | tf_op jit(solution)/shard_map/ppermute | solution.py:399
  21.7 15.3 %collective-permute-start.6 = (bf16[972,128]{1,0:T(8,128)(2,1)S(1)}, bf16[972,128]{1,0:T(8,128)(2,1)S(1)}, u32[]{:S(2)}, u32[]{:S(2)}) collective-permute-start(bf16[972,128]{1,0:T(8,128)(2,1)S(1)} %get-tuple-element.35), channel_id=1, source_target_pairs={{0,8},{1,9},{2,10},{3,11},{4,12},{5,13},{6,14},{7,15},{8,0},{9,1},... | collective-permute-start | bytes 746504 | tf_op jit(solution)/shard_map/ppermute | solution.py:399
  23.9 13.5 %collective-permute-start.3 = (bf16[972,128]{1,0:T(8,128)(2,1)S(1)}, bf16[972,128]{1,0:T(8,128)(2,1)S(1)}, u32[]{:S(2)}, u32[]{:S(2)}) collective-permute-start(bf16[972,128]{1,0:T(8,128)(2,1)S(1)} %get-tuple-element.31.own), channel_id=1, source_target_pairs={{0,2},{1,3},{2,0},{3,1},{4,6},{5,7},{6,4},{7,5},{8,10},{9,11},{10,... | collective-permute-start | bytes 746504 | tf_op jit(solution)/shard_map/ppermute | solution.py:399
  36.9 1.5 %collective-permute-start.9 = (bf16[972,128]{1,0:T(8,128)(2,1)S(1)}, bf16[972,128]{1,0:T(8,128)(2,1)S(1)}, u32[]{:S(2)}, u32[]{:S(2)}) collective-permute-start(bf16[972,128]{1,0:T(8,128)(2,1)S(1)} %collective-permute-done.8.own), channel_id=1, source_target_pairs={{0,2},{1,3},{2,0},{3,1},{4,6},{5,7},{6,4},{7,5},{8,10},{9,11},{10,... | collective-permute-start | bytes 746504 | tf_op jit(solution)/shard_map/ppermute | solution.py:399
  37.0 1.7 %collective-permute-start.7 = (bf16[972,128]{1,0:T(8,128)(2,1)S(1)}, bf16[972,128]{1,0:T(8,128)(2,1)S(1)}, u32[]{:S(2)}, u32[]{:S(2)}) collective-permute-start(bf16[972,128]{1,0:T(8,128)(2,1)S(1)} %collective-permute-done.6.own), channel_id=1, source_target_pairs={{0,2},{1,3},{2,0},{3,1},{4,6},{5,7},{6,4},{7,5},{8,10},{9,11},{10,... | collective-permute-start | bytes 746504 | tf_op jit(solution)/shard_map/ppermute | solution.py:399
  37.4 1.7 %collective-permute-start.5 = (bf16[972,128]{1,0:T(8,128)(2,1)S(1)}, bf16[972,128]{1,0:T(8,128)(2,1)S(1)}, u32[]{:S(2)}, u32[]{:S(2)}) collective-permute-start(bf16[972,128]{1,0:T(8,128)(2,1)S(1)} %collective-permute-done.4.own), channel_id=1, source_target_pairs={{0,2},{1,3},{2,0},{3,1},{4,6},{5,7},{6,4},{7,5},{8,10},{9,11},{10,... | collective-permute-start | bytes 746504 | tf_op jit(solution)/shard_map/ppermute | solution.py:399
  45.9 3.5 %collective-permute-start.10 = (bf16[2928,128]{1,0:T(8,128)(2,1)S(1)}, bf16[2928,128]{1,0:T(8,128)(2,1)S(1)}, u32[]{:S(2)}, u32[]{:S(2)}) collective-permute-start(bf16[2928,128]{1,0:T(8,128)(2,1)S(1)} %get-tuple-element.47), channel_id=1, source_target_pairs={{0,2},{1,3},{2,0},{3,1},{4,6},{5,7},{6,4},{7,5},{8,10},{9,11},{10,... | collective-permute-start | bytes 2248712 | tf_op jit(solution)/shard_map/ppermute | solution.py:399
  46.1 2.5 %collective-permute-start.11 = (bf16[976,128]{1,0:T(8,128)(2,1)S(1)}, bf16[976,128]{1,0:T(8,128)(2,1)S(1)}, u32[]{:S(2)}, u32[]{:S(2)}) collective-permute-start(bf16[976,128]{1,0:T(8,128)(2,1)S(1)} %get-tuple-element.45.refs_0_), channel_id=1, source_target_pairs={{0,2},{1,3},{2,0},{3,1},{4,6},{5,7},{6,4},{7,5},{8,10},{9,11},{10,... | collective-permute-start | bytes 749576 | tf_op jit(solution)/shard_map/ppermute | solution.py:399
  48.6 8.2 %collective-permute-start.12 = (bf16[972,128]{1,0:T(8,128)(2,1)S(1)}, bf16[972,128]{1,0:T(8,128)(2,1)S(1)}, u32[]{:S(2)}, u32[]{:S(2)}) collective-permute-start(bf16[972,128]{1,0:T(8,128)(2,1)S(1)} %total.2.refs_0_), channel_id=1, source_target_pairs={{0,1},{1,0},{2,3},{3,2},{4,5},{5,4},{6,7},{7,6},{8,9},{9,8},{10,11... | collective-permute-start | bytes 746504 | tf_op jit(solution)/shard_map/ppermute | solution.py:399
  49.5 9.1 %collective-permute-start.15 = (bf16[972,128]{1,0:T(8,128)(2,1)S(1)}, bf16[972,128]{1,0:T(8,128)(2,1)S(1)}, u32[]{:S(2)}, u32[]{:S(2)}) collective-permute-start(bf16[972,128]{1,0:T(8,128)(2,1)S(1)} %get-tuple-element.50), channel_id=1, source_target_pairs={{0,4},{1,5},{2,6},{3,7},{4,8},{5,9},{6,10},{7,11},{8,12},{9,13},{1... | collective-permute-start | bytes 746504 | tf_op jit(solution)/shard_map/ppermute | solution.py:399
  49.6 13.7 %collective-permute-start.17 = (bf16[972,128]{1,0:T(8,128)(2,1)S(1)}, bf16[972,128]{1,0:T(8,128)(2,1)S(1)}, u32[]{:S(2)}, u32[]{:S(2)}) collective-permute-start(bf16[972,128]{1,0:T(8,128)(2,1)S(1)} %get-tuple-element.51), channel_id=1, source_target_pairs={{0,12},{1,13},{2,14},{3,15},{4,0},{5,1},{6,2},{7,3},{8,4},{9,5},{1... | collective-permute-start | bytes 746504 | tf_op jit(solution)/shard_map/ppermute | solution.py:399
  56.8 19.5 %copy-start.1 = (bf16[8,972,128]{2,0,1:T(8,128)(2,1)S(1)}, bf16[8,972,128]{2,0,1:T(8,128)(2,1)}, u32[]{:S(2)}) copy-start(bf16[8,972,128]{2,0,1:T(8,128)(2,1)} %param.4) | copy-start | bytes 5971972
  56.8 8.8 %collective-permute-start.13 = (bf16[972,128]{1,0:T(8,128)(2,1)S(1)}, bf16[972,128]{1,0:T(8,128)(2,1)S(1)}, u32[]{:S(2)}, u32[]{:S(2)}) collective-permute-start(bf16[972,128]{1,0:T(8,128)(2,1)S(1)} %follow.1), channel_id=1, source_target_pairs={{0,8},{1,9},{2,10},{3,11},{4,12},{5,13},{6,14},{7,15},{8,0},{9,1},... | collective-permute-start | bytes 746504 | tf_op jit(solution)/shard_map/ppermute | solution.py:399
  58.7 9.0 %collective-permute-start.16 = (bf16[972,128]{1,0:T(8,128)(2,1)S(1)}, bf16[972,128]{1,0:T(8,128)(2,1)S(1)}, u32[]{:S(2)}, u32[]{:S(2)}) collective-permute-start(bf16[972,128]{1,0:T(8,128)(2,1)S(1)} %collective-permute-done.15.refs_2_), channel_id=1, source_target_pairs={{0,1},{1,0},{2,3},{3,2},{4,5},{5,4},{6,7},{7,6},{8,9},{9,8},{10,11... | collective-permute-start | bytes 746504 | tf_op jit(solution)/shard_map/ppermute | solution.py:399
  63.3 9.7 %collective-permute-start.18 = (bf16[972,128]{1,0:T(8,128)(2,1)S(1)}, bf16[972,128]{1,0:T(8,128)(2,1)S(1)}, u32[]{:S(2)}, u32[]{:S(2)}) collective-permute-start(bf16[972,128]{1,0:T(8,128)(2,1)S(1)} %collective-permute-done.17.refs_4_), channel_id=1, source_target_pairs={{0,1},{1,0},{2,3},{3,2},{4,5},{5,4},{6,7},{7,6},{8,9},{9,8},{10,11... | collective-permute-start | bytes 746504 | tf_op jit(solution)/shard_map/ppermute | solution.py:399
  65.7 10.7 %collective-permute-start.14 = (bf16[972,128]{1,0:T(8,128)(2,1)S(1)}, bf16[972,128]{1,0:T(8,128)(2,1)S(1)}, u32[]{:S(2)}, u32[]{:S(2)}) collective-permute-start(bf16[972,128]{1,0:T(8,128)(2,1)S(1)} %collective-permute-done.13.refs_0_), channel_id=1, source_target_pairs={{0,1},{1,0},{2,3},{3,2},{4,5},{5,4},{6,7},{7,6},{8,9},{9,8},{10,11... | collective-permute-start | bytes 746504 | tf_op jit(solution)/shard_map/ppermute | solution.py:399

commit v9 on v4

--- a/solution.py
+++ b/solution.py
@@ -421,19 +421,15 @@
 
     pieces = {}
     inner = weights.shape[1]
-    after_piece, after_total = (), ()
-    for shifts in ((0,), (1, 3, 2)):
-        home, away = piece(shifts, pe, mr, after_piece)
-        after_piece = (away,)
+    for s in (0, 1, 3, 2):
+        home, away = piece((s,), pe, mr)
         away = send(away, lambda t, y, k, d: (t, y, 1 - k, d))
-        blocks_here = total(home, away, len(shifts), inner, after_total)
-        after_total = (blocks_here[0],)
-        for s, block in zip(shifts, blocks_here):
-            if s:
-                block = send(block, lambda t, y, k, d: (t, y + s, k, d))
-            if s == 1:
-                block = follow(block, pieces[0][1])
-            pieces[s] = [block, send(block, lambda t, y, k, d: (t, y, k, 1 - d))]
+        (block,) = total(home, away, 1, inner, ())
+        if s == 2:
+            block = follow(block, pieces[0][1])
+        if s:
+            block = send(block, lambda t, y, k, d: (t, y + s, k, d))
+        pieces[s] = [block, send(block, lambda t, y, k, d: (t, y, k, 1 - d))]
     early, late = (0, 1, 3), (2,)
     full = gather(sum([pieces[s] for s in early], []), early, rows_y, dps)
     return finish(sum([pieces[s] for s in late], []), late, weights, full, rows_y, dps)

time: 84.3 us -> 76.6 us (0.909)
  waiting for transfers between devices: 41.7 us -> 35.2 us
  starting transfers between devices: 23.6 us -> 22.7 us
    ppermute x19 -> x21, waiting for transfers between devices: 41.7 us -> 35.2 us  [send(): return lax.ppermute(x, AXES, table(mesh_shape, move))]
    ppermute x19 -> x21, starting transfers between devices: 23.6 us -> 22.7 us  [send(): return lax.ppermute(x, AXES, table(mesh_shape, move))]
    pallas_call x2 -> x4, Pallas kernels: 2.06 us -> 2.44 us  [piece(): pl.pallas_call(functools.partial(piece_kernel, shifts, 1.0 / depth), out_...]
  transfers between devices with their start and end apart: 19 -> 21, of which waited for: 11 -> 12; matrix products, arithmetic and copies ran while one was open for 0% -> 0% of each run, Pallas kernels for 5% -> 8%
where the time goes in v9:
time: 76.6 us; the launch traced here: 76.4 us
  waiting for transfers between devices  35.2 us (46%)
  starting transfers between devices  22.7 us (30%)
  Pallas kernels  16.9 us (22%)
  between operations  0.97 us (1%)
    ppermute x21, waiting for transfers between devices, send(): return lax.ppermute(x, AXES, table(mesh_shape, move))  35.2 us
    ppermute x21, starting transfers between devices, send(): return lax.ppermute(x, AXES, table(mesh_shape, move))  22.7 us
    pallas_call x2, Pallas kernels, cut(): pl.pallas_call(functools.partial(cut_kernel, above), out_shape=[jax.Shape...  4.68 us
    pallas_call x1, Pallas kernels, column(): pl.pallas_call(functools.partial(column_kernel, rows_y), out_shape=[jax.S...  4.1 us
    pallas_call x1, Pallas kernels, finish(): pl.pallas_call(functools.partial(finish_kernel, rows_y, dps, shifts), out...  2.5 us
    pallas_call x4, Pallas kernels, piece(): pl.pallas_call(functools.partial(piece_kernel, shifts, 1.0 / depth), out_...  2.44 us
  transfers between devices with their start and end apart: 21, of which 12 were waited for; matrix products, arithmetic and copies ran while one was open for 0% of the time, Pallas kernels for 8%

profile of v9, /device:TPU:4, one launch (start us, length us, event | category | flops | bytes accessed | tf_op | source)
XLA Modules:
  0.0 76.4 jit_solution(15049065586094709153)
XLA Ops:
  0.6 3.8 %collective-permute-start.1 = (s32[2,8]{1,0:T(2,128)}, s32[2,8]{1,0:T(2,128)S(1)}, u32[]{:S(2)}, u32[]{:S(2)}) collective-permute-start(s32[2,8]{1,0:T(2,128)} %bitcast.12), channel_id=1, source_target_pairs={{0,16},{1,17},{2,18},{3,19},{4,20},{5,21},{6,22},{7,23},{8,24},{9,... | collective-permute-start | bytes 200 | tf_op jit(solution)/shard_map/ppermute | solution.py:399
  4.5 0.7 copy-done.1
  5.2 2.3 %cut_above.1 = (bf16[972,384]{1,0:T(8,128)(2,1)S(1)}, f32[8,128]{1,0:T(8,128)S(1)}) custom-call(s32[2,8]{1,0:T(2,128)S(1)} %bitcast.13, bf16[3,20,128,384]{3,2,1,0:T(8,128)(2,1)} %frames.3), custom_call_target="tpu_custom_call" | custom-call | tf_op jit(solution)/shard_map/cut_above/pallas_call | solution.py:95
  7.5 2.6 %collective-permute-done.1.places = s32[2,8]{1,0:T(2,128)S(1)} collective-permute-done((s32[2,8]{1,0:T(2,128)}, s32[2,8]{1,0:T(2,128)S(1)}, u32[]{:S(2)}, u32[]{:S(2)}) %collective-permute-start.1) | collective-permute-done | bytes 96 | tf_op jit(solution)/shard_map/ppermute | solution.py:399
  10.1 2.4 %cut_below.1 = (bf16[972,384]{1,0:T(8,128)(2,1)S(1)}, f32[8,128]{1,0:T(8,128)S(1)}) custom-call(s32[2,8]{1,0:T(2,128)S(1)} %collective-permute-done.1.places, bf16[3,20,128,384]{3,2,1,0:T(8,128)(2,1)} %frames.3, f32[8,128]{1,0:T(8,128)S(1)} %get-tuple-element.31.refs_0_), custom_call_target="tpu_custom_call" | custom-call | tf_op jit(solution)/shard_map/cut_below/pallas_call | solution.py:95
  12.5 0.8 %blocks.1 = (bf16[972,128]{1,0:T(8,128)(2,1)S(1)}, bf16[972,128]{1,0:T(8,128)(2,1)S(1)}, bf16[972,128]{1,0:T(8,128)(2,1)S(1)}, bf16[972,128]{1,0:T(8,128)(2,1)S(1)}) custom-call(bf16[7776,128]{1,0:T(8,128)(2,1)S(1)} %bitcast.10, f32[8,128]{1,0:T(8,128)S(1)} %get-tuple-element.33.refs_0_), custom_call_target="tpu_custom_call" | custom-call | tf_op jit(solution)/shard_map/blocks/pallas_call | solution.py:127
  13.2 3.1 %collective-permute-start.4 = (bf16[972,128]{1,0:T(8,128)(2,1)S(1)}, bf16[972,128]{1,0:T(8,128)(2,1)S(1)}, u32[]{:S(2)}, u32[]{:S(2)}) collective-permute-start(bf16[972,128]{1,0:T(8,128)(2,1)S(1)} %get-tuple-element.36), channel_id=1, source_target_pairs={{0,12},{1,13},{2,14},{3,15},{4,0},{5,1},{6,2},{7,3},{8,4},{9,5},{1... | collective-permute-start | bytes 746504 | tf_op jit(solution)/shard_map/ppermute | solution.py:399
  16.3 0.7 collective-permute-start
  17.0 3.9 %collective-permute-start.2 = (bf16[972,384]{1,0:T(8,128)(2,1)S(1)}, bf16[972,384]{1,0:T(8,128)(2,1)S(1)}, u32[]{:S(2)}, u32[]{:S(2)}) collective-permute-start(bf16[972,384]{1,0:T(8,128)(2,1)S(1)} %get-tuple-element.32), channel_id=1, source_target_pairs={{16,0},{17,2},{18,1},{19,3},{20,4},{21,6},{22,5},{23,7},{24,8},{25... | collective-permute-start | bytes 2239496 | tf_op jit(solution)/shard_map/ppermute | solution.py:399
  21.1 2.2 %collective-permute-start.6 = (bf16[972,128]{1,0:T(8,128)(2,1)S(1)}, bf16[972,128]{1,0:T(8,128)(2,1)S(1)}, u32[]{:S(2)}, u32[]{:S(2)}) collective-permute-start(bf16[972,128]{1,0:T(8,128)(2,1)S(1)} %get-tuple-element.38), channel_id=1, source_target_pairs={{0,8},{1,9},{2,10},{3,11},{4,12},{5,13},{6,14},{7,15},{8,0},{9,1},... | collective-permute-start | bytes 746504 | tf_op jit(solution)/shard_map/ppermute | solution.py:399
  23.2 0.9 %collective-permute-start.3 = (bf16[972,128]{1,0:T(8,128)(2,1)S(1)}, bf16[972,128]{1,0:T(8,128)(2,1)S(1)}, u32[]{:S(2)}, u32[]{:S(2)}) collective-permute-start(bf16[972,128]{1,0:T(8,128)(2,1)S(1)} %get-tuple-element.34.own), channel_id=1, source_target_pairs={{0,2},{1,3},{2,0},{3,1},{4,6},{5,7},{6,4},{7,5},{8,10},{9,11},{10,... | collective-permute-start | bytes 746504 | tf_op jit(solution)/shard_map/ppermute | solution.py:399
  24.1 12.1 %collective-permute-done.8.own = bf16[972,128]{1,0:T(8,128)(2,1)S(1)} collective-permute-done((bf16[972,128]{1,0:T(8,128)(2,1)S(1)}, bf16[972,128]{1,0:T(8,128)(2,1)S(1)}, u32[]{:S(2)}, u32[]{:S(2)}) %collective-permute-start.8) | collective-permute-done | bytes 248864 | tf_op jit(solution)/shard_map/ppermute | solution.py:399
  36.2 0.2 collective-permute-start.9
  36.4 0.3 collective-permute-start.7
  36.7 0.2 collective-permute-start.5
  36.9 0.2 filters.4
  37.1 0.6 collective-permute-done.9.other
  37.7 0.2 filters.7
  37.9 0.1 collective-permute-done.7.other
  38.1 0.2 filters.6
  38.3 0.1 collective-permute-done.5.other
  38.4 0.2 filters.5
  38.7 0.3 join.1.patch_in
  39.0 4.1 %column.1 = (bf16[972,768]{1,0:T(8,128)(2,1)S(1)}, bf16[1024,768]{1,0:T(8,128)(2,1)S(1)}) custom-call(bf16[972,384]{1,0:T(8,128)(2,1)S(1)} %join.1.patch_in, bf16[972,256]{1,0:T(8,128)(2,1)S(1)} %get-tuple-element.35.refs_0_, bf16[972,256]{1,0:T(8,128)(2,1)S(1)} %get-tuple-element.37.refs_1_, bf16[972,256]{1,0:T(8,128)(2,1)S(1)} %get-tuple-element.39.refs_2_, ...), custom_call_target="tpu_custom_call" | custom-call | tf_op jit(solution)/shard_map/column/pallas_call | solution.py:231
  43.1 0.6 piece.5
  43.7 0.3 collective-permute-start.11
  44.0 0.6 piece.7
  44.6 0.4 collective-permute-start.18
  45.0 0.6 piece.6
  45.6 0.2 collective-permute-start.15
  45.9 0.6 piece.4
  46.5 0.4 collective-permute-start.10
  47.0 1.4 %collective-permute-start.12 = (bf16[972,128]{1,0:T(8,128)(2,1)S(1)}, bf16[972,128]{1,0:T(8,128)(2,1)S(1)}, u32[]{:S(2)}, u32[]{:S(2)}) collective-permute-start(bf16[972,128]{1,0:T(8,128)(2,1)S(1)} %total.5.refs_0_), channel_id=1, source_target_pairs={{0,1},{1,0},{2,3},{3,2},{4,5},{5,4},{6,7},{7,6},{8,9},{9,8},{10,11... | collective-permute-start | bytes 746504 | tf_op jit(solution)/shard_map/ppermute | solution.py:399
  48.4 0.8 %collective-permute-start.19 = (bf16[972,128]{1,0:T(8,128)(2,1)S(1)}, bf16[972,128]{1,0:T(8,128)(2,1)S(1)}, u32[]{:S(2)}, u32[]{:S(2)}) collective-permute-start(bf16[972,128]{1,0:T(8,128)(2,1)S(1)} %total.7), channel_id=1, source_target_pairs={{0,12},{1,13},{2,14},{3,15},{4,0},{5,1},{6,2},{7,3},{8,4},{9,5},{1... | collective-permute-start | bytes 746504 | tf_op jit(solution)/shard_map/ppermute | solution.py:399
  49.3 1.3 %collective-permute-start.16 = (bf16[972,128]{1,0:T(8,128)(2,1)S(1)}, bf16[972,128]{1,0:T(8,128)(2,1)S(1)}, u32[]{:S(2)}, u32[]{:S(2)}) collective-permute-start(bf16[972,128]{1,0:T(8,128)(2,1)S(1)} %total.6), channel_id=1, source_target_pairs={{0,4},{1,5},{2,6},{3,7},{4,8},{5,9},{6,10},{7,11},{8,12},{9,13},{1... | collective-permute-start | bytes 746504 | tf_op jit(solution)/shard_map/ppermute | solution.py:399
  50.8 4.4 %collective-permute-done.12.after.refs_1_ = bf16[972,128]{1,0:T(8,128)(2,1)S(1)} collective-permute-done((bf16[972,128]{1,0:T(8,128)(2,1)S(1)}, bf16[972,128]{1,0:T(8,128)(2,1)S(1)}, u32[]{:S(2)}, u32[]{:S(2)}) %collective-permute-start.12) | collective-permute-done | bytes 248864 | tf_op jit(solution)/shard_map/ppermute | solution.py:399
  55.2 0.1 collective-permute-start.13
  55.3 0.9 %collective-permute-done.19.refs_4_ = bf16[972,128]{1,0:T(8,128)(2,1)S(1)} collective-permute-done((bf16[972,128]{1,0:T(8,128)(2,1)S(1)}, bf16[972,128]{1,0:T(8,128)(2,1)S(1)}, u32[]{:S(2)}, u32[]{:S(2)}) %collective-permute-start.19) | collective-permute-done | bytes 248864 | tf_op jit(solution)/shard_map/ppermute | solution.py:399
  56.2 0.9 %collective-permute-start.20 = (bf16[972,128]{1,0:T(8,128)(2,1)S(1)}, bf16[972,128]{1,0:T(8,128)(2,1)S(1)}, u32[]{:S(2)}, u32[]{:S(2)}) collective-permute-start(bf16[972,128]{1,0:T(8,128)(2,1)S(1)} %collective-permute-done.19.refs_4_), channel_id=1, source_target_pairs={{0,1},{1,0},{2,3},{3,2},{4,5},{5,4},{6,7},{7,6},{8,9},{9,8},{10,11... | collective-permute-start | bytes 746504 | tf_op jit(solution)/shard_map/ppermute | solution.py:399
  57.1 0.9 %collective-permute-done.16.refs_2_ = bf16[972,128]{1,0:T(8,128)(2,1)S(1)} collective-permute-done((bf16[972,128]{1,0:T(8,128)(2,1)S(1)}, bf16[972,128]{1,0:T(8,128)(2,1)S(1)}, u32[]{:S(2)}, u32[]{:S(2)}) %collective-permute-start.16) | collective-permute-done | bytes 248864 | tf_op jit(solution)/shard_map/ppermute | solution.py:399
  58.0 0.4 collective-permute-start.17
  58.5 5.6 %collective-permute-done.13.refs_0_ = bf16[972,128]{1,0:T(8,128)(2,1)S(1)} collective-permute-done((bf16[972,128]{1,0:T(8,128)(2,1)S(1)}, bf16[972,128]{1,0:T(8,128)(2,1)S(1)}, u32[]{:S(2)}, u32[]{:S(2)}) %collective-permute-start.13) | collective-permute-done | bytes 248864 | tf_op jit(solution)/shard_map/ppermute | solution.py:399
  64.1 1.0 %collective-permute-start.14 = (bf16[972,128]{1,0:T(8,128)(2,1)S(1)}, bf16[972,128]{1,0:T(8,128)(2,1)S(1)}, u32[]{:S(2)}, u32[]{:S(2)}) collective-permute-start(bf16[972,128]{1,0:T(8,128)(2,1)S(1)} %collective-permute-done.13.refs_0_), channel_id=1, source_target_pairs={{0,1},{1,0},{2,3},{3,2},{4,5},{5,4},{6,7},{7,6},{8,9},{9,8},{10,11... | collective-permute-start | bytes 746504 | tf_op jit(solution)/shard_map/ppermute | solution.py:399
  65.1 0.1 collective-permute-done.20.refs_5_
  65.2 5.4 %collective-permute-done.17.refs_3_ = bf16[972,128]{1,0:T(8,128)(2,1)S(1)} collective-permute-done((bf16[972,128]{1,0:T(8,128)(2,1)S(1)}, bf16[972,128]{1,0:T(8,128)(2,1)S(1)}, u32[]{:S(2)}, u32[]{:S(2)}) %collective-permute-start.17) | collective-permute-done | bytes 248864 | tf_op jit(solution)/shard_map/ppermute | solution.py:399
  70.6 0.8 %gather.1.refs_3_ = f32[7776,128]{1,0:T(8,128)S(1)} custom-call(bf16[972,128]{1,0:T(8,128)(2,1)S(1)} %total.5.refs_0_, bf16[972,128]{1,0:T(8,128)(2,1)S(1)} %collective-permute-done.12.after.refs_1_, bf16[972,128]{1,0:T(8,128)(2,1)S(1)} %collective-permute-done.16.refs_2_, bf16[972,128]{1,0:T(8,128)(2,1)S(1)} %collective-permute-done.17.refs_3_, ...), custom_call_target="tpu_custom_call" | custom-call | tf_op jit(solution)/shard_map/gather/pallas_call | solution.py:339
  71.4 2.3 %collective-permute-done.14.refs_1_ = bf16[972,128]{1,0:T(8,128)(2,1)S(1)} collective-permute-done((bf16[972,128]{1,0:T(8,128)(2,1)S(1)}, bf16[972,128]{1,0:T(8,128)(2,1)S(1)}, u32[]{:S(2)}, u32[]{:S(2)}) %collective-permute-start.14) | collective-permute-done | bytes 248864 | tf_op jit(solution)/shard_map/ppermute | solution.py:399
  73.7 2.5 %finish.1 = (f32[3888,128]{1,0:T(8,128)}, bf16[7776,128]{1,0:T(8,128)(2,1)}) custom-call(bf16[972,128]{1,0:T(8,128)(2,1)S(1)} %collective-permute-done.13.refs_0_, bf16[972,128]{1,0:T(8,128)(2,1)S(1)} %collective-permute-done.14.refs_1_, bf16[7776,128]{1,0:T(8,128)(2,1)S(1)} %bitcast.11, f32[7776,128]{1,0:T(8,128)S(1)} %gather.1.refs_3_), custom_call_target="tpu_custom_call" | custom-call | tf_op jit(solution)/shard_map/finish/pallas_call | solution.py:375
  (18 shorter events, 0.4 us)
Async XLA Ops:
  0.6 9.5 %collective-permute-start.1 = (s32[2,8]{1,0:T(2,128)}, s32[2,8]{1,0:T(2,128)S(1)}, u32[]{:S(2)}, u32[]{:S(2)}) collective-permute-start(s32[2,8]{1,0:T(2,128)} %bitcast.12), channel_id=1, source_target_pairs={{0,16},{1,17},{2,18},{3,19},{4,20},{5,21},{6,22},{7,23},{8,24},{9,... | collective-permute-start | bytes 200 | tf_op jit(solution)/shard_map/ppermute | solution.py:399
  4.5 0.7 copy-start.1
  10.1 2.4 %copy-start = (bf16[8,972,128]{2,0,1:T(8,128)(2,1)S(1)}, bf16[8,972,128]{2,0,1:T(8,128)(2,1)}, u32[]{:S(2)}) copy-start(bf16[8,972,128]{2,0,1:T(8,128)(2,1)} %param.4) | copy-start | bytes 5971972
  13.2 10.0 %collective-permute-start.4 = (bf16[972,128]{1,0:T(8,128)(2,1)S(1)}, bf16[972,128]{1,0:T(8,128)(2,1)S(1)}, u32[]{:S(2)}, u32[]{:S(2)}) collective-permute-start(bf16[972,128]{1,0:T(8,128)(2,1)S(1)} %get-tuple-element.36), channel_id=1, source_target_pairs={{0,12},{1,13},{2,14},{3,15},{4,0},{5,1},{6,2},{7,3},{8,4},{9,5},{1... | collective-permute-start | bytes 746504 | tf_op jit(solution)/shard_map/ppermute | solution.py:399
  16.3 22.3 %collective-permute-start = (bf16[972,384]{1,0:T(8,128)(2,1)S(1)}, bf16[972,384]{1,0:T(8,128)(2,1)S(1)}, u32[]{:S(2)}, u32[]{:S(2)}) collective-permute-start(bf16[972,384]{1,0:T(8,128)(2,1)S(1)} %get-tuple-element.30.above), channel_id=1, source_target_pairs={{1,2},{2,1},{5,6},{6,5},{9,10},{10,9},{13,14},{14,13},{17,18},{18,... | collective-permute-start | bytes 2239496 | tf_op jit(solution)/shard_map/ppermute | solution.py:399
  17.0 21.6 %collective-permute-start.2 = (bf16[972,384]{1,0:T(8,128)(2,1)S(1)}, bf16[972,384]{1,0:T(8,128)(2,1)S(1)}, u32[]{:S(2)}, u32[]{:S(2)}) collective-permute-start(bf16[972,384]{1,0:T(8,128)(2,1)S(1)} %get-tuple-element.32), channel_id=1, source_target_pairs={{16,0},{17,2},{18,1},{19,3},{20,4},{21,6},{22,5},{23,7},{24,8},{25... | collective-permute-start | bytes 2239496 | tf_op jit(solution)/shard_map/ppermute | solution.py:399
  21.0 15.2 %collective-permute-start.8 = (bf16[972,128]{1,0:T(8,128)(2,1)S(1)}, bf16[972,128]{1,0:T(8,128)(2,1)S(1)}, u32[]{:S(2)}, u32[]{:S(2)}) collective-permute-start(bf16[972,128]{1,0:T(8,128)(2,1)S(1)} %get-tuple-element.40), channel_id=1, source_target_pairs={{0,4},{1,5},{2,6},{3,7},{4,8},{5,9},{6,10},{7,11},{8,12},{9,13},{1... | collective-permute-start | bytes 746504 | tf_op jit(solution)/shard_map/ppermute | solution.py:399
  21.1 15.3 %collective-permute-start.6 = (bf16[972,128]{1,0:T(8,128)(2,1)S(1)}, bf16[972,128]{1,0:T(8,128)(2,1)S(1)}, u32[]{:S(2)}, u32[]{:S(2)}) collective-permute-start(bf16[972,128]{1,0:T(8,128)(2,1)S(1)} %get-tuple-element.38), channel_id=1, source_target_pairs={{0,8},{1,9},{2,10},{3,11},{4,12},{5,13},{6,14},{7,15},{8,0},{9,1},... | collective-permute-start | bytes 746504 | tf_op jit(solution)/shard_map/ppermute | solution.py:399
  23.2 13.4 %collective-permute-start.3 = (bf16[972,128]{1,0:T(8,128)(2,1)S(1)}, bf16[972,128]{1,0:T(8,128)(2,1)S(1)}, u32[]{:S(2)}, u32[]{:S(2)}) collective-permute-start(bf16[972,128]{1,0:T(8,128)(2,1)S(1)} %get-tuple-element.34.own), channel_id=1, source_target_pairs={{0,2},{1,3},{2,0},{3,1},{4,6},{5,7},{6,4},{7,5},{8,10},{9,11},{10,... | collective-permute-start | bytes 746504 | tf_op jit(solution)/shard_map/ppermute | solution.py:399
  36.2 1.5 %collective-permute-start.9 = (bf16[972,128]{1,0:T(8,128)(2,1)S(1)}, bf16[972,128]{1,0:T(8,128)(2,1)S(1)}, u32[]{:S(2)}, u32[]{:S(2)}) collective-permute-start(bf16[972,128]{1,0:T(8,128)(2,1)S(1)} %collective-permute-done.8.own), channel_id=1, source_target_pairs={{0,2},{1,3},{2,0},{3,1},{4,6},{5,7},{6,4},{7,5},{8,10},{9,11},{10,... | collective-permute-start | bytes 746504 | tf_op jit(solution)/shard_map/ppermute | solution.py:399
  36.4 1.7 %collective-permute-start.7 = (bf16[972,128]{1,0:T(8,128)(2,1)S(1)}, bf16[972,128]{1,0:T(8,128)(2,1)S(1)}, u32[]{:S(2)}, u32[]{:S(2)}) collective-permute-start(bf16[972,128]{1,0:T(8,128)(2,1)S(1)} %collective-permute-done.6.own), channel_id=1, source_target_pairs={{0,2},{1,3},{2,0},{3,1},{4,6},{5,7},{6,4},{7,5},{8,10},{9,11},{10,... | collective-permute-start | bytes 746504 | tf_op jit(solution)/shard_map/ppermute | solution.py:399
  36.7 1.7 %collective-permute-start.5 = (bf16[972,128]{1,0:T(8,128)(2,1)S(1)}, bf16[972,128]{1,0:T(8,128)(2,1)S(1)}, u32[]{:S(2)}, u32[]{:S(2)}) collective-permute-start(bf16[972,128]{1,0:T(8,128)(2,1)S(1)} %collective-permute-done.4.own), channel_id=1, source_target_pairs={{0,2},{1,3},{2,0},{3,1},{4,6},{5,7},{6,4},{7,5},{8,10},{9,11},{10,... | collective-permute-start | bytes 746504 | tf_op jit(solution)/shard_map/ppermute | solution.py:399
  43.7 3.2 %collective-permute-start.11 = (bf16[976,128]{1,0:T(8,128)(2,1)S(1)}, bf16[976,128]{1,0:T(8,128)(2,1)S(1)}, u32[]{:S(2)}, u32[]{:S(2)}) collective-permute-start(bf16[976,128]{1,0:T(8,128)(2,1)S(1)} %get-tuple-element.51), channel_id=1, source_target_pairs={{0,2},{1,3},{2,0},{3,1},{4,6},{5,7},{6,4},{7,5},{8,10},{9,11},{10,... | collective-permute-start | bytes 749576 | tf_op jit(solution)/shard_map/ppermute | solution.py:399
  44.6 3.8 %collective-permute-start.18 = (bf16[976,128]{1,0:T(8,128)(2,1)S(1)}, bf16[976,128]{1,0:T(8,128)(2,1)S(1)}, u32[]{:S(2)}, u32[]{:S(2)}) collective-permute-start(bf16[976,128]{1,0:T(8,128)(2,1)S(1)} %get-tuple-element.55), channel_id=1, source_target_pairs={{0,2},{1,3},{2,0},{3,1},{4,6},{5,7},{6,4},{7,5},{8,10},{9,11},{10,... | collective-permute-start | bytes 749576 | tf_op jit(solution)/shard_map/ppermute | solution.py:399
  45.6 3.6 %collective-permute-start.15 = (bf16[976,128]{1,0:T(8,128)(2,1)S(1)}, bf16[976,128]{1,0:T(8,128)(2,1)S(1)}, u32[]{:S(2)}, u32[]{:S(2)}) collective-permute-start(bf16[976,128]{1,0:T(8,128)(2,1)S(1)} %get-tuple-element.53), channel_id=1, source_target_pairs={{0,2},{1,3},{2,0},{3,1},{4,6},{5,7},{6,4},{7,5},{8,10},{9,11},{10,... | collective-permute-start | bytes 749576 | tf_op jit(solution)/shard_map/ppermute | solution.py:399
  46.5 4.2 %collective-permute-start.10 = (bf16[976,128]{1,0:T(8,128)(2,1)S(1)}, bf16[976,128]{1,0:T(8,128)(2,1)S(1)}, u32[]{:S(2)}, u32[]{:S(2)}) collective-permute-start(bf16[976,128]{1,0:T(8,128)(2,1)S(1)} %get-tuple-element.49), channel_id=1, source_target_pairs={{0,2},{1,3},{2,0},{3,1},{4,6},{5,7},{6,4},{7,5},{8,10},{9,11},{10,... | collective-permute-start | bytes 749576 | tf_op jit(solution)/shard_map/ppermute | solution.py:399
  47.0 8.2 %collective-permute-start.12 = (bf16[972,128]{1,0:T(8,128)(2,1)S(1)}, bf16[972,128]{1,0:T(8,128)(2,1)S(1)}, u32[]{:S(2)}, u32[]{:S(2)}) collective-permute-start(bf16[972,128]{1,0:T(8,128)(2,1)S(1)} %total.5.refs_0_), channel_id=1, source_target_pairs={{0,1},{1,0},{2,3},{3,2},{4,5},{5,4},{6,7},{7,6},{8,9},{9,8},{10,11... | collective-permute-start | bytes 746504 | tf_op jit(solution)/shard_map/ppermute | solution.py:399
  48.4 7.8 %collective-permute-start.19 = (bf16[972,128]{1,0:T(8,128)(2,1)S(1)}, bf16[972,128]{1,0:T(8,128)(2,1)S(1)}, u32[]{:S(2)}, u32[]{:S(2)}) collective-permute-start(bf16[972,128]{1,0:T(8,128)(2,1)S(1)} %total.7), channel_id=1, source_target_pairs={{0,12},{1,13},{2,14},{3,15},{4,0},{5,1},{6,2},{7,3},{8,4},{9,5},{1... | collective-permute-start | bytes 746504 | tf_op jit(solution)/shard_map/ppermute | solution.py:399
  49.3 8.7 %collective-permute-start.16 = (bf16[972,128]{1,0:T(8,128)(2,1)S(1)}, bf16[972,128]{1,0:T(8,128)(2,1)S(1)}, u32[]{:S(2)}, u32[]{:S(2)}) collective-permute-start(bf16[972,128]{1,0:T(8,128)(2,1)S(1)} %total.6), channel_id=1, source_target_pairs={{0,4},{1,5},{2,6},{3,7},{4,8},{5,9},{6,10},{7,11},{8,12},{9,13},{1... | collective-permute-start | bytes 746504 | tf_op jit(solution)/shard_map/ppermute | solution.py:399
  55.2 8.9 %collective-permute-start.13 = (bf16[972,128]{1,0:T(8,128)(2,1)S(1)}, bf16[972,128]{1,0:T(8,128)(2,1)S(1)}, u32[]{:S(2)}, u32[]{:S(2)}) collective-permute-start(bf16[972,128]{1,0:T(8,128)(2,1)S(1)} %follow.1), channel_id=1, source_target_pairs={{0,8},{1,9},{2,10},{3,11},{4,12},{5,13},{6,14},{7,15},{8,0},{9,1},... | collective-permute-start | bytes 746504 | tf_op jit(solution)/shard_map/ppermute | solution.py:399
  56.2 9.0 %collective-permute-start.20 = (bf16[972,128]{1,0:T(8,128)(2,1)S(1)}, bf16[972,128]{1,0:T(8,128)(2,1)S(1)}, u32[]{:S(2)}, u32[]{:S(2)}) collective-permute-start(bf16[972,128]{1,0:T(8,128)(2,1)S(1)} %collective-permute-done.19.refs_4_), channel_id=1, source_target_pairs={{0,1},{1,0},{2,3},{3,2},{4,5},{5,4},{6,7},{7,6},{8,9},{9,8},{10,11... | collective-permute-start | bytes 746504 | tf_op jit(solution)/shard_map/ppermute | solution.py:399
  58.0 12.5 %collective-permute-start.17 = (bf16[972,128]{1,0:T(8,128)(2,1)S(1)}, bf16[972,128]{1,0:T(8,128)(2,1)S(1)}, u32[]{:S(2)}, u32[]{:S(2)}) collective-permute-start(bf16[972,128]{1,0:T(8,128)(2,1)S(1)} %collective-permute-done.16.refs_2_), channel_id=1, source_target_pairs={{0,1},{1,0},{2,3},{3,2},{4,5},{5,4},{6,7},{7,6},{8,9},{9,8},{10,11... | collective-permute-start | bytes 746504 | tf_op jit(solution)/shard_map/ppermute | solution.py:399
  64.1 9.6 %collective-permute-start.14 = (bf16[972,128]{1,0:T(8,128)(2,1)S(1)}, bf16[972,128]{1,0:T(8,128)(2,1)S(1)}, u32[]{:S(2)}, u32[]{:S(2)}) collective-permute-start(bf16[972,128]{1,0:T(8,128)(2,1)S(1)} %collective-permute-done.13.refs_0_), channel_id=1, source_target_pairs={{0,1},{1,0},{2,3},{3,2},{4,5},{5,4},{6,7},{7,6},{8,9},{9,8},{10,11... | collective-permute-start | bytes 746504 | tf_op jit(solution)/shard_map/ppermute | solution.py:399

commit v10 on v9

--- a/solution.py
+++ b/solution.py
@@ -426,9 +426,11 @@
         away = send(away, lambda t, y, k, d: (t, y, 1 - k, d))
         (block,) = total(home, away, 1, inner, ())
         if s == 2:
-            block = follow(block, pieces[0][1])
+            block = follow(block, pieces[1][0])
         if s:
             block = send(block, lambda t, y, k, d: (t, y + s, k, d))
+        if s == 3:
+            block = follow(block, pieces[0][1])
         pieces[s] = [block, send(block, lambda t, y, k, d: (t, y, k, 1 - d))]
     early, late = (0, 1, 3), (2,)
     full = gather(sum([pieces[s] for s in early], []), early, rows_y, dps)

time: 76.6 us -> 78.6 us (1.026)
  starting transfers between devices: 22.7 us -> 24.7 us
    ppermute x21, starting transfers between devices: 22.7 us -> 24.7 us  [send(): return lax.ppermute(x, AXES, table(mesh_shape, move))]
  transfers between devices with their start and end apart: 21 -> 21, of which waited for: 12 -> 11; matrix products, arithmetic and copies ran while one was open for 0% -> 0% of each run, Pallas kernels for 8% -> 8%
where the time goes in v10:
time: 78.6 us; the launch traced here: 78.3 us
  waiting for transfers between devices  35.1 us (45%)
  starting transfers between devices  24.7 us (31%)
  Pallas kernels  16.9 us (22%)
  between operations  1 us (1%)
    ppermute x21, waiting for transfers between devices, send(): return lax.ppermute(x, AXES, table(mesh_shape, move))  35.1 us
    ppermute x21, starting transfers between devices, send(): return lax.ppermute(x, AXES, table(mesh_shape, move))  24.7 us
    pallas_call x2, Pallas kernels, cut(): pl.pallas_call(functools.partial(cut_kernel, above), out_shape=[jax.Shape...  4.66 us
    pallas_call x1, Pallas kernels, column(): pl.pallas_call(functools.partial(column_kernel, rows_y), out_shape=[jax.S...  4.1 us
    pallas_call x1, Pallas kernels, finish(): pl.pallas_call(functools.partial(finish_kernel, rows_y, dps, shifts), out...  2.5 us
    pallas_call x4, Pallas kernels, piece(): pl.pallas_call(functools.partial(piece_kernel, shifts, 1.0 / depth), out_...  2.44 us
  transfers between devices with their start and end apart: 21, of which 11 were waited for; matrix products, arithmetic and copies ran while one was open for 0% of the time, Pallas kernels for 8%

profile of v10, /device:TPU:4, one launch (start us, length us, event | category | flops | bytes accessed | tf_op | source)
XLA Modules:
  0.0 78.3 jit_solution(4865873265521913786)
XLA Ops:
  0.6 3.8 %collective-permute-start.1 = (s32[2,8]{1,0:T(2,128)}, s32[2,8]{1,0:T(2,128)S(1)}, u32[]{:S(2)}, u32[]{:S(2)}) collective-permute-start(s32[2,8]{1,0:T(2,128)} %bitcast.12), channel_id=1, source_target_pairs={{0,16},{1,17},{2,18},{3,19},{4,20},{5,21},{6,22},{7,23},{8,24},{9,... | collective-permute-start | bytes 200 | tf_op jit(solution)/shard_map/ppermute | solution.py:399
  4.5 0.7 copy-done.1
  5.2 2.3 %cut_above.1 = (bf16[972,384]{1,0:T(8,128)(2,1)S(1)}, f32[8,128]{1,0:T(8,128)S(1)}) custom-call(s32[2,8]{1,0:T(2,128)S(1)} %bitcast.13, bf16[3,20,128,384]{3,2,1,0:T(8,128)(2,1)} %frames.3), custom_call_target="tpu_custom_call" | custom-call | tf_op jit(solution)/shard_map/cut_above/pallas_call | solution.py:95
  7.5 2.6 %collective-permute-done.1.places = s32[2,8]{1,0:T(2,128)S(1)} collective-permute-done((s32[2,8]{1,0:T(2,128)}, s32[2,8]{1,0:T(2,128)S(1)}, u32[]{:S(2)}, u32[]{:S(2)}) %collective-permute-start.1) | collective-permute-done | bytes 96 | tf_op jit(solution)/shard_map/ppermute | solution.py:399
  10.1 2.3 %cut_below.1 = (bf16[972,384]{1,0:T(8,128)(2,1)S(1)}, f32[8,128]{1,0:T(8,128)S(1)}) custom-call(s32[2,8]{1,0:T(2,128)S(1)} %collective-permute-done.1.places, bf16[3,20,128,384]{3,2,1,0:T(8,128)(2,1)} %frames.3, f32[8,128]{1,0:T(8,128)S(1)} %get-tuple-element.31.refs_0_), custom_call_target="tpu_custom_call" | custom-call | tf_op jit(solution)/shard_map/cut_below/pallas_call | solution.py:95
  12.5 0.8 blocks.1
  13.2 3.1 %collective-permute-start.4 = (bf16[972,128]{1,0:T(8,128)(2,1)S(1)}, bf16[972,128]{1,0:T(8,128)(2,1)S(1)}, u32[]{:S(2)}, u32[]{:S(2)}) collective-permute-start(bf16[972,128]{1,0:T(8,128)(2,1)S(1)} %get-tuple-element.36), channel_id=1, source_target_pairs={{0,12},{1,13},{2,14},{3,15},{4,0},{5,1},{6,2},{7,3},{8,4},{9,5},{1... | collective-permute-start | bytes 746504 | tf_op jit(solution)/shard_map/ppermute | solution.py:399
  16.3 0.7 collective-permute-start
  17.0 3.9 %collective-permute-start.2 = (bf16[972,384]{1,0:T(8,128)(2,1)S(1)}, bf16[972,384]{1,0:T(8,128)(2,1)S(1)}, u32[]{:S(2)}, u32[]{:S(2)}) collective-permute-start(bf16[972,384]{1,0:T(8,128)(2,1)S(1)} %get-tuple-element.32), channel_id=1, source_target_pairs={{16,0},{17,2},{18,1},{19,3},{20,4},{21,6},{22,5},{23,7},{24,8},{25... | collective-permute-start | bytes 2239496 | tf_op jit(solution)/shard_map/ppermute | solution.py:399
  21.0 0.1 collective-permute-start.8
  21.1 2.2 %collective-permute-start.6 = (bf16[972,128]{1,0:T(8,128)(2,1)S(1)}, bf16[972,128]{1,0:T(8,128)(2,1)S(1)}, u32[]{:S(2)}, u32[]{:S(2)}) collective-permute-start(bf16[972,128]{1,0:T(8,128)(2,1)S(1)} %get-tuple-element.38), channel_id=1, source_target_pairs={{0,8},{1,9},{2,10},{3,11},{4,12},{5,13},{6,14},{7,15},{8,0},{9,1},... | collective-permute-start | bytes 746504 | tf_op jit(solution)/shard_map/ppermute | solution.py:399
  23.3 0.9 %collective-permute-start.3 = (bf16[972,128]{1,0:T(8,128)(2,1)S(1)}, bf16[972,128]{1,0:T(8,128)(2,1)S(1)}, u32[]{:S(2)}, u32[]{:S(2)}) collective-permute-start(bf16[972,128]{1,0:T(8,128)(2,1)S(1)} %get-tuple-element.34.own), channel_id=1, source_target_pairs={{0,2},{1,3},{2,0},{3,1},{4,6},{5,7},{6,4},{7,5},{8,10},{9,11},{10,... | collective-permute-start | bytes 746504 | tf_op jit(solution)/shard_map/ppermute | solution.py:399
  24.1 12.0 %collective-permute-done.8.own = bf16[972,128]{1,0:T(8,128)(2,1)S(1)} collective-permute-done((bf16[972,128]{1,0:T(8,128)(2,1)S(1)}, bf16[972,128]{1,0:T(8,128)(2,1)S(1)}, u32[]{:S(2)}, u32[]{:S(2)}) %collective-permute-start.8) | collective-permute-done | bytes 248864 | tf_op jit(solution)/shard_map/ppermute | solution.py:399
  36.1 0.2 collective-permute-start.9
  36.4 0.3 collective-permute-start.7
  36.7 0.2 collective-permute-start.5
  36.9 0.2 filters.4
  37.1 0.6 collective-permute-done.9.other
  37.7 0.2 filters.7
  37.9 0.1 collective-permute-done.7.other
  38.0 0.2 filters.6
  38.3 0.1 collective-permute-done.5.other
  38.4 0.2 filters.5
  38.7 0.3 join.1.patch_in
  39.0 4.1 %column.1 = (bf16[972,768]{1,0:T(8,128)(2,1)S(1)}, bf16[1024,768]{1,0:T(8,128)(2,1)S(1)}) custom-call(bf16[972,384]{1,0:T(8,128)(2,1)S(1)} %join.1.patch_in, bf16[972,256]{1,0:T(8,128)(2,1)S(1)} %get-tuple-element.35.refs_0_, bf16[972,256]{1,0:T(8,128)(2,1)S(1)} %get-tuple-element.37.refs_1_, bf16[972,256]{1,0:T(8,128)(2,1)S(1)} %get-tuple-element.39.refs_2_, ...), custom_call_target="tpu_custom_call" | custom-call | tf_op jit(solution)/shard_map/column/pallas_call | solution.py:231
  43.1 0.6 piece.5
  43.7 0.3 collective-permute-start.11
  44.0 0.6 piece.7
  44.6 0.4 collective-permute-start.18
  45.0 0.6 piece.6
  45.6 0.3 collective-permute-start.15
  45.9 0.6 piece.4
  46.5 0.4 collective-permute-start.10
  47.0 0.1 collective-permute-start.12
  47.1 3.3 %collective-permute-start.19 = (bf16[972,128]{1,0:T(8,128)(2,1)S(1)}, bf16[972,128]{1,0:T(8,128)(2,1)S(1)}, u32[]{:S(2)}, u32[]{:S(2)}) collective-permute-start(bf16[972,128]{1,0:T(8,128)(2,1)S(1)} %total.7), channel_id=1, source_target_pairs={{0,12},{1,13},{2,14},{3,15},{4,0},{5,1},{6,2},{7,3},{8,4},{9,5},{1... | collective-permute-start | bytes 746504 | tf_op jit(solution)/shard_map/ppermute | solution.py:399
  50.5 1.4 %collective-permute-start.16 = (bf16[972,128]{1,0:T(8,128)(2,1)S(1)}, bf16[972,128]{1,0:T(8,128)(2,1)S(1)}, u32[]{:S(2)}, u32[]{:S(2)}) collective-permute-start(bf16[972,128]{1,0:T(8,128)(2,1)S(1)} %total.6.refs_0_), channel_id=1, source_target_pairs={{0,1},{1,0},{2,3},{3,2},{4,5},{5,4},{6,7},{7,6},{8,9},{9,8},{10,11... | collective-permute-start | bytes 746504 | tf_op jit(solution)/shard_map/ppermute | solution.py:399
  52.0 4.4 %collective-permute-done.12.after.refs_2_ = bf16[972,128]{1,0:T(8,128)(2,1)S(1)} collective-permute-done((bf16[972,128]{1,0:T(8,128)(2,1)S(1)}, bf16[972,128]{1,0:T(8,128)(2,1)S(1)}, u32[]{:S(2)}, u32[]{:S(2)}) %collective-permute-start.12) | collective-permute-done | bytes 248864 | tf_op jit(solution)/shard_map/ppermute | solution.py:399
  56.4 0.1 collective-permute-start.13
  56.5 1.6 %collective-permute-done.16.after.refs_1_ = bf16[972,128]{1,0:T(8,128)(2,1)S(1)} collective-permute-done((bf16[972,128]{1,0:T(8,128)(2,1)S(1)}, bf16[972,128]{1,0:T(8,128)(2,1)S(1)}, u32[]{:S(2)}, u32[]{:S(2)}) %collective-permute-start.16) | collective-permute-done | bytes 248864 | tf_op jit(solution)/shard_map/ppermute | solution.py:399
  58.2 1.2 %collective-permute-start.20 = (bf16[972,128]{1,0:T(8,128)(2,1)S(1)}, bf16[972,128]{1,0:T(8,128)(2,1)S(1)}, u32[]{:S(2)}, u32[]{:S(2)}) collective-permute-start(bf16[972,128]{1,0:T(8,128)(2,1)S(1)} %follow.3.refs_4_), channel_id=1, source_target_pairs={{0,1},{1,0},{2,3},{3,2},{4,5},{5,4},{6,7},{7,6},{8,9},{9,8},{10,11... | collective-permute-start | bytes 746504 | tf_op jit(solution)/shard_map/ppermute | solution.py:399
  59.4 0.9 %collective-permute-start.17 = (bf16[972,128]{1,0:T(8,128)(2,1)S(1)}, bf16[972,128]{1,0:T(8,128)(2,1)S(1)}, u32[]{:S(2)}, u32[]{:S(2)}) collective-permute-start(bf16[972,128]{1,0:T(8,128)(2,1)S(1)} %collective-permute-done.12.after.refs_2_), channel_id=1, source_target_pairs={{0,1},{1,0},{2,3},{3,2},{4,5},{5,4},{6,7},{7,6},{8,9},{9,8},{10,11... | collective-permute-start | bytes 746504 | tf_op jit(solution)/shard_map/ppermute | solution.py:399
  60.3 5.0 %collective-permute-done.13.refs_0_ = bf16[972,128]{1,0:T(8,128)(2,1)S(1)} collective-permute-done((bf16[972,128]{1,0:T(8,128)(2,1)S(1)}, bf16[972,128]{1,0:T(8,128)(2,1)S(1)}, u32[]{:S(2)}, u32[]{:S(2)}) %collective-permute-start.13) | collective-permute-done | bytes 248864 | tf_op jit(solution)/shard_map/ppermute | solution.py:399
  65.3 1.0 %collective-permute-start.14 = (bf16[972,128]{1,0:T(8,128)(2,1)S(1)}, bf16[972,128]{1,0:T(8,128)(2,1)S(1)}, u32[]{:S(2)}, u32[]{:S(2)}) collective-permute-start(bf16[972,128]{1,0:T(8,128)(2,1)S(1)} %collective-permute-done.13.refs_0_), channel_id=1, source_target_pairs={{0,1},{1,0},{2,3},{3,2},{4,5},{5,4},{6,7},{7,6},{8,9},{9,8},{10,11... | collective-permute-start | bytes 746504 | tf_op jit(solution)/shard_map/ppermute | solution.py:399
  66.3 1.0 %collective-permute-done.20.refs_5_ = bf16[972,128]{1,0:T(8,128)(2,1)S(1)} collective-permute-done((bf16[972,128]{1,0:T(8,128)(2,1)S(1)}, bf16[972,128]{1,0:T(8,128)(2,1)S(1)}, u32[]{:S(2)}, u32[]{:S(2)}) %collective-permute-start.20) | collective-permute-done | bytes 248864 | tf_op jit(solution)/shard_map/ppermute | solution.py:399
  67.2 5.4 %collective-permute-done.17.refs_3_ = bf16[972,128]{1,0:T(8,128)(2,1)S(1)} collective-permute-done((bf16[972,128]{1,0:T(8,128)(2,1)S(1)}, bf16[972,128]{1,0:T(8,128)(2,1)S(1)}, u32[]{:S(2)}, u32[]{:S(2)}) %collective-permute-start.17) | collective-permute-done | bytes 248864 | tf_op jit(solution)/shard_map/ppermute | solution.py:399
  72.6 0.8 %gather.1.refs_3_ = f32[7776,128]{1,0:T(8,128)S(1)} custom-call(bf16[972,128]{1,0:T(8,128)(2,1)S(1)} %total.6.refs_0_, bf16[972,128]{1,0:T(8,128)(2,1)S(1)} %collective-permute-done.16.after.refs_1_, bf16[972,128]{1,0:T(8,128)(2,1)S(1)} %collective-permute-done.12.after.refs_2_, bf16[972,128]{1,0:T(8,128)(2,1)S(1)} %collective-permute-done.17.refs_3_, ...), custom_call_target="tpu_custom_call" | custom-call | tf_op jit(solution)/shard_map/gather/pallas_call | solution.py:339
  73.4 2.2 %collective-permute-done.14.refs_1_ = bf16[972,128]{1,0:T(8,128)(2,1)S(1)} collective-permute-done((bf16[972,128]{1,0:T(8,128)(2,1)S(1)}, bf16[972,128]{1,0:T(8,128)(2,1)S(1)}, u32[]{:S(2)}, u32[]{:S(2)}) %collective-permute-start.14) | collective-permute-done | bytes 248864 | tf_op jit(solution)/shard_map/ppermute | solution.py:399
  75.6 2.5 %finish.1 = (f32[3888,128]{1,0:T(8,128)}, bf16[7776,128]{1,0:T(8,128)(2,1)}) custom-call(bf16[972,128]{1,0:T(8,128)(2,1)S(1)} %collective-permute-done.13.refs_0_, bf16[972,128]{1,0:T(8,128)(2,1)S(1)} %collective-permute-done.14.refs_1_, bf16[7776,128]{1,0:T(8,128)(2,1)S(1)} %bitcast.11, f32[7776,128]{1,0:T(8,128)S(1)} %gather.1.refs_3_), custom_call_target="tpu_custom_call" | custom-call | tf_op jit(solution)/shard_map/finish/pallas_call | solution.py:375
  (19 shorter events, 0.3 us)
Async XLA Ops:
  0.6 9.5 %collective-permute-start.1 = (s32[2,8]{1,0:T(2,128)}, s32[2,8]{1,0:T(2,128)S(1)}, u32[]{:S(2)}, u32[]{:S(2)}) collective-permute-start(s32[2,8]{1,0:T(2,128)} %bitcast.12), channel_id=1, source_target_pairs={{0,16},{1,17},{2,18},{3,19},{4,20},{5,21},{6,22},{7,23},{8,24},{9,... | collective-permute-start | bytes 200 | tf_op jit(solution)/shard_map/ppermute | solution.py:399
  4.5 0.7 copy-start.1
  10.1 2.4 %copy-start = (bf16[8,972,128]{2,0,1:T(8,128)(2,1)S(1)}, bf16[8,972,128]{2,0,1:T(8,128)(2,1)}, u32[]{:S(2)}) copy-start(bf16[8,972,128]{2,0,1:T(8,128)(2,1)} %param.4) | copy-start | bytes 5971972
  13.2 10.0 %collective-permute-start.4 = (bf16[972,128]{1,0:T(8,128)(2,1)S(1)}, bf16[972,128]{1,0:T(8,128)(2,1)S(1)}, u32[]{:S(2)}, u32[]{:S(2)}) collective-permute-start(bf16[972,128]{1,0:T(8,128)(2,1)S(1)} %get-tuple-element.36), channel_id=1, source_target_pairs={{0,12},{1,13},{2,14},{3,15},{4,0},{5,1},{6,2},{7,3},{8,4},{9,5},{1... | collective-permute-start | bytes 746504 | tf_op jit(solution)/shard_map/ppermute | solution.py:399
  16.3 22.3 %collective-permute-start = (bf16[972,384]{1,0:T(8,128)(2,1)S(1)}, bf16[972,384]{1,0:T(8,128)(2,1)S(1)}, u32[]{:S(2)}, u32[]{:S(2)}) collective-permute-start(bf16[972,384]{1,0:T(8,128)(2,1)S(1)} %get-tuple-element.30.above), channel_id=1, source_target_pairs={{1,2},{2,1},{5,6},{6,5},{9,10},{10,9},{13,14},{14,13},{17,18},{18,... | collective-permute-start | bytes 2239496 | tf_op jit(solution)/shard_map/ppermute | solution.py:399
  17.0 21.6 %collective-permute-start.2 = (bf16[972,384]{1,0:T(8,128)(2,1)S(1)}, bf16[972,384]{1,0:T(8,128)(2,1)S(1)}, u32[]{:S(2)}, u32[]{:S(2)}) collective-permute-start(bf16[972,384]{1,0:T(8,128)(2,1)S(1)} %get-tuple-element.32), channel_id=1, source_target_pairs={{16,0},{17,2},{18,1},{19,3},{20,4},{21,6},{22,5},{23,7},{24,8},{25... | collective-permute-start | bytes 2239496 | tf_op jit(solution)/shard_map/ppermute | solution.py:399
  21.0 15.2 %collective-permute-start.8 = (bf16[972,128]{1,0:T(8,128)(2,1)S(1)}, bf16[972,128]{1,0:T(8,128)(2,1)S(1)}, u32[]{:S(2)}, u32[]{:S(2)}) collective-permute-start(bf16[972,128]{1,0:T(8,128)(2,1)S(1)} %get-tuple-element.40), channel_id=1, source_target_pairs={{0,4},{1,5},{2,6},{3,7},{4,8},{5,9},{6,10},{7,11},{8,12},{9,13},{1... | collective-permute-start | bytes 746504 | tf_op jit(solution)/shard_map/ppermute | solution.py:399
  21.1 15.3 %collective-permute-start.6 = (bf16[972,128]{1,0:T(8,128)(2,1)S(1)}, bf16[972,128]{1,0:T(8,128)(2,1)S(1)}, u32[]{:S(2)}, u32[]{:S(2)}) collective-permute-start(bf16[972,128]{1,0:T(8,128)(2,1)S(1)} %get-tuple-element.38), channel_id=1, source_target_pairs={{0,8},{1,9},{2,10},{3,11},{4,12},{5,13},{6,14},{7,15},{8,0},{9,1},... | collective-permute-start | bytes 746504 | tf_op jit(solution)/shard_map/ppermute | solution.py:399
  23.3 13.4 %collective-permute-start.3 = (bf16[972,128]{1,0:T(8,128)(2,1)S(1)}, bf16[972,128]{1,0:T(8,128)(2,1)S(1)}, u32[]{:S(2)}, u32[]{:S(2)}) collective-permute-start(bf16[972,128]{1,0:T(8,128)(2,1)S(1)} %get-tuple-element.34.own), channel_id=1, source_target_pairs={{0,2},{1,3},{2,0},{3,1},{4,6},{5,7},{6,4},{7,5},{8,10},{9,11},{10,... | collective-permute-start | bytes 746504 | tf_op jit(solution)/shard_map/ppermute | solution.py:399
  36.1 1.5 %collective-permute-start.9 = (bf16[972,128]{1,0:T(8,128)(2,1)S(1)}, bf16[972,128]{1,0:T(8,128)(2,1)S(1)}, u32[]{:S(2)}, u32[]{:S(2)}) collective-permute-start(bf16[972,128]{1,0:T(8,128)(2,1)S(1)} %collective-permute-done.8.own), channel_id=1, source_target_pairs={{0,2},{1,3},{2,0},{3,1},{4,6},{5,7},{6,4},{7,5},{8,10},{9,11},{10,... | collective-permute-start | bytes 746504 | tf_op jit(solution)/shard_map/ppermute | solution.py:399
  36.4 1.7 %collective-permute-start.7 = (bf16[972,128]{1,0:T(8,128)(2,1)S(1)}, bf16[972,128]{1,0:T(8,128)(2,1)S(1)}, u32[]{:S(2)}, u32[]{:S(2)}) collective-permute-start(bf16[972,128]{1,0:T(8,128)(2,1)S(1)} %collective-permute-done.6.own), channel_id=1, source_target_pairs={{0,2},{1,3},{2,0},{3,1},{4,6},{5,7},{6,4},{7,5},{8,10},{9,11},{10,... | collective-permute-start | bytes 746504 | tf_op jit(solution)/shard_map/ppermute | solution.py:399
  36.7 1.7 %collective-permute-start.5 = (bf16[972,128]{1,0:T(8,128)(2,1)S(1)}, bf16[972,128]{1,0:T(8,128)(2,1)S(1)}, u32[]{:S(2)}, u32[]{:S(2)}) collective-permute-start(bf16[972,128]{1,0:T(8,128)(2,1)S(1)} %collective-permute-done.4.own), channel_id=1, source_target_pairs={{0,2},{1,3},{2,0},{3,1},{4,6},{5,7},{6,4},{7,5},{8,10},{9,11},{10,... | collective-permute-start | bytes 746504 | tf_op jit(solution)/shard_map/ppermute | solution.py:399
  43.7 3.2 %collective-permute-start.11 = (bf16[976,128]{1,0:T(8,128)(2,1)S(1)}, bf16[976,128]{1,0:T(8,128)(2,1)S(1)}, u32[]{:S(2)}, u32[]{:S(2)}) collective-permute-start(bf16[976,128]{1,0:T(8,128)(2,1)S(1)} %get-tuple-element.51), channel_id=1, source_target_pairs={{0,2},{1,3},{2,0},{3,1},{4,6},{5,7},{6,4},{7,5},{8,10},{9,11},{10,... | collective-permute-start | bytes 749576 | tf_op jit(solution)/shard_map/ppermute | solution.py:399
  44.6 2.5 %collective-permute-start.18 = (bf16[976,128]{1,0:T(8,128)(2,1)S(1)}, bf16[976,128]{1,0:T(8,128)(2,1)S(1)}, u32[]{:S(2)}, u32[]{:S(2)}) collective-permute-start(bf16[976,128]{1,0:T(8,128)(2,1)S(1)} %get-tuple-element.55), channel_id=1, source_target_pairs={{0,2},{1,3},{2,0},{3,1},{4,6},{5,7},{6,4},{7,5},{8,10},{9,11},{10,... | collective-permute-start | bytes 749576 | tf_op jit(solution)/shard_map/ppermute | solution.py:399
  45.6 4.8 %collective-permute-start.15 = (bf16[976,128]{1,0:T(8,128)(2,1)S(1)}, bf16[976,128]{1,0:T(8,128)(2,1)S(1)}, u32[]{:S(2)}, u32[]{:S(2)}) collective-permute-start(bf16[976,128]{1,0:T(8,128)(2,1)S(1)} %get-tuple-element.53), channel_id=1, source_target_pairs={{0,2},{1,3},{2,0},{3,1},{4,6},{5,7},{6,4},{7,5},{8,10},{9,11},{10,... | collective-permute-start | bytes 749576 | tf_op jit(solution)/shard_map/ppermute | solution.py:399
  46.5 5.4 %collective-permute-start.10 = (bf16[976,128]{1,0:T(8,128)(2,1)S(1)}, bf16[976,128]{1,0:T(8,128)(2,1)S(1)}, u32[]{:S(2)}, u32[]{:S(2)}) collective-permute-start(bf16[976,128]{1,0:T(8,128)(2,1)S(1)} %get-tuple-element.49), channel_id=1, source_target_pairs={{0,2},{1,3},{2,0},{3,1},{4,6},{5,7},{6,4},{7,5},{8,10},{9,11},{10,... | collective-permute-start | bytes 749576 | tf_op jit(solution)/shard_map/ppermute | solution.py:399
  47.0 9.4 %collective-permute-start.12 = (bf16[972,128]{1,0:T(8,128)(2,1)S(1)}, bf16[972,128]{1,0:T(8,128)(2,1)S(1)}, u32[]{:S(2)}, u32[]{:S(2)}) collective-permute-start(bf16[972,128]{1,0:T(8,128)(2,1)S(1)} %total.5), channel_id=1, source_target_pairs={{0,4},{1,5},{2,6},{3,7},{4,8},{5,9},{6,10},{7,11},{8,12},{9,13},{1... | collective-permute-start | bytes 746504 | tf_op jit(solution)/shard_map/ppermute | solution.py:399
  47.1 9.4 %collective-permute-start.19 = (bf16[972,128]{1,0:T(8,128)(2,1)S(1)}, bf16[972,128]{1,0:T(8,128)(2,1)S(1)}, u32[]{:S(2)}, u32[]{:S(2)}) collective-permute-start(bf16[972,128]{1,0:T(8,128)(2,1)S(1)} %total.7), channel_id=1, source_target_pairs={{0,12},{1,13},{2,14},{3,15},{4,0},{5,1},{6,2},{7,3},{8,4},{9,5},{1... | collective-permute-start | bytes 746504 | tf_op jit(solution)/shard_map/ppermute | solution.py:399
  50.5 7.7 %collective-permute-start.16 = (bf16[972,128]{1,0:T(8,128)(2,1)S(1)}, bf16[972,128]{1,0:T(8,128)(2,1)S(1)}, u32[]{:S(2)}, u32[]{:S(2)}) collective-permute-start(bf16[972,128]{1,0:T(8,128)(2,1)S(1)} %total.6.refs_0_), channel_id=1, source_target_pairs={{0,1},{1,0},{2,3},{3,2},{4,5},{5,4},{6,7},{7,6},{8,9},{9,8},{10,11... | collective-permute-start | bytes 746504 | tf_op jit(solution)/shard_map/ppermute | solution.py:399
  56.4 8.9 %collective-permute-start.13 = (bf16[972,128]{1,0:T(8,128)(2,1)S(1)}, bf16[972,128]{1,0:T(8,128)(2,1)S(1)}, u32[]{:S(2)}, u32[]{:S(2)}) collective-permute-start(bf16[972,128]{1,0:T(8,128)(2,1)S(1)} %follow.2), channel_id=1, source_target_pairs={{0,8},{1,9},{2,10},{3,11},{4,12},{5,13},{6,14},{7,15},{8,0},{9,1},... | collective-permute-start | bytes 746504 | tf_op jit(solution)/shard_map/ppermute | solution.py:399
  58.2 9.1 %collective-permute-start.20 = (bf16[972,128]{1,0:T(8,128)(2,1)S(1)}, bf16[972,128]{1,0:T(8,128)(2,1)S(1)}, u32[]{:S(2)}, u32[]{:S(2)}) collective-permute-start(bf16[972,128]{1,0:T(8,128)(2,1)S(1)} %follow.3.refs_4_), channel_id=1, source_target_pairs={{0,1},{1,0},{2,3},{3,2},{4,5},{5,4},{6,7},{7,6},{8,9},{9,8},{10,11... | collective-permute-start | bytes 746504 | tf_op jit(solution)/shard_map/ppermute | solution.py:399
  59.4 13.2 %collective-permute-start.17 = (bf16[972,128]{1,0:T(8,128)(2,1)S(1)}, bf16[972,128]{1,0:T(8,128)(2,1)S(1)}, u32[]{:S(2)}, u32[]{:S(2)}) collective-permute-start(bf16[972,128]{1,0:T(8,128)(2,1)S(1)} %collective-permute-done.12.after.refs_2_), channel_id=1, source_target_pairs={{0,1},{1,0},{2,3},{3,2},{4,5},{5,4},{6,7},{7,6},{8,9},{9,8},{10,11... | collective-permute-start | bytes 746504 | tf_op jit(solution)/shard_map/ppermute | solution.py:399
  65.3 10.3 %collective-permute-start.14 = (bf16[972,128]{1,0:T(8,128)(2,1)S(1)}, bf16[972,128]{1,0:T(8,128)(2,1)S(1)}, u32[]{:S(2)}, u32[]{:S(2)}) collective-permute-start(bf16[972,128]{1,0:T(8,128)(2,1)S(1)} %collective-permute-done.13.refs_0_), channel_id=1, source_target_pairs={{0,1},{1,0},{2,3},{3,2},{4,5},{5,4},{6,7},{7,6},{8,9},{9,8},{10,11... | collective-permute-start | bytes 746504 | tf_op jit(solution)/shard_map/ppermute | solution.py:399

commit v11 on v9

--- a/solution.py
+++ b/solution.py
@@ -15,6 +15,7 @@
 LANES = 128
 MIB = 1 << 20
 CUT_MIB = 50
+FIRST = (0, 2, 1, 3)
 OUT_ROWS = 2048
 
 smoothing = 1.0
@@ -186,7 +187,8 @@
 
 
 def column_kernel(rows_y, patch_in, *refs):
-    weight, turned = refs[:rows_y], refs[rows_y : 2 * rows_y]
+    weight = [refs[p] for p in FIRST]
+    turned = [refs[rows_y + p] for p in FIRST]
     pe, mr, res, sq, inv = refs[2 * rows_y :]
     inner, count = patch_in.shape
     tile = weight[0].shape[1]
@@ -243,7 +245,7 @@
         ],
         compiler_params=params(40),
         name="column",
-    )(patch, *weight, *turned)
+    )(patch, *[weight[p] for p in FIRST], *[turned[p] for p in FIRST])
 
 
 def padded(rows):
@@ -406,15 +408,14 @@
     own = blocks(weights, rows_y, dps, (token,))
     below = send(below, lambda t, y, k, d: (t - 1, y, d, k))
 
-    weight, turned = [], []
-    for s in range(rows_y):
+    pairs = {}
+    for s in FIRST:
         block = own[s]
         if s:
             block = send(block, lambda t, y, k, d: (t, y - s, k, d))
         other = send(block, lambda t, y, k, d: (t, y, 1 - k, d))
-        pair = filters(block, other)
-        weight.append(pair[0])
-        turned.append(pair[1])
+        pairs[s] = filters(block, other)
+    weight, turned = zip(*(pairs[s] for s in range(rows_y)))
     above_in = send(above, lambda t, y, k, d: (t, y, d, k) if k != d else None)
 
     pe, mr = column(join(above, above_in, below), weight, turned)

time: 76.6 us -> 76.8 us (level)
  starting transfers between devices: 22.7 us -> 25.4 us
  waiting for transfers between devices: 35.2 us -> 32.7 us
    ppermute x21, starting transfers between devices: 22.7 us -> 25.4 us  [send(): return lax.ppermute(x, AXES, table(mesh_shape, move))]
    ppermute x21, waiting for transfers between devices: 35.2 us -> 32.7 us  [send(): return lax.ppermute(x, AXES, table(mesh_shape, move))]
  transfers between devices with their start and end apart: 21 -> 21, of which waited for: 12 -> 13; matrix products, arithmetic and copies ran while one was open for 0% -> 0% of each run, Pallas kernels for 8% -> 8%
where the time goes in v11:
time: 76.8 us; the launch traced here: 76.6 us
  waiting for transfers between devices  32.7 us (43%)
  starting transfers between devices  25.4 us (33%)
  Pallas kernels  16.8 us (22%)
  between operations  0.98 us (1%)
    ppermute x21, waiting for transfers between devices, send(): return lax.ppermute(x, AXES, table(mesh_shape, move))  32.7 us
    ppermute x21, starting transfers between devices, send(): return lax.ppermute(x, AXES, table(mesh_shape, move))  25.4 us
    pallas_call x2, Pallas kernels, cut(): pl.pallas_call(functools.partial(cut_kernel, above), out_shape=[jax.Shape...  4.65 us
    pallas_call x1, Pallas kernels, column(): pl.pallas_call(functools.partial(column_kernel, rows_y), out_shape=[jax.S...  4.09 us
    pallas_call x1, Pallas kernels, finish(): pl.pallas_call(functools.partial(finish_kernel, rows_y, dps, shifts), out...  2.5 us
    pallas_call x4, Pallas kernels, piece(): pl.pallas_call(functools.partial(piece_kernel, shifts, 1.0 / depth), out_...  2.44 us
  transfers between devices with their start and end apart: 21, of which 13 were waited for; matrix products, arithmetic and copies ran while one was open for 0% of the time, Pallas kernels for 8%

profile of v11, /device:TPU:4, one launch (start us, length us, event | category | flops | bytes accessed | tf_op | source)
XLA Modules:
  0.0 76.6 jit_solution(519748509114125027)
XLA Ops:
  0.6 3.8 %collective-permute-start.1 = (s32[2,8]{1,0:T(2,128)}, s32[2,8]{1,0:T(2,128)S(1)}, u32[]{:S(2)}, u32[]{:S(2)}) collective-permute-start(s32[2,8]{1,0:T(2,128)} %bitcast.12), channel_id=1, source_target_pairs={{0,16},{1,17},{2,18},{3,19},{4,20},{5,21},{6,22},{7,23},{8,24},{9,... | collective-permute-start | bytes 200 | tf_op jit(solution)/shard_map/ppermute | solution.py:401
  4.5 0.7 copy-done.1
  5.2 2.3 %cut_above.1 = (bf16[972,384]{1,0:T(8,128)(2,1)S(1)}, f32[8,128]{1,0:T(8,128)S(1)}) custom-call(s32[2,8]{1,0:T(2,128)S(1)} %bitcast.13, bf16[3,20,128,384]{3,2,1,0:T(8,128)(2,1)} %frames.3), custom_call_target="tpu_custom_call" | custom-call | tf_op jit(solution)/shard_map/cut_above/pallas_call | solution.py:96
  7.5 2.6 %collective-permute-done.1.places = s32[2,8]{1,0:T(2,128)S(1)} collective-permute-done((s32[2,8]{1,0:T(2,128)}, s32[2,8]{1,0:T(2,128)S(1)}, u32[]{:S(2)}, u32[]{:S(2)}) %collective-permute-start.1) | collective-permute-done | bytes 96 | tf_op jit(solution)/shard_map/ppermute | solution.py:401
  10.1 2.3 %cut_below.1 = (bf16[972,384]{1,0:T(8,128)(2,1)S(1)}, f32[8,128]{1,0:T(8,128)S(1)}) custom-call(s32[2,8]{1,0:T(2,128)S(1)} %collective-permute-done.1.places, bf16[3,20,128,384]{3,2,1,0:T(8,128)(2,1)} %frames.3, f32[8,128]{1,0:T(8,128)S(1)} %get-tuple-element.31.refs_0_), custom_call_target="tpu_custom_call" | custom-call | tf_op jit(solution)/shard_map/cut_below/pallas_call | solution.py:96
  12.5 0.8 %blocks.1 = (bf16[972,128]{1,0:T(8,128)(2,1)S(1)}, bf16[972,128]{1,0:T(8,128)(2,1)S(1)}, bf16[972,128]{1,0:T(8,128)(2,1)S(1)}, bf16[972,128]{1,0:T(8,128)(2,1)S(1)}) custom-call(bf16[7776,128]{1,0:T(8,128)(2,1)S(1)} %bitcast.10, f32[8,128]{1,0:T(8,128)S(1)} %get-tuple-element.33.refs_0_), custom_call_target="tpu_custom_call" | custom-call | tf_op jit(solution)/shard_map/blocks/pallas_call | solution.py:128
  13.2 3.3 %collective-permute-start.4 = (bf16[972,128]{1,0:T(8,128)(2,1)S(1)}, bf16[972,128]{1,0:T(8,128)(2,1)S(1)}, u32[]{:S(2)}, u32[]{:S(2)}) collective-permute-start(bf16[972,128]{1,0:T(8,128)(2,1)S(1)} %get-tuple-element.36), channel_id=1, source_target_pairs={{0,8},{1,9},{2,10},{3,11},{4,12},{5,13},{6,14},{7,15},{8,0},{9,1},... | collective-permute-start | bytes 746504 | tf_op jit(solution)/shard_map/ppermute | solution.py:401
  16.5 0.7 collective-permute-start
  17.2 3.9 %collective-permute-start.2 = (bf16[972,384]{1,0:T(8,128)(2,1)S(1)}, bf16[972,384]{1,0:T(8,128)(2,1)S(1)}, u32[]{:S(2)}, u32[]{:S(2)}) collective-permute-start(bf16[972,384]{1,0:T(8,128)(2,1)S(1)} %get-tuple-element.32), channel_id=1, source_target_pairs={{16,0},{17,2},{18,1},{19,3},{20,4},{21,6},{22,5},{23,7},{24,8},{25... | collective-permute-start | bytes 2239496 | tf_op jit(solution)/shard_map/ppermute | solution.py:401
  21.2 0.7 collective-permute-start.8
  21.9 2.6 %collective-permute-start.6 = (bf16[972,128]{1,0:T(8,128)(2,1)S(1)}, bf16[972,128]{1,0:T(8,128)(2,1)S(1)}, u32[]{:S(2)}, u32[]{:S(2)}) collective-permute-start(bf16[972,128]{1,0:T(8,128)(2,1)S(1)} %get-tuple-element.38), channel_id=1, source_target_pairs={{0,12},{1,13},{2,14},{3,15},{4,0},{5,1},{6,2},{7,3},{8,4},{9,5},{1... | collective-permute-start | bytes 746504 | tf_op jit(solution)/shard_map/ppermute | solution.py:401
  24.5 0.8 %collective-permute-start.3 = (bf16[972,128]{1,0:T(8,128)(2,1)S(1)}, bf16[972,128]{1,0:T(8,128)(2,1)S(1)}, u32[]{:S(2)}, u32[]{:S(2)}) collective-permute-start(bf16[972,128]{1,0:T(8,128)(2,1)S(1)} %get-tuple-element.34.own), channel_id=1, source_target_pairs={{0,2},{1,3},{2,0},{3,1},{4,6},{5,7},{6,4},{7,5},{8,10},{9,11},{10,... | collective-permute-start | bytes 746504 | tf_op jit(solution)/shard_map/ppermute | solution.py:401
  25.3 5.7 %collective-permute-done.8.own = bf16[972,128]{1,0:T(8,128)(2,1)S(1)} collective-permute-done((bf16[972,128]{1,0:T(8,128)(2,1)S(1)}, bf16[972,128]{1,0:T(8,128)(2,1)S(1)}, u32[]{:S(2)}, u32[]{:S(2)}) %collective-permute-start.8) | collective-permute-done | bytes 248864 | tf_op jit(solution)/shard_map/ppermute | solution.py:401
  31.0 0.2 collective-permute-start.9
  31.2 0.3 collective-permute-start.7
  31.5 0.2 collective-permute-start.5
  31.7 0.2 filters.4
  32.0 0.6 collective-permute-done.9.other
  32.5 0.2 filters.7
  32.8 0.1 collective-permute-done.7.other
  32.9 0.2 filters.6
  33.1 0.1 collective-permute-done.5.other
  33.2 0.2 filters.5
  33.5 4.1 %collective-permute-done.2.below = bf16[972,384]{1,0:T(8,128)(2,1)S(1)} collective-permute-done((bf16[972,384]{1,0:T(8,128)(2,1)S(1)}, bf16[972,384]{1,0:T(8,128)(2,1)S(1)}, u32[]{:S(2)}, u32[]{:S(2)}) %collective-permute-start.2) | collective-permute-done | bytes 746528 | tf_op jit(solution)/shard_map/ppermute | solution.py:401
  37.6 0.3 join.1.patch_in
  37.9 4.1 %column.1 = (bf16[972,768]{1,0:T(8,128)(2,1)S(1)}, bf16[1024,768]{1,0:T(8,128)(2,1)S(1)}) custom-call(bf16[972,384]{1,0:T(8,128)(2,1)S(1)} %join.1.patch_in, bf16[972,256]{1,0:T(8,128)(2,1)S(1)} %get-tuple-element.35.refs_0_, bf16[972,256]{1,0:T(8,128)(2,1)S(1)} %get-tuple-element.37.refs_1_, bf16[972,256]{1,0:T(8,128)(2,1)S(1)} %get-tuple-element.39.refs_2_, ...), custom_call_target="tpu_custom_call" | custom-call | tf_op jit(solution)/shard_map/column/pallas_call | solution.py:233
  42.0 0.6 piece.5
  42.6 0.9 %collective-permute-start.11 = (bf16[976,128]{1,0:T(8,128)(2,1)S(1)}, bf16[976,128]{1,0:T(8,128)(2,1)S(1)}, u32[]{:S(2)}, u32[]{:S(2)}) collective-permute-start(bf16[976,128]{1,0:T(8,128)(2,1)S(1)} %get-tuple-element.51), channel_id=1, source_target_pairs={{0,2},{1,3},{2,0},{3,1},{4,6},{5,7},{6,4},{7,5},{8,10},{9,11},{10,... | collective-permute-start | bytes 749576 | tf_op jit(solution)/shard_map/ppermute | solution.py:401
  43.5 0.6 piece.7
  44.2 0.6 piece.6
  44.8 0.6 collective-permute-start.15
  45.4 0.6 piece.4
  46.2 2.4 %collective-permute-start.12 = (bf16[972,128]{1,0:T(8,128)(2,1)S(1)}, bf16[972,128]{1,0:T(8,128)(2,1)S(1)}, u32[]{:S(2)}, u32[]{:S(2)}) collective-permute-start(bf16[972,128]{1,0:T(8,128)(2,1)S(1)} %total.5.refs_0_), channel_id=1, source_target_pairs={{0,1},{1,0},{2,3},{3,2},{4,5},{5,4},{6,7},{7,6},{8,9},{9,8},{10,11... | collective-permute-start | bytes 746504 | tf_op jit(solution)/shard_map/ppermute | solution.py:401
  48.7 1.1 %collective-permute-start.19 = (bf16[972,128]{1,0:T(8,128)(2,1)S(1)}, bf16[972,128]{1,0:T(8,128)(2,1)S(1)}, u32[]{:S(2)}, u32[]{:S(2)}) collective-permute-start(bf16[972,128]{1,0:T(8,128)(2,1)S(1)} %total.7), channel_id=1, source_target_pairs={{0,12},{1,13},{2,14},{3,15},{4,0},{5,1},{6,2},{7,3},{8,4},{9,5},{1... | collective-permute-start | bytes 746504 | tf_op jit(solution)/shard_map/ppermute | solution.py:401
  49.8 1.1 %collective-permute-start.16 = (bf16[972,128]{1,0:T(8,128)(2,1)S(1)}, bf16[972,128]{1,0:T(8,128)(2,1)S(1)}, u32[]{:S(2)}, u32[]{:S(2)}) collective-permute-start(bf16[972,128]{1,0:T(8,128)(2,1)S(1)} %total.6), channel_id=1, source_target_pairs={{0,4},{1,5},{2,6},{3,7},{4,8},{5,9},{6,10},{7,11},{8,12},{9,13},{1... | collective-permute-start | bytes 746504 | tf_op jit(solution)/shard_map/ppermute | solution.py:401
  51.0 3.9 %collective-permute-done.12.after.refs_1_ = bf16[972,128]{1,0:T(8,128)(2,1)S(1)} collective-permute-done((bf16[972,128]{1,0:T(8,128)(2,1)S(1)}, bf16[972,128]{1,0:T(8,128)(2,1)S(1)}, u32[]{:S(2)}, u32[]{:S(2)}) %collective-permute-start.12) | collective-permute-done | bytes 248864 | tf_op jit(solution)/shard_map/ppermute | solution.py:401
  54.8 0.4 collective-permute-start.13
  55.2 1.2 %collective-permute-done.19.refs_4_ = bf16[972,128]{1,0:T(8,128)(2,1)S(1)} collective-permute-done((bf16[972,128]{1,0:T(8,128)(2,1)S(1)}, bf16[972,128]{1,0:T(8,128)(2,1)S(1)}, u32[]{:S(2)}, u32[]{:S(2)}) %collective-permute-start.19) | collective-permute-done | bytes 248864 | tf_op jit(solution)/shard_map/ppermute | solution.py:401
  56.4 0.6 collective-permute-start.20
  57.0 1.6 %collective-permute-done.16.refs_2_ = bf16[972,128]{1,0:T(8,128)(2,1)S(1)} collective-permute-done((bf16[972,128]{1,0:T(8,128)(2,1)S(1)}, bf16[972,128]{1,0:T(8,128)(2,1)S(1)}, u32[]{:S(2)}, u32[]{:S(2)}) %collective-permute-start.16) | collective-permute-done | bytes 248864 | tf_op jit(solution)/shard_map/ppermute | solution.py:401
  58.5 0.3 collective-permute-start.17
  58.8 5.1 %collective-permute-done.13.refs_0_ = bf16[972,128]{1,0:T(8,128)(2,1)S(1)} collective-permute-done((bf16[972,128]{1,0:T(8,128)(2,1)S(1)}, bf16[972,128]{1,0:T(8,128)(2,1)S(1)}, u32[]{:S(2)}, u32[]{:S(2)}) %collective-permute-start.13) | collective-permute-done | bytes 248864 | tf_op jit(solution)/shard_map/ppermute | solution.py:401
  63.9 1.4 %collective-permute-start.14 = (bf16[972,128]{1,0:T(8,128)(2,1)S(1)}, bf16[972,128]{1,0:T(8,128)(2,1)S(1)}, u32[]{:S(2)}, u32[]{:S(2)}) collective-permute-start(bf16[972,128]{1,0:T(8,128)(2,1)S(1)} %collective-permute-done.13.refs_0_), channel_id=1, source_target_pairs={{0,1},{1,0},{2,3},{3,2},{4,5},{5,4},{6,7},{7,6},{8,9},{9,8},{10,11... | collective-permute-start | bytes 746504 | tf_op jit(solution)/shard_map/ppermute | solution.py:401
  65.3 0.1 collective-permute-done.20.refs_5_
  65.4 5.4 %collective-permute-done.17.refs_3_ = bf16[972,128]{1,0:T(8,128)(2,1)S(1)} collective-permute-done((bf16[972,128]{1,0:T(8,128)(2,1)S(1)}, bf16[972,128]{1,0:T(8,128)(2,1)S(1)}, u32[]{:S(2)}, u32[]{:S(2)}) %collective-permute-start.17) | collective-permute-done | bytes 248864 | tf_op jit(solution)/shard_map/ppermute | solution.py:401
  70.8 0.8 %gather.1.refs_3_ = f32[7776,128]{1,0:T(8,128)S(1)} custom-call(bf16[972,128]{1,0:T(8,128)(2,1)S(1)} %total.5.refs_0_, bf16[972,128]{1,0:T(8,128)(2,1)S(1)} %collective-permute-done.12.after.refs_1_, bf16[972,128]{1,0:T(8,128)(2,1)S(1)} %collective-permute-done.16.refs_2_, bf16[972,128]{1,0:T(8,128)(2,1)S(1)} %collective-permute-done.17.refs_3_, ...), custom_call_target="tpu_custom_call" | custom-call | tf_op jit(solution)/shard_map/gather/pallas_call | solution.py:341
  71.6 2.4 %collective-permute-done.14.refs_1_ = bf16[972,128]{1,0:T(8,128)(2,1)S(1)} collective-permute-done((bf16[972,128]{1,0:T(8,128)(2,1)S(1)}, bf16[972,128]{1,0:T(8,128)(2,1)S(1)}, u32[]{:S(2)}, u32[]{:S(2)}) %collective-permute-start.14) | collective-permute-done | bytes 248864 | tf_op jit(solution)/shard_map/ppermute | solution.py:401
  73.9 2.5 %finish.1 = (f32[3888,128]{1,0:T(8,128)}, bf16[7776,128]{1,0:T(8,128)(2,1)}) custom-call(bf16[972,128]{1,0:T(8,128)(2,1)S(1)} %collective-permute-done.13.refs_0_, bf16[972,128]{1,0:T(8,128)(2,1)S(1)} %collective-permute-done.14.refs_1_, bf16[7776,128]{1,0:T(8,128)(2,1)S(1)} %bitcast.11, f32[7776,128]{1,0:T(8,128)S(1)} %gather.1.refs_3_), custom_call_target="tpu_custom_call" | custom-call | tf_op jit(solution)/shard_map/finish/pallas_call | solution.py:377
  (18 shorter events, 0.5 us)
Async XLA Ops:
  0.6 9.5 %collective-permute-start.1 = (s32[2,8]{1,0:T(2,128)}, s32[2,8]{1,0:T(2,128)S(1)}, u32[]{:S(2)}, u32[]{:S(2)}) collective-permute-start(s32[2,8]{1,0:T(2,128)} %bitcast.12), channel_id=1, source_target_pairs={{0,16},{1,17},{2,18},{3,19},{4,20},{5,21},{6,22},{7,23},{8,24},{9,... | collective-permute-start | bytes 200 | tf_op jit(solution)/shard_map/ppermute | solution.py:401
  4.5 0.7 copy-start.1
  10.1 2.4 %copy-start = (bf16[8,972,128]{2,0,1:T(8,128)(2,1)S(1)}, bf16[8,972,128]{2,0,1:T(8,128)(2,1)}, u32[]{:S(2)}) copy-start(bf16[8,972,128]{2,0,1:T(8,128)(2,1)} %param.4) | copy-start | bytes 5971972
  13.2 11.2 %collective-permute-start.4 = (bf16[972,128]{1,0:T(8,128)(2,1)S(1)}, bf16[972,128]{1,0:T(8,128)(2,1)S(1)}, u32[]{:S(2)}, u32[]{:S(2)}) collective-permute-start(bf16[972,128]{1,0:T(8,128)(2,1)S(1)} %get-tuple-element.36), channel_id=1, source_target_pairs={{0,8},{1,9},{2,10},{3,11},{4,12},{5,13},{6,14},{7,15},{8,0},{9,1},... | collective-permute-start | bytes 746504 | tf_op jit(solution)/shard_map/ppermute | solution.py:401
  16.5 17.0 %collective-permute-start = (bf16[972,384]{1,0:T(8,128)(2,1)S(1)}, bf16[972,384]{1,0:T(8,128)(2,1)S(1)}, u32[]{:S(2)}, u32[]{:S(2)}) collective-permute-start(bf16[972,384]{1,0:T(8,128)(2,1)S(1)} %get-tuple-element.30.above), channel_id=1, source_target_pairs={{1,2},{2,1},{5,6},{6,5},{9,10},{10,9},{13,14},{14,13},{17,18},{18,... | collective-permute-start | bytes 2239496 | tf_op jit(solution)/shard_map/ppermute | solution.py:401
  17.2 20.4 %collective-permute-start.2 = (bf16[972,384]{1,0:T(8,128)(2,1)S(1)}, bf16[972,384]{1,0:T(8,128)(2,1)S(1)}, u32[]{:S(2)}, u32[]{:S(2)}) collective-permute-start(bf16[972,384]{1,0:T(8,128)(2,1)S(1)} %get-tuple-element.32), channel_id=1, source_target_pairs={{16,0},{17,2},{18,1},{19,3},{20,4},{21,6},{22,5},{23,7},{24,8},{25... | collective-permute-start | bytes 2239496 | tf_op jit(solution)/shard_map/ppermute | solution.py:401
  21.2 9.8 %collective-permute-start.8 = (bf16[972,128]{1,0:T(8,128)(2,1)S(1)}, bf16[972,128]{1,0:T(8,128)(2,1)S(1)}, u32[]{:S(2)}, u32[]{:S(2)}) collective-permute-start(bf16[972,128]{1,0:T(8,128)(2,1)S(1)} %get-tuple-element.40), channel_id=1, source_target_pairs={{0,4},{1,5},{2,6},{3,7},{4,8},{5,9},{6,10},{7,11},{8,12},{9,13},{1... | collective-permute-start | bytes 746504 | tf_op jit(solution)/shard_map/ppermute | solution.py:401
  21.9 9.3 %collective-permute-start.6 = (bf16[972,128]{1,0:T(8,128)(2,1)S(1)}, bf16[972,128]{1,0:T(8,128)(2,1)S(1)}, u32[]{:S(2)}, u32[]{:S(2)}) collective-permute-start(bf16[972,128]{1,0:T(8,128)(2,1)S(1)} %get-tuple-element.38), channel_id=1, source_target_pairs={{0,12},{1,13},{2,14},{3,15},{4,0},{5,1},{6,2},{7,3},{8,4},{9,5},{1... | collective-permute-start | bytes 746504 | tf_op jit(solution)/shard_map/ppermute | solution.py:401
  24.5 7.0 %collective-permute-start.3 = (bf16[972,128]{1,0:T(8,128)(2,1)S(1)}, bf16[972,128]{1,0:T(8,128)(2,1)S(1)}, u32[]{:S(2)}, u32[]{:S(2)}) collective-permute-start(bf16[972,128]{1,0:T(8,128)(2,1)S(1)} %get-tuple-element.34.own), channel_id=1, source_target_pairs={{0,2},{1,3},{2,0},{3,1},{4,6},{5,7},{6,4},{7,5},{8,10},{9,11},{10,... | collective-permute-start | bytes 746504 | tf_op jit(solution)/shard_map/ppermute | solution.py:401
  31.0 1.5 %collective-permute-start.9 = (bf16[972,128]{1,0:T(8,128)(2,1)S(1)}, bf16[972,128]{1,0:T(8,128)(2,1)S(1)}, u32[]{:S(2)}, u32[]{:S(2)}) collective-permute-start(bf16[972,128]{1,0:T(8,128)(2,1)S(1)} %collective-permute-done.8.own), channel_id=1, source_target_pairs={{0,2},{1,3},{2,0},{3,1},{4,6},{5,7},{6,4},{7,5},{8,10},{9,11},{10,... | collective-permute-start | bytes 746504 | tf_op jit(solution)/shard_map/ppermute | solution.py:401
  31.2 1.7 %collective-permute-start.7 = (bf16[972,128]{1,0:T(8,128)(2,1)S(1)}, bf16[972,128]{1,0:T(8,128)(2,1)S(1)}, u32[]{:S(2)}, u32[]{:S(2)}) collective-permute-start(bf16[972,128]{1,0:T(8,128)(2,1)S(1)} %collective-permute-done.6.own), channel_id=1, source_target_pairs={{0,2},{1,3},{2,0},{3,1},{4,6},{5,7},{6,4},{7,5},{8,10},{9,11},{10,... | collective-permute-start | bytes 746504 | tf_op jit(solution)/shard_map/ppermute | solution.py:401
  31.5 1.7 %collective-permute-start.5 = (bf16[972,128]{1,0:T(8,128)(2,1)S(1)}, bf16[972,128]{1,0:T(8,128)(2,1)S(1)}, u32[]{:S(2)}, u32[]{:S(2)}) collective-permute-start(bf16[972,128]{1,0:T(8,128)(2,1)S(1)} %collective-permute-done.4.own), channel_id=1, source_target_pairs={{0,2},{1,3},{2,0},{3,1},{4,6},{5,7},{6,4},{7,5},{8,10},{9,11},{10,... | collective-permute-start | bytes 746504 | tf_op jit(solution)/shard_map/ppermute | solution.py:401
  42.6 3.5 %collective-permute-start.11 = (bf16[976,128]{1,0:T(8,128)(2,1)S(1)}, bf16[976,128]{1,0:T(8,128)(2,1)S(1)}, u32[]{:S(2)}, u32[]{:S(2)}) collective-permute-start(bf16[976,128]{1,0:T(8,128)(2,1)S(1)} %get-tuple-element.51), channel_id=1, source_target_pairs={{0,2},{1,3},{2,0},{3,1},{4,6},{5,7},{6,4},{7,5},{8,10},{9,11},{10,... | collective-permute-start | bytes 749576 | tf_op jit(solution)/shard_map/ppermute | solution.py:401
  44.1 4.5 %collective-permute-start.18 = (bf16[976,128]{1,0:T(8,128)(2,1)S(1)}, bf16[976,128]{1,0:T(8,128)(2,1)S(1)}, u32[]{:S(2)}, u32[]{:S(2)}) collective-permute-start(bf16[976,128]{1,0:T(8,128)(2,1)S(1)} %get-tuple-element.55), channel_id=1, source_target_pairs={{0,2},{1,3},{2,0},{3,1},{4,6},{5,7},{6,4},{7,5},{8,10},{9,11},{10,... | collective-permute-start | bytes 749576 | tf_op jit(solution)/shard_map/ppermute | solution.py:401
  44.8 4.9 %collective-permute-start.15 = (bf16[976,128]{1,0:T(8,128)(2,1)S(1)}, bf16[976,128]{1,0:T(8,128)(2,1)S(1)}, u32[]{:S(2)}, u32[]{:S(2)}) collective-permute-start(bf16[976,128]{1,0:T(8,128)(2,1)S(1)} %get-tuple-element.53), channel_id=1, source_target_pairs={{0,2},{1,3},{2,0},{3,1},{4,6},{5,7},{6,4},{7,5},{8,10},{9,11},{10,... | collective-permute-start | bytes 749576 | tf_op jit(solution)/shard_map/ppermute | solution.py:401
  46.0 4.9 %collective-permute-start.10 = (bf16[976,128]{1,0:T(8,128)(2,1)S(1)}, bf16[976,128]{1,0:T(8,128)(2,1)S(1)}, u32[]{:S(2)}, u32[]{:S(2)}) collective-permute-start(bf16[976,128]{1,0:T(8,128)(2,1)S(1)} %get-tuple-element.49), channel_id=1, source_target_pairs={{0,2},{1,3},{2,0},{3,1},{4,6},{5,7},{6,4},{7,5},{8,10},{9,11},{10,... | collective-permute-start | bytes 749576 | tf_op jit(solution)/shard_map/ppermute | solution.py:401
  46.2 8.6 %collective-permute-start.12 = (bf16[972,128]{1,0:T(8,128)(2,1)S(1)}, bf16[972,128]{1,0:T(8,128)(2,1)S(1)}, u32[]{:S(2)}, u32[]{:S(2)}) collective-permute-start(bf16[972,128]{1,0:T(8,128)(2,1)S(1)} %total.5.refs_0_), channel_id=1, source_target_pairs={{0,1},{1,0},{2,3},{3,2},{4,5},{5,4},{6,7},{7,6},{8,9},{9,8},{10,11... | collective-permute-start | bytes 746504 | tf_op jit(solution)/shard_map/ppermute | solution.py:401
  48.7 7.8 %collective-permute-start.19 = (bf16[972,128]{1,0:T(8,128)(2,1)S(1)}, bf16[972,128]{1,0:T(8,128)(2,1)S(1)}, u32[]{:S(2)}, u32[]{:S(2)}) collective-permute-start(bf16[972,128]{1,0:T(8,128)(2,1)S(1)} %total.7), channel_id=1, source_target_pairs={{0,12},{1,13},{2,14},{3,15},{4,0},{5,1},{6,2},{7,3},{8,4},{9,5},{1... | collective-permute-start | bytes 746504 | tf_op jit(solution)/shard_map/ppermute | solution.py:401
  49.8 8.7 %collective-permute-start.16 = (bf16[972,128]{1,0:T(8,128)(2,1)S(1)}, bf16[972,128]{1,0:T(8,128)(2,1)S(1)}, u32[]{:S(2)}, u32[]{:S(2)}) collective-permute-start(bf16[972,128]{1,0:T(8,128)(2,1)S(1)} %total.6), channel_id=1, source_target_pairs={{0,4},{1,5},{2,6},{3,7},{4,8},{5,9},{6,10},{7,11},{8,12},{9,13},{1... | collective-permute-start | bytes 746504 | tf_op jit(solution)/shard_map/ppermute | solution.py:401
  54.8 9.1 %collective-permute-start.13 = (bf16[972,128]{1,0:T(8,128)(2,1)S(1)}, bf16[972,128]{1,0:T(8,128)(2,1)S(1)}, u32[]{:S(2)}, u32[]{:S(2)}) collective-permute-start(bf16[972,128]{1,0:T(8,128)(2,1)S(1)} %follow.1), channel_id=1, source_target_pairs={{0,8},{1,9},{2,10},{3,11},{4,12},{5,13},{6,14},{7,15},{8,0},{9,1},... | collective-permute-start | bytes 746504 | tf_op jit(solution)/shard_map/ppermute | solution.py:401
  56.4 9.0 %collective-permute-start.20 = (bf16[972,128]{1,0:T(8,128)(2,1)S(1)}, bf16[972,128]{1,0:T(8,128)(2,1)S(1)}, u32[]{:S(2)}, u32[]{:S(2)}) collective-permute-start(bf16[972,128]{1,0:T(8,128)(2,1)S(1)} %collective-permute-done.19.refs_4_), channel_id=1, source_target_pairs={{0,1},{1,0},{2,3},{3,2},{4,5},{5,4},{6,7},{7,6},{8,9},{9,8},{10,11... | collective-permute-start | bytes 746504 | tf_op jit(solution)/shard_map/ppermute | solution.py:401
  58.5 12.2 %collective-permute-start.17 = (bf16[972,128]{1,0:T(8,128)(2,1)S(1)}, bf16[972,128]{1,0:T(8,128)(2,1)S(1)}, u32[]{:S(2)}, u32[]{:S(2)}) collective-permute-start(bf16[972,128]{1,0:T(8,128)(2,1)S(1)} %collective-permute-done.16.refs_2_), channel_id=1, source_target_pairs={{0,1},{1,0},{2,3},{3,2},{4,5},{5,4},{6,7},{7,6},{8,9},{9,8},{10,11... | collective-permute-start | bytes 746504 | tf_op jit(solution)/shard_map/ppermute | solution.py:401
  63.9 10.0 %collective-permute-start.14 = (bf16[972,128]{1,0:T(8,128)(2,1)S(1)}, bf16[972,128]{1,0:T(8,128)(2,1)S(1)}, u32[]{:S(2)}, u32[]{:S(2)}) collective-permute-start(bf16[972,128]{1,0:T(8,128)(2,1)S(1)} %collective-permute-done.13.refs_0_), channel_id=1, source_target_pairs={{0,1},{1,0},{2,3},{3,2},{4,5},{5,4},{6,7},{7,6},{8,9},{9,8},{10,11... | collective-permute-start | bytes 746504 | tf_op jit(solution)/shard_map/ppermute | solution.py:401
